TPU v7x, 128 devices: a whole 4x4x4 slice. The times are simulated.
128 devices in a mesh: leaf: 64 (over z, x, y), rhs: 2 (over core).
Axes of the slice: x: 4, y: 4, z: 4, core: 2. Of those that a mesh axis runs over, the one named last changes fastest.
Arguments:
- points: float32 [3, 524288], P(None, 'leaf'), may hold values from -6 to 6
- values: float32 [64, 524288], P('rhs', 'leaf'), may hold values from -6 to 6
- near_list: int32 [4096, 27], P('leaf'), may hold values from 0 to 4095, as said below
- near_count: int32 [4096], P('leaf'), may hold values from 2 to 27, as said below
- basis: float32 [4096, 64, 128], P('leaf'), may hold values from -0.5 to 0.5
- transfer: float32 [8128, 64, 64], P('leaf'), may hold values from -0.75 to 0.75
- coupling: float32 [8128, 4, 64, 64], P('leaf'), may hold values from -1 to 1
- partners: int32 [8128, 4], P('leaf'), may hold values from 0 to 4095, as said below
- transfer_top: float32 [62, 64, 64], replicated, may hold values from -0.75 to 0.75
- coupling_top: float32 [60, 4, 64, 64], replicated, may hold values from -1 to 1
- partners_top: int32 [60, 4], replicated, may hold values from 0 to 31, as said below
Outputs:
- potential: float32 [64, 524288], P('rhs', 'leaf')
Inputs may be any that keep to these rules, and one draw needn't show every extreme that they name: near_list[i, 0] = i; near_list[i, 1] = i - 1 where i > 0 is the first leaf of its subtree, and i + 1 where i < 4095 is the last leaf of its subtree; every entry names a leaf at most 64 positions from i. `near_count`: some leaf has 27 live slots. `partners`: a partner lies on its cluster's level, differs from it, and is at most 64 >> l positions from it on level l. `partners_top`: a partner lies on its cluster's level and differs from it.
All inputs are finite; a program needn't handle non-finite values.
Results may differ from a plain program's by a relative error of at most 0.0003.
Values sent between devices are 32-bit elements; how exact they have to be, the bound alone decides.
No kernel may reach another device: no remote copies, remote signals or barrier semaphores. Data moves between devices by JAX's collectives and lax.ppermute only.
A program may use at most 256 MiB of HBM per device.

v0:
```python
import jax
import jax.numpy as jnp
from jax import lax
from jax.sharding import PartitionSpec as P

near_weight = 0.1
smoothing = 0.0025
highest = lax.Precision.HIGHEST


def padded(block, sides, width):
    for axis, dim in sides:
        count = lax.axis_size(axis)
        forward = [(i, i + 1) for i in range(count - 1)]
        backward = [(target, source) for source, target in forward]
        low = lax.ppermute(
            lax.slice_in_dim(block, block.shape[dim] - width, None, axis=dim), axis, forward
        )
        high = lax.ppermute(lax.slice_in_dim(block, 0, width, axis=dim), axis, backward)
        block = jnp.concatenate([low, block, high], axis=dim)
    return block


def block_kernel(targets, sources, counts):
    squared = jnp.zeros(
        (targets.shape[1], sources.shape[2], targets.shape[2], sources.shape[3]), jnp.float32
    )
    for comp_id in range(3):
        differ = targets[comp_id][:, None, :, None] - sources[comp_id][:, :, None, :]
        squared = squared + differ * differ
    kernel = near_weight / jnp.sqrt(squared + smoothing)
    live_mask = (jnp.arange(sources.shape[2])[None, :] < counts[:, None]).astype(jnp.float32)
    kernel = kernel * live_mask[:, :, None, None]
    return jnp.einsum("gsab,cgsb->cga", kernel, sources[3:], precision=highest)


def near_field(sources, targets, near_lists, counts):
    leaf_total = near_lists.shape[0]
    group_size = min(8, leaf_total)
    blocks = leaf_total // group_size
    leaf_size = targets.shape[2]

    def one_block(pieces):
        return block_kernel(pieces[0], jnp.take(sources, pieces[1], axis=1), pieces[2])

    result = lax.map(
        one_block,
        (
            targets.reshape(3, blocks, group_size, leaf_size).transpose(1, 0, 2, 3),
            near_lists.reshape(blocks, group_size, near_lists.shape[1]),
            counts.reshape(blocks, group_size),
        ),
    )
    return result.transpose(1, 0, 2, 3).reshape(result.shape[1], leaf_total * leaf_size)


def lift_up(matrices, coeffs):
    return jnp.einsum("nrq,nrc->nqc", matrices, coeffs, precision=highest)


def pair_sum(coeffs):
    return coeffs[0::2] + coeffs[1::2]


def push_down(matrices, parents):
    repeat_by = matrices.shape[0] // parents.shape[0]
    return jnp.einsum(
        "nrq,nqc->nrc", matrices, jnp.repeat(parents, repeat_by, axis=0), precision=highest
    )


def couple(matrices, indices, sources):
    result = jnp.zeros((indices.shape[0], sources.shape[1], sources.shape[2]), jnp.float32)
    for slot_id in range(indices.shape[1]):
        picked = jnp.take(sources, indices[:, slot_id], axis=0)
        result = result + jnp.einsum(
            "nrq,nqc->nrc", matrices[:, slot_id], picked, precision=highest
        )
    return result


def upper_tree(first, transfer_top, coupling_top, partners_top):
    levels = [first]
    matrices = []
    used_rows = 0
    while levels[-1].shape[0] > 1:
        level_width = levels[-1].shape[0]
        chosen = transfer_top[used_rows : used_rows + level_width]
        used_rows = used_rows + level_width
        matrices.append(chosen)
        levels.append(pair_sum(lift_up(chosen, levels[-1])))
    offsets = []
    taken_rows = 0
    for coeffs in levels:
        offsets.append(taken_rows)
        if coeffs.shape[0] >= 4:
            taken_rows = taken_rows + coeffs.shape[0]
    parents = jnp.zeros_like(levels[-1])
    for section_id in range(len(levels) - 2, -1, -1):
        parents = push_down(matrices[section_id], parents)
        level_width = levels[section_id].shape[0]
        if level_width >= 4:
            begin_row = offsets[section_id]
            parents = parents + couple(
                coupling_top[begin_row : begin_row + level_width],
                partners_top[begin_row : begin_row + level_width],
                levels[section_id],
            )
    return parents


def level_slice(array, leaf_dev, level_id):
    span_width = leaf_dev >> level_id
    begin_row = 2 * leaf_dev - 2 * span_width
    return array[begin_row : begin_row + span_width]


def local(
    points,
    values,
    near_list,
    near_count,
    basis,
    transfer,
    coupling,
    partners,
    transfer_top,
    coupling_top,
    partners_top,
):
    leaf_dev = basis.shape[0]
    leaf_size = basis.shape[2]
    columns = values.shape[0]
    tree_depth = leaf_dev.bit_length() - 1
    position = lax.axis_index("leaf")
    sources = jnp.concatenate([points, values], axis=0)
    extended = padded(sources, (("leaf", 1),), leaf_dev * leaf_size)
    extended = extended.reshape(extended.shape[0], 3 * leaf_dev, leaf_size)
    local_lists = near_list - (position * leaf_dev - leaf_dev)
    targets = points.reshape(3, leaf_dev, leaf_size)
    near_part = near_field(extended, targets, local_lists, near_count)
    coeffs = [
        jnp.einsum(
            "irb,cib->irc", basis, values.reshape(columns, leaf_dev, leaf_size), precision=highest
        )
    ]
    for level_id in range(tree_depth):
        coeffs.append(pair_sum(lift_up(level_slice(transfer, leaf_dev, level_id), coeffs[-1])))
    couplings = []
    for level_id in range(tree_depth + 1):
        span_width = leaf_dev >> level_id
        nearby = padded(coeffs[level_id], (("leaf", 0),), span_width)
        local_partners = level_slice(partners, leaf_dev, level_id) - (
            position * span_width - span_width
        )
        couplings.append(couple(level_slice(coupling, leaf_dev, level_id), local_partners, nearby))
    own_top = lift_up(level_slice(transfer, leaf_dev, tree_depth), coeffs[tree_depth])
    every_top = lax.all_gather(own_top, "leaf", axis=0, tiled=True)
    parents_all = upper_tree(pair_sum(every_top), transfer_top, coupling_top, partners_top)
    parents = lax.dynamic_slice_in_dim(parents_all, position // 2, 1, 0)
    for level_id in range(tree_depth, -1, -1):
        parents = (
            push_down(level_slice(transfer, leaf_dev, level_id), parents) + couplings[level_id]
        )
    far_part = jnp.einsum("irb,irc->cib", basis, parents, precision=highest).reshape(
        columns, leaf_dev * leaf_size
    )
    return near_part + far_part


def solution(mesh):
    placed = (
        P(None, "leaf"),
        P("rhs", "leaf"),
        P("leaf", None),
        P("leaf"),
        P("leaf", None, None),
        P("leaf", None, None),
        P("leaf", None, None, None),
        P("leaf", None),
        P(),
        P(),
        P(),
    )
    return jax.shard_map(
        local, mesh=mesh, in_specs=placed, out_specs=P("rhs", "leaf"), check_vma=False
    )
```

profile of v0, /device:TPU:0, one launch (start us, length us, event | category | flops | bytes accessed | tf_op | source)
XLA Modules:
  0.0 880.3 jit_solution(13365979181906678584)
XLA Ops:
  0.0 3.7 slice.494
  11.6 4.1 copy.249
  15.6 4.4 fusion.73
  45.3 4.2 collective-permute-start.2
  50.8 5.1 collective-permute-start.4
  57.2 5.5 collective-permute-start.6
  68.3 9.1 %fusion.365 = (f32[1,1,64,64]{0,3,2,1:T(8,128)}, f32[1,1,64,64]{0,3,2,1:T(8,128)}, f32[1,1,64,64]{0,3,2,1:T(8,128)}, f32[1,1,64,64]{0,3,2,1:T(8,128)}) fusion(f32[127,4,64,64]{0,3,2,1:T(8,128)} %param.41), kind=kLoop, calls=%fused_computation.594 | loop fusion | bytes 131072 | tf_op jit(solution)/shard_map/slice | solution.py:77
  77.5 9.2 %fusion.364 = (f32[2,1,64,64]{0,3,2,1:T(8,128)}, f32[2,1,64,64]{0,3,2,1:T(8,128)}, f32[2,1,64,64]{0,3,2,1:T(8,128)}, f32[2,1,64,64]{0,3,2,1:T(8,128)}) fusion(f32[127,4,64,64]{0,3,2,1:T(8,128)} %param.41), kind=kLoop, calls=%fused_computation.593 | loop fusion | bytes 262144 | tf_op jit(solution)/shard_map/slice | solution.py:77
  86.6 5.5 fusion.363
  92.1 5.5 fusion.362
  97.6 5.7 fusion.361
  103.4 8.9 %fusion.360 = (f32[32,1,64,64]{0,3,2,1:T(8,128)}, f32[32,1,64,64]{0,3,2,1:T(8,128)}, f32[32,1,64,64]{0,3,2,1:T(8,128)}, f32[32,1,64,64]{0,3,2,1:T(8,128)}) fusion(f32[127,4,64,64]{0,3,2,1:T(8,128)} %param.41), kind=kLoop, calls=%fused_computation.589 | loop fusion | bytes 4194304 | tf_op jit(solution)/shard_map/slice | solution.py:77
  112.3 7.6 fusion.359
  123.4 180.9 %all-gather.1 = f32[64,64,32]{1,2,0:T(8,128)S(1)} all-gather(f32[1,64,32]{1,2,0:T(8,128)S(1)} %convolution_bitcast_fusion.11), channel_id=2, replica_groups=mesh['leaf'=64,'rhs'=2] {'leaf'}, dimensions={0}, use_global_device_ids=true | all-gather | bytes 532480 | tf_op jit(solution)/shard_map/all_gather | solution.py:158
  454.9 3.8 copy.299
  458.8 3.8 copy.298
  462.6 3.8 copy.297
  466.4 3.9 copy.296
  473.6 5.2 collective-permute-start.8
  481.8 5.3 collective-permute-start.10
  497.0 5.4 collective-permute-start.12
  513.7 5.5 collective-permute-start.14
  535.2 5.6 collective-permute-start
  580.2 4.4 fusion.371
  584.6 3.9 pad_maximum_fusion.1
  588.5 3.6 gather_fusion.40
  594.8 6.6 fusion.34
  601.4 4.4 fusion.36
  612.1 5.5 fusion.38
  617.6 4.7 fusion.51
  627.7 4.0 copy.188
  631.7 244.7 %while.11 = (s32[]{:T(128)}, f32[8,32,8,128]{3,1,2,0:T(8,128)}, s32[8,8,27]{2,1,0:T(8,128)}, f32[35,192,128]{2,0,1:T(8,128)}, f32[8,3,8,128]{3,2,0,1:T(8,128)}, /*index=5*/s32[8,8]{1,0:T(8,128)}, s32[]{:T(128)}) while((s32[]{:T(128)}, f32[8,32,8,128]{3,1,2,0:T(8,128)}, s32[8,8,27]{2,1,0:T(8,128)}, f32[35,192,128]{2,0,1:T(8,128)}, ...), condition=%wide.region_1.2_spmd, body=%wide.region_0.1_spmd.sunk | while | flops 1395315072 | bytes 20950892 | solution.py:46
  632.5 5.0 gather_fusion
  642.6 19.7 %fusion.417 = f32[8,32,8,128]{3,1,2,0:T(8,128)} fusion(f32[8,32,8,128]{3,1,2,0:T(8,128)} %get-tuple-element.369, s32[]{:T(128)} %get-tuple-element.368, f32[8,27]{1,0:T(8,128)S(1)} %fusion.415, f32[8,27,128]{2,1,0:T(8,128)S(1)} %get-tuple-element.355, f32[8,128]{1,0:T(8,128)S(1)} %get-tuple-element.356, f32[8,27,128]{2,1,0:T(8,128)S(1)} %get-tuple-element.357, ...), kind=kOutput, calls=%fused_computation.64.clone.1 | convolution fusion | flops 1394343936 | bytes 4080128 | tf_op jit(solution)/shard_map/while/body/eval_jaxpr/gsab,cgsb->cga/dot_general | solution.py:34
  663.1 5.0 gather_fusion
  673.2 19.7 %fusion.417 = f32[8,32,8,128]{3,1,2,0:T(8,128)} fusion(f32[8,32,8,128]{3,1,2,0:T(8,128)} %get-tuple-element.369, s32[]{:T(128)} %get-tuple-element.368, f32[8,27]{1,0:T(8,128)S(1)} %fusion.415, f32[8,27,128]{2,1,0:T(8,128)S(1)} %get-tuple-element.355, f32[8,128]{1,0:T(8,128)S(1)} %get-tuple-element.356, f32[8,27,128]{2,1,0:T(8,128)S(1)} %get-tuple-element.357, ...), kind=kOutput, calls=%fused_computation.64.clone.1 | convolution fusion | flops 1394343936 | bytes 4080128 | tf_op jit(solution)/shard_map/while/body/eval_jaxpr/gsab,cgsb->cga/dot_general | solution.py:34
  693.6 5.0 gather_fusion
  703.8 19.7 %fusion.417 = f32[8,32,8,128]{3,1,2,0:T(8,128)} fusion(f32[8,32,8,128]{3,1,2,0:T(8,128)} %get-tuple-element.369, s32[]{:T(128)} %get-tuple-element.368, f32[8,27]{1,0:T(8,128)S(1)} %fusion.415, f32[8,27,128]{2,1,0:T(8,128)S(1)} %get-tuple-element.355, f32[8,128]{1,0:T(8,128)S(1)} %get-tuple-element.356, f32[8,27,128]{2,1,0:T(8,128)S(1)} %get-tuple-element.357, ...), kind=kOutput, calls=%fused_computation.64.clone.1 | convolution fusion | flops 1394343936 | bytes 4080128 | tf_op jit(solution)/shard_map/while/body/eval_jaxpr/gsab,cgsb->cga/dot_general | solution.py:34
  724.2 5.0 gather_fusion
  734.3 19.7 %fusion.417 = f32[8,32,8,128]{3,1,2,0:T(8,128)} fusion(f32[8,32,8,128]{3,1,2,0:T(8,128)} %get-tuple-element.369, s32[]{:T(128)} %get-tuple-element.368, f32[8,27]{1,0:T(8,128)S(1)} %fusion.415, f32[8,27,128]{2,1,0:T(8,128)S(1)} %get-tuple-element.355, f32[8,128]{1,0:T(8,128)S(1)} %get-tuple-element.356, f32[8,27,128]{2,1,0:T(8,128)S(1)} %get-tuple-element.357, ...), kind=kOutput, calls=%fused_computation.64.clone.1 | convolution fusion | flops 1394343936 | bytes 4080128 | tf_op jit(solution)/shard_map/while/body/eval_jaxpr/gsab,cgsb->cga/dot_general | solution.py:34
  754.8 5.0 gather_fusion
  764.9 19.7 %fusion.417 = f32[8,32,8,128]{3,1,2,0:T(8,128)} fusion(f32[8,32,8,128]{3,1,2,0:T(8,128)} %get-tuple-element.369, s32[]{:T(128)} %get-tuple-element.368, f32[8,27]{1,0:T(8,128)S(1)} %fusion.415, f32[8,27,128]{2,1,0:T(8,128)S(1)} %get-tuple-element.355, f32[8,128]{1,0:T(8,128)S(1)} %get-tuple-element.356, f32[8,27,128]{2,1,0:T(8,128)S(1)} %get-tuple-element.357, ...), kind=kOutput, calls=%fused_computation.64.clone.1 | convolution fusion | flops 1394343936 | bytes 4080128 | tf_op jit(solution)/shard_map/while/body/eval_jaxpr/gsab,cgsb->cga/dot_general | solution.py:34
  785.4 5.0 gather_fusion
  795.5 19.7 %fusion.417 = f32[8,32,8,128]{3,1,2,0:T(8,128)} fusion(f32[8,32,8,128]{3,1,2,0:T(8,128)} %get-tuple-element.369, s32[]{:T(128)} %get-tuple-element.368, f32[8,27]{1,0:T(8,128)S(1)} %fusion.415, f32[8,27,128]{2,1,0:T(8,128)S(1)} %get-tuple-element.355, f32[8,128]{1,0:T(8,128)S(1)} %get-tuple-element.356, f32[8,27,128]{2,1,0:T(8,128)S(1)} %get-tuple-element.357, ...), kind=kOutput, calls=%fused_computation.64.clone.1 | convolution fusion | flops 1394343936 | bytes 4080128 | tf_op jit(solution)/shard_map/while/body/eval_jaxpr/gsab,cgsb->cga/dot_general | solution.py:34
  816.0 5.0 gather_fusion
  826.1 19.7 %fusion.417 = f32[8,32,8,128]{3,1,2,0:T(8,128)} fusion(f32[8,32,8,128]{3,1,2,0:T(8,128)} %get-tuple-element.369, s32[]{:T(128)} %get-tuple-element.368, f32[8,27]{1,0:T(8,128)S(1)} %fusion.415, f32[8,27,128]{2,1,0:T(8,128)S(1)} %get-tuple-element.355, f32[8,128]{1,0:T(8,128)S(1)} %get-tuple-element.356, f32[8,27,128]{2,1,0:T(8,128)S(1)} %get-tuple-element.357, ...), kind=kOutput, calls=%fused_computation.64.clone.1 | convolution fusion | flops 1394343936 | bytes 4080128 | tf_op jit(solution)/shard_map/while/body/eval_jaxpr/gsab,cgsb->cga/dot_general | solution.py:34
  846.6 5.0 gather_fusion
  856.7 19.7 %fusion.417 = f32[8,32,8,128]{3,1,2,0:T(8,128)} fusion(f32[8,32,8,128]{3,1,2,0:T(8,128)} %get-tuple-element.369, s32[]{:T(128)} %get-tuple-element.368, f32[8,27]{1,0:T(8,128)S(1)} %fusion.415, f32[8,27,128]{2,1,0:T(8,128)S(1)} %get-tuple-element.355, f32[8,128]{1,0:T(8,128)S(1)} %get-tuple-element.356, f32[8,27,128]{2,1,0:T(8,128)S(1)} %get-tuple-element.357, ...), kind=kOutput, calls=%fused_computation.64.clone.1 | convolution fusion | flops 1394343936 | bytes 4080128 | tf_op jit(solution)/shard_map/while/body/eval_jaxpr/gsab,cgsb->cga/dot_general | solution.py:34
  (506 shorter events, 333.7 us)
Async XLA Ops:
  0.0 15.6 %copy-start = (f32[64,64,128]{2,1,0:T(8,128)S(1)}, f32[64,64,128]{2,1,0:T(8,128)}, u32[]{:S(2)}) copy-start(f32[64,64,128]{2,1,0:T(8,128)} %param.39) | copy-start | bytes 6291460
  37.0 7.3 copy-start.24
  40.3 26.0 %copy-start.35 = (f32[4,64,64]{2,1,0:T(8,128)}, f32[4,64,64]{2,1,0:T(8,128)S(1)}, u32[]{:S(2)}) copy-start(f32[4,64,64]{2,1,0:T(8,128)S(1)} %copy.253) | copy-start | bytes 196612
  44.3 21.9 %copy-start.42 = (f32[2,64,64]{2,1,0:T(8,128)}, f32[2,64,64]{2,1,0:T(8,128)S(1)}, u32[]{:S(2)}) copy-start(f32[2,64,64]{2,1,0:T(8,128)S(1)} %copy.254) | copy-start | bytes 98308
  45.3 427.0 %collective-permute-start.2 = (f32[1,64,32]{1,2,0:T(8,128)S(1)}, f32[1,64,32]{1,2,0:T(8,128)}, u32[]{:S(2)}, u32[]{:S(2)}) collective-permute-start(f32[1,64,32]{1,2,0:T(8,128)S(1)} %slice_add_fusion.9), channel_id=1, source_target_pairs={{0,2},{2,4},{4,6},{6,8},{8,10},{10,12},{12,14},{14,16},{16,18},{18... | collective-permute-start | bytes 24584 | tf_op jit(solution)/shard_map/ppermute | solution.py:16
  49.5 424.1 %collective-permute-start.3 = (f32[1,64,32]{1,2,0:T(8,128)S(1)}, f32[1,64,32]{1,2,0:T(8,128)}, u32[]{:S(2)}, u32[]{:S(2)}) collective-permute-start(f32[1,64,32]{1,2,0:T(8,128)S(1)} %slice_add_fusion.9), channel_id=1, source_target_pairs={{2,0},{4,2},{6,4},{8,6},{10,8},{12,10},{14,12},{16,14},{18,16},{20... | collective-permute-start | bytes 24584 | tf_op jit(solution)/shard_map/ppermute | solution.py:19
  50.8 429.8 %collective-permute-start.4 = (f32[2,64,32]{1,2,0:T(8,128)}, f32[2,64,32]{1,2,0:T(8,128)}, u32[]{:S(2)}, u32[]{:S(2)}) collective-permute-start(f32[2,64,32]{1,2,0:T(8,128)} %slice_add_fusion.8), channel_id=1, source_target_pairs={{0,2},{2,4},{4,6},{6,8},{8,10},{10,12},{12,14},{14,16},{16,18},{18... | collective-permute-start | bytes 49160 | tf_op jit(solution)/shard_map/ppermute | solution.py:16
  55.9 425.9 %collective-permute-start.5 = (f32[2,64,32]{1,2,0:T(8,128)}, f32[2,64,32]{1,2,0:T(8,128)}, u32[]{:S(2)}, u32[]{:S(2)}) collective-permute-start(f32[2,64,32]{1,2,0:T(8,128)} %slice_add_fusion.8), channel_id=1, source_target_pairs={{2,0},{4,2},{6,4},{8,6},{10,8},{12,10},{14,12},{16,14},{18,16},{20... | collective-permute-start | bytes 49160 | tf_op jit(solution)/shard_map/ppermute | solution.py:19
  57.2 438.5 %collective-permute-start.6 = (f32[4,64,32]{1,2,0:T(8,128)}, f32[4,64,32]{1,2,0:T(8,128)}, u32[]{:S(2)}, u32[]{:S(2)}) collective-permute-start(f32[4,64,32]{1,2,0:T(8,128)} %slice_add_fusion.7), channel_id=1, source_target_pairs={{0,2},{2,4},{4,6},{6,8},{8,10},{10,12},{12,14},{14,16},{16,18},{18... | collective-permute-start | bytes 98312 | tf_op jit(solution)/shard_map/ppermute | solution.py:16
  68.3 18.3 %slice-start = ((s8[8388608]{0:T(1024)(128)(4,1)}), s8[4194304]{0:T(1024)(128)(4,1)S(1)}, s32[]{:S(2)}) async-start(s8[8388608]{0:T(1024)(128)(4,1)} %bitcast.504), calls=%async_computation | async-start | bytes 8388608
  77.4 9.2 %slice-start.1 = ((s8[8388608]{0:T(1024)(128)(4,1)}), s8[4194304]{0:T(1024)(128)(4,1)S(1)}, s32[]{:S(2)}) async-start(s8[8388608]{0:T(1024)(128)(4,1)} %bitcast.504), calls=%async_computation.1 | async-start | bytes 8388608
  112.3 7.6 copy-start.47
  122.8 181.6 %copy-start.11 = (f32[62,64,64]{2,1,0:T(8,128)S(1)}, f32[62,64,64]{2,1,0:T(8,128)}, u32[]{:S(2)}) copy-start(f32[62,64,64]{2,1,0:T(8,128)} %param.43) | copy-start | bytes 3047428
  310.2 12.2 %copy-start.78 = (s32[16]{0:T(128)S(1)}, s32[16]{0:T(128)}, u32[]{:S(2)}) copy-start(s32[16]{0:T(128)} %get-tuple-element.269) | copy-start | bytes 196
  326.8 7.0 copy-start.73
  326.9 9.1 %copy-start.26 = (f32[16,64,32]{1,2,0:T(8,128)S(1)}, f32[16,64,32]{1,2,0:T(8,128)}, u32[]{:S(2)}) copy-start(f32[16,64,32]{1,2,0:T(8,128)} %gather_fusion.11) | copy-start | bytes 393220
  326.9 9.1 %copy-start.72 = (pred[16]{0:T(512)(128)(4,1)S(1)}, pred[16]{0:T(512)(128)(4,1)}, u32[]{:S(2)}) copy-start(pred[16]{0:T(512)(128)(4,1)} %get-tuple-element.264) | copy-start | bytes 52
  330.6 7.5 copy-start.71
  347.4 7.4 copy-start.51
  347.4 8.0 copy-start.32
  348.8 9.0 %copy-start.70 = (pred[32]{0:T(512)(128)(4,1)S(1)}, pred[32]{0:T(512)(128)(4,1)}, u32[]{:S(2)}) copy-start(pred[32]{0:T(512)(128)(4,1)} %get-tuple-element.248) | copy-start | bytes 100
  364.4 12.1 %copy-start.46 = (f32[1,64,64]{2,1,0:T(8,128)S(1)}, f32[1,64,64]{2,1,0:T(8,128)}, u32[]{:S(2)}) copy-start(f32[1,64,64]{2,1,0:T(8,128)} %copy-done.45) | copy-start | bytes 49156
  466.4 7.2 copy-start.40
  466.4 13.9 %copy-start.43 = (f32[2,64,64]{2,1,0:T(8,128)S(1)}, f32[2,64,64]{2,1,0:T(8,128)}, u32[]{:S(2)}) copy-start(f32[2,64,64]{2,1,0:T(8,128)} %copy-done.42) | copy-start | bytes 98308
  470.3 24.5 %copy-start.36 = (f32[4,64,64]{2,1,0:T(8,128)S(1)}, f32[4,64,64]{2,1,0:T(8,128)}, u32[]{:S(2)}) copy-start(f32[4,64,64]{2,1,0:T(8,128)} %copy-done.35) | copy-start | bytes 196612
  470.3 26.7 %copy-start.18 = (f32[32,64,32]{1,2,0:T(8,128)S(1)}, f32[32,64,32]{1,2,0:T(8,128)}, u32[]{:S(2)}) copy-start(f32[32,64,32]{1,2,0:T(8,128)} %slice_add_fusion.1) | copy-start | bytes 786436
  472.3 24.7 %collective-permute-start.7 = (f32[4,64,32]{1,2,0:T(8,128)}, f32[4,64,32]{1,2,0:T(8,128)}, u32[]{:S(2)}, u32[]{:S(2)}) collective-permute-start(f32[4,64,32]{1,2,0:T(8,128)} %slice_add_fusion.7), channel_id=1, source_target_pairs={{2,0},{4,2},{6,4},{8,6},{10,8},{12,10},{14,12},{16,14},{18,16},{20... | collective-permute-start | bytes 98312 | tf_op jit(solution)/shard_map/ppermute | solution.py:19
  473.6 38.8 %collective-permute-start.8 = (f32[8,64,32]{1,2,0:T(8,128)S(1)}, f32[8,64,32]{1,2,0:T(8,128)}, u32[]{:S(2)}, u32[]{:S(2)}) collective-permute-start(f32[8,64,32]{1,2,0:T(8,128)S(1)} %copy-done.40), channel_id=1, source_target_pairs={{0,2},{2,4},{4,6},{6,8},{8,10},{10,12},{12,14},{14,16},{16,18},{18... | collective-permute-start | bytes 196616 | tf_op jit(solution)/shard_map/ppermute | solution.py:16
  479.7 28.9 %copy-start.66 = (pred[4]{0:T(512)(128)(4,1)S(1)}, pred[4]{0:T(512)(128)(4,1)}, u32[]{:S(2)}) copy-start(pred[4]{0:T(512)(128)(4,1)} %get-tuple-element.230) | copy-start | bytes 16
  480.3 29.6 %copy-start.65 = (pred[4]{0:T(512)(128)(4,1)S(1)}, pred[4]{0:T(512)(128)(4,1)}, u32[]{:S(2)}) copy-start(pred[4]{0:T(512)(128)(4,1)} %get-tuple-element.122) | copy-start | bytes 16
  480.5 33.2 %collective-permute-start.9 = (f32[8,64,32]{1,2,0:T(8,128)S(1)}, f32[8,64,32]{1,2,0:T(8,128)}, u32[]{:S(2)}, u32[]{:S(2)}) collective-permute-start(f32[8,64,32]{1,2,0:T(8,128)S(1)} %copy-done.40), channel_id=1, source_target_pairs={{2,0},{4,2},{6,4},{8,6},{10,8},{12,10},{14,12},{16,14},{18,16},{20... | collective-permute-start | bytes 196616 | tf_op jit(solution)/shard_map/ppermute | solution.py:19
  481.8 52.0 %collective-permute-start.10 = (f32[16,64,32]{1,2,0:T(8,128)}, f32[16,64,32]{1,2,0:T(8,128)}, u32[]{:S(2)}, u32[]{:S(2)}) collective-permute-start(f32[16,64,32]{1,2,0:T(8,128)} %slice_add_fusion.3), channel_id=1, source_target_pairs={{0,2},{2,4},{4,6},{6,8},{8,10},{10,12},{12,14},{14,16},{16,18},{18... | collective-permute-start | bytes 393224 | tf_op jit(solution)/shard_map/ppermute | solution.py:16
  489.7 21.6 %copy-start.25 = (f32[8,64,64]{2,1,0:T(8,128)S(1)}, f32[8,64,64]{2,1,0:T(8,128)}, u32[]{:S(2)}) copy-start(f32[8,64,64]{2,1,0:T(8,128)} %copy-done.24) | copy-start | bytes 393220
  495.7 39.4 %collective-permute-start.11 = (f32[16,64,32]{1,2,0:T(8,128)}, f32[16,64,32]{1,2,0:T(8,128)}, u32[]{:S(2)}, u32[]{:S(2)}) collective-permute-start(f32[16,64,32]{1,2,0:T(8,128)} %slice_add_fusion.3), channel_id=1, source_target_pairs={{2,0},{4,2},{6,4},{8,6},{10,8},{12,10},{14,12},{16,14},{18,16},{20... | collective-permute-start | bytes 393224 | tf_op jit(solution)/shard_map/ppermute | solution.py:19
  497.0 59.8 %collective-permute-start.12 = (f32[32,64,32]{1,2,0:T(8,128)S(1)}, f32[32,64,32]{1,2,0:T(8,128)}, u32[]{:S(2)}, u32[]{:S(2)}) collective-permute-start(f32[32,64,32]{1,2,0:T(8,128)S(1)} %copy-done.18), channel_id=1, source_target_pairs={{0,2},{2,4},{4,6},{6,8},{8,10},{10,12},{12,14},{14,16},{16,18},{18... | collective-permute-start | bytes 786440 | tf_op jit(solution)/shard_map/ppermute | solution.py:16
  508.6 17.1 %copy-start.64 = (pred[8]{0:T(512)(128)(4,1)S(1)}, pred[8]{0:T(512)(128)(4,1)}, u32[]{:S(2)}) copy-start(pred[8]{0:T(512)(128)(4,1)} %get-tuple-element.226) | copy-start | bytes 28
  511.2 16.1 %copy-start.81 = (pred[8]{0:T(512)(128)(4,1)S(1)}, pred[8]{0:T(512)(128)(4,1)}, u32[]{:S(2)}) copy-start(pred[8]{0:T(512)(128)(4,1)} %get-tuple-element.228) | copy-start | bytes 28
  512.4 16.5 %copy-start.80 = (pred[8]{0:T(512)(128)(4,1)S(1)}, pred[8]{0:T(512)(128)(4,1)}, u32[]{:S(2)}) copy-start(pred[8]{0:T(512)(128)(4,1)} %get-tuple-element.224) | copy-start | bytes 28
  512.4 46.1 %collective-permute-start.13 = (f32[32,64,32]{1,2,0:T(8,128)S(1)}, f32[32,64,32]{1,2,0:T(8,128)}, u32[]{:S(2)}, u32[]{:S(2)}) collective-permute-start(f32[32,64,32]{1,2,0:T(8,128)S(1)} %copy-done.18), channel_id=1, source_target_pairs={{2,0},{4,2},{6,4},{8,6},{10,8},{12,10},{14,12},{16,14},{18,16},{20... | collective-permute-start | bytes 786440 | tf_op jit(solution)/shard_map/ppermute | solution.py:19
  513.7 70.9 %collective-permute-start.14 = (f32[64,64,32]{1,2,0:T(8,128)}, f32[64,64,32]{1,2,0:T(8,128)}, u32[]{:S(2)}, u32[]{:S(2)}) collective-permute-start(f32[64,64,32]{1,2,0:T(8,128)} %fusion.73), channel_id=1, source_target_pairs={{0,2},{2,4},{4,6},{6,8},{8,10},{10,12},{12,14},{14,16},{16,18},{18... | collective-permute-start | bytes 1572872 | tf_op jit(solution)/shard_map/ppermute | solution.py:16
  520.3 10.3 %copy-start.79 = (pred[8]{0:T(512)(128)(4,1)S(1)}, pred[8]{0:T(512)(128)(4,1)}, u32[]{:S(2)}) copy-start(pred[8]{0:T(512)(128)(4,1)} %get-tuple-element.114) | copy-start | bytes 28
  522.9 9.3 %copy-start.17 = (f32[16,64,64]{2,1,0:T(8,128)S(1)}, f32[16,64,64]{2,1,0:T(8,128)}, u32[]{:S(2)}) copy-start(f32[16,64,64]{2,1,0:T(8,128)} %copy.251) | copy-start | bytes 786436
  533.9 50.7 %collective-permute-start.15 = (f32[64,64,32]{1,2,0:T(8,128)}, f32[64,64,32]{1,2,0:T(8,128)}, u32[]{:S(2)}, u32[]{:S(2)}) collective-permute-start(f32[64,64,32]{1,2,0:T(8,128)} %fusion.73), channel_id=1, source_target_pairs={{2,0},{4,2},{6,4},{8,6},{10,8},{12,10},{14,12},{16,14},{18,16},{20... | collective-permute-start | bytes 1572872 | tf_op jit(solution)/shard_map/ppermute | solution.py:19
  535.2 89.2 %collective-permute-start = (f32[35,8192]{1,0:T(8,128)}, f32[35,8192]{1,0:T(8,128)}, u32[]{:S(2)}, u32[]{:S(2)}) collective-permute-start(f32[35,8192]{1,0:T(8,128)} %pad_maximum_fusion.3), channel_id=1, source_target_pairs={{0,2},{2,4},{4,6},{6,8},{8,10},{10,12},{12,14},{14,16},{16,18},{18... | collective-permute-start | bytes 3440648 | tf_op jit(solution)/shard_map/ppermute | solution.py:16
  543.4 6.7 copy-start.62
  544.9 7.3 copy-start.61
  556.9 67.5 %collective-permute-start.1 = (f32[35,8192]{1,0:T(8,128)}, f32[35,8192]{1,0:T(8,128)}, u32[]{:S(2)}, u32[]{:S(2)}) collective-permute-start(f32[35,8192]{1,0:T(8,128)} %pad_maximum_fusion.3), channel_id=1, source_target_pairs={{2,0},{4,2},{6,4},{8,6},{10,8},{12,10},{14,12},{16,14},{18,16},{20... | collective-permute-start | bytes 3440648 | tf_op jit(solution)/shard_map/ppermute | solution.py:19
  594.8 6.6 copy-start.9
  (55 other events, 246.2 us)
where the time goes:
time: 892 us; the launch traced here: 880 us
  local copies, waits for them, and re-layouts  289 us (32%)
  matrix products  280 us (31%)
  blocking collectives  181 us (20%)
  other arithmetic  68 us (8%)
  starting transfers between devices  52.5 us (6%)
  between operations  9.61 us (1%)
    all_gather x1, blocking collectives, local(): every_top = lax.all_gather(own_top, 'leaf', axis=0, tiled=True)  181 us
    dot_general x8, matrix products, block_kernel(): return jnp.einsum('gsab,cgsb->cga', kernel, sources[3:], precision=highest)  158 us
    unnamed x211, local copies, waits for them, and re-layouts  106 us
    dot_general x44, matrix products, couple(): jnp.einsum('nrq,nqc->nrc', matrices[:, slot_id], picked, precision=highest)  85.1 us
    gather x40, local copies, waits for them, and re-layouts, couple(): picked = jnp.take(sources, indices[:, slot_id], axis=0)  53.9 us
    slice x7, local copies, waits for them, and re-layouts, couple(): matrices[:, slot_id]  51.5 us
    ppermute x8, starting transfers between devices, padded(): lax.ppermute(lax.slice_in_dim(block, block.shape[dim] - width, None, axis...  41.9 us
    gather x8, local copies, waits for them, and re-layouts, one_block(): jnp.take(sources, pieces[1], axis=1)  40.3 us
  transfers between devices with their start and end apart: 16, of which 0 were waited for; matrix products, arithmetic and copies ran while one was open for 38% of the time, Pallas kernels for 0%

commit v1 on v0

v1 whole, which is shorter than its diff:
```python
import jax, jax.numpy as jnp, functools
from jax import lax
from jax.sharding import PartitionSpec as P
from jax.experimental import pallas as pl
from jax.experimental.pallas import tpu as pltpu
NT = (((1,), (1,)), ((), ()))
SM = pl.BlockSpec(memory_space=pltpu.SMEM)
VM = pl.BlockSpec(memory_space=pltpu.VMEM)
f32 = jnp.float32
bf16 = jnp.bfloat16

def split(x):
    hi = x.astype(bf16)
    return hi, (x - hi.astype(f32)).astype(bf16)

def stack(x):
    hi, lo = split(x)
    return jnp.concatenate([hi, lo], axis=0)

def fold(x):
    half = x.shape[0] // 2
    return x[:half] + x[half:]

def both(x):
    return x + pltpu.roll(x, 64, 1)

def low_lanes(shape):
    return lax.broadcasted_iota(jnp.int32, shape, 1) < 64

def up_body(basis, values, moves, up, top, trans, rows):
    leaves = basis.shape[0]
    columns = values.shape[0]
    nodes = moves.shape[2]
    @pl.loop(0, 64, unroll=4)
    def _(r):
        block = jnp.transpose(moves[r])
        rows[r, 0:nodes] = jnp.concatenate([block, block], axis=1)
    left = low_lanes((64, 128))
    @pl.loop(0, nodes, unroll=4)
    def _(n):
        x = rows[:, n, :]
        hi = x.astype(bf16).astype(f32)
        trans[n] = jnp.where(left, hi, x - hi).astype(bf16)
    half = low_lanes((columns, 128))
    def leaf_up(i):
        v = stack(values[:, pl.ds(pl.multiple_of(i * 128, 128), 128)])
        return both(fold(lax.dot_general(v, stack(basis[i]), NT, preferred_element_type=f32)))
    @pl.loop(0, leaves // 2, unroll=4)
    def _(p):
        up[p] = jnp.where(half, leaf_up(2 * p), leaf_up(2 * p + 1))
    def lift(tile, row):
        t = jnp.concatenate([trans[row], trans[row + 1]], axis=0)
        return both(fold(jnp.dot(stack(up[tile]), t, preferred_element_type=f32)))
    tile0, row0, width = 0, 0, leaves
    while width > 1:
        nxt = tile0 + width // 2
        if width >= 4:
            @pl.loop(0, width // 4, unroll=min(4, width // 4))
            def _(p, tile0=tile0, row0=row0, nxt=nxt):
                up[nxt + p] = jnp.where(half, lift(tile0 + 2 * p, row0 + 4 * p), lift(tile0 + 2 * p + 1, row0 + 4 * p + 2))
        else:
            up[nxt] = lift(tile0, row0)
        tile0, row0, width = nxt, row0 + width, width // 2
    top[...] = both(fold(jnp.dot(stack(up[tile0])[:, 0:64], trans[row0], preferred_element_type=f32)))

def up_pass(basis, values, moves):
    leaves, rank, size = basis.shape
    columns = values.shape[0]
    nodes = moves.shape[2]
    return pl.pallas_call(
        up_body,
        out_shape=(
            jax.ShapeDtypeStruct((leaves, columns, 128), f32),
            jax.ShapeDtypeStruct((columns, 128), f32),
            jax.ShapeDtypeStruct((nodes + 1, 64, 128), bf16),
        ),
        in_specs=[VM, VM, VM],
        out_specs=(VM, VM, VM),
        scratch_shapes=[pltpu.VMEM((64, 128, 128), f32)],
        compiler_params=pltpu.CompilerParams(vmem_limit_bytes=32 << 20),
        cost_estimate=pl.CostEstimate(flops=400_000_000, bytes_accessed=8_000_000, transcendentals=0),
        name="up_pass",
    )(basis, values, moves)

def unbatch_body(matrices, out, rows):
    nodes = matrices.shape[3]
    @pl.loop(0, 64, unroll=2)
    def _(r):
        for h in range(2):
            x = jnp.concatenate([matrices[2 * h, r], matrices[2 * h + 1, r]], axis=0)
            rows[h, r, 0:nodes] = jnp.transpose(x)
    @pl.loop(0, nodes, unroll=2)
    def _(n):
        for h in range(2):
            hi, lo = split(rows[h, :, n, :])
            out[n, 0:64, 128 * h : 128 * h + 128] = hi
            out[n, 64:128, 128 * h : 128 * h + 128] = lo

def unbatch(matrices):
    nodes = matrices.shape[3]
    return pl.pallas_call(
        unbatch_body,
        out_shape=jax.ShapeDtypeStruct((nodes, 128, 256), bf16),
        in_specs=[VM],
        out_specs=VM,
        scratch_shapes=[pltpu.VMEM((2, 64, 128, 128), f32)],
        compiler_params=pltpu.CompilerParams(vmem_limit_bytes=40 << 20),
        cost_estimate=pl.CostEstimate(flops=100_000_000, bytes_accessed=17_000_000, transcendentals=0),
        name="unbatch",
    )(matrices)

def top_body(place, partners, first, moves, matrices, parent, up, block, sem):
    spot = place[0]
    columns = first.shape[1]
    copies = []
    width, row = 32, 0
    for level in range(4):
        index = row + spot // (2 << level)
        copies.append(pltpu.make_async_copy(matrices.at[index], block.at[level], sem.at[level]))
        copies[-1].start()
        row, width = row + width, width // 2
    half = low_lanes((columns, 128))
    up[0:16] = first[...]
    def lift(tile, r):
        t = jnp.concatenate([moves[r], moves[r + 1]], axis=0)
        hi, lo = split(t)
        x = stack(up[tile])
        z = fold(jnp.dot(x, hi, preferred_element_type=f32)) + jnp.dot(x[:columns], lo, preferred_element_type=f32)
        return jnp.concatenate([z, z], axis=1)
    tile0, row, width = 0, 0, 32
    tiles, rows = [], []
    while width >= 4:
        tiles.append(tile0)
        rows.append(row)
        nxt = tile0 + width // 2
        if width > 4:
            for p in range(width // 4):
                up[nxt + p] = jnp.where(half, lift(tile0 + 2 * p, row + 4 * p), lift(tile0 + 2 * p + 1, row + 4 * p + 2))
        tile0, row, width = nxt, row + width, width // 2
    def push(d, r):
        hi, lo = split(moves[r])
        x = stack(d)
        return fold(lax.dot_general(x, hi, NT, preferred_element_type=f32)) + lax.dot_general(x[:columns], lo, NT, preferred_element_type=f32)
    down = jnp.zeros((columns, 64), f32)
    down = push(down, row + spot // 32)
    for level in range(3, -1, -1):
        index = rows[level] + spot // (2 << level)
        down = push(down, index)
        copies[level].wait()
        for k in range(4):
            p = partners[index * 4 + k]
            tile = up[tiles[level] + p // 2]
            x = stack(jnp.where(p % 2 == 0, tile, pltpu.roll(tile, 64, 1))[:, 0:64])
            hi, lo = split(block[level, k])
            down = down + fold(lax.dot_general(x, hi, NT, preferred_element_type=f32)) + lax.dot_general(x[:columns], lo, NT, preferred_element_type=f32)
    parent[...] = jnp.concatenate([down, down], axis=1)

def top_pass(place, partners, first, moves, matrices):
    columns = first.shape[1]
    return pl.pallas_call(
        top_body,
        out_shape=jax.ShapeDtypeStruct((columns, 128), f32),
        in_specs=[SM, SM, VM, VM, pl.BlockSpec(memory_space=pl.ANY)],
        out_specs=VM,
        scratch_shapes=[pltpu.VMEM((32, columns, 128), f32), pltpu.VMEM((4, 4, 64, 64), f32), pltpu.SemaphoreType.DMA((4,))],
        compiler_params=pltpu.CompilerParams(vmem_limit_bytes=16 << 20),
        cost_estimate=pl.CostEstimate(flops=50_000_000, bytes_accessed=2_000_000, transcendentals=0),
        name="top_pass",
    )(place, partners, first, moves, matrices)

def tail_body(core, partners, low, own, high, parent, matrices, trans, basis, near_a, near_b, out, gather, far, down):
    leaves = basis.shape[0]
    columns = out.shape[0]
    nodes = matrices.shape[0]
    half = low_lanes((columns, 128))
    for side, ref in enumerate((low, own, high)):
        @pl.loop(0, leaves, unroll=4)
        def _(t, side=side, ref=ref):
            x = ref[t]
            gather[0, side * leaves + t] = stack(x)
            gather[1, side * leaves + t] = stack(pltpu.roll(x, 64, 1))
    left = low_lanes((2 * columns, 128))
    def pick(n, k, side):
        code = partners[4 * n + k]
        return gather[(code & 1) ^ side, code >> 1]
    @pl.loop(0, nodes, unroll=4)
    def _(n):
        x = jnp.concatenate(
            [jnp.where(left, pick(n, 0, 0), pick(n, 1, 1)), jnp.where(left, pick(n, 2, 0), pick(n, 3, 1))], axis=1)
        far[n] = both(fold(lax.dot_general(x, matrices[n], NT, preferred_element_type=f32)))
    def push(d, n):
        t = trans[n]
        return fold(lax.dot_general(stack(d), jnp.concatenate([t, t], axis=0), NT, preferred_element_type=f32)) + far[n]
    row = nodes - 1
    down[row] = push(parent[...], row)
    width = 2
    while width <= leaves:
        begin = row - width
        if begin < 0:
            break
        @pl.loop(0, width, unroll=min(8, width))
        def _(i, begin=begin, row=row):
            down[begin + i] = push(down[row + i // 2], begin + i)
        row, width = begin, 2 * width
    @pl.loop(0, leaves, unroll=4)
    def _(i):
        at = pl.ds(pl.multiple_of(i * 128, 128), 128)
        out[:, at] = fold(jnp.dot(stack(down[i]), stack(basis[i]), preferred_element_type=f32))
    width = near_a.shape[1]
    out[:, pl.ds(pl.multiple_of(core[0] * width, width), width)] += near_a[...]
    out[:, pl.ds(pl.multiple_of((1 - core[0]) * width, width), width)] += near_b[...]

def tail(core, partners, low, own, high, parent, matrices, trans, basis, near_a, near_b):
    leaves = basis.shape[0]
    columns = own.shape[1]
    nodes = matrices.shape[0]
    return pl.pallas_call(
        tail_body,
        out_shape=jax.ShapeDtypeStruct((columns, leaves * 128), f32),
        in_specs=[SM, SM] + [VM] * 9,
        out_specs=VM,
        scratch_shapes=[pltpu.VMEM((2, 3 * leaves, 2 * columns, 128), bf16), pltpu.VMEM((nodes, columns, 128), f32), pltpu.VMEM((nodes, columns, 128), f32)],
        compiler_params=pltpu.CompilerParams(vmem_limit_bytes=50 << 20),
        cost_estimate=pl.CostEstimate(flops=400_000_000, bytes_accessed=20_000_000, transcendentals=0),
        name="tail",
    )(core, partners, low, own, high, parent, matrices, trans, basis, near_a, near_b)

near_weight = 0.1
smoothing = 0.0025
SLOTS = 28
PAIR = 2


def near_body(unroll, kinds, lists, counts, targets, *refs):
    sources = refs[:kinds]
    refs = refs[kinds:]
    begin = refs[0] if kinds == 4 else None
    if kinds == 4:
        refs = refs[1:]
    mine, other, columns_of, total, first, second, weights, places = refs
    leaves = mine.shape[1] // 128
    width = sources[0].shape[1] // 128
    chunks = kinds // 2
    for c in range(chunks):
        near_ref, far_ref = sources[2 * c], sources[2 * c + 1]

        @pl.loop(0, width, unroll=4)
        def _(j, c=c, near_ref=near_ref, far_ref=far_ref):
            at = pl.ds(pl.multiple_of(j * 128, 128), 128)
            x = near_weight * jnp.concatenate([near_ref[0:32, at], far_ref[0:32, at]], axis=0)
            weights[c * width + j] = stack(x)
            places[c * width + j, 0:3] = near_ref[32:35, at] if chunks == 2 else targets[:, at]

    weights[chunks * width] = jnp.zeros(weights.shape[1:], bf16)
    places[chunks * width] = jnp.zeros(places.shape[1:], f32)
    offset = counts[leaves] * leaves

    @pl.loop(0, leaves, unroll=4)
    def _(leaf):
        at = pl.ds(pl.multiple_of((offset + leaf) * 128, 128), 128)
        row = jnp.concatenate([targets[:, at], jnp.zeros((5, 128), f32)], axis=0)
        t = jnp.transpose(row)
        for c in range(3):
            columns_of[leaf, c] = jnp.broadcast_to(t[:, c : c + 1], (128, 128))
        total[leaf] = jnp.zeros((128, 128), f32)

    items = lax.fori_loop(
        0, leaves, lambda i, s: s + jnp.maximum((counts[i] + PAIR - 1) // PAIR, 1), jnp.int32(0)
    )

    def make(buf, leaf, slot):
        for u in range(PAIR):
            s = places[lists[leaf * SLOTS + slot + u]]
            for r in range(0, 128, 32):
                d = columns_of[leaf, 0, r : r + 32] - s[0:1]
                squared = d * d + smoothing
                d = columns_of[leaf, 1, r : r + 32] - s[1:2]
                squared = squared + d * d
                d = columns_of[leaf, 2, r : r + 32] - s[2:3]
                squared = squared + d * d
                hi, lo = split(lax.rsqrt(squared))
                buf[r : r + 32, u * 256 : u * 256 + 128] = hi
                buf[r : r + 32, u * 256 + 128 : u * 256 + 256] = lo

    def use(buf, leaf, slot):
        parts = []
        for u in range(PAIR):
            x = weights[lists[leaf * SLOTS + slot + u]]
            parts += [x, x]
        total[leaf] += lax.dot_general(
            buf[...], jnp.concatenate(parts, axis=1), NT, preferred_element_type=f32
        )

    def take(leaf, slot):
        found = []
        for u in range(unroll):
            found += [leaf, slot]
            done = slot + PAIR >= counts[leaf]
            leaf = jnp.where(done, jnp.minimum(leaf + 1, leaves - 1), leaf)
            slot = jnp.where(done, 0, slot + PAIR)
        return found, leaf, slot

    def half(carry, source, dest):
        found, leaf, slot = take(carry[-2], carry[-1])
        for u in range(unroll):
            use(source.at[u], carry[2 * u], carry[2 * u + 1])
            make(dest.at[u], found[2 * u], found[2 * u + 1])
        return (*found, leaf, slot)

    def finish(buf, carry, start):
        for u in range(unroll):

            @pl.when(start * unroll + u < items)
            def _(u=u):
                use(buf.at[u], carry[2 * u], carry[2 * u + 1])

    found, leaf, slot = take(jnp.int32(0), jnp.int32(0))
    for u in range(unroll):
        make(first.at[u], found[2 * u], found[2 * u + 1])
    batches = (items + unroll - 1) // unroll
    steps = (batches - 1) // 2
    carry = lax.fori_loop(
        0, steps, lambda b, c: half(half(c, first, second), second, first), (*found, leaf, slot)
    )

    @pl.when(batches - 1 == 2 * steps)
    def _():
        finish(first, carry, 2 * steps)

    @pl.when(batches - 1 > 2 * steps)
    def _():
        finish(second, half(carry, first, second), 2 * steps + 1)

    @pl.loop(0, leaves, unroll=4)
    def _(leaf):
        at = pl.ds(pl.multiple_of(leaf * 128, 128), 128)
        x = jnp.transpose(both(total[leaf]))
        if begin is None:
            mine[:, at] = x[0:32]
            other[:, at] = x[32:64]
        else:
            mine[:, at] = begin[0:32, at] + x[0:32]
            other[:, at] = begin[32:64, at] + x[32:64]


def near_pass(unroll, lists, counts, targets, sources, begin=None):
    leaves = lists.shape[0] // SLOTS
    held = 64 * (len(sources) // 2) + 1
    side = jax.ShapeDtypeStruct((32, leaves * 128), f32)
    extra = [] if begin is None else list(begin)
    if begin is not None:
        extra = [jnp.concatenate(begin, axis=0)]
    return pl.pallas_call(
        functools.partial(near_body, unroll, len(sources)),
        out_shape=(side, side),
        in_specs=[SM, SM] + [VM] * (1 + len(sources) + len(extra)),
        out_specs=(VM, VM),
        scratch_shapes=[
            pltpu.VMEM((leaves, 3, 128, 128), f32),
            pltpu.VMEM((leaves, 128, 128), f32),
            pltpu.VMEM((unroll, 128, PAIR * 256), bf16),
            pltpu.VMEM((unroll, 128, PAIR * 256), bf16),
            pltpu.VMEM((held, 128, 128), bf16),
            pltpu.VMEM((held, 8, 128), f32),
        ],
        compiler_params=pltpu.CompilerParams(vmem_limit_bytes=40 << 20),
        cost_estimate=pl.CostEstimate(flops=16_000_000_000, bytes_accessed=8_000_000, transcendentals=8_000_000),
        name="near_pass",
    )(lists, counts, targets, *sources, *extra)


def arranged(picked, leaf_ids, empty):
    slots = picked.shape[1]
    before = jnp.arange(slots)[:, None] < jnp.arange(slots)[None, :]
    rank = jnp.sum(jnp.where(picked[:, :, None] & before[None], 1, 0), axis=1)
    to = jnp.arange(SLOTS)[None, None, :]
    here = picked[:, :, None] & (rank[:, :, None] == to)
    found = jnp.sum(jnp.where(here, leaf_ids[:, :, None], 0), axis=1)
    count = jnp.sum(picked.astype(jnp.int32), axis=1)
    lists = jnp.where(jnp.arange(SLOTS)[None, :] < count[:, None], found, empty)
    return lists.astype(jnp.int32).reshape(-1), count


def partner_codes(partners, position, leaves):
    spans, starts = [], []
    width, tile = leaves, 0
    while width >= 1:
        spans += [width] * width
        starts += [2 * tile] * width
        tile, width = tile + max(1, width // 2), width // 2
    spans = jnp.array(spans, jnp.int32)[:, None]
    starts = jnp.array(starts, jnp.int32)[:, None]
    local = partners - position * spans
    side = jnp.where(local < 0, 0, jnp.where(local < spans, 1, 2))
    return (side * (2 * leaves) + starts + local - (side - 1) * spans).reshape(-1)


def local(
    points,
    values,
    near_list,
    near_count,
    basis,
    transfer,
    coupling,
    partners,
    transfer_top,
    coupling_top,
    partners_top,
):
    leaves = basis.shape[0]
    position = lax.axis_index("leaf")
    core = lax.axis_index("rhs")
    count = lax.axis_size("leaf")
    forward = [(i, i + 1) for i in range(count - 1)]
    backward = [(target, source) for source, target in forward]
    swap = [(0, 1), (1, 0)]
    packed = jnp.concatenate([values, points], axis=0)
    low = lax.ppermute(packed, "leaf", forward)
    high = lax.ppermute(packed, "leaf", backward)
    across = lax.ppermute(values, "rhs", swap)

    half = leaves // 2
    chosen = lax.dynamic_slice_in_dim(near_list, core * half, half, 0) - position * leaves
    live = lax.dynamic_slice_in_dim(near_count, core * half, half, 0)
    alive = jnp.arange(chosen.shape[1])[None, :] < live[:, None]
    inside = (chosen >= 0) & (chosen < leaves)
    near_ids, near_live = arranged(alive & inside, chosen, leaves)
    outside_ids = jnp.where(chosen < 0, chosen + leaves, chosen)
    far_ids, far_live = arranged(alive & ~inside, outside_ids, 2 * leaves)
    near_live = jnp.concatenate([near_live, core[None]]).astype(jnp.int32)
    far_live = jnp.concatenate([far_live, core[None]]).astype(jnp.int32)
    codes = partner_codes(partners, position, leaves)

    up, top, trans = up_pass(basis, values, transfer.transpose(1, 2, 0))
    up_low = lax.ppermute(up, "leaf", forward)
    up_high = lax.ppermute(up, "leaf", backward)

    def exchange(x, bit):
        return lax.ppermute(x, "leaf", [(i, i ^ (1 << bit)) for i in range(count)])

    def ordered(x, y, bit, axis):
        return jnp.where((position >> bit) & 1 == 0, jnp.concatenate([x, y], axis), jnp.concatenate([y, x], axis))

    level = top + exchange(top, 0)
    level = ordered(level[:, 0:64], exchange(level, 1)[:, 0:64], 1, 1)[None]
    for bit in range(2, count.bit_length() - 1):
        level = ordered(level, exchange(level, bit), bit, 0)

    begin = near_pass(4, near_ids, near_live, points, (values, across))
    matrices = unbatch(coupling.transpose(1, 2, 3, 0))
    parent = top_pass(position[None].astype(jnp.int32), partners_top.reshape(-1), level, transfer_top, coupling_top)
    low_across = lax.ppermute(low, "rhs", swap)
    high_across = lax.ppermute(high, "rhs", swap)
    mine, other = near_pass(4, far_ids, far_live, points, (low, low_across, high, high_across), begin)
    given = lax.ppermute(other, "rhs", swap)
    return tail(core[None].astype(jnp.int32), codes, up_low, up, up_high, parent, matrices, trans, basis, mine, given)


def solution(mesh):
    placed = (
        P(None, "leaf"),
        P("rhs", "leaf"),
        P("leaf", None),
        P("leaf"),
        P("leaf", None, None),
        P("leaf", None, None),
        P("leaf", None, None, None),
        P("leaf", None),
        P(),
        P(),
        P(),
    )
    return jax.shard_map(
        local, mesh=mesh, in_specs=placed, out_specs=P("rhs", "leaf"), check_vma=False
    )
```

time: 892 us -> 199 us (0.22)
  the two profiles are of different devices: /device:TPU:0 before, /device:TPU:33 now
where the time goes in v1:
time: 199 us; the launch traced here: 200 us
  Pallas kernels  128 us (64%)
  starting transfers between devices  41.6 us (21%)
  waiting for transfers between devices  19.1 us (10%)
  local copies, waits for them, and re-layouts  8.13 us (4%)
    pallas_call x1, Pallas kernels, tail(): pl.pallas_call(tail_body, out_shape=jax.ShapeDtypeStruct((columns, leaves...  37.6 us
    pallas_call x2, Pallas kernels, near_pass(): pl.pallas_call(functools.partial(near_body, unroll, len(sources)), out_sh...  36.7 us
    pallas_call x1, Pallas kernels, unbatch(): pl.pallas_call(unbatch_body, out_shape=jax.ShapeDtypeStruct((nodes, 128,...  30 us
    pallas_call x1, Pallas kernels, up_pass(): pl.pallas_call(up_body, out_shape=(jax.ShapeDtypeStruct((leaves, columns,...  20.6 us
    ppermute x6, waiting for transfers between devices, exchange(): return lax.ppermute(x, 'leaf', [(i, i ^ 1 << bit) for i in range(count)])  19 us
    ppermute x6, starting transfers between devices, exchange(): return lax.ppermute(x, 'leaf', [(i, i ^ 1 << bit) for i in range(count)])  13.9 us
    ppermute x1, starting transfers between devices, local(): up_high = lax.ppermute(up, 'leaf', backward)  7.57 us
    unnamed x34, local copies, waits for them, and re-layouts  6.65 us
  transfers between devices with their start and end apart: 14, of which 3 were waited for; matrix products, arithmetic and copies ran while one was open for 3% of the time, Pallas kernels for 46%

profile of v1, /device:TPU:33, one launch (start us, length us, event | category | flops | bytes accessed | tf_op | source)
XLA Modules:
  0.0 199.5 jit_solution(5193449702603080884)
XLA Ops:
  0.0 0.7 collective-permute-start.12
  0.7 2.3 %constant_dynamic-update-slice_fusion.1 = f32[35,8192]{1,0:T(8,128)} fusion(f32[32,8192]{1,0:T(8,128)} %refs_0_.1), kind=kLoop, calls=%fused_computation.30 | loop fusion | bytes 2097152
  3.0 0.7 constant_dynamic-update-slice_fusion
  3.7 6.4 %collective-permute-start.10 = (f32[35,8192]{1,0:T(8,128)}, f32[35,8192]{1,0:T(8,128)}, u32[]{:S(2)}, u32[]{:S(2)}) collective-permute-start(f32[35,8192]{1,0:T(8,128)} %constant_dynamic-update-slice_fusion), channel_id=1, source_target_pairs={{2,0},{4,2},{6,4},{8,6},{10,8},{12,10},{14,12},{16,14},{18,16},{20... | collective-permute-start | bytes 3440648 | tf_op jit(solution)/shard_map/ppermute | solution.py:420
  10.1 1.9 collective-permute-start.8
  12.0 1.2 copy-done.2
  13.2 1.6 copy-done.5
  14.8 20.6 %up_pass.1 = (f32[64,32,128]{2,1,0:T(8,128)}, f32[32,128]{1,0:T(8,128)S(1)}, bf16[128,64,128]{2,1,0:T(8,128)(2,1)S(1)}) custom-call(f32[64,64,128]{2,1,0:T(8,128)S(1)} %copy-done.1, f32[32,8192]{1,0:T(8,128)S(1)} %copy-done.2, f32[64,64,127]{2,1,0:T(8,128)S(1)} %bitcast.10), custom_call_target="tpu_custom_call" | custom-call | flops 400000000 | bytes 8000000 | tf_op jit(solution)/shard_map/up_pass/pallas_call | solution.py:70
  35.4 1.4 copy-done.4
  36.8 7.6 %collective-permute-start.1 = (f32[64,32,128]{2,1,0:T(8,128)}, f32[64,32,128]{2,1,0:T(8,128)}, u32[]{:S(2)}, u32[]{:S(2)}) collective-permute-start(f32[64,32,128]{2,1,0:T(8,128)} %get-tuple-element.12.own), channel_id=1, source_target_pairs={{2,0},{4,2},{6,4},{8,6},{10,8},{12,10},{14,12},{16,14},{18,16},{20... | collective-permute-start | bytes 3145736 | tf_op jit(solution)/shard_map/ppermute | solution.py:437
  44.4 0.1 dynamic_slice.6
  44.5 0.1 convert_reduce_fusion
  44.6 0.3 select_reduce_fusion.1
  44.9 0.1 copy.31
  45.0 0.5 select_reduce_fusion
  45.5 0.1 copy.30
  45.6 0.1 fusion.5
  45.6 0.5 select_reduce_fusion.2
  46.2 0.1 fusion.4
  46.2 0.1 collective-permute-start.3
  46.3 4.1 %collective-permute-done.3 = f32[32,128]{1,0:T(8,128)S(1)} collective-permute-done((f32[32,128]{1,0:T(8,128)S(1)}, f32[32,128]{1,0:T(8,128)S(1)}, u32[]{:S(2)}, u32[]{:S(2)}) %collective-permute-start.3) | collective-permute-done | bytes 16416 | tf_op jit(solution)/shard_map/ppermute | solution.py:440
  50.4 0.1 maximum_select_fusion.4
  50.5 0.0 collective-permute-start.4
  50.5 0.1 pad_add_fusion.1.counts
  50.6 13.9 %collective-permute-done.4 = f32[1,32,128]{2,1,0:T(8,128)S(1)} collective-permute-done((f32[1,32,128]{2,1,0:T(8,128)S(1)}, f32[1,32,128]{2,1,0:T(8,128)S(1)}, u32[]{:S(2)}, u32[]{:S(2)}) %collective-permute-start.4) | collective-permute-done | bytes 16416 | tf_op jit(solution)/shard_map/ppermute | solution.py:440
  64.5 3.0 %collective-permute-start.5 = (f32[2,32,128]{2,1,0:T(8,128)S(1)}, f32[2,32,128]{2,1,0:T(8,128)S(1)}, u32[]{:S(2)}, u32[]{:S(2)}) collective-permute-start(f32[2,32,128]{2,1,0:T(8,128)S(1)} %maximum_select_fusion.3), channel_id=1, source_target_pairs={{0,16},{2,18},{4,20},{6,22},{8,24},{10,26},{12,28},{14,30},{16,0},... | collective-permute-start | bytes 98312 | tf_op jit(solution)/shard_map/ppermute | solution.py:440
  67.5 0.1 pad_add_fusion.counts
  67.6 0.1 select_n.113.lists
  67.7 0.1 select_n.109.lists
  67.8 1.0 collective-permute-done.5
  68.8 6.4 %collective-permute-start = (f32[64,32,128]{2,1,0:T(8,128)}, f32[64,32,128]{2,1,0:T(8,128)S(1)}, u32[]{:S(2)}, u32[]{:S(2)}) collective-permute-start(f32[64,32,128]{2,1,0:T(8,128)} %get-tuple-element.12.own), channel_id=1, source_target_pairs={{0,2},{2,4},{4,6},{6,8},{8,10},{10,12},{12,14},{14,16},{16,18},{18... | collective-permute-start | bytes 3145736 | tf_op jit(solution)/shard_map/ppermute | solution.py:436
  75.2 0.1 collective-permute-start.6
  75.3 4.4 %collective-permute-start.11 = (f32[35,8192]{1,0:T(8,128)}, f32[35,8192]{1,0:T(8,128)S(1)}, u32[]{:S(2)}, u32[]{:S(2)}) collective-permute-start(f32[35,8192]{1,0:T(8,128)} %collective-permute-done.10.refs_2_), channel_id=1, source_target_pairs={{0,1},{1,0},{2,3},{3,2},{4,5},{5,4},{6,7},{7,6},{8,9},{9,8},{10,11... | collective-permute-start | bytes 3440648 | tf_op jit(solution)/shard_map/ppermute | solution.py:454
  79.7 0.1 collective-permute-start.9
  79.8 19.1 %near_pass.2 = (f32[32,4096]{1,0:T(8,128)S(1)}, f32[32,4096]{1,0:T(8,128)S(1)}) custom-call(s32[896]{0:T(1024)S(1)} %select_n.113.lists, s32[33]{0:T(128)S(1)} %pad_add_fusion.1.counts, f32[3,8192]{1,0:T(4,128)S(1)} %copy-done.7, f32[32,8192]{1,0:T(8,128)S(1)} %copy-done.3, f32[32,8192]{1,0:T(8,128)} %collective-permute-done.12.refs_1_), custom_call_target="tpu_custom_call" | custom-call | flops 16000000000 | bytes 8000000 | tf_op jit(solution)/shard_map/near_pass/pallas_call | solution.py:353
  98.9 0.1 pad_maximum_fusion.refs_4_
  99.0 0.0 copy-start.11
  99.0 0.0 copy-start.12
  99.1 17.7 %near_pass.3 = (f32[32,4096]{1,0:T(8,128)S(1)}, f32[32,4096]{1,0:T(8,128)S(1)}) custom-call(s32[896]{0:T(1024)S(1)} %select_n.109.lists, s32[33]{0:T(128)S(1)} %pad_add_fusion.counts, f32[3,8192]{1,0:T(4,128)S(1)} %copy-done.7, f32[35,8192]{1,0:T(8,128)} %collective-permute-done.8.refs_0_, f32[35,8192]{1,0:T(8,128)S(1)} %collective-permute-done.9.refs_1_, ...), custom_call_target="tpu_custom_call" | custom-call | flops 16000000000 | bytes 8000000 | tf_op jit(solution)/shard_map/near_pass/pallas_call | solution.py:353
  116.7 0.3 collective-permute-start.13
  117.0 0.1 copy.29
  117.1 0.1 reshape.101.partners
  117.3 10.7 %collective-permute-start.7 = (f32[8,32,128]{2,1,0:T(8,128)S(1)}, f32[8,32,128]{2,1,0:T(8,128)S(1)}, u32[]{:S(2)}, u32[]{:S(2)}) collective-permute-start(f32[8,32,128]{2,1,0:T(8,128)S(1)} %maximum_select_fusion.1), channel_id=1, source_target_pairs={{0,64},{2,66},{4,68},{6,70},{8,72},{10,74},{12,76},{14,78},{16,80}... | collective-permute-start | bytes 393224 | tf_op jit(solution)/shard_map/ppermute | solution.py:440
  128.0 0.1 copy.28
  128.1 0.1 reshape.100.partners
  128.3 30.0 %unbatch.1.matrices = bf16[127,128,256]{2,1,0:T(8,128)(2,1)S(1)} custom-call(f32[4,64,64,127]{3,2,1,0:T(8,128)} %bitcast.11), custom_call_target="tpu_custom_call" | custom-call | flops 100000000 | bytes 17000000 | tf_op jit(solution)/shard_map/unbatch/pallas_call | solution.py:101
  158.3 3.6 %top_pass.1.parent = f32[32,128]{1,0:T(8,128)S(1)} custom-call(s32[1]{0:T(128)} %bitcast.2.place, s32[240]{0:T(256)S(1)} %reshape.101.partners, f32[16,32,128]{2,1,0:T(8,128)S(1)} %maximum_select_fusion.first, f32[62,64,64]{2,1,0:T(8,128)S(1)} %copy-done.6, f32[60,4,64,64]{3,2,1,0:T(8,128)S(1)} %bitcast.9), custom_call_target="tpu_custom_call" | custom-call | flops 50000000 | bytes 2000000 | tf_op jit(solution)/shard_map/top_pass/pallas_call | solution.py:160
  162.0 37.6 %tail.1 = f32[32,8192]{1,0:T(8,128)} custom-call(s32[1]{0:T(128)} %bitcast.core, s32[508]{0:T(512)S(1)} %reshape.100.partners, f32[64,32,128]{2,1,0:T(8,128)S(1)} %collective-permute-done.low, f32[64,32,128]{2,1,0:T(8,128)} %get-tuple-element.12.own, f32[64,32,128]{2,1,0:T(8,128)} %collective-permute-done.1.high, f32[32,128]{1,0:T(8,128)S(1)} %top_pass.1.parent, ...), custom_call_target="tpu_custom_call" | custom-call | flops 400000000 | bytes 20000000 | tf_op jit(solution)/shard_map/tail/pallas_call | solution.py:217
  (51 shorter events, 0.2 us)
Async XLA Ops:
  0.0 3.0 %copy-start.7 = (f32[3,8192]{1,0:T(4,128)S(1)}, f32[3,8192]{1,0:T(4,128)}, u32[]{:S(2)}) copy-start(f32[3,8192]{1,0:T(4,128)} %targets.3) | copy-start | bytes 294916
  0.0 12.0 %copy-start.1 = (f32[64,64,128]{2,1,0:T(8,128)S(1)}, f32[64,64,128]{2,1,0:T(8,128)}, u32[]{:S(2)}) copy-start(f32[64,64,128]{2,1,0:T(8,128)} %basis.3) | copy-start | bytes 6291460
  0.0 75.2 %collective-permute-start.12 = (f32[32,8192]{1,0:T(8,128)}, f32[32,8192]{1,0:T(8,128)}, u32[]{:S(2)}, u32[]{:S(2)}) collective-permute-start(f32[32,8192]{1,0:T(8,128)} %refs_0_.1), channel_id=1, source_target_pairs={{0,1},{1,0},{2,3},{3,2},{4,5},{5,4},{6,7},{7,6},{8,9},{9,8},{10,11... | collective-permute-start | bytes 3145736 | tf_op jit(solution)/shard_map/ppermute | solution.py:421
  3.7 71.7 %collective-permute-start.10 = (f32[35,8192]{1,0:T(8,128)}, f32[35,8192]{1,0:T(8,128)}, u32[]{:S(2)}, u32[]{:S(2)}) collective-permute-start(f32[35,8192]{1,0:T(8,128)} %constant_dynamic-update-slice_fusion), channel_id=1, source_target_pairs={{2,0},{4,2},{6,4},{8,6},{10,8},{12,10},{14,12},{16,14},{18,16},{20... | collective-permute-start | bytes 3440648 | tf_op jit(solution)/shard_map/ppermute | solution.py:420
  10.1 69.7 %collective-permute-start.8 = (f32[35,8192]{1,0:T(8,128)}, f32[35,8192]{1,0:T(8,128)}, u32[]{:S(2)}, u32[]{:S(2)}) collective-permute-start(f32[35,8192]{1,0:T(8,128)} %constant_dynamic-update-slice_fusion), channel_id=1, source_target_pairs={{0,2},{2,4},{4,6},{6,8},{8,10},{10,12},{12,14},{14,16},{16,18},{18... | collective-permute-start | bytes 3440648 | tf_op jit(solution)/shard_map/ppermute | solution.py:419
  12.0 1.2 copy-start.2
  13.2 1.6 copy-start.5
  14.8 29.6 %copy-start.13 = (s32[64]{0:T(128)S(1)}, s32[64]{0:T(128)}, u32[]{:S(2)}) copy-start(s32[64]{0:T(128)} %param.16) | copy-start | bytes 772
  14.8 29.6 %copy-start.8 = (s32[64,27]{0,1:T(8,128)S(1)}, s32[64,27]{0,1:T(8,128)}, u32[]{:S(2)}) copy-start(s32[64,27]{0,1:T(8,128)} %param.15) | copy-start | bytes 20740
  14.8 65.0 %copy-start.3 = (f32[32,8192]{1,0:T(8,128)S(1)}, f32[32,8192]{1,0:T(8,128)}, u32[]{:S(2)}) copy-start(f32[32,8192]{1,0:T(8,128)} %refs_0_.1) | copy-start | bytes 3145732
  35.4 1.4 copy-start.4
  36.8 9.5 %collective-permute-start.2 = (f32[32,128]{1,0:T(8,128)S(1)}, f32[32,128]{1,0:T(8,128)S(1)}, u32[]{:S(2)}, u32[]{:S(2)}) collective-permute-start(f32[32,128]{1,0:T(8,128)S(1)} %get-tuple-element.13), channel_id=1, source_target_pairs={{0,2},{2,0},{4,6},{6,4},{8,10},{10,8},{12,14},{14,12},{16,18},{18,... | collective-permute-start | bytes 49160 | tf_op jit(solution)/shard_map/ppermute | solution.py:440
  36.8 125.1 %collective-permute-start.1 = (f32[64,32,128]{2,1,0:T(8,128)}, f32[64,32,128]{2,1,0:T(8,128)}, u32[]{:S(2)}, u32[]{:S(2)}) collective-permute-start(f32[64,32,128]{2,1,0:T(8,128)} %get-tuple-element.12.own), channel_id=1, source_target_pairs={{2,0},{4,2},{6,4},{8,6},{10,8},{12,10},{14,12},{16,14},{18,16},{20... | collective-permute-start | bytes 3145736 | tf_op jit(solution)/shard_map/ppermute | solution.py:437
  46.2 4.2 %collective-permute-start.3 = (f32[32,128]{1,0:T(8,128)S(1)}, f32[32,128]{1,0:T(8,128)S(1)}, u32[]{:S(2)}, u32[]{:S(2)}) collective-permute-start(f32[32,128]{1,0:T(8,128)S(1)} %add.25), channel_id=1, source_target_pairs={{0,4},{2,6},{4,0},{6,2},{8,12},{10,14},{12,8},{14,10},{16,20},{18,... | collective-permute-start | bytes 49160 | tf_op jit(solution)/shard_map/ppermute | solution.py:440
  50.5 14.0 %collective-permute-start.4 = (f32[1,32,128]{2,1,0:T(8,128)S(1)}, f32[1,32,128]{2,1,0:T(8,128)S(1)}, u32[]{:S(2)}, u32[]{:S(2)}) collective-permute-start(f32[1,32,128]{2,1,0:T(8,128)S(1)} %maximum_select_fusion.4), channel_id=1, source_target_pairs={{0,8},{2,10},{4,12},{6,14},{8,0},{10,2},{12,4},{14,6},{16,24},{18,... | collective-permute-start | bytes 49160 | tf_op jit(solution)/shard_map/ppermute | solution.py:440
  64.5 4.3 %collective-permute-start.5 = (f32[2,32,128]{2,1,0:T(8,128)S(1)}, f32[2,32,128]{2,1,0:T(8,128)S(1)}, u32[]{:S(2)}, u32[]{:S(2)}) collective-permute-start(f32[2,32,128]{2,1,0:T(8,128)S(1)} %maximum_select_fusion.3), channel_id=1, source_target_pairs={{0,16},{2,18},{4,20},{6,22},{8,24},{10,26},{12,28},{14,30},{16,0},... | collective-permute-start | bytes 98312 | tf_op jit(solution)/shard_map/ppermute | solution.py:440
  68.8 93.1 %collective-permute-start = (f32[64,32,128]{2,1,0:T(8,128)}, f32[64,32,128]{2,1,0:T(8,128)S(1)}, u32[]{:S(2)}, u32[]{:S(2)}) collective-permute-start(f32[64,32,128]{2,1,0:T(8,128)} %get-tuple-element.12.own), channel_id=1, source_target_pairs={{0,2},{2,4},{4,6},{6,8},{8,10},{10,12},{12,14},{14,16},{16,18},{18... | collective-permute-start | bytes 3145736 | tf_op jit(solution)/shard_map/ppermute | solution.py:436
  75.2 42.0 %collective-permute-start.6 = (f32[4,32,128]{2,1,0:T(8,128)S(1)}, f32[4,32,128]{2,1,0:T(8,128)S(1)}, u32[]{:S(2)}, u32[]{:S(2)}) collective-permute-start(f32[4,32,128]{2,1,0:T(8,128)S(1)} %maximum_select_fusion.2), channel_id=1, source_target_pairs={{0,32},{2,34},{4,36},{6,38},{8,40},{10,42},{12,44},{14,46},{16,48}... | collective-permute-start | bytes 196616 | tf_op jit(solution)/shard_map/ppermute | solution.py:440
  75.3 23.7 %collective-permute-start.11 = (f32[35,8192]{1,0:T(8,128)}, f32[35,8192]{1,0:T(8,128)S(1)}, u32[]{:S(2)}, u32[]{:S(2)}) collective-permute-start(f32[35,8192]{1,0:T(8,128)} %collective-permute-done.10.refs_2_), channel_id=1, source_target_pairs={{0,1},{1,0},{2,3},{3,2},{4,5},{5,4},{6,7},{7,6},{8,9},{9,8},{10,11... | collective-permute-start | bytes 3440648 | tf_op jit(solution)/shard_map/ppermute | solution.py:454
  79.7 19.3 %collective-permute-start.9 = (f32[35,8192]{1,0:T(8,128)}, f32[35,8192]{1,0:T(8,128)S(1)}, u32[]{:S(2)}, u32[]{:S(2)}) collective-permute-start(f32[35,8192]{1,0:T(8,128)} %collective-permute-done.8.refs_0_), channel_id=1, source_target_pairs={{0,1},{1,0},{2,3},{3,2},{4,5},{5,4},{6,7},{7,6},{8,9},{9,8},{10,11... | collective-permute-start | bytes 3440648 | tf_op jit(solution)/shard_map/ppermute | solution.py:453
  99.0 18.0 %copy-start.11 = (s32[127]{0:T(128)S(1)}, s32[127]{0:T(128)}, u32[]{:S(2)}) copy-start(s32[127]{0:T(128)} %constant.13.clone) | copy-start | bytes 1528
  99.0 18.0 %copy-start.9 = (s32[60,4]{0,1:T(4,128)S(1)}, s32[60,4]{0,1:T(4,128)}, u32[]{:S(2)}) copy-start(s32[60,4]{0,1:T(4,128)} %param.23) | copy-start | bytes 2884
  99.0 29.0 %copy-start.10 = (s32[127,4]{0,1:T(4,128)S(1)}, s32[127,4]{0,1:T(4,128)}, u32[]{:S(2)}) copy-start(s32[127,4]{0,1:T(4,128)} %param.20) | copy-start | bytes 6100
  99.0 29.0 %copy-start.12 = (s32[127]{0:T(128)S(1)}, s32[127]{0:T(128)}, u32[]{:S(2)}) copy-start(s32[127]{0:T(128)} %constant.38.clone) | copy-start | bytes 1528
  116.7 45.2 %collective-permute-start.13 = (f32[32,4096]{1,0:T(8,128)S(1)}, f32[32,4096]{1,0:T(8,128)S(1)}, u32[]{:S(2)}, u32[]{:S(2)}) collective-permute-start(f32[32,4096]{1,0:T(8,128)S(1)} %get-tuple-element.18), channel_id=1, source_target_pairs={{0,1},{1,0},{2,3},{3,2},{4,5},{5,4},{6,7},{7,6},{8,9},{9,8},{10,11... | collective-permute-start | bytes 1572872 | tf_op jit(solution)/shard_map/ppermute | solution.py:456
  117.3 41.0 %collective-permute-start.7 = (f32[8,32,128]{2,1,0:T(8,128)S(1)}, f32[8,32,128]{2,1,0:T(8,128)S(1)}, u32[]{:S(2)}, u32[]{:S(2)}) collective-permute-start(f32[8,32,128]{2,1,0:T(8,128)S(1)} %maximum_select_fusion.1), channel_id=1, source_target_pairs={{0,64},{2,66},{4,68},{6,70},{8,72},{10,74},{12,76},{14,78},{16,80}... | collective-permute-start | bytes 393224 | tf_op jit(solution)/shard_map/ppermute | solution.py:440
  128.2 30.1 %slice-start = ((s8[7864320]{0:T(1024)(128)(4,1)}), s8[4194304]{0:T(1024)(128)(4,1)S(1)}, s32[]{:S(2)}) async-start(s8[7864320]{0:T(1024)(128)(4,1)} %bitcast.8), calls=%async_computation | async-start | bytes 8388608
  128.2 30.1 %slice-start.1 = ((s8[7864320]{0:T(1024)(128)(4,1)}), s8[3670016]{0:T(1024)(128)(4,1)S(1)}, s32[]{:S(2)}) async-start(s8[7864320]{0:T(1024)(128)(4,1)} %bitcast.8), calls=%async_computation.1 | async-start | bytes 7340032
  128.3 30.1 %copy-start.6 = (f32[62,64,64]{2,1,0:T(8,128)S(1)}, f32[62,64,64]{2,1,0:T(8,128)}, u32[]{:S(2)}) copy-start(f32[62,64,64]{2,1,0:T(8,128)} %moves.1) | copy-start | bytes 3047428
  158.2 3.7 %copy-start = (bf16[127,128,256]{2,1,0:T(8,128)(2,1)}, bf16[127,128,256]{2,1,0:T(8,128)(2,1)S(1)}, u32[]{:S(2)}) copy-start(bf16[127,128,256]{2,1,0:T(8,128)(2,1)S(1)} %unbatch.1.matrices) | copy-start | bytes 24969220

commit v2 on v1

v2 whole, which is shorter than its diff:
```python
import jax, jax.numpy as jnp, functools
from jax import lax
from jax.sharding import PartitionSpec as P
from jax.experimental import pallas as pl
from jax.experimental.pallas import tpu as pltpu
NT = (((1,), (1,)), ((), ()))
SM = pl.BlockSpec(memory_space=pltpu.SMEM)
VM = pl.BlockSpec(memory_space=pltpu.VMEM)
ANY = pl.BlockSpec(memory_space=pl.ANY)
PITCH = 136
f32 = jnp.float32
bf16 = jnp.bfloat16

def split(x):
    hi = x.astype(bf16)
    return hi, (x - hi.astype(f32)).astype(bf16)

def stack(x):
    hi, lo = split(x)
    return jnp.concatenate([hi, lo], axis=0)

def fold(x):
    half = x.shape[0] // 2
    return x[:half] + x[half:]

def both(x):
    return x + pltpu.roll(x, 64, 1)

def low_lanes(shape):
    return lax.broadcasted_iota(jnp.int32, shape, 1) < 64

def up_body(basis, values, moves, up, trans, rows):
    leaves = basis.shape[0]
    columns = values.shape[0]
    nodes = moves.shape[2]

    @pl.loop(0, 64, unroll=4)
    def _(r):
        block = jnp.transpose(moves[r])
        rows[pl.ds(pl.multiple_of(r * PITCH, 8), nodes)] = jnp.concatenate([block, block], axis=1)

    left = low_lanes((64, 128))

    @pl.loop(0, nodes, unroll=4)
    def _(n):
        x = rows[pl.ds(n, 64, stride=PITCH), :]
        hi = x.astype(bf16).astype(f32)
        trans[n] = jnp.where(left, hi, x - hi).astype(bf16)

    half = low_lanes((columns, 128))

    def leaf_up(i):
        v = stack(values[:, pl.ds(pl.multiple_of(i * 128, 128), 128)])
        return both(fold(lax.dot_general(v, stack(basis[i]), NT, preferred_element_type=f32)))

    @pl.loop(0, leaves // 2, unroll=4)
    def _(p):
        up[p] = jnp.where(half, leaf_up(2 * p), leaf_up(2 * p + 1))

    def lift(tile, row):
        t = jnp.concatenate([trans[row], trans[row + 1]], axis=0)
        return both(fold(jnp.dot(stack(tile), t, preferred_element_type=f32)))

    def pair(tile_a, tile_b, row):
        return jnp.where(half, lift(tile_a, row), lift(tile_b, row + 2))

    start, row, width = 0, 0, leaves
    while width > 16:
        after = start + width // 2

        @pl.loop(0, width // 16)
        def _(g, start=start, row=row, after=after):
            made = []
            for p in range(4):
                q = 4 * g + p
                made.append(pair(up[start + 2 * q], up[start + 2 * q + 1], row + 4 * q))
            for p in range(4):
                up[after + 4 * g + p] = made[p]

        start, row, width = after, row + width, width // 2
    tiles = [up[start + p] for p in range(width // 2)]
    while width > 1:
        after = start + width // 2
        if width >= 4:
            tiles = [pair(tiles[2 * p], tiles[2 * p + 1], row + 4 * p) for p in range(width // 4)]
        else:
            tiles = [lift(tiles[0], row)]
        if after < leaves - 1:
            for p, tile in enumerate(tiles):
                up[after + p] = tile
        start, row, width = after, row + width, width // 2
    share = both(fold(jnp.dot(stack(tiles[0])[:, 0:64], trans[row], preferred_element_type=f32)))
    up[leaves - 1] = jnp.where(half, tiles[0], share)


def up_pass(basis, values, moves):
    leaves = basis.shape[0]
    columns = values.shape[0]
    nodes = moves.shape[2]
    return pl.pallas_call(
        up_body,
        out_shape=(
            jax.ShapeDtypeStruct((leaves, columns, 128), f32),
            jax.ShapeDtypeStruct((nodes + 1, 64, 128), bf16),
        ),
        in_specs=[VM, VM, VM],
        out_specs=(VM, VM),
        scratch_shapes=[pltpu.VMEM((64 * PITCH, 128), f32)],
        compiler_params=pltpu.CompilerParams(vmem_limit_bytes=24 << 20),
        cost_estimate=pl.CostEstimate(flops=400_000_000, bytes_accessed=8_000_000, transcendentals=0),
        name="up_pass",
    )(basis, values, moves)


CHUNK = 16


def unbatch_body(matrices, out, held, rows, made, in_sem, out_sem):
    nodes = matrices.shape[3]
    reads = [pltpu.make_async_copy(matrices.at[k], held.at[k], in_sem.at[k]) for k in range(4)]
    for read in reads:
        read.start()
    for h in range(2):
        reads[2 * h].wait()
        reads[2 * h + 1].wait()

        @pl.loop(0, 64, unroll=4)
        def _(r, h=h):
            x = jnp.concatenate([held[2 * h, r], held[2 * h + 1, r]], axis=0)
            rows[pl.ds(pl.multiple_of((h * 64 + r) * PITCH, 8), nodes)] = jnp.transpose(x)

    writes = []
    for begin in range(0, nodes, CHUNK):
        size = min(CHUNK, nodes - begin)

        def one(n):
            for h in range(2):
                hi, lo = split(rows[pl.ds(h * 64 * PITCH + n, 64, stride=PITCH), :])
                made[n, 0:64, 128 * h : 128 * h + 128] = hi
                made[n, 64:128, 128 * h : 128 * h + 128] = lo

        if size == CHUNK:
            pl.loop(begin, begin + size, unroll=4)(one)
        else:
            for n in range(begin, begin + size):
                one(n)
        at = pl.ds(begin, size)
        writes.append(pltpu.make_async_copy(made.at[at], out.at[at], out_sem.at[begin // CHUNK]))
        writes[-1].start()
    for write in writes:
        write.wait()


def unbatch(matrices):
    nodes = matrices.shape[3]
    return pl.pallas_call(
        unbatch_body,
        out_shape=jax.ShapeDtypeStruct((nodes, 128, 256), bf16),
        in_specs=[ANY],
        out_specs=ANY,
        scratch_shapes=[
            pltpu.VMEM(matrices.shape, f32),
            pltpu.VMEM((2 * 64 * PITCH, 128), f32),
            pltpu.VMEM((nodes, 128, 256), bf16),
            pltpu.SemaphoreType.DMA((4,)),
            pltpu.SemaphoreType.DMA((-(-nodes // CHUNK),)),
        ],
        compiler_params=pltpu.CompilerParams(vmem_limit_bytes=36 << 20),
        cost_estimate=pl.CostEstimate(flops=100_000_000, bytes_accessed=17_000_000, transcendentals=0),
        name="unbatch",
    )(matrices)


def top_body(place, partners, first, moves, matrices, parent, up, block, sem):
    spot = place[0]
    columns = first.shape[1]
    copies = []
    width, row = 32, 0
    for level in range(4):
        index = row + spot // (2 << level)
        copies.append(pltpu.make_async_copy(matrices.at[index], block.at[level], sem.at[level]))
        copies[-1].start()
        row, width = row + width, width // 2
    half = low_lanes((columns, 128))
    up[0:16] = first[...]
    def lift(tile, r):
        t = jnp.concatenate([moves[r], moves[r + 1]], axis=0)
        hi, lo = split(t)
        x = stack(up[tile])
        z = fold(jnp.dot(x, hi, preferred_element_type=f32)) + jnp.dot(x[:columns], lo, preferred_element_type=f32)
        return jnp.concatenate([z, z], axis=1)
    tile0, row, width = 0, 0, 32
    tiles, rows = [], []
    while width >= 4:
        tiles.append(tile0)
        rows.append(row)
        nxt = tile0 + width // 2
        if width > 4:
            for p in range(width // 4):
                up[nxt + p] = jnp.where(half, lift(tile0 + 2 * p, row + 4 * p), lift(tile0 + 2 * p + 1, row + 4 * p + 2))
        tile0, row, width = nxt, row + width, width // 2
    def push(d, r):
        hi, lo = split(moves[r])
        x = stack(d)
        return fold(lax.dot_general(x, hi, NT, preferred_element_type=f32)) + lax.dot_general(x[:columns], lo, NT, preferred_element_type=f32)
    down = jnp.zeros((columns, 64), f32)
    down = push(down, row + spot // 32)
    for level in range(3, -1, -1):
        index = rows[level] + spot // (2 << level)
        down = push(down, index)
        copies[level].wait()
        for k in range(4):
            p = partners[index * 4 + k]
            tile = up[tiles[level] + p // 2]
            x = stack(jnp.where(p % 2 == 0, tile, pltpu.roll(tile, 64, 1))[:, 0:64])
            hi, lo = split(block[level, k])
            down = down + fold(lax.dot_general(x, hi, NT, preferred_element_type=f32)) + lax.dot_general(x[:columns], lo, NT, preferred_element_type=f32)
    parent[...] = jnp.concatenate([down, down], axis=1)

def top_pass(place, partners, first, moves, matrices):
    columns = first.shape[1]
    return pl.pallas_call(
        top_body,
        out_shape=jax.ShapeDtypeStruct((columns, 128), f32),
        in_specs=[SM, SM, VM, VM, pl.BlockSpec(memory_space=pl.ANY)],
        out_specs=VM,
        scratch_shapes=[pltpu.VMEM((32, columns, 128), f32), pltpu.VMEM((4, 4, 64, 64), f32), pltpu.SemaphoreType.DMA((4,))],
        compiler_params=pltpu.CompilerParams(vmem_limit_bytes=16 << 20),
        cost_estimate=pl.CostEstimate(flops=50_000_000, bytes_accessed=2_000_000, transcendentals=0),
        name="top_pass",
    )(place, partners, first, moves, matrices)


def couple_body(codes, low, own, high, matrices, far, gather, held, sem):
    leaves = own.shape[0]
    columns = own.shape[1]
    nodes = matrices.shape[0]
    read = pltpu.make_async_copy(matrices, held, sem)
    read.start()
    half = low_lanes((columns, 128))
    left = low_lanes((2 * columns, 128))
    for side, ref in enumerate((low, own, high)):

        @pl.loop(0, leaves, unroll=16)
        def _(t, side=side, ref=ref):
            x = ref[t]
            gather[0, side * leaves + t] = stack(x)
            gather[1, side * leaves + t] = stack(pltpu.roll(x, 64, 1))

    read.wait()

    def pick(n, k, side):
        code = codes[4 * n + k]
        return gather[(code & 1) ^ side, code >> 1]

    def one(n):
        x = jnp.concatenate(
            [
                jnp.where(left, pick(n, 0, 0), pick(n, 1, 1)),
                jnp.where(left, pick(n, 2, 0), pick(n, 3, 1)),
            ],
            axis=1,
        )
        return both(fold(lax.dot_general(x, held[n], NT, preferred_element_type=f32)))

    @pl.loop(0, leaves - 1, unroll=7)
    def _(t):
        far[t] = jnp.where(half, one(2 * t), one(2 * t + 1))

    far[leaves - 1] = one(nodes - 1)


def couple_pass(codes, low, own, high, matrices):
    leaves, columns, _ = own.shape
    return pl.pallas_call(
        couple_body,
        out_shape=jax.ShapeDtypeStruct((leaves, columns, 128), f32),
        in_specs=[SM, VM, VM, VM, ANY],
        out_specs=VM,
        scratch_shapes=[
            pltpu.VMEM((2, 3 * leaves, 2 * columns, 128), bf16),
            pltpu.VMEM(matrices.shape, bf16),
            pltpu.SemaphoreType.DMA,
        ],
        compiler_params=pltpu.CompilerParams(vmem_limit_bytes=28 << 20),
        cost_estimate=pl.CostEstimate(flops=400_000_000, bytes_accessed=12_000_000, transcendentals=0),
        name="couple_pass",
    )(codes, low, own, high, matrices)


def down_body(core, parent, far, trans, basis, mine, given, out, held):
    leaves = basis.shape[0]
    columns = out.shape[0]
    half = low_lanes((columns, 128))

    def push(d, row, tile):
        t = jnp.concatenate([trans[row], trans[row + 1]], axis=0)
        return fold(lax.dot_general(stack(d), t, NT, preferred_element_type=f32)) + far[tile]

    def spread(tile):
        turned = pltpu.roll(tile, 64, 1)
        return jnp.where(half, tile, turned), jnp.where(half, turned, tile)

    last = leaves - 1
    t = trans[2 * last]
    d = fold(
        lax.dot_general(
            stack(parent[...]), jnp.concatenate([t, t], axis=0), NT, preferred_element_type=f32
        )
    )
    sources = [d + far[last]]
    start, width = last, 1
    while width < 16:
        start = start - max(1, width)
        made = [push(d, 2 * (start + i), start + i) for i, d in enumerate(sources)]
        sources = [d for tile in made for d in spread(tile)]
        width = 2 * width
    for i, tile in enumerate(made):
        held[i] = tile
    first = start - width

    @pl.loop(0, len(made), unroll=2)
    def _(i):
        results = []
        for j, d in enumerate(spread(held[i])):
            above = 2 * i + j
            for u, e in enumerate(spread(push(d, 2 * (first + above), first + above))):
                tile = 2 * above + u
                for w, x in enumerate(spread(push(e, 2 * tile, tile))):
                    leaf = 2 * tile + w
                    results.append(
                        (leaf, fold(jnp.dot(stack(x), stack(basis[leaf]), preferred_element_type=f32)))
                    )
        for leaf, x in results:
            out[:, pl.ds(pl.multiple_of(leaf * 128, 128), 128)] = x

    size = mine.shape[1]
    out[:, pl.ds(pl.multiple_of(core[0] * size, size), size)] += mine[...]
    out[:, pl.ds(pl.multiple_of((1 - core[0]) * size, size), size)] += given[...]


def down_pass(core, parent, far, trans, basis, mine, given):
    leaves = basis.shape[0]
    columns = parent.shape[0]
    return pl.pallas_call(
        down_body,
        out_shape=jax.ShapeDtypeStruct((columns, leaves * 128), f32),
        in_specs=[SM] + [VM] * 6,
        out_specs=VM,
        scratch_shapes=[pltpu.VMEM((8, columns, 128), f32)],
        compiler_params=pltpu.CompilerParams(vmem_limit_bytes=20 << 20),
        cost_estimate=pl.CostEstimate(flops=200_000_000, bytes_accessed=7_000_000, transcendentals=0),
        name="down_pass",
    )(core, parent, far, trans, basis, mine, given)


near_weight = 0.1
smoothing = 0.0025
SLOTS = 28
PAIR = 2

def near_body(unroll, kinds, lists, counts, targets, *refs):
    sources, refs = refs[:kinds], refs[kinds:]
    begin = None
    if kinds == 4:
        begin, refs = refs[0], refs[1:]
    mine, other, columns_of, total, weights, places = refs
    leaves = mine.shape[1] // 128
    width = sources[0].shape[1] // 128
    chunks = kinds // 2
    core = counts[leaves]
    for c in range(chunks):
        near_ref, far_ref = sources[2 * c], sources[2 * c + 1]
        lower = 0 if chunks == 1 or c == 1 else core * (leaves // 8)
        upper = width // 8 if chunks == 1 or c == 0 else (core + 1) * (leaves // 8)

        @pl.loop(lower, upper)
        def _(g, c=c, near_ref=near_ref, far_ref=far_ref):
            for u in range(8):
                j = 8 * g + u
                at = pl.ds(pl.multiple_of(j * 128, 128), 128)
                x = near_weight * jnp.concatenate([near_ref[0:32, at], far_ref[0:32, at]], axis=0)
                weights[c * width + j] = stack(x)
                places[c * width + j, 0:3] = near_ref[32:35, at] if chunks == 2 else targets[:, at]

    weights[chunks * width] = jnp.zeros(weights.shape[1:], bf16)
    places[chunks * width] = jnp.zeros(places.shape[1:], f32)
    blank = jnp.zeros((5, 128), f32)

    @pl.loop(0, leaves // 16)
    def _(g):
        rows = []
        for u in range(16):
            at = pl.ds(pl.multiple_of((core * leaves + 16 * g + u) * 128, 128), 128)
            rows += [targets[:, at], blank]
        t = jnp.transpose(jnp.concatenate(rows, axis=0))
        for u in range(16):
            for c in range(3):
                columns_of[16 * g + u, c] = jnp.broadcast_to(t[:, 8 * u + c : 8 * u + c + 1], (128, 128))
            total[16 * g + u] = jnp.zeros((128, 128), f32)

    items = lax.fori_loop(
        0, leaves, lambda i, s: s + jnp.maximum((counts[i] + PAIR - 1) // PAIR, 1), jnp.int32(0)
    )

    def block(leaf, slot):
        kernels, parts = [], []
        for u in range(PAIR):
            j = lists[leaf * SLOTS + slot + u]
            s = places[j]
            d = columns_of[leaf, 0] - s[0:1]
            squared = d * d + smoothing
            d = columns_of[leaf, 1] - s[1:2]
            squared = squared + d * d
            d = columns_of[leaf, 2] - s[2:3]
            squared = squared + d * d
            kernels += split(lax.rsqrt(squared))
            x = weights[j]
            parts += [x, x]
        return lax.dot_general(
            jnp.concatenate(kernels, axis=1),
            jnp.concatenate(parts, axis=1),
            NT,
            preferred_element_type=f32,
        )

    def step(b, carry):
        leaf, slot = carry
        made = []
        for u in range(unroll):
            place = jnp.where(b * unroll + u < items, leaf, leaves)
            made.append((place, block(leaf, slot)))
            done = slot + PAIR >= counts[leaf]
            leaf = jnp.where(done, jnp.minimum(leaf + 1, leaves - 1), leaf)
            slot = jnp.where(done, 0, slot + PAIR)
        for place, x in made:
            total[place] += x
        return leaf, slot

    lax.fori_loop(0, (items + unroll - 1) // unroll, step, (jnp.int32(0), jnp.int32(0)))

    @pl.loop(0, leaves, unroll=8)
    def _(leaf):
        at = pl.ds(pl.multiple_of(leaf * 128, 128), 128)
        x = jnp.transpose(both(total[leaf]))
        if begin is None:
            mine[:, at] = x[0:32]
            other[:, at] = x[32:64]
        else:
            mine[:, at] = begin[0:32, at] + x[0:32]
            other[:, at] = begin[32:64, at] + x[32:64]


def near_pass(unroll, lists, counts, targets, sources, begin=None):
    leaves = lists.shape[0] // SLOTS
    held = 64 * (len(sources) // 2) + 1
    side = jax.ShapeDtypeStruct((32, leaves * 128), f32)
    extra = [] if begin is None else list(begin)
    if begin is not None:
        extra = [jnp.concatenate(begin, axis=0)]
    return pl.pallas_call(
        functools.partial(near_body, unroll, len(sources)),
        out_shape=(side, side),
        in_specs=[SM, SM] + [VM] * (1 + len(sources) + len(extra)),
        out_specs=(VM, VM),
        scratch_shapes=[
            pltpu.VMEM((leaves, 3, 128, 128), f32),
            pltpu.VMEM((leaves + 1, 128, 128), f32),
            pltpu.VMEM((held, 128, 128), bf16),
            pltpu.VMEM((held, 8, 128), f32),
        ],
        compiler_params=pltpu.CompilerParams(vmem_limit_bytes=40 << 20),
        cost_estimate=pl.CostEstimate(flops=1_000, bytes_accessed=1_000, transcendentals=0),
        name="near_pass",
    )(lists, counts, targets, *sources, *extra)


def arranged(picked, leaf_ids, empty):
    slots = picked.shape[1]
    before = jnp.arange(slots)[:, None] < jnp.arange(slots)[None, :]
    rank = jnp.sum(jnp.where(picked[:, :, None] & before[None], 1, 0), axis=1)
    to = jnp.arange(SLOTS)[None, None, :]
    here = picked[:, :, None] & (rank[:, :, None] == to)
    found = jnp.sum(jnp.where(here, leaf_ids[:, :, None], 0), axis=1)
    count = jnp.sum(picked.astype(jnp.int32), axis=1)
    lists = jnp.where(jnp.arange(SLOTS)[None, :] < count[:, None], found, empty)
    return lists.astype(jnp.int32).reshape(-1), count


def partner_codes(partners, position, leaves):
    spans, starts = [], []
    width, tile = leaves, 0
    while width >= 1:
        spans += [width] * width
        starts += [2 * tile] * width
        tile, width = tile + max(1, width // 2), width // 2
    spans = jnp.array(spans, jnp.int32)[:, None]
    starts = jnp.array(starts, jnp.int32)[:, None]
    local = partners - position * spans
    side = jnp.where(local < 0, 0, jnp.where(local < spans, 1, 2))
    return (side * (2 * leaves) + starts + local - (side - 1) * spans).reshape(-1)


def local(
    points,
    values,
    near_list,
    near_count,
    basis,
    transfer,
    coupling,
    partners,
    transfer_top,
    coupling_top,
    partners_top,
):
    leaves = basis.shape[0]
    position = lax.axis_index("leaf")
    core = lax.axis_index("rhs")
    count = lax.axis_size("leaf")
    forward = [(i, i + 1) for i in range(count - 1)]
    backward = [(target, source) for source, target in forward]
    swap = [(0, 1), (1, 0)]
    packed = jnp.concatenate([values, points], axis=0)
    low = lax.ppermute(packed, "leaf", forward)
    high = lax.ppermute(packed, "leaf", backward)
    across = lax.ppermute(values, "rhs", swap)

    half = leaves // 2
    chosen = lax.dynamic_slice_in_dim(near_list, core * half, half, 0) - position * leaves
    live = lax.dynamic_slice_in_dim(near_count, core * half, half, 0)
    alive = jnp.arange(chosen.shape[1])[None, :] < live[:, None]
    inside = (chosen >= 0) & (chosen < leaves)
    near_ids, near_live = arranged(alive & inside, chosen, leaves)
    outside_ids = jnp.where(chosen < 0, chosen + leaves, chosen)
    far_ids, far_live = arranged(alive & ~inside, outside_ids, 2 * leaves)
    near_live = jnp.concatenate([near_live, core[None]]).astype(jnp.int32)
    far_live = jnp.concatenate([far_live, core[None]]).astype(jnp.int32)
    codes = partner_codes(partners, position, leaves)

    def exchange(x, bit):
        return lax.ppermute(x, "leaf", [(i, i ^ (1 << bit)) for i in range(count)])

    def ordered(x, y, bit, axis):
        return jnp.where(
            (position >> bit) & 1 == 0,
            jnp.concatenate([x, y], axis),
            jnp.concatenate([y, x], axis),
        )

    after = lax.optimization_barrier
    up, trans = up_pass(basis, values, transfer.transpose(1, 2, 0))
    up_low = lax.ppermute(up, "leaf", forward)
    up_high = lax.ppermute(up, "leaf", backward)
    near_ids, up = after((near_ids, up))
    begin = near_pass(8, near_ids, near_live, points, (values, across))
    low, high, coupling, begin = after((low, high, coupling, begin))
    low_across = lax.ppermute(low, "rhs", swap)
    high_across = lax.ppermute(high, "rhs", swap)
    matrices = unbatch(coupling.transpose(1, 2, 3, 0))
    far_ids, up_low, up_high, matrices = after((far_ids, up_low, up_high, matrices))
    sibling = jnp.where(position % 2 == 0, up_high[leaves - 1, :, 64:], up_low[leaves - 1, :, 64:])
    level = up[leaves - 1, :, 64:] + sibling
    pair = exchange(level, 1)
    mine, other = near_pass(8, far_ids, far_live, points, (low, low_across, high, high_across), begin)
    pair, mine, other = after((pair, mine, other))
    level = ordered(level, pair, 1, 1)[None]
    for bit in range(2, 5):
        level = ordered(level, exchange(level, bit), bit, 0)
    pair = exchange(level, 5)
    given = lax.ppermute(other, "rhs", swap)
    codes, level, mine = after((codes, level, mine))
    far = couple_pass(codes, up_low, up, up_high, matrices)
    pair, far = after((pair, far))
    level = ordered(level, pair, 5, 0)
    parent = top_pass(
        position[None].astype(jnp.int32), partners_top.reshape(-1), level, transfer_top, coupling_top
    )
    return down_pass(core[None].astype(jnp.int32), parent, far, trans, basis, mine, given)


def solution(mesh):
    placed = (
        P(None, "leaf"),
        P("rhs", "leaf"),
        P("leaf", None),
        P("leaf"),
        P("leaf", None, None),
        P("leaf", None, None),
        P("leaf", None, None, None),
        P("leaf", None),
        P(),
        P(),
        P(),
    )
    return jax.shard_map(
        local, mesh=mesh, in_specs=placed, out_specs=P("rhs", "leaf"), check_vma=False
    )
```

time: 199 us -> 139 us (0.70)
  the two profiles are of different devices: /device:TPU:33 before, /device:TPU:0 now
where the time goes in v2:
time: 139 us; the launch traced here: 138 us
  Pallas kernels  74 us (53%)
  starting transfers between devices  29.7 us (21%)
  local copies, waits for them, and re-layouts  22.9 us (16%)
  waiting for transfers between devices  8.14 us (6%)
  other arithmetic  2.75 us (2%)
    pallas_call x2, Pallas kernels, near_pass(): pl.pallas_call(functools.partial(near_body, unroll, len(sources)), out_sh...  30.5 us
    unnamed x44, local copies, waits for them, and re-layouts  21.4 us
    ppermute x5, starting transfers between devices, exchange(): return lax.ppermute(x, 'leaf', [(i, i ^ 1 << bit) for i in range(count)])  15.6 us
    pallas_call x1, Pallas kernels, up_pass(): pl.pallas_call(up_body, out_shape=(jax.ShapeDtypeStruct((leaves, columns,...  11.2 us
    pallas_call x1, Pallas kernels, down_pass(): pl.pallas_call(down_body, out_shape=jax.ShapeDtypeStruct((columns, leaves...  11.2 us
    pallas_call x1, Pallas kernels, couple_pass(): pl.pallas_call(couple_body, out_shape=jax.ShapeDtypeStruct((leaves, colum...  9.32 us
    pallas_call x1, Pallas kernels, unbatch(): pl.pallas_call(unbatch_body, out_shape=jax.ShapeDtypeStruct((nodes, 128,...  8.19 us
    ppermute x5, waiting for transfers between devices, exchange(): return lax.ppermute(x, 'leaf', [(i, i ^ 1 << bit) for i in range(count)])  8.12 us
  transfers between devices with their start and end apart: 13, of which 3 were waited for; matrix products, arithmetic and copies ran while one was open for 5% of the time, Pallas kernels for 46%

profile of v2, /device:TPU:0, one launch (start us, length us, event | category | flops | bytes accessed | tf_op | source)
XLA Modules:
  0.0 137.9 jit_solution(7963953761733072214)
XLA Ops:
  0.0 2.4 %constant_dynamic-update-slice_fusion.1 = f32[35,8192]{1,0:T(8,128)} fusion(f32[32,8192]{1,0:T(8,128)} %refs_0_.1), kind=kLoop, calls=%fused_computation.29 | loop fusion | bytes 2097152
  2.4 0.7 constant_dynamic-update-slice_fusion
  3.1 4.8 %collective-permute-start.2 = (f32[35,8192]{1,0:T(8,128)}, f32[35,8192]{1,0:T(8,128)}, u32[]{:S(2)}, u32[]{:S(2)}) collective-permute-start(f32[35,8192]{1,0:T(8,128)} %constant_dynamic-update-slice_fusion), channel_id=1, source_target_pairs={{0,2},{2,4},{4,6},{6,8},{8,10},{10,12},{12,14},{14,16},{16,18},{18... | collective-permute-start | bytes 3440648 | tf_op jit(solution)/shard_map/ppermute | solution.py:525
  7.9 1.3 collective-permute-start.3
  9.2 1.6 %copy-done.4 = f32[64,64,128]{2,1,0:T(8,128)S(1)} copy-done((f32[64,64,128]{2,1,0:T(8,128)S(1)}, f32[64,64,128]{2,1,0:T(8,128)}, u32[]{:S(2)}) %copy-start.4) | copy-done | bytes 2097176
  10.8 1.6 %copy-done.7 = f32[127,64,64]{0,2,1:T(8,128)S(1)} copy-done((f32[127,64,64]{0,2,1:T(8,128)S(1)}, f32[127,64,64]{0,2,1:T(8,128)}, u32[]{:S(2)}) %copy-start.7) | copy-done | bytes 2080792
  12.4 11.2 %up_pass.1 = (f32[64,32,128]{2,1,0:T(8,128)}, bf16[128,64,128]{2,1,0:T(8,128)(2,1)S(1)}) custom-call(f32[64,64,128]{2,1,0:T(8,128)S(1)} %copy-done.4, f32[32,8192]{1,0:T(8,128)S(1)} %copy-done.2, f32[64,64,127]{2,1,0:T(8,128)S(1)} %bitcast.7), custom_call_target="tpu_custom_call" | custom-call | flops 400000000 | bytes 8000000 | tf_op jit(solution)/shard_map/up_pass/pallas_call | solution.py:100
  23.6 5.5 %collective-permute-start = (f32[64,32,128]{2,1,0:T(8,128)}, f32[64,32,128]{2,1,0:T(8,128)}, u32[]{:S(2)}, u32[]{:S(2)}) collective-permute-start(f32[64,32,128]{2,1,0:T(8,128)} %get-tuple-element.31.own), channel_id=1, source_target_pairs={{0,2},{2,4},{4,6},{6,8},{8,10},{10,12},{12,14},{14,16},{16,18},{18... | collective-permute-start | bytes 3145736 | tf_op jit(solution)/shard_map/ppermute | solution.py:553
  29.1 1.3 collective-permute-start.1
  30.4 0.1 dynamic_slice.6
  30.5 0.1 convert_reduce_fusion.1
  30.6 0.3 select_reduce_fusion.3
  30.9 0.1 copy.30
  31.0 0.5 select_reduce_fusion.2
  31.6 0.1 select_n.120.lists
  31.7 0.1 copy.31
  31.8 0.1 pad_add_fusion.counts
  31.8 17.9 %near_pass.2 = (f32[32,4096]{1,0:T(8,128)S(1)}, f32[32,4096]{1,0:T(8,128)S(1)}) custom-call(s32[896]{0:T(1024)S(1)} %select_n.120.lists, s32[33]{0:T(128)S(1)} %pad_add_fusion.counts, f32[3,8192]{1,0:T(4,128)S(1)} %copy-done.9, f32[32,8192]{1,0:T(8,128)S(1)} %copy-done.2, f32[32,8192]{1,0:T(8,128)} %collective-permute-done.4.refs_1_), custom_call_target="tpu_custom_call" | custom-call | flops 1000 | bytes 1000 | tf_op jit(solution)/shard_map/near_pass/pallas_call | solution.py:461
  49.7 0.8 copy-done.10
  50.5 0.8 copy-done.12
  51.4 0.5 collective-permute-start.7
  51.9 0.5 select_reduce_fusion
  52.4 0.1 fusion.5
  52.5 0.1 select_n.127.lists
  52.6 0.1 pad_add_fusion.1.counts
  52.7 3.4 %copy-done.3 = f32[127,4,64,64]{0,3,2,1:T(8,128)S(1)} copy-done((f32[127,4,64,64]{0,3,2,1:T(8,128)S(1)}, f32[127,4,64,64]{0,3,2,1:T(8,128)}, u32[]{:S(2)}) %copy-start.3) | copy-done | bytes 8323096
  56.1 8.2 %unbatch.1.matrices = bf16[127,128,256]{2,1,0:T(8,128)(2,1)S(1)} custom-call(f32[4,64,64,127]{3,2,1,0:T(8,128)S(1)} %bitcast.6), custom_call_target="tpu_custom_call" | custom-call | flops 100000000 | bytes 17000000 | tf_op jit(solution)/shard_map/unbatch/pallas_call | solution.py:156
  64.3 3.2 %copy-done = bf16[127,128,256]{2,1,0:T(8,128)(2,1)} copy-done((bf16[127,128,256]{2,1,0:T(8,128)(2,1)}, bf16[127,128,256]{2,1,0:T(8,128)(2,1)S(1)}, u32[]{:S(2)}) %copy-start) | copy-done | bytes 8323096
  67.5 0.8 select_add_fusion
  68.5 12.6 %near_pass.3 = (f32[32,4096]{1,0:T(8,128)S(1)}, f32[32,4096]{1,0:T(8,128)S(1)}) custom-call(s32[896]{0:T(1024)S(1)} %select_n.127.lists, s32[33]{0:T(128)S(1)} %pad_add_fusion.1.counts, f32[3,8192]{1,0:T(4,128)S(1)} %copy-done.9, f32[35,8192]{1,0:T(8,128)} %collective-permute-done.2.refs_0_, f32[35,8192]{1,0:T(8,128)} %collective-permute-done.6.refs_1_, ...), custom_call_target="tpu_custom_call" | custom-call | flops 1000 | bytes 1000 | tf_op jit(solution)/shard_map/near_pass/pallas_call | solution.py:461
  81.2 0.8 copy-done.14
  82.0 0.1 maximum_select_fusion.4
  82.1 3.7 %collective-permute-done.8 = f32[1,32,128]{2,1,0:T(8,128)S(1)} collective-permute-done((f32[1,32,128]{2,1,0:T(8,128)S(1)}, f32[1,32,128]{2,1,0:T(8,128)S(1)}, u32[]{:S(2)}, u32[]{:S(2)}) %collective-permute-start.8) | collective-permute-done | bytes 16416 | tf_op jit(solution)/shard_map/ppermute | solution.py:542
  85.8 3.1 %collective-permute-start.9 = (f32[2,32,128]{2,1,0:T(8,128)S(1)}, f32[2,32,128]{2,1,0:T(8,128)S(1)}, u32[]{:S(2)}, u32[]{:S(2)}) collective-permute-start(f32[2,32,128]{2,1,0:T(8,128)S(1)} %maximum_select_fusion.3), channel_id=1, source_target_pairs={{0,16},{2,18},{4,20},{6,22},{8,24},{10,26},{12,28},{14,30},{16,0},... | collective-permute-start | bytes 98312 | tf_op jit(solution)/shard_map/ppermute | solution.py:542
  89.0 0.8 collective-permute-start.12
  89.8 1.5 %collective-permute-done.9 = f32[2,32,128]{2,1,0:T(8,128)S(1)} collective-permute-done((f32[2,32,128]{2,1,0:T(8,128)S(1)}, f32[2,32,128]{2,1,0:T(8,128)S(1)}, u32[]{:S(2)}, u32[]{:S(2)}) %collective-permute-start.9) | collective-permute-done | bytes 32800 | tf_op jit(solution)/shard_map/ppermute | solution.py:542
  91.3 12.1 %collective-permute-start.10 = (f32[4,32,128]{2,1,0:T(8,128)S(1)}, f32[4,32,128]{2,1,0:T(8,128)S(1)}, u32[]{:S(2)}, u32[]{:S(2)}) collective-permute-start(f32[4,32,128]{2,1,0:T(8,128)S(1)} %maximum_select_fusion.2), channel_id=1, source_target_pairs={{0,32},{2,34},{4,36},{6,38},{8,40},{10,42},{12,44},{14,46},{16,48}... | collective-permute-start | bytes 196616 | tf_op jit(solution)/shard_map/ppermute | solution.py:542
  103.4 2.9 %collective-permute-done.10 = f32[4,32,128]{2,1,0:T(8,128)S(1)} collective-permute-done((f32[4,32,128]{2,1,0:T(8,128)S(1)}, f32[4,32,128]{2,1,0:T(8,128)S(1)}, u32[]{:S(2)}, u32[]{:S(2)}) %collective-permute-start.10) | collective-permute-done | bytes 65568 | tf_op jit(solution)/shard_map/ppermute | solution.py:542
  106.3 0.3 collective-permute-start.11
  106.6 0.1 copy.29
  106.8 0.1 reshape.98.codes
  106.9 0.1 copy.28
  107.0 0.1 reshape.97.partners
  107.1 3.4 %copy-done.1 = bf16[127,128,256]{2,1,0:T(8,128)(2,1)S(1)} copy-done((bf16[127,128,256]{2,1,0:T(8,128)(2,1)S(1)}, bf16[127,128,256]{2,1,0:T(8,128)(2,1)}, u32[]{:S(2)}) %copy-start.1) | copy-done | bytes 8323096
  110.5 9.3 %couple_pass.1.far = f32[64,32,128]{2,1,0:T(8,128)S(1)} custom-call(s32[508]{0:T(512)S(1)} %reshape.98.codes, f32[64,32,128]{2,1,0:T(8,128)} %collective-permute-done.low, f32[64,32,128]{2,1,0:T(8,128)} %get-tuple-element.31.own, f32[64,32,128]{2,1,0:T(8,128)} %collective-permute-done.1.high, bf16[127,128,256]{2,1,0:T(8,128)(2,1)S(1)} %copy-done.1), custom_call_target="tpu_custom_call" | custom-call | flops 400000000 | bytes 12000000 | tf_op jit(solution)/shard_map/couple_pass/pallas_call | solution.py:275
  119.9 3.2 %copy-done.6 = f32[60,4,64,64]{3,2,1,0:T(8,128)S(1)} copy-done((f32[60,4,64,64]{3,2,1,0:T(8,128)S(1)}, f32[60,4,64,64]{3,2,1,0:T(8,128)}, u32[]{:S(2)}) %copy-start.6) | copy-done | bytes 3932184
  123.1 3.6 %top_pass.1.parent = f32[32,128]{1,0:T(8,128)S(1)} custom-call(s32[1]{0:T(128)} %bitcast.1.place, s32[240]{0:T(256)S(1)} %reshape.97.partners, f32[16,32,128]{2,1,0:T(8,128)S(1)} %maximum_select_fusion.first, f32[62,64,64]{2,1,0:T(8,128)S(1)} %copy-done.8, f32[60,4,64,64]{3,2,1,0:T(8,128)S(1)} %copy-done.6), custom_call_target="tpu_custom_call" | custom-call | flops 50000000 | bytes 2000000 | tf_op jit(solution)/shard_map/top_pass/pallas_call | solution.py:222
  126.7 11.2 %down_pass.1 = f32[32,8192]{1,0:T(8,128)} custom-call(s32[1]{0:T(128)} %bitcast.core, f32[32,128]{1,0:T(8,128)S(1)} %top_pass.1.parent, f32[64,32,128]{2,1,0:T(8,128)S(1)} %couple_pass.1.far, bf16[128,64,128]{2,1,0:T(8,128)(2,1)S(1)} %get-tuple-element.52.trans, f32[64,64,128]{2,1,0:T(8,128)S(1)} %copy-done.5, f32[32,4096]{1,0:T(8,128)S(1)} %get-tuple-element.53.mine, ...), custom_call_target="tpu_custom_call" | custom-call | flops 200000000 | bytes 7000000 | tf_op jit(solution)/shard_map/down_pass/pallas_call | solution.py:345
  (57 shorter events, 0.4 us)
Async XLA Ops:
  0.0 9.2 %copy-start.2 = (f32[32,8192]{1,0:T(8,128)S(1)}, f32[32,8192]{1,0:T(8,128)}, u32[]{:S(2)}) copy-start(f32[32,8192]{1,0:T(8,128)} %refs_0_.1) | copy-start | bytes 3145732
  0.0 2.4 %copy-start.9 = (f32[3,8192]{1,0:T(4,128)S(1)}, f32[3,8192]{1,0:T(4,128)}, u32[]{:S(2)}) copy-start(f32[3,8192]{1,0:T(4,128)} %targets.3) | copy-start | bytes 294916
  0.0 31.8 %collective-permute-start.4 = (f32[32,8192]{1,0:T(8,128)}, f32[32,8192]{1,0:T(8,128)}, u32[]{:S(2)}, u32[]{:S(2)}) collective-permute-start(f32[32,8192]{1,0:T(8,128)} %refs_0_.1), channel_id=1, source_target_pairs={{0,1},{1,0},{2,3},{3,2},{4,5},{5,4},{6,7},{7,6},{8,9},{9,8},{10,11... | collective-permute-start | bytes 3145736 | tf_op jit(solution)/shard_map/ppermute | solution.py:527
  3.1 48.3 %collective-permute-start.2 = (f32[35,8192]{1,0:T(8,128)}, f32[35,8192]{1,0:T(8,128)}, u32[]{:S(2)}, u32[]{:S(2)}) collective-permute-start(f32[35,8192]{1,0:T(8,128)} %constant_dynamic-update-slice_fusion), channel_id=1, source_target_pairs={{0,2},{2,4},{4,6},{6,8},{8,10},{10,12},{12,14},{14,16},{16,18},{18... | collective-permute-start | bytes 3440648 | tf_op jit(solution)/shard_map/ppermute | solution.py:525
  7.9 43.5 %collective-permute-start.3 = (f32[35,8192]{1,0:T(8,128)}, f32[35,8192]{1,0:T(8,128)}, u32[]{:S(2)}, u32[]{:S(2)}) collective-permute-start(f32[35,8192]{1,0:T(8,128)} %constant_dynamic-update-slice_fusion), channel_id=1, source_target_pairs={{2,0},{4,2},{6,4},{8,6},{10,8},{12,10},{14,12},{16,14},{18,16},{20... | collective-permute-start | bytes 3440648 | tf_op jit(solution)/shard_map/ppermute | solution.py:526
  9.2 1.6 %copy-start.4 = (f32[64,64,128]{2,1,0:T(8,128)S(1)}, f32[64,64,128]{2,1,0:T(8,128)}, u32[]{:S(2)}) copy-start(f32[64,64,128]{2,1,0:T(8,128)} %basis.3) | copy-start | bytes 6291460
  10.8 1.6 %copy-start.7 = (f32[127,64,64]{0,2,1:T(8,128)S(1)}, f32[127,64,64]{0,2,1:T(8,128)}, u32[]{:S(2)}) copy-start(f32[127,64,64]{0,2,1:T(8,128)} %param.18) | copy-start | bytes 6242308
  12.3 18.0 %copy-start.20 = (s32[64]{0:T(128)S(1)}, s32[64]{0:T(128)}, u32[]{:S(2)}) copy-start(s32[64]{0:T(128)} %param.16) | copy-start | bytes 772
  12.4 18.1 %copy-start.15 = (s32[64,27]{0,1:T(8,128)S(1)}, s32[64,27]{0,1:T(8,128)}, u32[]{:S(2)}) copy-start(s32[64,27]{0,1:T(8,128)} %param.15) | copy-start | bytes 20740
  23.6 43.9 %collective-permute-start = (f32[64,32,128]{2,1,0:T(8,128)}, f32[64,32,128]{2,1,0:T(8,128)}, u32[]{:S(2)}, u32[]{:S(2)}) collective-permute-start(f32[64,32,128]{2,1,0:T(8,128)} %get-tuple-element.31.own), channel_id=1, source_target_pairs={{0,2},{2,4},{4,6},{6,8},{8,10},{10,12},{12,14},{14,16},{16,18},{18... | collective-permute-start | bytes 3145736 | tf_op jit(solution)/shard_map/ppermute | solution.py:553
  29.1 38.4 %collective-permute-start.1 = (f32[64,32,128]{2,1,0:T(8,128)}, f32[64,32,128]{2,1,0:T(8,128)}, u32[]{:S(2)}, u32[]{:S(2)}) collective-permute-start(f32[64,32,128]{2,1,0:T(8,128)} %get-tuple-element.31.own), channel_id=1, source_target_pairs={{2,0},{4,2},{6,4},{8,6},{10,8},{12,10},{14,12},{16,14},{18,16},{20... | collective-permute-start | bytes 3145736 | tf_op jit(solution)/shard_map/ppermute | solution.py:554
  49.7 0.8 copy-start.10
  50.5 0.8 copy-start.12
  51.4 17.1 %collective-permute-start.6 = (f32[35,8192]{1,0:T(8,128)}, f32[35,8192]{1,0:T(8,128)}, u32[]{:S(2)}, u32[]{:S(2)}) collective-permute-start(f32[35,8192]{1,0:T(8,128)} %collective-permute-done.2.refs_0_), channel_id=1, source_target_pairs={{0,1},{1,0},{2,3},{3,2},{4,5},{5,4},{6,7},{7,6},{8,9},{9,8},{10,11... | collective-permute-start | bytes 3440648 | tf_op jit(solution)/shard_map/ppermute | solution.py:558
  51.4 17.1 %collective-permute-start.7 = (f32[35,8192]{1,0:T(8,128)}, f32[35,8192]{1,0:T(8,128)}, u32[]{:S(2)}, u32[]{:S(2)}) collective-permute-start(f32[35,8192]{1,0:T(8,128)} %collective-permute-done.3.refs_2_), channel_id=1, source_target_pairs={{0,1},{1,0},{2,3},{3,2},{4,5},{5,4},{6,7},{7,6},{8,9},{9,8},{10,11... | collective-permute-start | bytes 3440648 | tf_op jit(solution)/shard_map/ppermute | solution.py:559
  52.7 3.4 %copy-start.3 = (f32[127,4,64,64]{0,3,2,1:T(8,128)S(1)}, f32[127,4,64,64]{0,3,2,1:T(8,128)}, u32[]{:S(2)}) copy-start(f32[127,4,64,64]{0,3,2,1:T(8,128)} %param.19) | copy-start | bytes 24969220
  56.1 12.3 %copy-start.11 = (f32[32,4096]{1,0:T(8,128)S(1)}, f32[32,4096]{1,0:T(8,128)}, u32[]{:S(2)}) copy-start(f32[32,4096]{1,0:T(8,128)} %copy-done.10) | copy-start | bytes 1572868
  56.1 12.3 %copy-start.13 = (f32[32,4096]{1,0:T(8,128)S(1)}, f32[32,4096]{1,0:T(8,128)}, u32[]{:S(2)}) copy-start(f32[32,4096]{1,0:T(8,128)} %copy-done.12) | copy-start | bytes 1572868
  64.3 3.2 %copy-start = (bf16[127,128,256]{2,1,0:T(8,128)(2,1)}, bf16[127,128,256]{2,1,0:T(8,128)(2,1)S(1)}, u32[]{:S(2)}) copy-start(bf16[127,128,256]{2,1,0:T(8,128)(2,1)S(1)} %unbatch.1.matrices) | copy-start | bytes 24969220
  68.3 13.7 %collective-permute-start.5 = (f32[32,64]{1,0:T(8,128)S(1)}, f32[32,64]{1,0:T(8,128)S(1)}, u32[]{:S(2)}, u32[]{:S(2)}) collective-permute-start(f32[32,64]{1,0:T(8,128)S(1)} %bitcast.8), channel_id=1, source_target_pairs={{0,4},{2,6},{4,0},{6,2},{8,12},{10,14},{12,8},{14,10},{16,20},{18,... | collective-permute-start | bytes 24584 | tf_op jit(solution)/shard_map/ppermute | solution.py:542
  68.5 34.9 %copy-start.18 = (s32[127]{0:T(128)S(1)}, s32[127]{0:T(128)}, u32[]{:S(2)}) copy-start(s32[127]{0:T(128)} %constant.46.clone) | copy-start | bytes 1528
  68.5 38.1 %copy-start.17 = (s32[127,4]{0,1:T(4,128)S(1)}, s32[127,4]{0,1:T(4,128)}, u32[]{:S(2)}) copy-start(s32[127,4]{0,1:T(4,128)} %param.20) | copy-start | bytes 6100
  68.5 38.1 %copy-start.19 = (s32[127]{0:T(128)S(1)}, s32[127]{0:T(128)}, u32[]{:S(2)}) copy-start(s32[127]{0:T(128)} %constant.47.clone) | copy-start | bytes 1528
  68.5 38.4 %copy-start.16 = (s32[60,4]{0,1:T(4,128)S(1)}, s32[60,4]{0,1:T(4,128)}, u32[]{:S(2)}) copy-start(s32[60,4]{0,1:T(4,128)} %param.23) | copy-start | bytes 2884
  81.2 0.8 copy-start.14
  82.1 3.8 %collective-permute-start.8 = (f32[1,32,128]{2,1,0:T(8,128)S(1)}, f32[1,32,128]{2,1,0:T(8,128)S(1)}, u32[]{:S(2)}, u32[]{:S(2)}) collective-permute-start(f32[1,32,128]{2,1,0:T(8,128)S(1)} %maximum_select_fusion.4), channel_id=1, source_target_pairs={{0,8},{2,10},{4,12},{6,14},{8,0},{10,2},{12,4},{14,6},{16,24},{18,... | collective-permute-start | bytes 49160 | tf_op jit(solution)/shard_map/ppermute | solution.py:542
  85.8 5.4 %collective-permute-start.9 = (f32[2,32,128]{2,1,0:T(8,128)S(1)}, f32[2,32,128]{2,1,0:T(8,128)S(1)}, u32[]{:S(2)}, u32[]{:S(2)}) collective-permute-start(f32[2,32,128]{2,1,0:T(8,128)S(1)} %maximum_select_fusion.3), channel_id=1, source_target_pairs={{0,16},{2,18},{4,20},{6,22},{8,24},{10,26},{12,28},{14,30},{16,0},... | collective-permute-start | bytes 98312 | tf_op jit(solution)/shard_map/ppermute | solution.py:542
  89.0 37.7 %collective-permute-start.12 = (f32[32,4096]{1,0:T(8,128)}, f32[32,4096]{1,0:T(8,128)S(1)}, u32[]{:S(2)}, u32[]{:S(2)}) collective-permute-start(f32[32,4096]{1,0:T(8,128)} %copy-done.14), channel_id=1, source_target_pairs={{0,1},{1,0},{2,3},{3,2},{4,5},{5,4},{6,7},{7,6},{8,9},{9,8},{10,11... | collective-permute-start | bytes 1572872 | tf_op jit(solution)/shard_map/ppermute | solution.py:571
  91.3 15.0 %collective-permute-start.10 = (f32[4,32,128]{2,1,0:T(8,128)S(1)}, f32[4,32,128]{2,1,0:T(8,128)S(1)}, u32[]{:S(2)}, u32[]{:S(2)}) collective-permute-start(f32[4,32,128]{2,1,0:T(8,128)S(1)} %maximum_select_fusion.2), channel_id=1, source_target_pairs={{0,32},{2,34},{4,36},{6,38},{8,40},{10,42},{12,44},{14,46},{16,48}... | collective-permute-start | bytes 196616 | tf_op jit(solution)/shard_map/ppermute | solution.py:542
  106.3 13.5 %collective-permute-start.11 = (f32[8,32,128]{2,1,0:T(8,128)S(1)}, f32[8,32,128]{2,1,0:T(8,128)S(1)}, u32[]{:S(2)}, u32[]{:S(2)}) collective-permute-start(f32[8,32,128]{2,1,0:T(8,128)S(1)} %maximum_select_fusion.1), channel_id=1, source_target_pairs={{0,64},{2,66},{4,68},{6,70},{8,72},{10,74},{12,76},{14,78},{16,80}... | collective-permute-start | bytes 393224 | tf_op jit(solution)/shard_map/ppermute | solution.py:542
  107.1 3.4 %copy-start.1 = (bf16[127,128,256]{2,1,0:T(8,128)(2,1)S(1)}, bf16[127,128,256]{2,1,0:T(8,128)(2,1)}, u32[]{:S(2)}) copy-start(bf16[127,128,256]{2,1,0:T(8,128)(2,1)} %copy-done) | copy-start | bytes 24969220
  110.5 9.4 %copy-start.8 = (f32[62,64,64]{2,1,0:T(8,128)S(1)}, f32[62,64,64]{2,1,0:T(8,128)}, u32[]{:S(2)}) copy-start(f32[62,64,64]{2,1,0:T(8,128)} %moves.1) | copy-start | bytes 3047428
  119.9 3.2 %copy-start.6 = (f32[60,4,64,64]{3,2,1,0:T(8,128)S(1)}, f32[60,4,64,64]{3,2,1,0:T(8,128)}, u32[]{:S(2)}) copy-start(f32[60,4,64,64]{3,2,1,0:T(8,128)} %matrices.1) | copy-start | bytes 11796484
  123.1 3.6 %copy-start.5 = (f32[64,64,128]{2,1,0:T(8,128)S(1)}, f32[64,64,128]{2,1,0:T(8,128)}, u32[]{:S(2)}) copy-start(f32[64,64,128]{2,1,0:T(8,128)} %basis.3) | copy-start | bytes 6291460

commit v3 on v2

--- a/solution.py
+++ b/solution.py
@@ -6,7 +6,7 @@
 NT = (((1,), (1,)), ((), ()))
 SM = pl.BlockSpec(memory_space=pltpu.SMEM)
 VM = pl.BlockSpec(memory_space=pltpu.VMEM)
-ANY = pl.BlockSpec(memory_space=pl.ANY)
+HBM = pl.BlockSpec(memory_space=pltpu.HBM)
 PITCH = 136
 f32 = jnp.float32
 bf16 = jnp.bfloat16
@@ -29,15 +29,25 @@
 def low_lanes(shape):
     return lax.broadcasted_iota(jnp.int32, shape, 1) < 64
 
-def up_body(basis, values, moves, up, trans, rows):
+def up_body(basis_hbm, values_hbm, moves_hbm, up, trans, rows, basis, values, moves, sem):
     leaves = basis.shape[0]
     columns = values.shape[0]
     nodes = moves.shape[2]
-
-    @pl.loop(0, 64, unroll=4)
-    def _(r):
-        block = jnp.transpose(moves[r])
-        rows[pl.ds(pl.multiple_of(r * PITCH, 8), nodes)] = jnp.concatenate([block, block], axis=1)
+    reads = []
+    for i in range(4):
+        at = pl.ds(16 * i, 16)
+        reads.append(pltpu.make_async_copy(moves_hbm.at[at], moves.at[at], sem.at[i]))
+    reads.append(pltpu.make_async_copy(values_hbm, values, sem.at[4]))
+    reads.append(pltpu.make_async_copy(basis_hbm, basis, sem.at[5]))
+    for read in reads:
+        read.start()
+    for i in range(4):
+        reads[i].wait()
+
+        @pl.loop(16 * i, 16 * i + 16, unroll=4)
+        def _(r):
+            block = jnp.transpose(moves[r])
+            rows[pl.ds(pl.multiple_of(r * PITCH, 8), nodes)] = jnp.concatenate([block, block], axis=1)
 
     left = low_lanes((64, 128))
 
@@ -48,6 +58,9 @@
         trans[n] = jnp.where(left, hi, x - hi).astype(bf16)
 
     half = low_lanes((columns, 128))
+
+    for read in reads[4:]:
+        read.wait()
 
     def leaf_up(i):
         v = stack(values[:, pl.ds(pl.multiple_of(i * 128, 128), 128)])
@@ -103,70 +116,50 @@
             jax.ShapeDtypeStruct((leaves, columns, 128), f32),
             jax.ShapeDtypeStruct((nodes + 1, 64, 128), bf16),
         ),
-        in_specs=[VM, VM, VM],
+        in_specs=[HBM, HBM, HBM],
         out_specs=(VM, VM),
-        scratch_shapes=[pltpu.VMEM((64 * PITCH, 128), f32)],
-        compiler_params=pltpu.CompilerParams(vmem_limit_bytes=24 << 20),
+        scratch_shapes=[
+            pltpu.VMEM((64 * PITCH, 128), f32),
+            pltpu.VMEM(basis.shape, f32),
+            pltpu.VMEM(values.shape, f32),
+            pltpu.VMEM(moves.shape, f32),
+            pltpu.SemaphoreType.DMA((6,)),
+        ],
+        compiler_params=pltpu.CompilerParams(vmem_limit_bytes=56 << 20),
         cost_estimate=pl.CostEstimate(flops=400_000_000, bytes_accessed=8_000_000, transcendentals=0),
         name="up_pass",
     )(basis, values, moves)
 
 
-CHUNK = 16
-
-
-def unbatch_body(matrices, out, held, rows, made, in_sem, out_sem):
+def unbatch_body(part, matrices, out, rows):
     nodes = matrices.shape[3]
-    reads = [pltpu.make_async_copy(matrices.at[k], held.at[k], in_sem.at[k]) for k in range(4)]
-    for read in reads:
-        read.start()
-    for h in range(2):
-        reads[2 * h].wait()
-        reads[2 * h + 1].wait()
-
-        @pl.loop(0, 64, unroll=4)
-        def _(r, h=h):
-            x = jnp.concatenate([held[2 * h, r], held[2 * h + 1, r]], axis=0)
-            rows[pl.ds(pl.multiple_of((h * 64 + r) * PITCH, 8), nodes)] = jnp.transpose(x)
-
-    writes = []
-    for begin in range(0, nodes, CHUNK):
-        size = min(CHUNK, nodes - begin)
-
-        def one(n):
-            for h in range(2):
-                hi, lo = split(rows[pl.ds(h * 64 * PITCH + n, 64, stride=PITCH), :])
-                made[n, 0:64, 128 * h : 128 * h + 128] = hi
-                made[n, 64:128, 128 * h : 128 * h + 128] = lo
-
-        if size == CHUNK:
-            pl.loop(begin, begin + size, unroll=4)(one)
-        else:
-            for n in range(begin, begin + size):
-                one(n)
-        at = pl.ds(begin, size)
-        writes.append(pltpu.make_async_copy(made.at[at], out.at[at], out_sem.at[begin // CHUNK]))
-        writes[-1].start()
-    for write in writes:
-        write.wait()
-
-
-def unbatch(matrices):
+
+    @pl.loop(0, 64, unroll=4)
+    def _(r):
+        x = jnp.concatenate([matrices[2 * part, r], matrices[2 * part + 1, r]], axis=0)
+        rows[pl.ds(pl.multiple_of(r * PITCH, 8), nodes)] = jnp.transpose(x)
+
+    def one(n):
+        hi, lo = split(rows[pl.ds(n, 64, stride=PITCH), :])
+        out[n, 0:64] = hi
+        out[n, 64:128] = lo
+
+    whole = nodes // 8 * 8
+    pl.loop(0, whole, unroll=8)(one)
+    for n in range(whole, nodes):
+        one(n)
+
+
+def unbatch(matrices, part):
     nodes = matrices.shape[3]
     return pl.pallas_call(
-        unbatch_body,
-        out_shape=jax.ShapeDtypeStruct((nodes, 128, 256), bf16),
-        in_specs=[ANY],
-        out_specs=ANY,
-        scratch_shapes=[
-            pltpu.VMEM(matrices.shape, f32),
-            pltpu.VMEM((2 * 64 * PITCH, 128), f32),
-            pltpu.VMEM((nodes, 128, 256), bf16),
-            pltpu.SemaphoreType.DMA((4,)),
-            pltpu.SemaphoreType.DMA((-(-nodes // CHUNK),)),
-        ],
-        compiler_params=pltpu.CompilerParams(vmem_limit_bytes=36 << 20),
-        cost_estimate=pl.CostEstimate(flops=100_000_000, bytes_accessed=17_000_000, transcendentals=0),
+        functools.partial(unbatch_body, part),
+        out_shape=jax.ShapeDtypeStruct((nodes, 128, 128), bf16),
+        in_specs=[VM],
+        out_specs=VM,
+        scratch_shapes=[pltpu.VMEM((64 * PITCH, 128), f32)],
+        compiler_params=pltpu.CompilerParams(vmem_limit_bytes=20 << 20),
+        cost_estimate=pl.CostEstimate(flops=50_000_000, bytes_accessed=9_000_000, transcendentals=0),
         name="unbatch",
     )(matrices)
 
@@ -222,21 +215,19 @@
     return pl.pallas_call(
         top_body,
         out_shape=jax.ShapeDtypeStruct((columns, 128), f32),
-        in_specs=[SM, SM, VM, VM, pl.BlockSpec(memory_space=pl.ANY)],
+        in_specs=[SM, SM, VM, VM, HBM],
         out_specs=VM,
         scratch_shapes=[pltpu.VMEM((32, columns, 128), f32), pltpu.VMEM((4, 4, 64, 64), f32), pltpu.SemaphoreType.DMA((4,))],
-        compiler_params=pltpu.CompilerParams(vmem_limit_bytes=16 << 20),
+        compiler_params=pltpu.CompilerParams(vmem_limit_bytes=56 << 20),
         cost_estimate=pl.CostEstimate(flops=50_000_000, bytes_accessed=2_000_000, transcendentals=0),
         name="top_pass",
     )(place, partners, first, moves, matrices)
 
 
-def couple_body(codes, low, own, high, matrices, far, gather, held, sem):
+def couple_body(codes, low, own, high, first, second, far, gather):
     leaves = own.shape[0]
     columns = own.shape[1]
-    nodes = matrices.shape[0]
-    read = pltpu.make_async_copy(matrices, held, sem)
-    read.start()
+    nodes = first.shape[0]
     half = low_lanes((columns, 128))
     left = low_lanes((2 * columns, 128))
     for side, ref in enumerate((low, own, high)):
@@ -246,8 +237,6 @@
             x = ref[t]
             gather[0, side * leaves + t] = stack(x)
             gather[1, side * leaves + t] = stack(pltpu.roll(x, 64, 1))
-
-    read.wait()
 
     def pick(n, k, side):
         code = codes[4 * n + k]
@@ -261,7 +250,8 @@
             ],
             axis=1,
         )
-        return both(fold(lax.dot_general(x, held[n], NT, preferred_element_type=f32)))
+        m = jnp.concatenate([first[n], second[n]], axis=1)
+        return both(fold(lax.dot_general(x, m, NT, preferred_element_type=f32)))
 
     @pl.loop(0, leaves - 1, unroll=7)
     def _(t):
@@ -270,22 +260,18 @@
     far[leaves - 1] = one(nodes - 1)
 
 
-def couple_pass(codes, low, own, high, matrices):
+def couple_pass(codes, low, own, high, first, second):
     leaves, columns, _ = own.shape
     return pl.pallas_call(
         couple_body,
         out_shape=jax.ShapeDtypeStruct((leaves, columns, 128), f32),
-        in_specs=[SM, VM, VM, VM, ANY],
+        in_specs=[SM] + [VM] * 5,
         out_specs=VM,
-        scratch_shapes=[
-            pltpu.VMEM((2, 3 * leaves, 2 * columns, 128), bf16),
-            pltpu.VMEM(matrices.shape, bf16),
-            pltpu.SemaphoreType.DMA,
-        ],
-        compiler_params=pltpu.CompilerParams(vmem_limit_bytes=28 << 20),
+        scratch_shapes=[pltpu.VMEM((2, 3 * leaves, 2 * columns, 128), bf16)],
+        compiler_params=pltpu.CompilerParams(vmem_limit_bytes=24 << 20),
         cost_estimate=pl.CostEstimate(flops=400_000_000, bytes_accessed=12_000_000, transcendentals=0),
         name="couple_pass",
-    )(codes, low, own, high, matrices)
+    )(codes, low, own, high, first, second)
 
 
 def down_body(core, parent, far, trans, basis, mine, given, out, held):
@@ -348,7 +334,7 @@
         in_specs=[SM] + [VM] * 6,
         out_specs=VM,
         scratch_shapes=[pltpu.VMEM((8, columns, 128), f32)],
-        compiler_params=pltpu.CompilerParams(vmem_limit_bytes=20 << 20),
+        compiler_params=pltpu.CompilerParams(vmem_limit_bytes=14 << 20),
         cost_estimate=pl.CostEstimate(flops=200_000_000, bytes_accessed=7_000_000, transcendentals=0),
         name="down_pass",
     )(core, parent, far, trans, basis, mine, given)
@@ -359,15 +345,14 @@
 SLOTS = 28
 PAIR = 2
 
-def near_body(unroll, kinds, lists, counts, targets, *refs):
-    sources, refs = refs[:kinds], refs[kinds:]
-    begin = None
-    if kinds == 4:
-        begin, refs = refs[0], refs[1:]
+def near_body(unroll, chunks, lists, counts, targets, *refs):
+    sources, refs = refs[: 2 * chunks], refs[2 * chunks :]
+    begin, spots = None, [targets]
+    if chunks == 2:
+        begin, spots, refs = refs[0:2], refs[2:4], refs[4:]
     mine, other, columns_of, total, weights, places = refs
     leaves = mine.shape[1] // 128
     width = sources[0].shape[1] // 128
-    chunks = kinds // 2
     core = counts[leaves]
     for c in range(chunks):
         near_ref, far_ref = sources[2 * c], sources[2 * c + 1]
@@ -379,9 +364,9 @@
             for u in range(8):
                 j = 8 * g + u
                 at = pl.ds(pl.multiple_of(j * 128, 128), 128)
-                x = near_weight * jnp.concatenate([near_ref[0:32, at], far_ref[0:32, at]], axis=0)
+                x = near_weight * jnp.concatenate([near_ref[:, at], far_ref[:, at]], axis=0)
                 weights[c * width + j] = stack(x)
-                places[c * width + j, 0:3] = near_ref[32:35, at] if chunks == 2 else targets[:, at]
+                places[c * width + j, 0:3] = spots[c][:, at]
 
     weights[chunks * width] = jnp.zeros(weights.shape[1:], bf16)
     places[chunks * width] = jnp.zeros(places.shape[1:], f32)
@@ -447,21 +432,20 @@
             mine[:, at] = x[0:32]
             other[:, at] = x[32:64]
         else:
-            mine[:, at] = begin[0:32, at] + x[0:32]
-            other[:, at] = begin[32:64, at] + x[32:64]
-
-
-def near_pass(unroll, lists, counts, targets, sources, begin=None):
+            mine[:, at] = begin[0][:, at] + x[0:32]
+            other[:, at] = begin[1][:, at] + x[32:64]
+
+
+def near_pass(unroll, lists, counts, targets, sources, begin=(), spots=()):
     leaves = lists.shape[0] // SLOTS
-    held = 64 * (len(sources) // 2) + 1
+    chunks = len(sources) // 2
+    held = chunks * (sources[0].shape[1] // 128) + 1
     side = jax.ShapeDtypeStruct((32, leaves * 128), f32)
-    extra = [] if begin is None else list(begin)
-    if begin is not None:
-        extra = [jnp.concatenate(begin, axis=0)]
+    arrays = (targets, *sources, *begin, *spots)
     return pl.pallas_call(
-        functools.partial(near_body, unroll, len(sources)),
+        functools.partial(near_body, unroll, chunks),
         out_shape=(side, side),
-        in_specs=[SM, SM] + [VM] * (1 + len(sources) + len(extra)),
+        in_specs=[SM, SM] + [VM] * len(arrays),
         out_specs=(VM, VM),
         scratch_shapes=[
             pltpu.VMEM((leaves, 3, 128, 128), f32),
@@ -469,10 +453,10 @@
             pltpu.VMEM((held, 128, 128), bf16),
             pltpu.VMEM((held, 8, 128), f32),
         ],
-        compiler_params=pltpu.CompilerParams(vmem_limit_bytes=40 << 20),
+        compiler_params=pltpu.CompilerParams(vmem_limit_bytes=24 << 20),
         cost_estimate=pl.CostEstimate(flops=1_000, bytes_accessed=1_000, transcendentals=0),
         name="near_pass",
-    )(lists, counts, targets, *sources, *extra)
+    )(lists, counts, *arrays)
 
 
 def arranged(picked, leaf_ids, empty):
@@ -521,9 +505,8 @@
     forward = [(i, i + 1) for i in range(count - 1)]
     backward = [(target, source) for source, target in forward]
     swap = [(0, 1), (1, 0)]
-    packed = jnp.concatenate([values, points], axis=0)
-    low = lax.ppermute(packed, "leaf", forward)
-    high = lax.ppermute(packed, "leaf", backward)
+    low = lax.ppermute(values, "leaf", forward)
+    high = lax.ppermute(values, "leaf", backward)
     across = lax.ppermute(values, "rhs", swap)
 
     half = leaves // 2
@@ -538,41 +521,52 @@
     far_live = jnp.concatenate([far_live, core[None]]).astype(jnp.int32)
     codes = partner_codes(partners, position, leaves)
 
-    def exchange(x, bit):
-        return lax.ppermute(x, "leaf", [(i, i ^ (1 << bit)) for i in range(count)])
-
-    def ordered(x, y, bit, axis):
-        return jnp.where(
-            (position >> bit) & 1 == 0,
-            jnp.concatenate([x, y], axis),
-            jnp.concatenate([y, x], axis),
-        )
+    def ring(x, stride):
+        spot = (position // stride) % 4
+        turned = []
+        for shift in range(3, 0, -1):
+            to = [(i, i + stride * ((i // stride + shift) % 4 - i // stride % 4)) for i in range(count)]
+            turned.append(lax.ppermute(x, "leaf", to))
+        return turned, spot
+
+    def in_order(turned, x, spot):
+        both_rounds = jnp.concatenate([*turned, x, *turned, x], axis=0)
+        return lax.dynamic_slice_in_dim(both_rounds, (3 - spot) * x.shape[0], 4 * x.shape[0], 0)
 
     after = lax.optimization_barrier
     up, trans = up_pass(basis, values, transfer.transpose(1, 2, 0))
     up_low = lax.ppermute(up, "leaf", forward)
     up_high = lax.ppermute(up, "leaf", backward)
+    spots = (lax.ppermute(points, "leaf", forward), lax.ppermute(points, "leaf", backward))
     near_ids, up = after((near_ids, up))
     begin = near_pass(8, near_ids, near_live, points, (values, across))
     low, high, coupling, begin = after((low, high, coupling, begin))
     low_across = lax.ppermute(low, "rhs", swap)
     high_across = lax.ppermute(high, "rhs", swap)
-    matrices = unbatch(coupling.transpose(1, 2, 3, 0))
-    far_ids, up_low, up_high, matrices = after((far_ids, up_low, up_high, matrices))
+    coupling = coupling.transpose(1, 2, 3, 0)
+    first = unbatch(coupling, 0)
+    far_ids, up_low, up_high, first = after((far_ids, up_low, up_high, first))
     sibling = jnp.where(position % 2 == 0, up_high[leaves - 1, :, 64:], up_low[leaves - 1, :, 64:])
     level = up[leaves - 1, :, 64:] + sibling
-    pair = exchange(level, 1)
-    mine, other = near_pass(8, far_ids, far_live, points, (low, low_across, high, high_across), begin)
-    pair, mine, other = after((pair, mine, other))
-    level = ordered(level, pair, 1, 1)[None]
-    for bit in range(2, 5):
-        level = ordered(level, exchange(level, bit), bit, 0)
-    pair = exchange(level, 5)
+    pair = lax.ppermute(level, "leaf", [(i, i ^ 2) for i in range(count)])
+    mine, other = near_pass(
+        8, far_ids, far_live, points, (low, low_across, high, high_across), begin, spots
+    )
+    pair, mine, other, coupling = after((pair, mine, other, coupling))
     given = lax.ppermute(other, "rhs", swap)
-    codes, level, mine = after((codes, level, mine))
-    far = couple_pass(codes, up_low, up, up_high, matrices)
-    pair, far = after((pair, far))
-    level = ordered(level, pair, 5, 0)
+    level = jnp.where(
+        position & 2 == 0,
+        jnp.concatenate([level, pair], axis=1),
+        jnp.concatenate([pair, level], axis=1),
+    )[None]
+    turned, spot = ring(level, 4)
+    second = unbatch(coupling, 1)
+    turned, codes, second = after((turned, codes, second))
+    level = in_order(turned, level, spot)
+    turned, spot = ring(level, 16)
+    far = couple_pass(codes, up_low, up, up_high, first, second)
+    turned, far = after((turned, far))
+    level = in_order(turned, level, spot)
     parent = top_pass(
         position[None].astype(jnp.int32), partners_top.reshape(-1), level, transfer_top, coupling_top
     )

time: 139 us -> 147 us (1.058)
  the two profiles are of different devices: /device:TPU:0 before, /device:TPU:5 now
where the time goes in v3:
time: 147 us; the launch traced here: 145 us
  Pallas kernels  64 us (44%)
  starting transfers between devices  51.8 us (35%)
  local copies, waits for them, and re-layouts  24.1 us (16%)
  other arithmetic  4.59 us (3%)
    unnamed x63, local copies, waits for them, and re-layouts  21.3 us
    pallas_call x2, Pallas kernels, near_pass(): pl.pallas_call(functools.partial(near_body, unroll, chunks), out_shape=(s...  21 us
    ppermute x6, starting transfers between devices, ring(): turned.append(lax.ppermute(x, 'leaf', to))  19 us
    pallas_call x1, Pallas kernels, up_pass(): pl.pallas_call(up_body, out_shape=(jax.ShapeDtypeStruct((leaves, columns,...  12.3 us
    pallas_call x1, Pallas kernels, down_pass(): pl.pallas_call(down_body, out_shape=jax.ShapeDtypeStruct((columns, leaves...  12.2 us
    pallas_call x1, Pallas kernels, couple_pass(): pl.pallas_call(couple_body, out_shape=jax.ShapeDtypeStruct((leaves, colum...  7.04 us
    pallas_call x2, Pallas kernels, unbatch(): pl.pallas_call(functools.partial(unbatch_body, part), out_shape=jax.Shape...  5.97 us
    ppermute x1, starting transfers between devices, local(): lax.ppermute(points, 'leaf', backward)  5.59 us
  transfers between devices with their start and end apart: 17, of which 0 were waited for; matrix products, arithmetic and copies ran while one was open for 4% of the time, Pallas kernels for 36%

profile of v3, /device:TPU:5, one launch (start us, length us, event | category | flops | bytes accessed | tf_op | source)
XLA Modules:
  0.0 145.1 jit_solution(11866420127417560892)
XLA Ops:
  0.0 0.8 collective-permute-start.4
  0.8 3.2 %collective-permute-start.2 = (f32[32,8192]{1,0:T(8,128)}, f32[32,8192]{1,0:T(8,128)}, u32[]{:S(2)}, u32[]{:S(2)}) collective-permute-start(f32[32,8192]{1,0:T(8,128)} %refs_0_.1), channel_id=1, source_target_pairs={{0,2},{2,4},{4,6},{6,8},{8,10},{10,12},{12,14},{14,16},{16,18},{18... | collective-permute-start | bytes 3145736 | tf_op jit(solution)/shard_map/ppermute | solution.py:508
  4.0 4.2 %collective-permute-start.3 = (f32[32,8192]{1,0:T(8,128)}, f32[32,8192]{1,0:T(8,128)}, u32[]{:S(2)}, u32[]{:S(2)}) collective-permute-start(f32[32,8192]{1,0:T(8,128)} %refs_0_.1), channel_id=1, source_target_pairs={{2,0},{4,2},{6,4},{8,6},{10,8},{12,10},{14,12},{16,14},{18,16},{20... | collective-permute-start | bytes 3145736 | tf_op jit(solution)/shard_map/ppermute | solution.py:509
  8.2 12.3 %up_pass.1 = (f32[64,32,128]{2,1,0:T(8,128)}, bf16[128,64,128]{2,1,0:T(8,128)(2,1)}) custom-call(f32[64,64,128]{2,1,0:T(8,128)} %basis.1, f32[32,8192]{1,0:T(8,128)} %refs_0_.1, f32[64,64,127]{2,1,0:T(8,128)} %bitcast.8), custom_call_target="tpu_custom_call" | custom-call | flops 400000000 | bytes 8000000 | tf_op jit(solution)/shard_map/up_pass/pallas_call | solution.py:113
  20.5 1.9 %collective-permute-start = (f32[64,32,128]{2,1,0:T(8,128)}, f32[64,32,128]{2,1,0:T(8,128)S(1)}, u32[]{:S(2)}, u32[]{:S(2)}) collective-permute-start(f32[64,32,128]{2,1,0:T(8,128)} %get-tuple-element.36.own), channel_id=1, source_target_pairs={{0,2},{2,4},{4,6},{6,8},{8,10},{10,12},{12,14},{14,16},{16,18},{18... | collective-permute-start | bytes 3145736 | tf_op jit(solution)/shard_map/ppermute | solution.py:538
  22.4 5.5 %collective-permute-start.1 = (f32[64,32,128]{2,1,0:T(8,128)}, f32[64,32,128]{2,1,0:T(8,128)S(1)}, u32[]{:S(2)}, u32[]{:S(2)}) collective-permute-start(f32[64,32,128]{2,1,0:T(8,128)} %get-tuple-element.36.own), channel_id=1, source_target_pairs={{2,0},{4,2},{6,4},{8,6},{10,8},{12,10},{14,12},{16,14},{18,16},{20... | collective-permute-start | bytes 3145736 | tf_op jit(solution)/shard_map/ppermute | solution.py:539
  28.1 0.3 select_reduce_fusion.3
  28.5 0.5 select_reduce_fusion.2
  29.3 10.5 %near_pass.2 = (f32[32,4096]{1,0:T(8,128)S(1)}, f32[32,4096]{1,0:T(8,128)S(1)}) custom-call(s32[896]{0:T(1024)S(1)} %select_n.103.lists, s32[33]{0:T(128)S(1)} %pad_add_fusion.counts, f32[3,8192]{1,0:T(4,128)S(1)} %copy-done.14, f32[32,8192]{1,0:T(8,128)S(1)} %copy-done.7, f32[32,8192]{1,0:T(8,128)} %collective-permute-done.4.refs_1_), custom_call_target="tpu_custom_call" | custom-call | flops 1000 | bytes 1000 | tf_op jit(solution)/shard_map/near_pass/pallas_call | solution.py:445
  39.8 0.8 copy-done.10
  40.6 0.8 copy-done.12
  41.4 1.9 %collective-permute-start.6 = (f32[32,8192]{1,0:T(8,128)}, f32[32,8192]{1,0:T(8,128)}, u32[]{:S(2)}, u32[]{:S(2)}) collective-permute-start(f32[32,8192]{1,0:T(8,128)} %collective-permute-done.2.refs_0_), channel_id=1, source_target_pairs={{0,1},{1,0},{2,3},{3,2},{4,5},{5,4},{6,7},{7,6},{8,9},{9,8},{10,11... | collective-permute-start | bytes 3145736 | tf_op jit(solution)/shard_map/ppermute | solution.py:544
  43.4 1.9 %collective-permute-start.8 = (f32[3,8192]{1,0:T(4,128)S(1)}, f32[3,8192]{1,0:T(4,128)S(1)}, u32[]{:S(2)}, u32[]{:S(2)}) collective-permute-start(f32[3,8192]{1,0:T(4,128)S(1)} %copy-done.14), channel_id=1, source_target_pairs={{0,2},{2,4},{4,6},{6,8},{8,10},{10,12},{12,14},{14,16},{16,18},{18... | collective-permute-start | bytes 294920 | tf_op jit(solution)/shard_map/ppermute | solution.py:540
  45.4 0.5 select_reduce_fusion
  46.1 0.6 broadcast_multiply_fusion
  46.7 3.4 %copy-done = f32[127,4,64,64]{0,3,2,1:T(8,128)S(1)} copy-done((f32[127,4,64,64]{0,3,2,1:T(8,128)S(1)}, f32[127,4,64,64]{0,3,2,1:T(8,128)}, u32[]{:S(2)}) %copy-start) | copy-done | bytes 8323096
  50.1 3.0 %unbatch.2.first = bf16[127,128,128]{2,1,0:T(8,128)(2,1)S(1)} custom-call(f32[4,64,64,127]{3,2,1,0:T(8,128)S(1)} %bitcast.6), custom_call_target="tpu_custom_call" | custom-call | flops 50000000 | bytes 9000000 | tf_op jit(solution)/shard_map/unbatch/pallas_call | solution.py:155
  53.1 2.0 %copy-done.2 = bf16[127,128,128]{2,1,0:T(8,128)(2,1)} copy-done((bf16[127,128,128]{2,1,0:T(8,128)(2,1)}, bf16[127,128,128]{2,1,0:T(8,128)(2,1)S(1)}, u32[]{:S(2)}) %copy-start.2) | copy-done | bytes 4161560
  55.1 5.6 %collective-permute-start.9 = (f32[3,8192]{1,0:T(4,128)S(1)}, f32[3,8192]{1,0:T(4,128)S(1)}, u32[]{:S(2)}, u32[]{:S(2)}) collective-permute-start(f32[3,8192]{1,0:T(4,128)S(1)} %copy-done.14), channel_id=1, source_target_pairs={{2,0},{4,2},{6,4},{8,6},{10,8},{12,10},{14,12},{16,14},{18,16},{20... | collective-permute-start | bytes 294920 | tf_op jit(solution)/shard_map/ppermute | solution.py:540
  60.7 0.7 select_add_fusion
  61.4 3.2 %collective-permute-start.5 = (f32[32,64]{1,0:T(8,128)}, f32[32,64]{1,0:T(8,128)}, u32[]{:S(2)}, u32[]{:S(2)}) collective-permute-start(f32[32,64]{1,0:T(8,128)} %bitcast.4), channel_id=1, source_target_pairs={{0,4},{2,6},{4,0},{6,2},{8,12},{10,14},{12,8},{14,10},{16,20},{18,... | collective-permute-start | bytes 24584 | tf_op jit(solution)/shard_map/ppermute | solution.py:551
  64.7 1.0 copy-done.11
  65.8 1.0 copy-done.13
  66.8 10.4 %near_pass.3 = (f32[32,4096]{1,0:T(8,128)S(1)}, f32[32,4096]{1,0:T(8,128)S(1)}) custom-call(s32[896]{0:T(1024)S(1)} %select_n.110.lists, s32[33]{0:T(128)S(1)} %pad_add_fusion.1.counts, f32[3,8192]{1,0:T(4,128)S(1)} %copy-done.14, f32[32,8192]{1,0:T(8,128)} %collective-permute-done.2.refs_0_, f32[32,8192]{1,0:T(8,128)} %collective-permute-done.6.refs_1_, ...), custom_call_target="tpu_custom_call" | custom-call | flops 1000 | bytes 1000 | tf_op jit(solution)/shard_map/near_pass/pallas_call | solution.py:445
  77.3 0.8 copy-done.15
  78.1 0.8 copy-done.18
  78.9 0.9 maximum_select_fusion
  79.8 2.2 %collective-permute-start.11 = (f32[1,32,128]{2,1,0:T(8,128)S(1)}, f32[1,32,128]{2,1,0:T(8,128)S(1)}, u32[]{:S(2)}, u32[]{:S(2)}) collective-permute-start(f32[1,32,128]{2,1,0:T(8,128)S(1)} %maximum_select_fusion), channel_id=1, source_target_pairs={{0,16},{2,18},{4,20},{6,22},{8,24},{10,26},{12,28},{14,30},{16,0},... | collective-permute-start | bytes 49160 | tf_op jit(solution)/shard_map/ppermute | solution.py:529
  82.0 0.7 multiply_subtract_fusion
  82.7 0.1 copy.31
  82.8 0.1 reshape.98.codes
  83.0 3.4 %copy-done.1 = f32[127,4,64,64]{0,3,2,1:T(8,128)S(1)} copy-done((f32[127,4,64,64]{0,3,2,1:T(8,128)S(1)}, f32[127,4,64,64]{0,3,2,1:T(8,128)}, u32[]{:S(2)}) %copy-start.1) | copy-done | bytes 8323096
  86.3 3.0 %unbatch.3.second = bf16[127,128,128]{2,1,0:T(8,128)(2,1)S(1)} custom-call(f32[4,64,64,127]{3,2,1,0:T(8,128)S(1)} %bitcast.7), custom_call_target="tpu_custom_call" | custom-call | flops 50000000 | bytes 9000000 | tf_op jit(solution)/shard_map/unbatch/pallas_call | solution.py:155
  89.3 2.0 %copy-done.4 = bf16[127,128,128]{2,1,0:T(8,128)(2,1)} copy-done((bf16[127,128,128]{2,1,0:T(8,128)(2,1)}, bf16[127,128,128]{2,1,0:T(8,128)(2,1)S(1)}, u32[]{:S(2)}) %copy-start.4) | copy-done | bytes 4161560
  91.5 0.6 constant_dynamic-slice_fusion.1
  92.1 16.2 %collective-permute-start.13 = (f32[4,32,128]{2,1,0:T(8,128)}, f32[4,32,128]{2,1,0:T(8,128)S(1)}, u32[]{:S(2)}, u32[]{:S(2)}) collective-permute-start(f32[4,32,128]{2,1,0:T(8,128)} %constant_dynamic-slice_fusion.1), channel_id=1, source_target_pairs={{0,96},{2,98},{4,100},{6,102},{8,104},{10,106},{12,108},{14,110},{... | collective-permute-start | bytes 196616 | tf_op jit(solution)/shard_map/ppermute | solution.py:529
  108.3 0.3 collective-permute-start.14
  108.6 0.3 collective-permute-start.15
  108.9 0.1 copy.28
  109.0 0.6 reshape.97.partners
  109.7 4.6 %collective-permute-start.16 = (f32[32,4096]{1,0:T(8,128)}, f32[32,4096]{1,0:T(8,128)}, u32[]{:S(2)}, u32[]{:S(2)}) collective-permute-start(f32[32,4096]{1,0:T(8,128)} %copy-done.18), channel_id=1, source_target_pairs={{0,1},{1,0},{2,3},{3,2},{4,5},{5,4},{6,7},{7,6},{8,9},{9,8},{10,11... | collective-permute-start | bytes 1572872 | tf_op jit(solution)/shard_map/ppermute | solution.py:556
  114.2 2.2 %copy-done.3 = bf16[127,128,128]{2,1,0:T(8,128)(2,1)S(1)} copy-done((bf16[127,128,128]{2,1,0:T(8,128)(2,1)S(1)}, bf16[127,128,128]{2,1,0:T(8,128)(2,1)}, u32[]{:S(2)}) %copy-start.3) | copy-done | bytes 4161560
  116.4 2.2 %copy-done.5 = bf16[127,128,128]{2,1,0:T(8,128)(2,1)S(1)} copy-done((bf16[127,128,128]{2,1,0:T(8,128)(2,1)S(1)}, bf16[127,128,128]{2,1,0:T(8,128)(2,1)}, u32[]{:S(2)}) %copy-start.5) | copy-done | bytes 4161560
  118.6 7.0 %couple_pass.1.far = f32[64,32,128]{2,1,0:T(8,128)S(1)} custom-call(s32[508]{0:T(512)S(1)} %reshape.98.codes, f32[64,32,128]{2,1,0:T(8,128)S(1)} %collective-permute-done.low, f32[64,32,128]{2,1,0:T(8,128)S(1)} %copy-done.9, f32[64,32,128]{2,1,0:T(8,128)S(1)} %collective-permute-done.1.high, bf16[127,128,128]{2,1,0:T(8,128)(2,1)S(1)} %copy-done.3, ...), custom_call_target="tpu_custom_call" | custom-call | flops 400000000 | bytes 12000000 | tf_op jit(solution)/shard_map/couple_pass/pallas_call | solution.py:265
  125.8 0.7 constant_dynamic-slice_fusion.first
  126.6 5.5 %top_pass.1.parent = f32[32,128]{1,0:T(8,128)} custom-call(s32[1]{0:T(128)} %bitcast.1.place, s32[240]{0:T(256)} %reshape.97.partners, f32[16,32,128]{2,1,0:T(8,128)} %constant_dynamic-slice_fusion.first, f32[62,64,64]{2,1,0:T(8,128)} %moves.1, f32[60,4,64,64]{3,2,1,0:T(8,128)} %matrices.1), custom_call_target="tpu_custom_call" | custom-call | flops 50000000 | bytes 2000000 | tf_op jit(solution)/shard_map/top_pass/pallas_call | solution.py:215
  132.2 0.7 copy-done.17
  132.9 12.2 %down_pass.1 = f32[32,8192]{1,0:T(8,128)} custom-call(s32[1]{0:T(128)} %bitcast.core, f32[32,128]{1,0:T(8,128)S(1)} %copy-done.17, f32[64,32,128]{2,1,0:T(8,128)S(1)} %couple_pass.1.far, bf16[128,64,128]{2,1,0:T(8,128)(2,1)S(1)} %copy-done.8, f32[64,64,128]{2,1,0:T(8,128)S(1)} %copy-done.6, f32[32,4096]{1,0:T(8,128)S(1)} %copy-done.16, ...), custom_call_target="tpu_custom_call" | custom-call | flops 200000000 | bytes 7000000 | tf_op jit(solution)/shard_map/down_pass/pallas_call | solution.py:331
  (83 shorter events, 1.2 us)
Async XLA Ops:
  0.0 46.1 %copy-start.22 = (s32[127]{0:T(128)S(1)}, s32[127]{0:T(128)}, u32[]{:S(2)}) copy-start(s32[127]{0:T(128)} %constant.78.clone) | copy-start | bytes 1528
  0.0 29.3 %copy-start.7 = (f32[32,8192]{1,0:T(8,128)S(1)}, f32[32,8192]{1,0:T(8,128)}, u32[]{:S(2)}) copy-start(f32[32,8192]{1,0:T(8,128)} %refs_0_.1) | copy-start | bytes 3145732
  0.0 27.9 %copy-start.23 = (s32[64]{0:T(128)S(1)}, s32[64]{0:T(128)}, u32[]{:S(2)}) copy-start(s32[64]{0:T(128)} %param.16) | copy-start | bytes 772
  0.0 28.0 %copy-start.19 = (s32[64,27]{0,1:T(8,128)S(1)}, s32[64,27]{0,1:T(8,128)}, u32[]{:S(2)}) copy-start(s32[64,27]{0,1:T(8,128)} %param.15) | copy-start | bytes 20740
  0.0 29.3 %copy-start.14 = (f32[3,8192]{1,0:T(4,128)S(1)}, f32[3,8192]{1,0:T(4,128)}, u32[]{:S(2)}) copy-start(f32[3,8192]{1,0:T(4,128)} %targets.3) | copy-start | bytes 294916
  0.0 29.2 %collective-permute-start.4 = (f32[32,8192]{1,0:T(8,128)}, f32[32,8192]{1,0:T(8,128)}, u32[]{:S(2)}, u32[]{:S(2)}) collective-permute-start(f32[32,8192]{1,0:T(8,128)} %refs_0_.1), channel_id=1, source_target_pairs={{0,1},{1,0},{2,3},{3,2},{4,5},{5,4},{6,7},{7,6},{8,9},{9,8},{10,11... | collective-permute-start | bytes 3145736 | tf_op jit(solution)/shard_map/ppermute | solution.py:510
  0.8 40.6 %collective-permute-start.2 = (f32[32,8192]{1,0:T(8,128)}, f32[32,8192]{1,0:T(8,128)}, u32[]{:S(2)}, u32[]{:S(2)}) collective-permute-start(f32[32,8192]{1,0:T(8,128)} %refs_0_.1), channel_id=1, source_target_pairs={{0,2},{2,4},{4,6},{6,8},{8,10},{10,12},{12,14},{14,16},{16,18},{18... | collective-permute-start | bytes 3145736 | tf_op jit(solution)/shard_map/ppermute | solution.py:508
  4.0 37.4 %collective-permute-start.3 = (f32[32,8192]{1,0:T(8,128)}, f32[32,8192]{1,0:T(8,128)}, u32[]{:S(2)}, u32[]{:S(2)}) collective-permute-start(f32[32,8192]{1,0:T(8,128)} %refs_0_.1), channel_id=1, source_target_pairs={{2,0},{4,2},{6,4},{8,6},{10,8},{12,10},{14,12},{16,14},{18,16},{20... | collective-permute-start | bytes 3145736 | tf_op jit(solution)/shard_map/ppermute | solution.py:509
  20.5 34.6 %collective-permute-start = (f32[64,32,128]{2,1,0:T(8,128)}, f32[64,32,128]{2,1,0:T(8,128)S(1)}, u32[]{:S(2)}, u32[]{:S(2)}) collective-permute-start(f32[64,32,128]{2,1,0:T(8,128)} %get-tuple-element.36.own), channel_id=1, source_target_pairs={{0,2},{2,4},{4,6},{6,8},{8,10},{10,12},{12,14},{14,16},{16,18},{18... | collective-permute-start | bytes 3145736 | tf_op jit(solution)/shard_map/ppermute | solution.py:538
  22.4 38.3 %collective-permute-start.1 = (f32[64,32,128]{2,1,0:T(8,128)}, f32[64,32,128]{2,1,0:T(8,128)S(1)}, u32[]{:S(2)}, u32[]{:S(2)}) collective-permute-start(f32[64,32,128]{2,1,0:T(8,128)} %get-tuple-element.36.own), channel_id=1, source_target_pairs={{2,0},{4,2},{6,4},{8,6},{10,8},{12,10},{14,12},{16,14},{18,16},{20... | collective-permute-start | bytes 3145736 | tf_op jit(solution)/shard_map/ppermute | solution.py:539
  39.8 0.8 copy-start.10
  40.6 0.8 copy-start.12
  41.4 23.3 %collective-permute-start.6 = (f32[32,8192]{1,0:T(8,128)}, f32[32,8192]{1,0:T(8,128)}, u32[]{:S(2)}, u32[]{:S(2)}) collective-permute-start(f32[32,8192]{1,0:T(8,128)} %collective-permute-done.2.refs_0_), channel_id=1, source_target_pairs={{0,1},{1,0},{2,3},{3,2},{4,5},{5,4},{6,7},{7,6},{8,9},{9,8},{10,11... | collective-permute-start | bytes 3145736 | tf_op jit(solution)/shard_map/ppermute | solution.py:544
  43.3 21.4 %collective-permute-start.7 = (f32[32,8192]{1,0:T(8,128)}, f32[32,8192]{1,0:T(8,128)}, u32[]{:S(2)}, u32[]{:S(2)}) collective-permute-start(f32[32,8192]{1,0:T(8,128)} %collective-permute-done.3.refs_2_), channel_id=1, source_target_pairs={{0,1},{1,0},{2,3},{3,2},{4,5},{5,4},{6,7},{7,6},{8,9},{9,8},{10,11... | collective-permute-start | bytes 3145736 | tf_op jit(solution)/shard_map/ppermute | solution.py:545
  43.4 21.3 %collective-permute-start.8 = (f32[3,8192]{1,0:T(4,128)S(1)}, f32[3,8192]{1,0:T(4,128)S(1)}, u32[]{:S(2)}, u32[]{:S(2)}) collective-permute-start(f32[3,8192]{1,0:T(4,128)S(1)} %copy-done.14), channel_id=1, source_target_pairs={{0,2},{2,4},{4,6},{6,8},{8,10},{10,12},{12,14},{14,16},{16,18},{18... | collective-permute-start | bytes 294920 | tf_op jit(solution)/shard_map/ppermute | solution.py:540
  46.7 3.4 %copy-start = (f32[127,4,64,64]{0,3,2,1:T(8,128)S(1)}, f32[127,4,64,64]{0,3,2,1:T(8,128)}, u32[]{:S(2)}) copy-start(f32[127,4,64,64]{0,3,2,1:T(8,128)} %param.19) | copy-start | bytes 24969220
  50.1 10.6 %copy-start.9 = (f32[64,32,128]{2,1,0:T(8,128)S(1)}, f32[64,32,128]{2,1,0:T(8,128)}, u32[]{:S(2)}) copy-start(f32[64,32,128]{2,1,0:T(8,128)} %get-tuple-element.36.own) | copy-start | bytes 3145732
  53.1 2.0 %copy-start.2 = (bf16[127,128,128]{2,1,0:T(8,128)(2,1)}, bf16[127,128,128]{2,1,0:T(8,128)(2,1)S(1)}, u32[]{:S(2)}) copy-start(bf16[127,128,128]{2,1,0:T(8,128)(2,1)S(1)} %unbatch.2.first) | copy-start | bytes 12484612
  55.1 26.9 %copy-start.21 = (s32[127,4]{0,1:T(4,128)S(1)}, s32[127,4]{0,1:T(4,128)}, u32[]{:S(2)}) copy-start(s32[127,4]{0,1:T(4,128)} %param.20) | copy-start | bytes 6100
  55.1 9.6 %collective-permute-start.9 = (f32[3,8192]{1,0:T(4,128)S(1)}, f32[3,8192]{1,0:T(4,128)S(1)}, u32[]{:S(2)}, u32[]{:S(2)}) collective-permute-start(f32[3,8192]{1,0:T(4,128)S(1)} %copy-done.14), channel_id=1, source_target_pairs={{2,0},{4,2},{6,4},{8,6},{10,8},{12,10},{14,12},{16,14},{18,16},{20... | collective-permute-start | bytes 294920 | tf_op jit(solution)/shard_map/ppermute | solution.py:540
  61.4 17.5 %collective-permute-start.5 = (f32[32,64]{1,0:T(8,128)}, f32[32,64]{1,0:T(8,128)}, u32[]{:S(2)}, u32[]{:S(2)}) collective-permute-start(f32[32,64]{1,0:T(8,128)} %bitcast.4), channel_id=1, source_target_pairs={{0,4},{2,6},{4,0},{6,2},{8,12},{10,14},{12,8},{14,10},{16,20},{18,... | collective-permute-start | bytes 24584 | tf_op jit(solution)/shard_map/ppermute | solution.py:551
  64.7 1.0 copy-start.11
  65.8 1.0 copy-start.13
  77.3 0.8 copy-start.15
  78.1 0.8 copy-start.18
  79.8 11.6 %collective-permute-start.10 = (f32[1,32,128]{2,1,0:T(8,128)S(1)}, f32[1,32,128]{2,1,0:T(8,128)S(1)}, u32[]{:S(2)}, u32[]{:S(2)}) collective-permute-start(f32[1,32,128]{2,1,0:T(8,128)S(1)} %maximum_select_fusion), channel_id=1, source_target_pairs={{0,24},{2,26},{4,28},{6,30},{8,0},{10,2},{12,4},{14,6},{16,8},{18,... | collective-permute-start | bytes 49160 | tf_op jit(solution)/shard_map/ppermute | solution.py:529
  79.8 11.6 %collective-permute-start.11 = (f32[1,32,128]{2,1,0:T(8,128)S(1)}, f32[1,32,128]{2,1,0:T(8,128)S(1)}, u32[]{:S(2)}, u32[]{:S(2)}) collective-permute-start(f32[1,32,128]{2,1,0:T(8,128)S(1)} %maximum_select_fusion), channel_id=1, source_target_pairs={{0,16},{2,18},{4,20},{6,22},{8,24},{10,26},{12,28},{14,30},{16,0},... | collective-permute-start | bytes 49160 | tf_op jit(solution)/shard_map/ppermute | solution.py:529
  82.0 9.4 %collective-permute-start.12 = (f32[1,32,128]{2,1,0:T(8,128)S(1)}, f32[1,32,128]{2,1,0:T(8,128)S(1)}, u32[]{:S(2)}, u32[]{:S(2)}) collective-permute-start(f32[1,32,128]{2,1,0:T(8,128)S(1)} %maximum_select_fusion), channel_id=1, source_target_pairs={{0,8},{2,10},{4,12},{6,14},{8,16},{10,18},{12,20},{14,22},{16,24},... | collective-permute-start | bytes 49160 | tf_op jit(solution)/shard_map/ppermute | solution.py:529
  83.0 3.4 %copy-start.1 = (f32[127,4,64,64]{0,3,2,1:T(8,128)S(1)}, f32[127,4,64,64]{0,3,2,1:T(8,128)}, u32[]{:S(2)}) copy-start(f32[127,4,64,64]{0,3,2,1:T(8,128)} %param.19) | copy-start | bytes 24969220
  86.3 22.6 %copy-start.20 = (s32[60,4]{0,1:T(4,128)S(1)}, s32[60,4]{0,1:T(4,128)}, u32[]{:S(2)}) copy-start(s32[60,4]{0,1:T(4,128)} %param.23) | copy-start | bytes 2884
  89.3 2.0 %copy-start.4 = (bf16[127,128,128]{2,1,0:T(8,128)(2,1)}, bf16[127,128,128]{2,1,0:T(8,128)(2,1)S(1)}, u32[]{:S(2)}) copy-start(bf16[127,128,128]{2,1,0:T(8,128)(2,1)S(1)} %unbatch.3.second) | copy-start | bytes 12484612
  92.1 33.5 %collective-permute-start.13 = (f32[4,32,128]{2,1,0:T(8,128)}, f32[4,32,128]{2,1,0:T(8,128)S(1)}, u32[]{:S(2)}, u32[]{:S(2)}) collective-permute-start(f32[4,32,128]{2,1,0:T(8,128)} %constant_dynamic-slice_fusion.1), channel_id=1, source_target_pairs={{0,96},{2,98},{4,100},{6,102},{8,104},{10,106},{12,108},{14,110},{... | collective-permute-start | bytes 196616 | tf_op jit(solution)/shard_map/ppermute | solution.py:529
  108.3 17.3 %collective-permute-start.14 = (f32[4,32,128]{2,1,0:T(8,128)}, f32[4,32,128]{2,1,0:T(8,128)S(1)}, u32[]{:S(2)}, u32[]{:S(2)}) collective-permute-start(f32[4,32,128]{2,1,0:T(8,128)} %constant_dynamic-slice_fusion.1), channel_id=1, source_target_pairs={{0,64},{2,66},{4,68},{6,70},{8,72},{10,74},{12,76},{14,78},{16,80}... | collective-permute-start | bytes 196616 | tf_op jit(solution)/shard_map/ppermute | solution.py:529
  108.6 17.0 %collective-permute-start.15 = (f32[4,32,128]{2,1,0:T(8,128)}, f32[4,32,128]{2,1,0:T(8,128)S(1)}, u32[]{:S(2)}, u32[]{:S(2)}) collective-permute-start(f32[4,32,128]{2,1,0:T(8,128)} %constant_dynamic-slice_fusion.1), channel_id=1, source_target_pairs={{0,32},{2,34},{4,36},{6,38},{8,40},{10,42},{12,44},{14,46},{16,48}... | collective-permute-start | bytes 196616 | tf_op jit(solution)/shard_map/ppermute | solution.py:529
  109.7 22.4 %collective-permute-start.16 = (f32[32,4096]{1,0:T(8,128)}, f32[32,4096]{1,0:T(8,128)}, u32[]{:S(2)}, u32[]{:S(2)}) collective-permute-start(f32[32,4096]{1,0:T(8,128)} %copy-done.18), channel_id=1, source_target_pairs={{0,1},{1,0},{2,3},{3,2},{4,5},{5,4},{6,7},{7,6},{8,9},{9,8},{10,11... | collective-permute-start | bytes 1572872 | tf_op jit(solution)/shard_map/ppermute | solution.py:556
  114.2 2.2 %copy-start.3 = (bf16[127,128,128]{2,1,0:T(8,128)(2,1)S(1)}, bf16[127,128,128]{2,1,0:T(8,128)(2,1)}, u32[]{:S(2)}) copy-start(bf16[127,128,128]{2,1,0:T(8,128)(2,1)} %copy-done.2) | copy-start | bytes 12484612
  116.4 2.2 %copy-start.5 = (bf16[127,128,128]{2,1,0:T(8,128)(2,1)S(1)}, bf16[127,128,128]{2,1,0:T(8,128)(2,1)}, u32[]{:S(2)}) copy-start(bf16[127,128,128]{2,1,0:T(8,128)(2,1)} %copy-done.4) | copy-start | bytes 12484612
  126.6 5.6 %copy-start.6 = (f32[64,64,128]{2,1,0:T(8,128)S(1)}, f32[64,64,128]{2,1,0:T(8,128)}, u32[]{:S(2)}) copy-start(f32[64,64,128]{2,1,0:T(8,128)} %basis.1) | copy-start | bytes 6291460
  126.6 5.6 %copy-start.8 = (bf16[128,64,128]{2,1,0:T(8,128)(2,1)S(1)}, bf16[128,64,128]{2,1,0:T(8,128)(2,1)}, u32[]{:S(2)}) copy-start(bf16[128,64,128]{2,1,0:T(8,128)(2,1)} %get-tuple-element.62.trans) | copy-start | bytes 6291460
  126.6 5.6 %copy-start.16 = (f32[32,4096]{1,0:T(8,128)S(1)}, f32[32,4096]{1,0:T(8,128)}, u32[]{:S(2)}) copy-start(f32[32,4096]{1,0:T(8,128)} %copy-done.15) | copy-start | bytes 1572868
  132.2 0.7 copy-start.17

commit v4 on v3

--- a/solution.py
+++ b/solution.py
@@ -8,6 +8,7 @@
 VM = pl.BlockSpec(memory_space=pltpu.VMEM)
 HBM = pl.BlockSpec(memory_space=pltpu.HBM)
 PITCH = 136
+VMEM_BYTES = 58 << 20
 f32 = jnp.float32
 bf16 = jnp.bfloat16
 
@@ -29,7 +30,7 @@
 def low_lanes(shape):
     return lax.broadcasted_iota(jnp.int32, shape, 1) < 64
 
-def up_body(basis_hbm, values_hbm, moves_hbm, up, trans, rows, basis, values, moves, sem):
+def up_body(points, basis_hbm, values_hbm, moves_hbm, up, trans, packed, rows, basis, values, moves, sem):
     leaves = basis.shape[0]
     columns = values.shape[0]
     nodes = moves.shape[2]
@@ -61,6 +62,8 @@
 
     for read in reads[4:]:
         read.wait()
+    packed[0:columns] = values[...]
+    packed[columns:] = points[...]
 
     def leaf_up(i):
         v = stack(values[:, pl.ds(pl.multiple_of(i * 128, 128), 128)])
@@ -106,7 +109,7 @@
     up[leaves - 1] = jnp.where(half, tiles[0], share)
 
 
-def up_pass(basis, values, moves):
+def up_pass(points, basis, values, moves):
     leaves = basis.shape[0]
     columns = values.shape[0]
     nodes = moves.shape[2]
@@ -115,9 +118,10 @@
         out_shape=(
             jax.ShapeDtypeStruct((leaves, columns, 128), f32),
             jax.ShapeDtypeStruct((nodes + 1, 64, 128), bf16),
+            jax.ShapeDtypeStruct((columns + 3, values.shape[1]), f32),
         ),
-        in_specs=[HBM, HBM, HBM],
-        out_specs=(VM, VM),
+        in_specs=[VM, HBM, HBM, HBM],
+        out_specs=(VM, VM, VM),
         scratch_shapes=[
             pltpu.VMEM((64 * PITCH, 128), f32),
             pltpu.VMEM(basis.shape, f32),
@@ -125,41 +129,77 @@
             pltpu.VMEM(moves.shape, f32),
             pltpu.SemaphoreType.DMA((6,)),
         ],
-        compiler_params=pltpu.CompilerParams(vmem_limit_bytes=56 << 20),
+        compiler_params=pltpu.CompilerParams(vmem_limit_bytes=VMEM_BYTES),
         cost_estimate=pl.CostEstimate(flops=400_000_000, bytes_accessed=8_000_000, transcendentals=0),
         name="up_pass",
-    )(basis, values, moves)
-
-
-def unbatch_body(part, matrices, out, rows):
+    )(points, basis, values, moves)
+
+
+CHUNK = 32
+
+
+def unbatch_body(matrices, out, held, rows, made, in_sem, out_sem):
     nodes = matrices.shape[3]
-
-    @pl.loop(0, 64, unroll=4)
-    def _(r):
-        x = jnp.concatenate([matrices[2 * part, r], matrices[2 * part + 1, r]], axis=0)
-        rows[pl.ds(pl.multiple_of(r * PITCH, 8), nodes)] = jnp.transpose(x)
-
-    def one(n):
-        hi, lo = split(rows[pl.ds(n, 64, stride=PITCH), :])
-        out[n, 0:64] = hi
-        out[n, 64:128] = lo
-
-    whole = nodes // 8 * 8
-    pl.loop(0, whole, unroll=8)(one)
-    for n in range(whole, nodes):
-        one(n)
-
-
-def unbatch(matrices, part):
+    pieces = 4
+    step = matrices.shape[1] // pieces
+    reads = []
+    for h in range(2):
+        for i in range(pieces):
+            at = pl.ds(i * step, step)
+            pair = pl.ds(2 * h, 2)
+            reads.append(
+                pltpu.make_async_copy(
+                    matrices.at[pair, at], held.at[pair, at], in_sem.at[pieces * h + i]
+                )
+            )
+    for read in reads:
+        read.start()
+    writes = []
+    for h in range(2):
+        for i in range(pieces):
+            reads[pieces * h + i].wait()
+
+            @pl.loop(i * step, (i + 1) * step, unroll=4)
+            def _(r, h=h):
+                x = jnp.concatenate([held[2 * h, r], held[2 * h + 1, r]], axis=0)
+                rows[pl.ds(pl.multiple_of((h * 64 + r) * PITCH, 8), nodes)] = jnp.transpose(x)
+
+        def one(n, h=h):
+            hi, lo = split(rows[pl.ds(h * 64 * PITCH + n, 64, stride=PITCH), :])
+            made[h, n, 0:64] = hi
+            made[h, n, 64:128] = lo
+
+        for c, begin in enumerate(range(0, nodes, CHUNK)):
+            size = min(CHUNK, nodes - begin)
+            whole = begin + size // 8 * 8
+            pl.loop(begin, whole, unroll=8)(one)
+            for n in range(whole, begin + size):
+                one(n)
+            at = pl.ds(begin, size)
+            writes.append(
+                pltpu.make_async_copy(made.at[h, at], out.at[h, at], out_sem.at[h, c])
+            )
+            writes[-1].start()
+    for write in writes:
+        write.wait()
+
+
+def unbatch(matrices):
     nodes = matrices.shape[3]
     return pl.pallas_call(
-        functools.partial(unbatch_body, part),
-        out_shape=jax.ShapeDtypeStruct((nodes, 128, 128), bf16),
-        in_specs=[VM],
-        out_specs=VM,
-        scratch_shapes=[pltpu.VMEM((64 * PITCH, 128), f32)],
-        compiler_params=pltpu.CompilerParams(vmem_limit_bytes=20 << 20),
-        cost_estimate=pl.CostEstimate(flops=50_000_000, bytes_accessed=9_000_000, transcendentals=0),
+        unbatch_body,
+        out_shape=jax.ShapeDtypeStruct((2, nodes, 128, 128), bf16),
+        in_specs=[HBM],
+        out_specs=HBM,
+        scratch_shapes=[
+            pltpu.VMEM(matrices.shape, f32),
+            pltpu.VMEM((2 * 64 * PITCH, 128), f32),
+            pltpu.VMEM((2, nodes, 128, 128), bf16),
+            pltpu.SemaphoreType.DMA((8,)),
+            pltpu.SemaphoreType.DMA((2, -(-nodes // CHUNK))),
+        ],
+        compiler_params=pltpu.CompilerParams(vmem_limit_bytes=VMEM_BYTES),
+        cost_estimate=pl.CostEstimate(flops=100_000_000, bytes_accessed=17_000_000, transcendentals=0),
         name="unbatch",
     )(matrices)
 
@@ -218,16 +258,22 @@
         in_specs=[SM, SM, VM, VM, HBM],
         out_specs=VM,
         scratch_shapes=[pltpu.VMEM((32, columns, 128), f32), pltpu.VMEM((4, 4, 64, 64), f32), pltpu.SemaphoreType.DMA((4,))],
-        compiler_params=pltpu.CompilerParams(vmem_limit_bytes=56 << 20),
+        compiler_params=pltpu.CompilerParams(vmem_limit_bytes=VMEM_BYTES),
         cost_estimate=pl.CostEstimate(flops=50_000_000, bytes_accessed=2_000_000, transcendentals=0),
         name="top_pass",
     )(place, partners, first, moves, matrices)
 
 
-def couple_body(codes, low, own, high, first, second, far, gather):
+def couple_body(codes, low, own, high, matrices, far, gather, held, sem):
     leaves = own.shape[0]
     columns = own.shape[1]
-    nodes = first.shape[0]
+    nodes = matrices.shape[1]
+    reads = []
+    for i in range(3):
+        begin = 42 * i
+        at = pl.ds(begin, nodes - begin if i == 2 else 42)
+        reads.append(pltpu.make_async_copy(matrices.at[:, at], held.at[:, at], sem.at[i]))
+        reads[-1].start()
     half = low_lanes((columns, 128))
     left = low_lanes((2 * columns, 128))
     for side, ref in enumerate((low, own, high)):
@@ -250,28 +296,35 @@
             ],
             axis=1,
         )
-        m = jnp.concatenate([first[n], second[n]], axis=1)
+        m = jnp.concatenate([held[0, n], held[1, n]], axis=1)
         return both(fold(lax.dot_general(x, m, NT, preferred_element_type=f32)))
 
-    @pl.loop(0, leaves - 1, unroll=7)
-    def _(t):
-        far[t] = jnp.where(half, one(2 * t), one(2 * t + 1))
+    for i in range(3):
+        reads[i].wait()
+
+        @pl.loop(21 * i, 21 * i + 21, unroll=7)
+        def _(t):
+            far[t] = jnp.where(half, one(2 * t), one(2 * t + 1))
 
     far[leaves - 1] = one(nodes - 1)
 
 
-def couple_pass(codes, low, own, high, first, second):
+def couple_pass(codes, low, own, high, matrices):
     leaves, columns, _ = own.shape
     return pl.pallas_call(
         couple_body,
         out_shape=jax.ShapeDtypeStruct((leaves, columns, 128), f32),
-        in_specs=[SM] + [VM] * 5,
+        in_specs=[SM] + [VM] * 3 + [HBM],
         out_specs=VM,
-        scratch_shapes=[pltpu.VMEM((2, 3 * leaves, 2 * columns, 128), bf16)],
-        compiler_params=pltpu.CompilerParams(vmem_limit_bytes=24 << 20),
+        scratch_shapes=[
+            pltpu.VMEM((2, 3 * leaves, 2 * columns, 128), bf16),
+            pltpu.VMEM(matrices.shape, bf16),
+            pltpu.SemaphoreType.DMA((3,)),
+        ],
+        compiler_params=pltpu.CompilerParams(vmem_limit_bytes=VMEM_BYTES),
         cost_estimate=pl.CostEstimate(flops=400_000_000, bytes_accessed=12_000_000, transcendentals=0),
         name="couple_pass",
-    )(codes, low, own, high, first, second)
+    )(codes, low, own, high, matrices)
 
 
 def down_body(core, parent, far, trans, basis, mine, given, out, held):
@@ -334,7 +387,7 @@
         in_specs=[SM] + [VM] * 6,
         out_specs=VM,
         scratch_shapes=[pltpu.VMEM((8, columns, 128), f32)],
-        compiler_params=pltpu.CompilerParams(vmem_limit_bytes=14 << 20),
+        compiler_params=pltpu.CompilerParams(vmem_limit_bytes=VMEM_BYTES),
         cost_estimate=pl.CostEstimate(flops=200_000_000, bytes_accessed=7_000_000, transcendentals=0),
         name="down_pass",
     )(core, parent, far, trans, basis, mine, given)
@@ -347,9 +400,9 @@
 
 def near_body(unroll, chunks, lists, counts, targets, *refs):
     sources, refs = refs[: 2 * chunks], refs[2 * chunks :]
-    begin, spots = None, [targets]
+    begin = None
     if chunks == 2:
-        begin, spots, refs = refs[0:2], refs[2:4], refs[4:]
+        begin, refs = refs[0:2], refs[2:]
     mine, other, columns_of, total, weights, places = refs
     leaves = mine.shape[1] // 128
     width = sources[0].shape[1] // 128
@@ -364,9 +417,9 @@
             for u in range(8):
                 j = 8 * g + u
                 at = pl.ds(pl.multiple_of(j * 128, 128), 128)
-                x = near_weight * jnp.concatenate([near_ref[:, at], far_ref[:, at]], axis=0)
+                x = near_weight * jnp.concatenate([near_ref[0:32, at], far_ref[0:32, at]], axis=0)
                 weights[c * width + j] = stack(x)
-                places[c * width + j, 0:3] = spots[c][:, at]
+                places[c * width + j, 0:3] = near_ref[32:35, at]
 
     weights[chunks * width] = jnp.zeros(weights.shape[1:], bf16)
     places[chunks * width] = jnp.zeros(places.shape[1:], f32)
@@ -436,12 +489,12 @@
             other[:, at] = begin[1][:, at] + x[32:64]
 
 
-def near_pass(unroll, lists, counts, targets, sources, begin=(), spots=()):
+def near_pass(unroll, lists, counts, targets, sources, begin=()):
     leaves = lists.shape[0] // SLOTS
     chunks = len(sources) // 2
     held = chunks * (sources[0].shape[1] // 128) + 1
     side = jax.ShapeDtypeStruct((32, leaves * 128), f32)
-    arrays = (targets, *sources, *begin, *spots)
+    arrays = (targets, *sources, *begin)
     return pl.pallas_call(
         functools.partial(near_body, unroll, chunks),
         out_shape=(side, side),
@@ -453,7 +506,7 @@
             pltpu.VMEM((held, 128, 128), bf16),
             pltpu.VMEM((held, 8, 128), f32),
         ],
-        compiler_params=pltpu.CompilerParams(vmem_limit_bytes=24 << 20),
+        compiler_params=pltpu.CompilerParams(vmem_limit_bytes=VMEM_BYTES),
         cost_estimate=pl.CostEstimate(flops=1_000, bytes_accessed=1_000, transcendentals=0),
         name="near_pass",
     )(lists, counts, *arrays)
@@ -505,10 +558,7 @@
     forward = [(i, i + 1) for i in range(count - 1)]
     backward = [(target, source) for source, target in forward]
     swap = [(0, 1), (1, 0)]
-    low = lax.ppermute(values, "leaf", forward)
-    high = lax.ppermute(values, "leaf", backward)
     across = lax.ppermute(values, "rhs", swap)
-
     half = leaves // 2
     chosen = lax.dynamic_slice_in_dim(near_list, core * half, half, 0) - position * leaves
     live = lax.dynamic_slice_in_dim(near_count, core * half, half, 0)
@@ -534,42 +584,36 @@
         return lax.dynamic_slice_in_dim(both_rounds, (3 - spot) * x.shape[0], 4 * x.shape[0], 0)
 
     after = lax.optimization_barrier
-    up, trans = up_pass(basis, values, transfer.transpose(1, 2, 0))
+    up, trans, packed = up_pass(points, basis, values, transfer.transpose(1, 2, 0))
+    share = up[leaves - 1, :, 64:]
+    shares, spot = ring(share[None], 1)
+    low = lax.ppermute(packed, "leaf", forward)
+    high = lax.ppermute(packed, "leaf", backward)
     up_low = lax.ppermute(up, "leaf", forward)
     up_high = lax.ppermute(up, "leaf", backward)
-    spots = (lax.ppermute(points, "leaf", forward), lax.ppermute(points, "leaf", backward))
-    near_ids, up = after((near_ids, up))
-    begin = near_pass(8, near_ids, near_live, points, (values, across))
-    low, high, coupling, begin = after((low, high, coupling, begin))
+    near_ids, far_ids, codes, up = after((near_ids, far_ids, codes, up))
+    begin = near_pass(8, near_ids, near_live, points, (packed, across))
+    shares, low, high, coupling, begin = after((shares, low, high, coupling, begin))
+    level = in_order(shares, share[None], spot)
+    level = jnp.concatenate([level[0] + level[1], level[2] + level[3]], axis=1)[None]
     low_across = lax.ppermute(low, "rhs", swap)
     high_across = lax.ppermute(high, "rhs", swap)
-    coupling = coupling.transpose(1, 2, 3, 0)
-    first = unbatch(coupling, 0)
-    far_ids, up_low, up_high, first = after((far_ids, up_low, up_high, first))
-    sibling = jnp.where(position % 2 == 0, up_high[leaves - 1, :, 64:], up_low[leaves - 1, :, 64:])
-    level = up[leaves - 1, :, 64:] + sibling
-    pair = lax.ppermute(level, "leaf", [(i, i ^ 2) for i in range(count)])
-    mine, other = near_pass(
-        8, far_ids, far_live, points, (low, low_across, high, high_across), begin, spots
-    )
-    pair, mine, other, coupling = after((pair, mine, other, coupling))
-    given = lax.ppermute(other, "rhs", swap)
-    level = jnp.where(
-        position & 2 == 0,
-        jnp.concatenate([level, pair], axis=1),
-        jnp.concatenate([pair, level], axis=1),
-    )[None]
     turned, spot = ring(level, 4)
-    second = unbatch(coupling, 1)
-    turned, codes, second = after((turned, codes, second))
+    matrices = unbatch(coupling.transpose(1, 2, 3, 0))
+    turned, far_ids, matrices = after((turned, far_ids, matrices))
     level = in_order(turned, level, spot)
     turned, spot = ring(level, 16)
-    far = couple_pass(codes, up_low, up, up_high, first, second)
-    turned, far = after((turned, far))
+    mine, other = near_pass(
+        8, far_ids, far_live, points, (low, low_across, high, high_across), begin
+    )
+    turned, mine, other = after((turned, mine, other))
+    given = lax.ppermute(other, "rhs", swap)
     level = in_order(turned, level, spot)
     parent = top_pass(
         position[None].astype(jnp.int32), partners_top.reshape(-1), level, transfer_top, coupling_top
     )
+    up_low, up_high, parent = after((up_low, up_high, parent))
+    far = couple_pass(codes, up_low, up, up_high, matrices)
     return down_pass(core[None].astype(jnp.int32), parent, far, trans, basis, mine, given)
 
 

time: 147 us -> 139 us (0.946)
  the two profiles are of different devices: /device:TPU:5 before, /device:TPU:0 now
where the time goes in v4:
time: 139 us; the launch traced here: 137 us
  Pallas kernels  72.6 us (52%)
  starting transfers between devices  30.3 us (22%)
  waiting for transfers between devices  23.2 us (17%)
  local copies, waits for them, and re-layouts  7.31 us (5%)
  other arithmetic  2.94 us (2%)
    ppermute x9, waiting for transfers between devices, ring(): turned.append(lax.ppermute(x, 'leaf', to))  23.2 us
    pallas_call x2, Pallas kernels, near_pass(): pl.pallas_call(functools.partial(near_body, unroll, chunks), out_shape=(s...  21.7 us
    ppermute x9, starting transfers between devices, ring(): turned.append(lax.ppermute(x, 'leaf', to))  20.2 us
    pallas_call x1, Pallas kernels, down_pass(): pl.pallas_call(down_body, out_shape=jax.ShapeDtypeStruct((columns, leaves...  14 us
    pallas_call x1, Pallas kernels, up_pass(): pl.pallas_call(up_body, out_shape=(jax.ShapeDtypeStruct((leaves, columns,...  13.3 us
    pallas_call x1, Pallas kernels, couple_pass(): pl.pallas_call(couple_body, out_shape=jax.ShapeDtypeStruct((leaves, colum...  9.51 us
    pallas_call x1, Pallas kernels, unbatch(): pl.pallas_call(unbatch_body, out_shape=jax.ShapeDtypeStruct((2, nodes, 12...  8.67 us
    pallas_call x1, Pallas kernels, top_pass(): pl.pallas_call(top_body, out_shape=jax.ShapeDtypeStruct((columns, 128), f...  5.41 us
  transfers between devices with their start and end apart: 17, of which 2 were waited for; matrix products, arithmetic and copies ran while one was open for 6% of the time, Pallas kernels for 43%

profile of v4, /device:TPU:0, one launch (start us, length us, event | category | flops | bytes accessed | tf_op | source)
XLA Modules:
  0.0 136.7 jit_solution(7672591558372680269)
XLA Ops:
  0.0 0.0 collective-permute-start.7
  0.0 0.0 copy-start.7
  0.0 13.3 %up_pass.1 = (f32[64,32,128]{2,1,0:T(8,128)}, bf16[128,64,128]{2,1,0:T(8,128)(2,1)}, f32[35,8192]{1,0:T(8,128)}) custom-call(f32[3,8192]{1,0:T(4,128)} %targets.3, f32[64,64,128]{2,1,0:T(8,128)} %basis.1, f32[32,8192]{1,0:T(8,128)} %values_hbm.1, f32[64,64,127]{2,1,0:T(8,128)} %bitcast.11), custom_call_target="tpu_custom_call" | custom-call | flops 400000000 | bytes 8000000 | tf_op jit(solution)/shard_map/up_pass/pallas_call | solution.py:116
  13.4 0.8 slice.15
  14.2 3.1 %collective-permute-start.2 = (f32[1,32,64]{2,1,0:T(8,128)S(1)}, f32[1,32,64]{2,1,0:T(8,128)S(1)}, u32[]{:S(2)}, u32[]{:S(2)}) collective-permute-start(f32[1,32,64]{2,1,0:T(8,128)S(1)} %slice.15), channel_id=1, source_target_pairs={{0,6},{2,0},{4,2},{6,4},{8,14},{10,8},{12,10},{14,12},{16,22},{18,... | collective-permute-start | bytes 24584 | tf_op jit(solution)/shard_map/ppermute | solution.py:579
  17.3 0.6 collective-permute-start.3
  17.9 2.9 %collective-permute-start.5 = (f32[35,8192]{1,0:T(8,128)}, f32[35,8192]{1,0:T(8,128)S(1)}, u32[]{:S(2)}, u32[]{:S(2)}) collective-permute-start(f32[35,8192]{1,0:T(8,128)} %get-tuple-element.38.refs_0_), channel_id=1, source_target_pairs={{0,2},{2,4},{4,6},{6,8},{8,10},{10,12},{12,14},{14,16},{16,18},{18... | collective-permute-start | bytes 3440648 | tf_op jit(solution)/shard_map/ppermute | solution.py:590
  20.8 1.3 collective-permute-start.6
  22.2 0.1 dynamic_slice.15
  22.3 0.1 convert_reduce_fusion
  22.4 0.3 select_reduce_fusion.1
  22.7 0.1 copy.29
  22.8 0.1 copy.30
  22.9 1.0 select_reduce_fusion
  23.9 0.1 fusion.6
  24.0 0.1 fusion.7
  24.1 2.7 %collective-permute-start.4 = (f32[1,32,64]{2,1,0:T(8,128)S(1)}, f32[1,32,64]{2,1,0:T(8,128)S(1)}, u32[]{:S(2)}, u32[]{:S(2)}) collective-permute-start(f32[1,32,64]{2,1,0:T(8,128)S(1)} %slice.15), channel_id=1, source_target_pairs={{0,2},{2,4},{4,6},{6,0},{8,10},{10,12},{12,14},{14,8},{16,18},{18,... | collective-permute-start | bytes 24584 | tf_op jit(solution)/shard_map/ppermute | solution.py:579
  26.7 0.6 pad_add_fusion.counts
  27.3 0.7 select_n.81.lists
  28.0 0.7 select_n.86.lists
  28.7 0.1 copy.31
  28.9 0.7 reshape.48.codes
  29.5 10.7 %near_pass.2 = (f32[32,4096]{1,0:T(8,128)}, f32[32,4096]{1,0:T(8,128)}) custom-call(s32[896]{0:T(1024)} %select_n.81.lists, s32[33]{0:T(128)} %pad_add_fusion.counts, f32[3,8192]{1,0:T(4,128)} %targets.3, f32[35,8192]{1,0:T(8,128)} %get-tuple-element.38.refs_0_, f32[32,8192]{1,0:T(8,128)} %collective-permute-done.7.refs_1_), custom_call_target="tpu_custom_call" | custom-call | flops 1000 | bytes 1000 | tf_op jit(solution)/shard_map/near_pass/pallas_call | solution.py:498
  40.2 0.0 collective-permute-done.2
  40.2 15.4 %collective-permute-done.4 = f32[1,32,64]{2,1,0:T(8,128)S(1)} collective-permute-done((f32[1,32,64]{2,1,0:T(8,128)S(1)}, f32[1,32,64]{2,1,0:T(8,128)S(1)}, u32[]{:S(2)}, u32[]{:S(2)}) %collective-permute-start.4) | collective-permute-done | bytes 8224 | tf_op jit(solution)/shard_map/ppermute | solution.py:579
  55.7 0.8 constant_dynamic-update-slice_fusion.4
  56.5 0.8 constant_dynamic-update-slice_fusion
  57.3 0.0 collective-permute-start.14
  57.4 0.5 collective-permute-start.15
  57.9 0.1 maximum_bitcast_fusion
  57.9 0.0 collective-permute-start.10
  57.9 3.2 %collective-permute-start.8 = (f32[1,32,128]{2,1,0:T(8,128)S(1)}, f32[1,32,128]{2,1,0:T(8,128)S(1)}, u32[]{:S(2)}, u32[]{:S(2)}) collective-permute-start(f32[1,32,128]{2,1,0:T(8,128)S(1)} %maximum_bitcast_fusion), channel_id=1, source_target_pairs={{0,24},{2,26},{4,28},{6,30},{8,0},{10,2},{12,4},{14,6},{16,8},{18,... | collective-permute-start | bytes 49160 | tf_op jit(solution)/shard_map/ppermute | solution.py:579
  61.2 0.1 collective-permute-start.9
  61.3 8.7 %unbatch.1.matrices = bf16[2,127,128,128]{3,2,1,0:T(8,128)(2,1)} custom-call(f32[4,64,64,127]{3,2,1,0:T(8,128)} %bitcast.10), custom_call_target="tpu_custom_call" | custom-call | flops 100000000 | bytes 17000000 | tf_op jit(solution)/shard_map/unbatch/pallas_call | solution.py:189
  70.0 4.0 %collective-permute-start = (f32[64,32,128]{2,1,0:T(8,128)}, f32[64,32,128]{2,1,0:T(8,128)}, u32[]{:S(2)}, u32[]{:S(2)}) collective-permute-start(f32[64,32,128]{2,1,0:T(8,128)} %get-tuple-element.63.own), channel_id=1, source_target_pairs={{0,2},{2,4},{4,6},{6,8},{8,10},{10,12},{12,14},{14,16},{16,18},{18... | collective-permute-start | bytes 3145736 | tf_op jit(solution)/shard_map/ppermute | solution.py:592
  74.0 1.3 collective-permute-start.1
  75.4 9.2 %collective-permute-start.11 = (f32[4,32,128]{2,1,0:T(8,128)S(1)}, f32[4,32,128]{2,1,0:T(8,128)S(1)}, u32[]{:S(2)}, u32[]{:S(2)}) collective-permute-start(f32[4,32,128]{2,1,0:T(8,128)S(1)} %constant_dynamic-slice_fusion.1), channel_id=1, source_target_pairs={{0,96},{2,98},{4,100},{6,102},{8,104},{10,106},{12,108},{14,110},{... | collective-permute-start | bytes 196616 | tf_op jit(solution)/shard_map/ppermute | solution.py:579
  84.7 1.3 collective-permute-start.13
  85.9 0.6 pad_add_fusion.1.counts
  86.6 0.1 copy.28
  86.7 0.7 reshape.47.partners
  87.3 11.0 %near_pass.3 = (f32[32,4096]{1,0:T(8,128)}, f32[32,4096]{1,0:T(8,128)}) custom-call(s32[896]{0:T(1024)} %select_n.86.lists, s32[33]{0:T(128)} %pad_add_fusion.1.counts, f32[3,8192]{1,0:T(4,128)} %targets.3, f32[35,8192]{1,0:T(8,128)} %copy-done, f32[35,8192]{1,0:T(8,128)} %collective-permute-done.14.refs_1_, f32[35,8192]{1,0:T(8,128)} %copy-done.1, ...), custom_call_target="tpu_custom_call" | custom-call | flops 1000 | bytes 1000 | tf_op jit(solution)/shard_map/near_pass/pallas_call | solution.py:498
  98.3 7.8 %collective-permute-done.12 = f32[4,32,128]{2,1,0:T(8,128)S(1)} collective-permute-done((f32[4,32,128]{2,1,0:T(8,128)S(1)}, f32[4,32,128]{2,1,0:T(8,128)S(1)}, u32[]{:S(2)}, u32[]{:S(2)}) %collective-permute-start.12) | collective-permute-done | bytes 65568 | tf_op jit(solution)/shard_map/ppermute | solution.py:579
  106.3 0.7 constant_dynamic-slice_fusion.first
  107.0 5.4 %top_pass.1.parent = f32[32,128]{1,0:T(8,128)} custom-call(s32[1]{0:T(128)} %bitcast.2.place, s32[240]{0:T(256)} %reshape.47.partners, f32[16,32,128]{2,1,0:T(8,128)} %constant_dynamic-slice_fusion.first, f32[62,64,64]{2,1,0:T(8,128)} %moves.1, f32[60,4,64,64]{3,2,1,0:T(8,128)} %matrices.1), custom_call_target="tpu_custom_call" | custom-call | flops 50000000 | bytes 2000000 | tf_op jit(solution)/shard_map/top_pass/pallas_call | solution.py:255
  112.5 9.5 %couple_pass.1.far = f32[64,32,128]{2,1,0:T(8,128)} custom-call(s32[508]{0:T(512)} %reshape.48.codes, f32[64,32,128]{2,1,0:T(8,128)} %collective-permute-done.low, f32[64,32,128]{2,1,0:T(8,128)} %get-tuple-element.63.own, f32[64,32,128]{2,1,0:T(8,128)} %collective-permute-done.1.high, bf16[2,127,128,128]{3,2,1,0:T(8,128)(2,1)} %unbatch.1.matrices), custom_call_target="tpu_custom_call" | custom-call | flops 400000000 | bytes 12000000 | tf_op jit(solution)/shard_map/couple_pass/pallas_call | solution.py:314
  122.0 0.8 copy-done.2
  122.8 14.0 %down_pass.1 = f32[32,8192]{1,0:T(8,128)} custom-call(s32[1]{0:T(128)} %bitcast.core, f32[32,128]{1,0:T(8,128)} %top_pass.1.parent, f32[64,32,128]{2,1,0:T(8,128)} %couple_pass.1.far, bf16[128,64,128]{2,1,0:T(8,128)(2,1)} %get-tuple-element.66.trans, f32[64,64,128]{2,1,0:T(8,128)} %basis.1, f32[32,4096]{1,0:T(8,128)} %get-tuple-element.67.mine, ...), custom_call_target="tpu_custom_call" | custom-call | flops 200000000 | bytes 7000000 | tf_op jit(solution)/shard_map/down_pass/pallas_call | solution.py:384
  (61 shorter events, 0.3 us)
Async XLA Ops:
  0.0 24.1 %collective-permute-start.7 = (f32[32,8192]{1,0:T(8,128)}, f32[32,8192]{1,0:T(8,128)}, u32[]{:S(2)}, u32[]{:S(2)}) collective-permute-start(f32[32,8192]{1,0:T(8,128)} %values_hbm.1), channel_id=1, source_target_pairs={{0,1},{1,0},{2,3},{3,2},{4,5},{5,4},{6,7},{7,6},{8,9},{9,8},{10,11... | collective-permute-start | bytes 3145736 | tf_op jit(solution)/shard_map/ppermute | solution.py:561
  0.0 22.2 %copy-start.8 = (s32[64]{0:T(128)S(1)}, s32[64]{0:T(128)}, u32[]{:S(2)}) copy-start(s32[64]{0:T(128)} %param.16) | copy-start | bytes 772
  0.0 22.2 %copy-start.3 = (s32[64,27]{0,1:T(8,128)S(1)}, s32[64,27]{0,1:T(8,128)}, u32[]{:S(2)}) copy-start(s32[64,27]{0,1:T(8,128)} %param.15) | copy-start | bytes 20740
  0.0 23.9 %copy-start.6 = (s32[127]{0:T(128)S(1)}, s32[127]{0:T(128)}, u32[]{:S(2)}) copy-start(s32[127]{0:T(128)} %constant.84.clone) | copy-start | bytes 1528
  0.0 23.9 %copy-start.5 = (s32[127,4]{0,1:T(4,128)S(1)}, s32[127,4]{0,1:T(4,128)}, u32[]{:S(2)}) copy-start(s32[127,4]{0,1:T(4,128)} %param.20) | copy-start | bytes 6100
  0.0 23.9 %copy-start.7 = (s32[127]{0:T(128)S(1)}, s32[127]{0:T(128)}, u32[]{:S(2)}) copy-start(s32[127]{0:T(128)} %constant.85.clone) | copy-start | bytes 1528
  14.2 26.1 %collective-permute-start.2 = (f32[1,32,64]{2,1,0:T(8,128)S(1)}, f32[1,32,64]{2,1,0:T(8,128)S(1)}, u32[]{:S(2)}, u32[]{:S(2)}) collective-permute-start(f32[1,32,64]{2,1,0:T(8,128)S(1)} %slice.15), channel_id=1, source_target_pairs={{0,6},{2,0},{4,2},{6,4},{8,14},{10,8},{12,10},{14,12},{16,22},{18,... | collective-permute-start | bytes 24584 | tf_op jit(solution)/shard_map/ppermute | solution.py:579
  17.3 23.0 %collective-permute-start.3 = (f32[1,32,64]{2,1,0:T(8,128)S(1)}, f32[1,32,64]{2,1,0:T(8,128)S(1)}, u32[]{:S(2)}, u32[]{:S(2)}) collective-permute-start(f32[1,32,64]{2,1,0:T(8,128)S(1)} %slice.15), channel_id=1, source_target_pairs={{0,4},{2,6},{4,0},{6,2},{8,12},{10,14},{12,8},{14,10},{16,20},{18,... | collective-permute-start | bytes 24584 | tf_op jit(solution)/shard_map/ppermute | solution.py:579
  17.9 37.7 %collective-permute-start.5 = (f32[35,8192]{1,0:T(8,128)}, f32[35,8192]{1,0:T(8,128)S(1)}, u32[]{:S(2)}, u32[]{:S(2)}) collective-permute-start(f32[35,8192]{1,0:T(8,128)} %get-tuple-element.38.refs_0_), channel_id=1, source_target_pairs={{0,2},{2,4},{4,6},{6,8},{8,10},{10,12},{12,14},{14,16},{16,18},{18... | collective-permute-start | bytes 3440648 | tf_op jit(solution)/shard_map/ppermute | solution.py:590
  20.8 34.8 %collective-permute-start.6 = (f32[35,8192]{1,0:T(8,128)}, f32[35,8192]{1,0:T(8,128)S(1)}, u32[]{:S(2)}, u32[]{:S(2)}) collective-permute-start(f32[35,8192]{1,0:T(8,128)} %get-tuple-element.38.refs_0_), channel_id=1, source_target_pairs={{2,0},{4,2},{6,4},{8,6},{10,8},{12,10},{14,12},{16,14},{18,16},{20... | collective-permute-start | bytes 3440648 | tf_op jit(solution)/shard_map/ppermute | solution.py:591
  24.1 31.6 %collective-permute-start.4 = (f32[1,32,64]{2,1,0:T(8,128)S(1)}, f32[1,32,64]{2,1,0:T(8,128)S(1)}, u32[]{:S(2)}, u32[]{:S(2)}) collective-permute-start(f32[1,32,64]{2,1,0:T(8,128)S(1)} %slice.15), channel_id=1, source_target_pairs={{0,2},{2,4},{4,6},{6,0},{8,10},{10,12},{12,14},{14,8},{16,18},{18,... | collective-permute-start | bytes 24584 | tf_op jit(solution)/shard_map/ppermute | solution.py:579
  55.6 14.4 %copy-start = (f32[35,8192]{1,0:T(8,128)}, f32[35,8192]{1,0:T(8,128)S(1)}, u32[]{:S(2)}) copy-start(f32[35,8192]{1,0:T(8,128)S(1)} %collective-permute-done.5.refs_0_) | copy-start | bytes 3440644
  55.6 14.4 %copy-start.1 = (f32[35,8192]{1,0:T(8,128)}, f32[35,8192]{1,0:T(8,128)S(1)}, u32[]{:S(2)}) copy-start(f32[35,8192]{1,0:T(8,128)S(1)} %collective-permute-done.6.refs_2_) | copy-start | bytes 3440644
  57.3 27.3 %collective-permute-start.14 = (f32[35,8192]{1,0:T(8,128)S(1)}, f32[35,8192]{1,0:T(8,128)}, u32[]{:S(2)}, u32[]{:S(2)}) collective-permute-start(f32[35,8192]{1,0:T(8,128)S(1)} %collective-permute-done.5.refs_0_), channel_id=1, source_target_pairs={{0,1},{1,0},{2,3},{3,2},{4,5},{5,4},{6,7},{7,6},{8,9},{9,8},{10,11... | collective-permute-start | bytes 3440648 | tf_op jit(solution)/shard_map/ppermute | solution.py:599
  57.4 27.3 %collective-permute-start.15 = (f32[35,8192]{1,0:T(8,128)S(1)}, f32[35,8192]{1,0:T(8,128)}, u32[]{:S(2)}, u32[]{:S(2)}) collective-permute-start(f32[35,8192]{1,0:T(8,128)S(1)} %collective-permute-done.6.refs_2_), channel_id=1, source_target_pairs={{0,1},{1,0},{2,3},{3,2},{4,5},{5,4},{6,7},{7,6},{8,9},{9,8},{10,11... | collective-permute-start | bytes 3440648 | tf_op jit(solution)/shard_map/ppermute | solution.py:600
  57.9 12.1 %collective-permute-start.10 = (f32[1,32,128]{2,1,0:T(8,128)S(1)}, f32[1,32,128]{2,1,0:T(8,128)S(1)}, u32[]{:S(2)}, u32[]{:S(2)}) collective-permute-start(f32[1,32,128]{2,1,0:T(8,128)S(1)} %maximum_bitcast_fusion), channel_id=1, source_target_pairs={{0,8},{2,10},{4,12},{6,14},{8,16},{10,18},{12,20},{14,22},{16,24},... | collective-permute-start | bytes 49160 | tf_op jit(solution)/shard_map/ppermute | solution.py:579
  57.9 16.1 %collective-permute-start.8 = (f32[1,32,128]{2,1,0:T(8,128)S(1)}, f32[1,32,128]{2,1,0:T(8,128)S(1)}, u32[]{:S(2)}, u32[]{:S(2)}) collective-permute-start(f32[1,32,128]{2,1,0:T(8,128)S(1)} %maximum_bitcast_fusion), channel_id=1, source_target_pairs={{0,24},{2,26},{4,28},{6,30},{8,0},{10,2},{12,4},{14,6},{16,8},{18,... | collective-permute-start | bytes 49160 | tf_op jit(solution)/shard_map/ppermute | solution.py:579
  61.2 14.1 %collective-permute-start.9 = (f32[1,32,128]{2,1,0:T(8,128)S(1)}, f32[1,32,128]{2,1,0:T(8,128)S(1)}, u32[]{:S(2)}, u32[]{:S(2)}) collective-permute-start(f32[1,32,128]{2,1,0:T(8,128)S(1)} %maximum_bitcast_fusion), channel_id=1, source_target_pairs={{0,16},{2,18},{4,20},{6,22},{8,24},{10,26},{12,28},{14,30},{16,0},... | collective-permute-start | bytes 49160 | tf_op jit(solution)/shard_map/ppermute | solution.py:579
  61.3 25.2 %copy-start.4 = (s32[60,4]{0,1:T(4,128)S(1)}, s32[60,4]{0,1:T(4,128)}, u32[]{:S(2)}) copy-start(s32[60,4]{0,1:T(4,128)} %param.23) | copy-start | bytes 2884
  70.0 42.4 %collective-permute-start = (f32[64,32,128]{2,1,0:T(8,128)}, f32[64,32,128]{2,1,0:T(8,128)}, u32[]{:S(2)}, u32[]{:S(2)}) collective-permute-start(f32[64,32,128]{2,1,0:T(8,128)} %get-tuple-element.63.own), channel_id=1, source_target_pairs={{0,2},{2,4},{4,6},{6,8},{8,10},{10,12},{12,14},{14,16},{16,18},{18... | collective-permute-start | bytes 3145736 | tf_op jit(solution)/shard_map/ppermute | solution.py:592
  74.0 38.4 %collective-permute-start.1 = (f32[64,32,128]{2,1,0:T(8,128)}, f32[64,32,128]{2,1,0:T(8,128)}, u32[]{:S(2)}, u32[]{:S(2)}) collective-permute-start(f32[64,32,128]{2,1,0:T(8,128)} %get-tuple-element.63.own), channel_id=1, source_target_pairs={{2,0},{4,2},{6,4},{8,6},{10,8},{12,10},{14,12},{16,14},{18,16},{20... | collective-permute-start | bytes 3145736 | tf_op jit(solution)/shard_map/ppermute | solution.py:593
  75.4 22.9 %collective-permute-start.11 = (f32[4,32,128]{2,1,0:T(8,128)S(1)}, f32[4,32,128]{2,1,0:T(8,128)S(1)}, u32[]{:S(2)}, u32[]{:S(2)}) collective-permute-start(f32[4,32,128]{2,1,0:T(8,128)S(1)} %constant_dynamic-slice_fusion.1), channel_id=1, source_target_pairs={{0,96},{2,98},{4,100},{6,102},{8,104},{10,106},{12,108},{14,110},{... | collective-permute-start | bytes 196616 | tf_op jit(solution)/shard_map/ppermute | solution.py:579
  84.6 21.5 %collective-permute-start.12 = (f32[4,32,128]{2,1,0:T(8,128)S(1)}, f32[4,32,128]{2,1,0:T(8,128)S(1)}, u32[]{:S(2)}, u32[]{:S(2)}) collective-permute-start(f32[4,32,128]{2,1,0:T(8,128)S(1)} %constant_dynamic-slice_fusion.1), channel_id=1, source_target_pairs={{0,64},{2,66},{4,68},{6,70},{8,72},{10,74},{12,76},{14,78},{16,80}... | collective-permute-start | bytes 196616 | tf_op jit(solution)/shard_map/ppermute | solution.py:579
  84.7 21.5 %collective-permute-start.13 = (f32[4,32,128]{2,1,0:T(8,128)S(1)}, f32[4,32,128]{2,1,0:T(8,128)S(1)}, u32[]{:S(2)}, u32[]{:S(2)}) collective-permute-start(f32[4,32,128]{2,1,0:T(8,128)S(1)} %constant_dynamic-slice_fusion.1), channel_id=1, source_target_pairs={{0,32},{2,34},{4,36},{6,38},{8,40},{10,42},{12,44},{14,46},{16,48}... | collective-permute-start | bytes 196616 | tf_op jit(solution)/shard_map/ppermute | solution.py:579
  106.1 15.8 %collective-permute-start.16 = (f32[32,4096]{1,0:T(8,128)}, f32[32,4096]{1,0:T(8,128)S(1)}, u32[]{:S(2)}, u32[]{:S(2)}) collective-permute-start(f32[32,4096]{1,0:T(8,128)} %get-tuple-element.68), channel_id=1, source_target_pairs={{0,1},{1,0},{2,3},{3,2},{4,5},{5,4},{6,7},{7,6},{8,9},{9,8},{10,11... | collective-permute-start | bytes 1572872 | tf_op jit(solution)/shard_map/ppermute | solution.py:610
  122.0 0.8 copy-start.2

commit v5 on v4

--- a/solution.py
+++ b/solution.py
@@ -30,7 +30,9 @@
 def low_lanes(shape):
     return lax.broadcasted_iota(jnp.int32, shape, 1) < 64
 
-def up_body(points, basis_hbm, values_hbm, moves_hbm, up, trans, packed, rows, basis, values, moves, sem):
+def up_body(
+    points, basis_hbm, values_hbm, moves_hbm, up, trans_hbm, packed_hbm, rows, basis, values, moves, trans, packed, sem
+):
     leaves = basis.shape[0]
     columns = values.shape[0]
     nodes = moves.shape[2]
@@ -45,31 +47,39 @@
     for i in range(4):
         reads[i].wait()
 
-        @pl.loop(16 * i, 16 * i + 16, unroll=4)
+        @pl.loop(16 * i, 16 * i + 16, unroll=8)
         def _(r):
             block = jnp.transpose(moves[r])
             rows[pl.ds(pl.multiple_of(r * PITCH, 8), nodes)] = jnp.concatenate([block, block], axis=1)
 
     left = low_lanes((64, 128))
 
-    @pl.loop(0, nodes, unroll=4)
-    def _(n):
+    def node(n):
         x = rows[pl.ds(n, 64, stride=PITCH), :]
         hi = x.astype(bf16).astype(f32)
         trans[n] = jnp.where(left, hi, x - hi).astype(bf16)
 
+    whole = nodes // 8 * 8
+    pl.loop(0, whole, unroll=8)(node)
+    for n in range(whole, nodes):
+        node(n)
+    trans[nodes] = jnp.zeros(trans.shape[1:], bf16)
+    writes = [pltpu.make_async_copy(trans, trans_hbm, sem.at[6])]
+    writes[0].start()
+
     half = low_lanes((columns, 128))
 
     for read in reads[4:]:
         read.wait()
     packed[0:columns] = values[...]
-    packed[columns:] = points[...]
+    packed[columns : columns + 3] = points[...]
+    packed[columns + 4 :] = jnp.zeros((4, packed.shape[1]), f32)
 
     def leaf_up(i):
         v = stack(values[:, pl.ds(pl.multiple_of(i * 128, 128), 128)])
         return both(fold(lax.dot_general(v, stack(basis[i]), NT, preferred_element_type=f32)))
 
-    @pl.loop(0, leaves // 2, unroll=4)
+    @pl.loop(0, leaves // 2, unroll=8)
     def _(p):
         up[p] = jnp.where(half, leaf_up(2 * p), leaf_up(2 * p + 1))
 
@@ -105,8 +115,17 @@
             for p, tile in enumerate(tiles):
                 up[after + p] = tile
         start, row, width = after, row + width, width // 2
+    up[leaves - 1] = tiles[0]
     share = both(fold(jnp.dot(stack(tiles[0])[:, 0:64], trans[row], preferred_element_type=f32)))
-    up[leaves - 1] = jnp.where(half, tiles[0], share)
+    for c in range(columns):
+        packed[columns + 3 : columns + 4, 128 * c : 128 * c + 128] = share[c : c + 1]
+    packed[columns + 3 : columns + 4, 128 * columns :] = jnp.zeros(
+        (1, packed.shape[1] - 128 * columns), f32
+    )
+    writes.append(pltpu.make_async_copy(packed, packed_hbm, sem.at[7]))
+    writes[1].start()
+    for write in writes:
+        write.wait()
 
 
 def up_pass(points, basis, values, moves):
@@ -118,16 +137,18 @@
         out_shape=(
             jax.ShapeDtypeStruct((leaves, columns, 128), f32),
             jax.ShapeDtypeStruct((nodes + 1, 64, 128), bf16),
-            jax.ShapeDtypeStruct((columns + 3, values.shape[1]), f32),
+            jax.ShapeDtypeStruct((columns + 8, values.shape[1]), f32),
         ),
         in_specs=[VM, HBM, HBM, HBM],
-        out_specs=(VM, VM, VM),
+        out_specs=(VM, HBM, HBM),
         scratch_shapes=[
             pltpu.VMEM((64 * PITCH, 128), f32),
             pltpu.VMEM(basis.shape, f32),
             pltpu.VMEM(values.shape, f32),
             pltpu.VMEM(moves.shape, f32),
-            pltpu.SemaphoreType.DMA((6,)),
+            pltpu.VMEM((nodes + 1, 64, 128), bf16),
+            pltpu.VMEM((columns + 8, values.shape[1]), f32),
+            pltpu.SemaphoreType.DMA((8,)),
         ],
         compiler_params=pltpu.CompilerParams(vmem_limit_bytes=VMEM_BYTES),
         cost_estimate=pl.CostEstimate(flops=400_000_000, bytes_accessed=8_000_000, transcendentals=0),
@@ -199,14 +220,14 @@
             pltpu.SemaphoreType.DMA((2, -(-nodes // CHUNK))),
         ],
         compiler_params=pltpu.CompilerParams(vmem_limit_bytes=VMEM_BYTES),
-        cost_estimate=pl.CostEstimate(flops=100_000_000, bytes_accessed=17_000_000, transcendentals=0),
+        cost_estimate=pl.CostEstimate(flops=1_000, bytes_accessed=1_000, transcendentals=0),
         name="unbatch",
     )(matrices)
 
 
-def top_body(place, partners, first, moves, matrices, parent, up, block, sem):
+def top_body(place, partners, far_three, far_two, far_one, own, moves, matrices, parent, up, block, sem):
     spot = place[0]
-    columns = first.shape[1]
+    columns = own.shape[1]
     copies = []
     width, row = 32, 0
     for level in range(4):
@@ -215,7 +236,8 @@
         copies[-1].start()
         row, width = row + width, width // 2
     half = low_lanes((columns, 128))
-    up[0:16] = first[...]
+    for j, ref in enumerate((far_three, far_two, far_one, own)):
+        up[pl.ds(4 * ((spot // 16 + 1 + j) % 4), 4)] = ref[...]
     def lift(tile, r):
         t = jnp.concatenate([moves[r], moves[r + 1]], axis=0)
         hi, lo = split(t)
@@ -236,38 +258,47 @@
         hi, lo = split(moves[r])
         x = stack(d)
         return fold(lax.dot_general(x, hi, NT, preferred_element_type=f32)) + lax.dot_general(x[:columns], lo, NT, preferred_element_type=f32)
+    for copy in copies:
+        copy.wait()
+    fars = []
+    for level in range(4):
+        index = rows[level] + spot // (2 << level)
+        far = jnp.zeros((columns, 64), f32)
+        for k in range(4):
+            p = partners[index, k]
+            tile = up[tiles[level] + p // 2]
+            x = stack(jnp.where(p % 2 == 0, tile, pltpu.roll(tile, 64, 1))[:, 0:64])
+            hi, lo = split(block[level, k])
+            far = far + fold(lax.dot_general(x, hi, NT, preferred_element_type=f32))
+            far = far + lax.dot_general(x[:columns], lo, NT, preferred_element_type=f32)
+        fars.append(far)
     down = jnp.zeros((columns, 64), f32)
     down = push(down, row + spot // 32)
     for level in range(3, -1, -1):
-        index = rows[level] + spot // (2 << level)
-        down = push(down, index)
-        copies[level].wait()
-        for k in range(4):
-            p = partners[index * 4 + k]
-            tile = up[tiles[level] + p // 2]
-            x = stack(jnp.where(p % 2 == 0, tile, pltpu.roll(tile, 64, 1))[:, 0:64])
-            hi, lo = split(block[level, k])
-            down = down + fold(lax.dot_general(x, hi, NT, preferred_element_type=f32)) + lax.dot_general(x[:columns], lo, NT, preferred_element_type=f32)
+        down = push(down, rows[level] + spot // (2 << level)) + fars[level]
     parent[...] = jnp.concatenate([down, down], axis=1)
 
-def top_pass(place, partners, first, moves, matrices):
-    columns = first.shape[1]
+def top_pass(place, partners, gathered, moves, matrices):
+    columns = gathered[0].shape[1]
     return pl.pallas_call(
         top_body,
         out_shape=jax.ShapeDtypeStruct((columns, 128), f32),
-        in_specs=[SM, SM, VM, VM, HBM],
+        in_specs=[SM, SM] + [VM] * 5 + [HBM],
         out_specs=VM,
         scratch_shapes=[pltpu.VMEM((32, columns, 128), f32), pltpu.VMEM((4, 4, 64, 64), f32), pltpu.SemaphoreType.DMA((4,))],
         compiler_params=pltpu.CompilerParams(vmem_limit_bytes=VMEM_BYTES),
         cost_estimate=pl.CostEstimate(flops=50_000_000, bytes_accessed=2_000_000, transcendentals=0),
         name="top_pass",
-    )(place, partners, first, moves, matrices)
-
-
-def couple_body(codes, low, own, high, matrices, far, gather, held, sem):
-    leaves = own.shape[0]
-    columns = own.shape[1]
+    )(place, partners, *gathered, moves, matrices)
+
+
+def couple_body(codes, low, own, high, matrices, far, gather, tiles, held, sem):
+    leaves, columns, _ = own.shape
     nodes = matrices.shape[1]
+    takes = []
+    for side, ref in enumerate((low, own, high)):
+        takes.append(pltpu.make_async_copy(ref, tiles.at[side], sem.at[3 + side]))
+        takes[-1].start()
     reads = []
     for i in range(3):
         begin = 42 * i
@@ -276,16 +307,17 @@
         reads[-1].start()
     half = low_lanes((columns, 128))
     left = low_lanes((2 * columns, 128))
-    for side, ref in enumerate((low, own, high)):
+    for side in range(3):
+        takes[side].wait()
 
         @pl.loop(0, leaves, unroll=16)
-        def _(t, side=side, ref=ref):
-            x = ref[t]
+        def _(t, side=side):
+            x = tiles[side, t]
             gather[0, side * leaves + t] = stack(x)
             gather[1, side * leaves + t] = stack(pltpu.roll(x, 64, 1))
 
     def pick(n, k, side):
-        code = codes[4 * n + k]
+        code = codes[n, k]
         return gather[(code & 1) ^ side, code >> 1]
 
     def one(n):
@@ -314,12 +346,13 @@
     return pl.pallas_call(
         couple_body,
         out_shape=jax.ShapeDtypeStruct((leaves, columns, 128), f32),
-        in_specs=[SM] + [VM] * 3 + [HBM],
+        in_specs=[SM] + [HBM] * 4,
         out_specs=VM,
         scratch_shapes=[
             pltpu.VMEM((2, 3 * leaves, 2 * columns, 128), bf16),
+            pltpu.VMEM((3, leaves, columns, 128), f32),
             pltpu.VMEM(matrices.shape, bf16),
-            pltpu.SemaphoreType.DMA((3,)),
+            pltpu.SemaphoreType.DMA((6,)),
         ],
         compiler_params=pltpu.CompilerParams(vmem_limit_bytes=VMEM_BYTES),
         cost_estimate=pl.CostEstimate(flops=400_000_000, bytes_accessed=12_000_000, transcendentals=0),
@@ -327,13 +360,17 @@
     )(codes, low, own, high, matrices)
 
 
-def down_body(core, parent, far, trans, basis, mine, given, out, held):
+def down_body(core, parent, far_hbm, trans_hbm, basis_hbm, mine, given, out, far, trans, basis, ones, twos, sem):
     leaves = basis.shape[0]
     columns = out.shape[0]
+    reads = []
+    for i, (source, dest) in enumerate(((far_hbm, far), (trans_hbm, trans), (basis_hbm, basis))):
+        reads.append(pltpu.make_async_copy(source, dest, sem.at[i]))
+        reads[-1].start()
     half = low_lanes((columns, 128))
 
-    def push(d, row, tile):
-        t = jnp.concatenate([trans[row], trans[row + 1]], axis=0)
+    def push(d, tile):
+        t = jnp.concatenate([trans[2 * tile], trans[2 * tile + 1]], axis=0)
         return fold(lax.dot_general(stack(d), t, NT, preferred_element_type=f32)) + far[tile]
 
     def spread(tile):
@@ -341,37 +378,36 @@
         return jnp.where(half, tile, turned), jnp.where(half, turned, tile)
 
     last = leaves - 1
+    above = stack(parent[...])
+    reads[0].wait()
+    reads[1].wait()
     t = trans[2 * last]
-    d = fold(
-        lax.dot_general(
-            stack(parent[...]), jnp.concatenate([t, t], axis=0), NT, preferred_element_type=f32
-        )
-    )
-    sources = [d + far[last]]
+    t = jnp.concatenate([t, t], axis=0)
+    sources = [fold(lax.dot_general(above, t, NT, preferred_element_type=f32)) + far[last]]
     start, width = last, 1
     while width < 16:
-        start = start - max(1, width)
-        made = [push(d, 2 * (start + i), start + i) for i, d in enumerate(sources)]
+        start = start - width
+        made = [push(d, start + i) for i, d in enumerate(sources)]
         sources = [d for tile in made for d in spread(tile)]
         width = 2 * width
-    for i, tile in enumerate(made):
-        held[i] = tile
-    first = start - width
-
-    @pl.loop(0, len(made), unroll=2)
+    start = start - width
+    for i, d in enumerate(sources):
+        ones[i] = push(d, start + i)
+
+    @pl.loop(0, width, unroll=8)
     def _(i):
-        results = []
-        for j, d in enumerate(spread(held[i])):
-            above = 2 * i + j
-            for u, e in enumerate(spread(push(d, 2 * (first + above), first + above))):
-                tile = 2 * above + u
-                for w, x in enumerate(spread(push(e, 2 * tile, tile))):
-                    leaf = 2 * tile + w
-                    results.append(
-                        (leaf, fold(jnp.dot(stack(x), stack(basis[leaf]), preferred_element_type=f32)))
-                    )
-        for leaf, x in results:
-            out[:, pl.ds(pl.multiple_of(leaf * 128, 128), 128)] = x
+        for u, d in enumerate(spread(ones[i])):
+            twos[2 * i + u] = push(d, 2 * i + u)
+
+    reads[2].wait()
+
+    @pl.loop(0, leaves // 2, unroll=4)
+    def _(i):
+        for u, d in enumerate(spread(twos[i])):
+            leaf = 2 * i + u
+            out[:, pl.ds(pl.multiple_of(leaf * 128, 128), 128)] = fold(
+                jnp.dot(stack(d), stack(basis[leaf]), preferred_element_type=f32)
+            )
 
     size = mine.shape[1]
     out[:, pl.ds(pl.multiple_of(core[0] * size, size), size)] += mine[...]
@@ -384,9 +420,16 @@
     return pl.pallas_call(
         down_body,
         out_shape=jax.ShapeDtypeStruct((columns, leaves * 128), f32),
-        in_specs=[SM] + [VM] * 6,
+        in_specs=[SM, VM, HBM, HBM, HBM, VM, VM],
         out_specs=VM,
-        scratch_shapes=[pltpu.VMEM((8, columns, 128), f32)],
+        scratch_shapes=[
+            pltpu.VMEM(far.shape, f32),
+            pltpu.VMEM(trans.shape, bf16),
+            pltpu.VMEM(basis.shape, f32),
+            pltpu.VMEM((leaves // 4, columns, 128), f32),
+            pltpu.VMEM((leaves // 2, columns, 128), f32),
+            pltpu.SemaphoreType.DMA((3,)),
+        ],
         compiler_params=pltpu.CompilerParams(vmem_limit_bytes=VMEM_BYTES),
         cost_estimate=pl.CostEstimate(flops=200_000_000, bytes_accessed=7_000_000, transcendentals=0),
         name="down_pass",
@@ -398,29 +441,19 @@
 SLOTS = 28
 PAIR = 2
 
-def near_body(unroll, chunks, lists, counts, targets, *refs):
-    sources, refs = refs[: 2 * chunks], refs[2 * chunks :]
+def near_body(unroll, chunks, core, lists, counts, targets, *refs):
+    origins, refs = refs[: 2 * chunks], refs[2 * chunks :]
     begin = None
     if chunks == 2:
         begin, refs = refs[0:2], refs[2:]
-    mine, other, columns_of, total, weights, places = refs
+    mine, other, columns_of, total, weights, places, sem, *sources = refs
     leaves = mine.shape[1] // 128
     width = sources[0].shape[1] // 128
-    core = counts[leaves]
-    for c in range(chunks):
-        near_ref, far_ref = sources[2 * c], sources[2 * c + 1]
-        lower = 0 if chunks == 1 or c == 1 else core * (leaves // 8)
-        upper = width // 8 if chunks == 1 or c == 0 else (core + 1) * (leaves // 8)
-
-        @pl.loop(lower, upper)
-        def _(g, c=c, near_ref=near_ref, far_ref=far_ref):
-            for u in range(8):
-                j = 8 * g + u
-                at = pl.ds(pl.multiple_of(j * 128, 128), 128)
-                x = near_weight * jnp.concatenate([near_ref[0:32, at], far_ref[0:32, at]], axis=0)
-                weights[c * width + j] = stack(x)
-                places[c * width + j, 0:3] = near_ref[32:35, at]
-
+    core = core[0]
+    reads = []
+    for i, (origin, source) in enumerate(zip(origins, sources)):
+        reads.append(pltpu.make_async_copy(origin, source, sem.at[i]))
+        reads[-1].start()
     weights[chunks * width] = jnp.zeros(weights.shape[1:], bf16)
     places[chunks * width] = jnp.zeros(places.shape[1:], f32)
     blank = jnp.zeros((5, 128), f32)
@@ -437,6 +470,22 @@
                 columns_of[16 * g + u, c] = jnp.broadcast_to(t[:, 8 * u + c : 8 * u + c + 1], (128, 128))
             total[16 * g + u] = jnp.zeros((128, 128), f32)
 
+    for read in reads:
+        read.wait()
+    for c in range(chunks):
+        near_ref, far_ref = sources[2 * c], sources[2 * c + 1]
+        lower = 0 if chunks == 1 or c == 1 else core * (leaves // 8)
+        upper = width // 8 if chunks == 1 or c == 0 else (core + 1) * (leaves // 8)
+
+        @pl.loop(lower, upper)
+        def _(g, c=c, near_ref=near_ref, far_ref=far_ref):
+            for u in range(8):
+                j = 8 * g + u
+                at = pl.ds(pl.multiple_of(j * 128, 128), 128)
+                x = near_weight * jnp.concatenate([near_ref[0:32, at], far_ref[0:32, at]], axis=0)
+                weights[c * width + j] = stack(x)
+                places[c * width + j, 0:3] = near_ref[32:35, at]
+
     items = lax.fori_loop(
         0, leaves, lambda i, s: s + jnp.maximum((counts[i] + PAIR - 1) // PAIR, 1), jnp.int32(0)
     )
@@ -444,7 +493,7 @@
     def block(leaf, slot):
         kernels, parts = [], []
         for u in range(PAIR):
-            j = lists[leaf * SLOTS + slot + u]
+            j = lists[leaf, slot + u]
             s = places[j]
             d = columns_of[leaf, 0] - s[0:1]
             squared = d * d + smoothing
@@ -489,8 +538,8 @@
             other[:, at] = begin[1][:, at] + x[32:64]
 
 
-def near_pass(unroll, lists, counts, targets, sources, begin=()):
-    leaves = lists.shape[0] // SLOTS
+def near_pass(unroll, core, lists, counts, targets, sources, begin=()):
+    leaves = lists.shape[0]
     chunks = len(sources) // 2
     held = chunks * (sources[0].shape[1] // 128) + 1
     side = jax.ShapeDtypeStruct((32, leaves * 128), f32)
@@ -498,18 +547,20 @@
     return pl.pallas_call(
         functools.partial(near_body, unroll, chunks),
         out_shape=(side, side),
-        in_specs=[SM, SM] + [VM] * len(arrays),
+        in_specs=[SM, SM, SM, VM] + [HBM] * len(sources) + [VM] * len(begin),
         out_specs=(VM, VM),
         scratch_shapes=[
             pltpu.VMEM((leaves, 3, 128, 128), f32),
             pltpu.VMEM((leaves + 1, 128, 128), f32),
             pltpu.VMEM((held, 128, 128), bf16),
             pltpu.VMEM((held, 8, 128), f32),
+            pltpu.SemaphoreType.DMA((len(sources),)),
+            *[pltpu.VMEM(x.shape, f32) for x in sources],
         ],
         compiler_params=pltpu.CompilerParams(vmem_limit_bytes=VMEM_BYTES),
         cost_estimate=pl.CostEstimate(flops=1_000, bytes_accessed=1_000, transcendentals=0),
         name="near_pass",
-    )(lists, counts, *arrays)
+    )(core, lists, counts, *arrays)
 
 
 def arranged(picked, leaf_ids, empty):
@@ -521,7 +572,7 @@
     found = jnp.sum(jnp.where(here, leaf_ids[:, :, None], 0), axis=1)
     count = jnp.sum(picked.astype(jnp.int32), axis=1)
     lists = jnp.where(jnp.arange(SLOTS)[None, :] < count[:, None], found, empty)
-    return lists.astype(jnp.int32).reshape(-1), count
+    return lists.astype(jnp.int32), count
 
 
 def partner_codes(partners, position, leaves):
@@ -535,7 +586,7 @@
     starts = jnp.array(starts, jnp.int32)[:, None]
     local = partners - position * spans
     side = jnp.where(local < 0, 0, jnp.where(local < spans, 1, 2))
-    return (side * (2 * leaves) + starts + local - (side - 1) * spans).reshape(-1)
+    return (side * (2 * leaves) + starts + local - (side - 1) * spans)
 
 
 def local(
@@ -567,8 +618,6 @@
     near_ids, near_live = arranged(alive & inside, chosen, leaves)
     outside_ids = jnp.where(chosen < 0, chosen + leaves, chosen)
     far_ids, far_live = arranged(alive & ~inside, outside_ids, 2 * leaves)
-    near_live = jnp.concatenate([near_live, core[None]]).astype(jnp.int32)
-    far_live = jnp.concatenate([far_live, core[None]]).astype(jnp.int32)
     codes = partner_codes(partners, position, leaves)
 
     def ring(x, stride):
@@ -580,41 +629,53 @@
         return turned, spot
 
     def in_order(turned, x, spot):
-        both_rounds = jnp.concatenate([*turned, x, *turned, x], axis=0)
-        return lax.dynamic_slice_in_dim(both_rounds, (3 - spot) * x.shape[0], 4 * x.shape[0], 0)
+        blocks = [*turned, x]
+        ordered = []
+        for k in range(4):
+            block = blocks[3]
+            for j in range(3):
+                block = jnp.where(spot == (k - j - 1) % 4, blocks[j], block)
+            ordered.append(block)
+        return jnp.concatenate(ordered, axis=0)
 
     after = lax.optimization_barrier
+    core = core[None].astype(jnp.int32)
+    columns = values.shape[0]
     up, trans, packed = up_pass(points, basis, values, transfer.transpose(1, 2, 0))
-    share = up[leaves - 1, :, 64:]
-    shares, spot = ring(share[None], 1)
     low = lax.ppermute(packed, "leaf", forward)
     high = lax.ppermute(packed, "leaf", backward)
+    near_ids, far_ids, codes, up = after((near_ids, far_ids, codes, up))
+    begin = near_pass(12, core, near_ids, near_live, points, (packed, across))
+    low, high, coupling, begin = after((low, high, coupling, begin))
+    row = slice(columns + 3, columns + 4)
+    lanes = 128 * columns
+    sibling = jnp.where(position % 2 == 0, high[row, 0:lanes], low[row, 0:lanes])
+    level = (packed[row, 0:lanes] + sibling).reshape(columns, 128)
+    pair = lax.ppermute(level, "leaf", [(i, i ^ 2) for i in range(count)])
+    low_across = lax.ppermute(low, "rhs", swap)
+    high_across = lax.ppermute(high, "rhs", swap)
+    pair, up, coupling = after((pair, up, coupling))
     up_low = lax.ppermute(up, "leaf", forward)
     up_high = lax.ppermute(up, "leaf", backward)
-    near_ids, far_ids, codes, up = after((near_ids, far_ids, codes, up))
-    begin = near_pass(8, near_ids, near_live, points, (packed, across))
-    shares, low, high, coupling, begin = after((shares, low, high, coupling, begin))
-    level = in_order(shares, share[None], spot)
-    level = jnp.concatenate([level[0] + level[1], level[2] + level[3]], axis=1)[None]
-    low_across = lax.ppermute(low, "rhs", swap)
-    high_across = lax.ppermute(high, "rhs", swap)
+    matrices = unbatch(coupling.transpose(1, 2, 3, 0))
+    pair, far_ids, matrices = after((pair, far_ids, matrices))
+    lower = jnp.arange(128) < 64
+    level = jnp.where(lower == (position & 2 == 0), level, pair)[None]
     turned, spot = ring(level, 4)
-    matrices = unbatch(coupling.transpose(1, 2, 3, 0))
-    turned, far_ids, matrices = after((turned, far_ids, matrices))
-    level = in_order(turned, level, spot)
-    turned, spot = ring(level, 16)
     mine, other = near_pass(
-        8, far_ids, far_live, points, (low, low_across, high, high_across), begin
+        12, core, far_ids, far_live, points, (low, low_across, high, high_across), begin
     )
     turned, mine, other = after((turned, mine, other))
     given = lax.ppermute(other, "rhs", swap)
     level = in_order(turned, level, spot)
+    turned, spot = ring(level, 16)
+    codes, mine = after((codes, mine))
+    far = couple_pass(codes, up_low, up, up_high, matrices)
+    turned, far = after((turned, far))
     parent = top_pass(
-        position[None].astype(jnp.int32), partners_top.reshape(-1), level, transfer_top, coupling_top
+        position[None].astype(jnp.int32), partners_top, (*turned, level), transfer_top, coupling_top
     )
-    up_low, up_high, parent = after((up_low, up_high, parent))
-    far = couple_pass(codes, up_low, up, up_high, matrices)
-    return down_pass(core[None].astype(jnp.int32), parent, far, trans, basis, mine, given)
+    return down_pass(core, parent, far, trans, basis, mine, given)
 
 
 def solution(mesh):

time: 139 us -> 130 us (0.935)
  the two profiles are of different devices: /device:TPU:0 before, /device:TPU:4 now
where the time goes in v5:
time: 130 us; the launch traced here: 128 us
  Pallas kernels  77.3 us (59%)
  starting transfers between devices  32.6 us (25%)
  waiting for transfers between devices  10.7 us (8%)
  other arithmetic  4.38 us (3%)
  local copies, waits for them, and re-layouts  2.67 us (2%)
    pallas_call x2, Pallas kernels, near_pass(): pl.pallas_call(functools.partial(near_body, unroll, chunks), out_shape=(s...  32.2 us
    ppermute x6, starting transfers between devices, ring(): turned.append(lax.ppermute(x, 'leaf', to))  13 us
    pallas_call x1, Pallas kernels, up_pass(): pl.pallas_call(up_body, out_shape=(jax.ShapeDtypeStruct((leaves, columns,...  12.7 us
    pallas_call x1, Pallas kernels, couple_pass(): pl.pallas_call(couple_body, out_shape=jax.ShapeDtypeStruct((leaves, colum...  10.5 us
    pallas_call x1, Pallas kernels, unbatch(): pl.pallas_call(unbatch_body, out_shape=jax.ShapeDtypeStruct((2, nodes, 12...  8.67 us
    pallas_call x1, Pallas kernels, down_pass(): pl.pallas_call(down_body, out_shape=jax.ShapeDtypeStruct((columns, leaves...  8.64 us
    ppermute x1, waiting for transfers between devices, local(): low = lax.ppermute(packed, 'leaf', forward)  6.87 us
    ppermute x1, starting transfers between devices, local(): up_high = lax.ppermute(up, 'leaf', backward)  4.86 us
  transfers between devices with their start and end apart: 15, of which 3 were waited for; matrix products, arithmetic and copies ran while one was open for 4% of the time, Pallas kernels for 54%

profile of v5, /device:TPU:4, one launch (start us, length us, event | category | flops | bytes accessed | tf_op | source)
XLA Modules:
  0.0 128.2 jit_solution(13720023704937748330)
XLA Ops:
  0.0 0.0 collective-permute-start.2
  0.0 0.0 copy-start.12
  0.0 0.0 copy-start.13
  0.0 12.7 %up_pass.1 = (f32[64,32,128]{2,1,0:T(8,128)}, bf16[128,64,128]{2,1,0:T(8,128)(2,1)}, f32[40,8192]{1,0:T(8,128)}) custom-call(f32[3,8192]{1,0:T(4,128)} %targets.3, f32[64,64,128]{2,1,0:T(8,128)} %basis_hbm.3, f32[32,8192]{1,0:T(8,128)} %values_hbm.1, f32[64,64,127]{2,1,0:T(8,128)} %bitcast.8), custom_call_target="tpu_custom_call" | custom-call | flops 400000000 | bytes 8000000 | tf_op jit(solution)/shard_map/up_pass/pallas_call | solution.py:135
  12.8 3.5 %collective-permute-start = (f32[40,8192]{1,0:T(8,128)}, f32[40,8192]{1,0:T(8,128)S(1)}, u32[]{:S(2)}, u32[]{:S(2)}) collective-permute-start(f32[40,8192]{1,0:T(8,128)} %get-tuple-element.38.refs_0_), channel_id=1, source_target_pairs={{0,2},{2,4},{4,6},{6,8},{8,10},{10,12},{12,14},{14,16},{16,18},{18... | collective-permute-start | bytes 3932168 | tf_op jit(solution)/shard_map/ppermute | solution.py:645
  16.3 4.5 %collective-permute-start.1 = (f32[40,8192]{1,0:T(8,128)}, f32[40,8192]{1,0:T(8,128)S(1)}, u32[]{:S(2)}, u32[]{:S(2)}) collective-permute-start(f32[40,8192]{1,0:T(8,128)} %get-tuple-element.38.refs_0_), channel_id=1, source_target_pairs={{2,0},{4,2},{6,4},{8,6},{10,8},{12,10},{14,12},{16,14},{18,16},{20... | collective-permute-start | bytes 3932168 | tf_op jit(solution)/shard_map/ppermute | solution.py:646
  20.8 0.1 dynamic_slice.6
  20.8 0.1 convert_reduce_fusion
  21.0 0.3 select_reduce_fusion.1
  21.3 0.1 copy.48
  21.4 0.1 copy.49
  21.5 0.1 copy.50
  21.6 0.1 copy.51
  21.8 0.6 sub.31.codes
  22.4 1.0 select_reduce_fusion
  23.4 0.7 fusion.5.lists
  24.1 0.7 fusion.6.lists
  24.7 16.5 %near_pass.2 = (f32[32,4096]{1,0:T(8,128)}, f32[32,4096]{1,0:T(8,128)}) custom-call(s32[1]{0:T(128)} %bitcast.core, s32[32,28]{1,0:T(8,128)} %fusion.5.lists, s32[32]{0:T(128)} %copy-done.8, f32[3,8192]{1,0:T(4,128)} %targets.3, f32[40,8192]{1,0:T(8,128)} %get-tuple-element.38.refs_0_, f32[32,8192]{1,0:T(8,128)} %collective-permute-done.2.refs_1_), custom_call_target="tpu_custom_call" | custom-call | flops 1000 | bytes 1000 | tf_op jit(solution)/shard_map/near_pass/pallas_call | solution.py:547
  41.3 6.9 %collective-permute-done.refs_0_ = f32[40,8192]{1,0:T(8,128)S(1)} collective-permute-done((f32[40,8192]{1,0:T(8,128)}, f32[40,8192]{1,0:T(8,128)S(1)}, u32[]{:S(2)}, u32[]{:S(2)}) %collective-permute-start) | collective-permute-done | bytes 1310752 | tf_op jit(solution)/shard_map/ppermute | solution.py:645
  48.2 1.3 %collective-permute-done.1.refs_2_ = f32[40,8192]{1,0:T(8,128)S(1)} collective-permute-done((f32[40,8192]{1,0:T(8,128)}, f32[40,8192]{1,0:T(8,128)S(1)}, u32[]{:S(2)}, u32[]{:S(2)}) %collective-permute-start.1) | collective-permute-done | bytes 1310752 | tf_op jit(solution)/shard_map/ppermute | solution.py:646
  49.5 0.0 collective-permute-start.7
  49.5 0.5 collective-permute-start.8
  50.0 0.9 fusion.2
  50.9 2.8 %collective-permute-start.3 = (f32[32,128]{1,0:T(8,128)S(1)}, f32[32,128]{1,0:T(8,128)S(1)}, u32[]{:S(2)}, u32[]{:S(2)}) collective-permute-start(f32[32,128]{1,0:T(8,128)S(1)} %bitcast.9), channel_id=1, source_target_pairs={{0,4},{2,6},{4,0},{6,2},{8,12},{10,14},{12,8},{14,10},{16,20},{18,... | collective-permute-start | bytes 49160 | tf_op jit(solution)/shard_map/ppermute | solution.py:654
  53.7 2.5 %collective-permute-done.3 = f32[32,128]{1,0:T(8,128)S(1)} collective-permute-done((f32[32,128]{1,0:T(8,128)S(1)}, f32[32,128]{1,0:T(8,128)S(1)}, u32[]{:S(2)}, u32[]{:S(2)}) %collective-permute-start.3) | collective-permute-done | bytes 16416 | tf_op jit(solution)/shard_map/ppermute | solution.py:654
  56.2 3.5 %collective-permute-start.12 = (f32[64,32,128]{2,1,0:T(8,128)}, f32[64,32,128]{2,1,0:T(8,128)}, u32[]{:S(2)}, u32[]{:S(2)}) collective-permute-start(f32[64,32,128]{2,1,0:T(8,128)} %get-tuple-element.62.own), channel_id=1, source_target_pairs={{0,2},{2,4},{4,6},{6,8},{8,10},{10,12},{12,14},{14,16},{16,18},{18... | collective-permute-start | bytes 3145736 | tf_op jit(solution)/shard_map/ppermute | solution.py:658
  59.7 4.9 %collective-permute-start.13 = (f32[64,32,128]{2,1,0:T(8,128)}, f32[64,32,128]{2,1,0:T(8,128)}, u32[]{:S(2)}, u32[]{:S(2)}) collective-permute-start(f32[64,32,128]{2,1,0:T(8,128)} %get-tuple-element.62.own), channel_id=1, source_target_pairs={{2,0},{4,2},{6,4},{8,6},{10,8},{12,10},{14,12},{16,14},{18,16},{20... | collective-permute-start | bytes 3145736 | tf_op jit(solution)/shard_map/ppermute | solution.py:659
  64.6 8.7 %unbatch.1.matrices = bf16[2,127,128,128]{3,2,1,0:T(8,128)(2,1)} custom-call(f32[4,64,64,127]{3,2,1,0:T(8,128)} %bitcast.7), custom_call_target="tpu_custom_call" | custom-call | flops 1000 | bytes 1000 | tf_op jit(solution)/shard_map/unbatch/pallas_call | solution.py:210
  73.3 0.0 copy-start.10
  73.3 0.6 collective-permute-start.4
  73.9 0.0 collective-permute-done.7.refs_1_
  73.9 2.7 %collective-permute-start.5 = (f32[1,32,128]{2,1,0:T(8,128)S(1)}, f32[1,32,128]{2,1,0:T(8,128)S(1)}, u32[]{:S(2)}, u32[]{:S(2)}) collective-permute-start(f32[1,32,128]{2,1,0:T(8,128)S(1)} %select_bitcast_fusion), channel_id=1, source_target_pairs={{0,16},{2,18},{4,20},{6,22},{8,24},{10,26},{12,28},{14,30},{16,0},... | collective-permute-start | bytes 49160 | tf_op jit(solution)/shard_map/ppermute | solution.py:628
  76.6 0.0 collective-permute-start.6
  76.6 15.7 %near_pass.3 = (f32[32,4096]{1,0:T(8,128)}, f32[32,4096]{1,0:T(8,128)}) custom-call(s32[1]{0:T(128)} %bitcast.core, s32[32,28]{1,0:T(8,128)} %fusion.6.lists, s32[32]{0:T(128)} %copy-done.9, f32[3,8192]{1,0:T(4,128)} %targets.3, f32[40,8192]{1,0:T(8,128)} %copy-done, f32[40,8192]{1,0:T(8,128)} %collective-permute-done.7.refs_1_, f32[40,8192]{1,0:T(8,128)} %copy-done.1, ...), custom_call_target="tpu_custom_call" | custom-call | flops 1000 | bytes 1000 | tf_op jit(solution)/shard_map/near_pass/pallas_call | solution.py:547
  92.3 0.0 collective-permute-done.5
  92.3 0.1 collective-permute-start.14
  92.5 2.1 %collective-permute-start.10 = (f32[4,32,128]{2,1,0:T(8,128)S(1)}, f32[4,32,128]{2,1,0:T(8,128)S(1)}, u32[]{:S(2)}, u32[]{:S(2)}) collective-permute-start(f32[4,32,128]{2,1,0:T(8,128)S(1)} %pad_maximum_fusion.own), channel_id=1, source_target_pairs={{0,64},{2,66},{4,68},{6,70},{8,72},{10,74},{12,76},{14,78},{16,80}... | collective-permute-start | bytes 196616 | tf_op jit(solution)/shard_map/ppermute | solution.py:628
  94.6 5.1 %collective-permute-start.11 = (f32[4,32,128]{2,1,0:T(8,128)S(1)}, f32[4,32,128]{2,1,0:T(8,128)S(1)}, u32[]{:S(2)}, u32[]{:S(2)}) collective-permute-start(f32[4,32,128]{2,1,0:T(8,128)S(1)} %pad_maximum_fusion.own), channel_id=1, source_target_pairs={{0,32},{2,34},{4,36},{6,38},{8,40},{10,42},{12,44},{14,46},{16,48}... | collective-permute-start | bytes 196616 | tf_op jit(solution)/shard_map/ppermute | solution.py:628
  99.7 2.4 %collective-permute-start.9 = (f32[4,32,128]{2,1,0:T(8,128)S(1)}, f32[4,32,128]{2,1,0:T(8,128)S(1)}, u32[]{:S(2)}, u32[]{:S(2)}) collective-permute-start(f32[4,32,128]{2,1,0:T(8,128)S(1)} %pad_maximum_fusion.own), channel_id=1, source_target_pairs={{0,96},{2,98},{4,100},{6,102},{8,104},{10,106},{12,108},{14,110},{... | collective-permute-start | bytes 196616 | tf_op jit(solution)/shard_map/ppermute | solution.py:628
  102.1 0.7 copy.52.partners
  102.8 10.5 %couple_pass.1.far_hbm = f32[64,32,128]{2,1,0:T(8,128)} custom-call(s32[127,4]{1,0:T(8,128)} %sub.31.codes, f32[64,32,128]{2,1,0:T(8,128)} %collective-permute-done.12.low, f32[64,32,128]{2,1,0:T(8,128)} %get-tuple-element.62.own, f32[64,32,128]{2,1,0:T(8,128)} %collective-permute-done.13.high, bf16[2,127,128,128]{3,2,1,0:T(8,128)(2,1)} %unbatch.1.matrices), custom_call_target="tpu_custom_call" | custom-call | flops 400000000 | bytes 12000000 | tf_op jit(solution)/shard_map/couple_pass/pallas_call | solution.py:346
  113.4 0.0 copy-start.6
  113.4 0.6 copy-done.4
  114.0 0.0 copy-done.5
  114.0 0.0 copy-done.6
  114.0 4.6 %top_pass.1.parent = f32[32,128]{1,0:T(8,128)} custom-call(s32[1]{0:T(128)} %bitcast.1.place, s32[60,4]{1,0:T(8,128)} %copy.52.partners, f32[4,32,128]{2,1,0:T(8,128)} %copy-done.6, f32[4,32,128]{2,1,0:T(8,128)} %copy-done.4, f32[4,32,128]{2,1,0:T(8,128)} %copy-done.5, f32[4,32,128]{2,1,0:T(8,128)} %copy-done.3, f32[62,64,64]{2,1,0:T(8,128)} %moves.1, ...), custom_call_target="tpu_custom_call" | custom-call | flops 50000000 | bytes 2000000 | tf_op jit(solution)/shard_map/top_pass/pallas_call | solution.py:283
  118.6 0.8 copy-done.2
  119.4 8.6 %down_pass.1 = f32[32,8192]{1,0:T(8,128)} custom-call(s32[1]{0:T(128)} %bitcast.core, f32[32,128]{1,0:T(8,128)} %top_pass.1.parent, f32[64,32,128]{2,1,0:T(8,128)} %couple_pass.1.far_hbm, bf16[128,64,128]{2,1,0:T(8,128)(2,1)} %get-tuple-element.68.trans_hbm, f32[64,64,128]{2,1,0:T(8,128)} %basis_hbm.3, f32[32,4096]{1,0:T(8,128)} %get-tuple-element.69.mine, ...), custom_call_target="tpu_custom_call" | custom-call | flops 200000000 | bytes 7000000 | tf_op jit(solution)/shard_map/down_pass/pallas_call | solution.py:420
  (41 shorter events, 0.2 us)
Async XLA Ops:
  0.0 24.7 %collective-permute-start.2 = (f32[32,8192]{1,0:T(8,128)}, f32[32,8192]{1,0:T(8,128)}, u32[]{:S(2)}, u32[]{:S(2)}) collective-permute-start(f32[32,8192]{1,0:T(8,128)} %values_hbm.1), channel_id=1, source_target_pairs={{0,1},{1,0},{2,3},{3,2},{4,5},{5,4},{6,7},{7,6},{8,9},{9,8},{10,11... | collective-permute-start | bytes 3145736 | tf_op jit(solution)/shard_map/ppermute | solution.py:612
  0.0 20.8 %copy-start.14 = (s32[64]{0:T(128)S(1)}, s32[64]{0:T(128)}, u32[]{:S(2)}) copy-start(s32[64]{0:T(128)} %param.16) | copy-start | bytes 772
  0.0 20.8 %copy-start.7 = (s32[64,27]{0,1:T(8,128)S(1)}, s32[64,27]{0,1:T(8,128)}, u32[]{:S(2)}) copy-start(s32[64,27]{0,1:T(8,128)} %param.15) | copy-start | bytes 20740
  0.0 21.5 %copy-start.12 = (s32[127]{0:T(128)S(1)}, s32[127]{0:T(128)}, u32[]{:S(2)}) copy-start(s32[127]{0:T(128)} %constant.62.clone) | copy-start | bytes 1528
  0.0 21.4 %copy-start.11 = (s32[127,4]{0,1:T(4,128)S(1)}, s32[127,4]{0,1:T(4,128)}, u32[]{:S(2)}) copy-start(s32[127,4]{0,1:T(4,128)} %param.20) | copy-start | bytes 6100
  0.0 21.4 %copy-start.13 = (s32[127]{0:T(128)S(1)}, s32[127]{0:T(128)}, u32[]{:S(2)}) copy-start(s32[127]{0:T(128)} %constant.63.clone) | copy-start | bytes 1528
  12.8 35.4 %collective-permute-start = (f32[40,8192]{1,0:T(8,128)}, f32[40,8192]{1,0:T(8,128)S(1)}, u32[]{:S(2)}, u32[]{:S(2)}) collective-permute-start(f32[40,8192]{1,0:T(8,128)} %get-tuple-element.38.refs_0_), channel_id=1, source_target_pairs={{0,2},{2,4},{4,6},{6,8},{8,10},{10,12},{12,14},{14,16},{16,18},{18... | collective-permute-start | bytes 3932168 | tf_op jit(solution)/shard_map/ppermute | solution.py:645
  16.3 33.2 %collective-permute-start.1 = (f32[40,8192]{1,0:T(8,128)}, f32[40,8192]{1,0:T(8,128)S(1)}, u32[]{:S(2)}, u32[]{:S(2)}) collective-permute-start(f32[40,8192]{1,0:T(8,128)} %get-tuple-element.38.refs_0_), channel_id=1, source_target_pairs={{2,0},{4,2},{6,4},{8,6},{10,8},{12,10},{14,12},{16,14},{18,16},{20... | collective-permute-start | bytes 3932168 | tf_op jit(solution)/shard_map/ppermute | solution.py:646
  20.9 20.3 %copy-start.9 = (s32[32]{0:T(128)}, s32[32]{0:T(128)S(1)}, u32[]{:S(2)}) copy-start(s32[32]{0:T(128)S(1)} %get-tuple-element.73.counts) | copy-start | bytes 388
  21.0 3.8 %copy-start.8 = (s32[32]{0:T(128)}, s32[32]{0:T(128)S(1)}, u32[]{:S(2)}) copy-start(s32[32]{0:T(128)S(1)} %get-tuple-element.77.counts) | copy-start | bytes 388
  48.2 25.1 %copy-start = (f32[40,8192]{1,0:T(8,128)}, f32[40,8192]{1,0:T(8,128)S(1)}, u32[]{:S(2)}) copy-start(f32[40,8192]{1,0:T(8,128)S(1)} %collective-permute-done.refs_0_) | copy-start | bytes 3932164
  49.5 23.8 %copy-start.1 = (f32[40,8192]{1,0:T(8,128)}, f32[40,8192]{1,0:T(8,128)S(1)}, u32[]{:S(2)}) copy-start(f32[40,8192]{1,0:T(8,128)S(1)} %collective-permute-done.1.refs_2_) | copy-start | bytes 3932164
  49.5 24.5 %collective-permute-start.7 = (f32[40,8192]{1,0:T(8,128)S(1)}, f32[40,8192]{1,0:T(8,128)}, u32[]{:S(2)}, u32[]{:S(2)}) collective-permute-start(f32[40,8192]{1,0:T(8,128)S(1)} %collective-permute-done.refs_0_), channel_id=1, source_target_pairs={{0,1},{1,0},{2,3},{3,2},{4,5},{5,4},{6,7},{7,6},{8,9},{9,8},{10,11... | collective-permute-start | bytes 3932168 | tf_op jit(solution)/shard_map/ppermute | solution.py:655
  49.5 27.2 %collective-permute-start.8 = (f32[40,8192]{1,0:T(8,128)S(1)}, f32[40,8192]{1,0:T(8,128)}, u32[]{:S(2)}, u32[]{:S(2)}) collective-permute-start(f32[40,8192]{1,0:T(8,128)S(1)} %collective-permute-done.1.refs_2_), channel_id=1, source_target_pairs={{0,1},{1,0},{2,3},{3,2},{4,5},{5,4},{6,7},{7,6},{8,9},{9,8},{10,11... | collective-permute-start | bytes 3932168 | tf_op jit(solution)/shard_map/ppermute | solution.py:656
  50.9 5.3 %collective-permute-start.3 = (f32[32,128]{1,0:T(8,128)S(1)}, f32[32,128]{1,0:T(8,128)S(1)}, u32[]{:S(2)}, u32[]{:S(2)}) collective-permute-start(f32[32,128]{1,0:T(8,128)S(1)} %bitcast.9), channel_id=1, source_target_pairs={{0,4},{2,6},{4,0},{6,2},{8,12},{10,14},{12,8},{14,10},{16,20},{18,... | collective-permute-start | bytes 49160 | tf_op jit(solution)/shard_map/ppermute | solution.py:654
  56.2 43.5 %collective-permute-start.12 = (f32[64,32,128]{2,1,0:T(8,128)}, f32[64,32,128]{2,1,0:T(8,128)}, u32[]{:S(2)}, u32[]{:S(2)}) collective-permute-start(f32[64,32,128]{2,1,0:T(8,128)} %get-tuple-element.62.own), channel_id=1, source_target_pairs={{0,2},{2,4},{4,6},{6,8},{8,10},{10,12},{12,14},{14,16},{16,18},{18... | collective-permute-start | bytes 3145736 | tf_op jit(solution)/shard_map/ppermute | solution.py:658
  59.7 43.2 %collective-permute-start.13 = (f32[64,32,128]{2,1,0:T(8,128)}, f32[64,32,128]{2,1,0:T(8,128)}, u32[]{:S(2)}, u32[]{:S(2)}) collective-permute-start(f32[64,32,128]{2,1,0:T(8,128)} %get-tuple-element.62.own), channel_id=1, source_target_pairs={{2,0},{4,2},{6,4},{8,6},{10,8},{12,10},{14,12},{16,14},{18,16},{20... | collective-permute-start | bytes 3145736 | tf_op jit(solution)/shard_map/ppermute | solution.py:659
  73.3 28.8 %copy-start.10 = (s32[60,4]{0,1:T(4,128)S(1)}, s32[60,4]{0,1:T(4,128)}, u32[]{:S(2)}) copy-start(s32[60,4]{0,1:T(4,128)} %param.23) | copy-start | bytes 2884
  73.3 19.0 %collective-permute-start.4 = (f32[1,32,128]{2,1,0:T(8,128)S(1)}, f32[1,32,128]{2,1,0:T(8,128)S(1)}, u32[]{:S(2)}, u32[]{:S(2)}) collective-permute-start(f32[1,32,128]{2,1,0:T(8,128)S(1)} %select_bitcast_fusion), channel_id=1, source_target_pairs={{0,24},{2,26},{4,28},{6,30},{8,0},{10,2},{12,4},{14,6},{16,8},{18,... | collective-permute-start | bytes 49160 | tf_op jit(solution)/shard_map/ppermute | solution.py:628
  73.9 18.4 %collective-permute-start.5 = (f32[1,32,128]{2,1,0:T(8,128)S(1)}, f32[1,32,128]{2,1,0:T(8,128)S(1)}, u32[]{:S(2)}, u32[]{:S(2)}) collective-permute-start(f32[1,32,128]{2,1,0:T(8,128)S(1)} %select_bitcast_fusion), channel_id=1, source_target_pairs={{0,16},{2,18},{4,20},{6,22},{8,24},{10,26},{12,28},{14,30},{16,0},... | collective-permute-start | bytes 49160 | tf_op jit(solution)/shard_map/ppermute | solution.py:628
  76.6 15.7 %collective-permute-start.6 = (f32[1,32,128]{2,1,0:T(8,128)S(1)}, f32[1,32,128]{2,1,0:T(8,128)S(1)}, u32[]{:S(2)}, u32[]{:S(2)}) collective-permute-start(f32[1,32,128]{2,1,0:T(8,128)S(1)} %select_bitcast_fusion), channel_id=1, source_target_pairs={{0,8},{2,10},{4,12},{6,14},{8,16},{10,18},{12,20},{14,22},{16,24},... | collective-permute-start | bytes 49160 | tf_op jit(solution)/shard_map/ppermute | solution.py:628
  92.3 26.3 %collective-permute-start.14 = (f32[32,4096]{1,0:T(8,128)}, f32[32,4096]{1,0:T(8,128)S(1)}, u32[]{:S(2)}, u32[]{:S(2)}) collective-permute-start(f32[32,4096]{1,0:T(8,128)} %get-tuple-element.70), channel_id=1, source_target_pairs={{0,1},{1,0},{2,3},{3,2},{4,5},{5,4},{6,7},{7,6},{8,9},{9,8},{10,11... | collective-permute-start | bytes 1572872 | tf_op jit(solution)/shard_map/ppermute | solution.py:669
  92.5 20.9 %copy-start.3 = (f32[4,32,128]{2,1,0:T(8,128)}, f32[4,32,128]{2,1,0:T(8,128)S(1)}, u32[]{:S(2)}) copy-start(f32[4,32,128]{2,1,0:T(8,128)S(1)} %pad_maximum_fusion.own) | copy-start | bytes 196612
  92.5 20.9 %collective-permute-start.10 = (f32[4,32,128]{2,1,0:T(8,128)S(1)}, f32[4,32,128]{2,1,0:T(8,128)S(1)}, u32[]{:S(2)}, u32[]{:S(2)}) collective-permute-start(f32[4,32,128]{2,1,0:T(8,128)S(1)} %pad_maximum_fusion.own), channel_id=1, source_target_pairs={{0,64},{2,66},{4,68},{6,70},{8,72},{10,74},{12,76},{14,78},{16,80}... | collective-permute-start | bytes 196616 | tf_op jit(solution)/shard_map/ppermute | solution.py:628
  94.6 18.8 %collective-permute-start.11 = (f32[4,32,128]{2,1,0:T(8,128)S(1)}, f32[4,32,128]{2,1,0:T(8,128)S(1)}, u32[]{:S(2)}, u32[]{:S(2)}) collective-permute-start(f32[4,32,128]{2,1,0:T(8,128)S(1)} %pad_maximum_fusion.own), channel_id=1, source_target_pairs={{0,32},{2,34},{4,36},{6,38},{8,40},{10,42},{12,44},{14,46},{16,48}... | collective-permute-start | bytes 196616 | tf_op jit(solution)/shard_map/ppermute | solution.py:628
  99.7 13.7 %collective-permute-start.9 = (f32[4,32,128]{2,1,0:T(8,128)S(1)}, f32[4,32,128]{2,1,0:T(8,128)S(1)}, u32[]{:S(2)}, u32[]{:S(2)}) collective-permute-start(f32[4,32,128]{2,1,0:T(8,128)S(1)} %pad_maximum_fusion.own), channel_id=1, source_target_pairs={{0,96},{2,98},{4,100},{6,102},{8,104},{10,106},{12,108},{14,110},{... | collective-permute-start | bytes 196616 | tf_op jit(solution)/shard_map/ppermute | solution.py:628
  113.4 0.6 copy-start.4
  113.4 0.6 copy-start.5
  113.4 0.6 copy-start.6
  118.6 0.8 copy-start.2

commit v6 on v5

--- a/solution.py
+++ b/solution.py
@@ -30,9 +30,7 @@
 def low_lanes(shape):
     return lax.broadcasted_iota(jnp.int32, shape, 1) < 64
 
-def up_body(
-    points, basis_hbm, values_hbm, moves_hbm, up, trans_hbm, packed_hbm, rows, basis, values, moves, trans, packed, sem
-):
+def up_body(basis_hbm, values_hbm, moves_hbm, up, share, trans_hbm, rows, basis, values, moves, trans, sem):
     leaves = basis.shape[0]
     columns = values.shape[0]
     nodes = moves.shape[2]
@@ -64,16 +62,13 @@
     for n in range(whole, nodes):
         node(n)
     trans[nodes] = jnp.zeros(trans.shape[1:], bf16)
-    writes = [pltpu.make_async_copy(trans, trans_hbm, sem.at[6])]
-    writes[0].start()
+    write = pltpu.make_async_copy(trans, trans_hbm, sem.at[6])
+    write.start()
 
     half = low_lanes((columns, 128))
 
     for read in reads[4:]:
         read.wait()
-    packed[0:columns] = values[...]
-    packed[columns : columns + 3] = points[...]
-    packed[columns + 4 :] = jnp.zeros((4, packed.shape[1]), f32)
 
     def leaf_up(i):
         v = stack(values[:, pl.ds(pl.multiple_of(i * 128, 128), 128)])
@@ -116,19 +111,11 @@
                 up[after + p] = tile
         start, row, width = after, row + width, width // 2
     up[leaves - 1] = tiles[0]
-    share = both(fold(jnp.dot(stack(tiles[0])[:, 0:64], trans[row], preferred_element_type=f32)))
-    for c in range(columns):
-        packed[columns + 3 : columns + 4, 128 * c : 128 * c + 128] = share[c : c + 1]
-    packed[columns + 3 : columns + 4, 128 * columns :] = jnp.zeros(
-        (1, packed.shape[1] - 128 * columns), f32
-    )
-    writes.append(pltpu.make_async_copy(packed, packed_hbm, sem.at[7]))
-    writes[1].start()
-    for write in writes:
-        write.wait()
-
-
-def up_pass(points, basis, values, moves):
+    share[...] = both(fold(jnp.dot(stack(tiles[0])[:, 0:64], trans[row], preferred_element_type=f32)))
+    write.wait()
+
+
+def up_pass(basis, values, moves):
     leaves = basis.shape[0]
     columns = values.shape[0]
     nodes = moves.shape[2]
@@ -136,88 +123,79 @@
         up_body,
         out_shape=(
             jax.ShapeDtypeStruct((leaves, columns, 128), f32),
+            jax.ShapeDtypeStruct((columns, 128), f32),
             jax.ShapeDtypeStruct((nodes + 1, 64, 128), bf16),
-            jax.ShapeDtypeStruct((columns + 8, values.shape[1]), f32),
         ),
-        in_specs=[VM, HBM, HBM, HBM],
-        out_specs=(VM, HBM, HBM),
+        in_specs=[HBM, HBM, HBM],
+        out_specs=(VM, VM, HBM),
         scratch_shapes=[
             pltpu.VMEM((64 * PITCH, 128), f32),
             pltpu.VMEM(basis.shape, f32),
             pltpu.VMEM(values.shape, f32),
             pltpu.VMEM(moves.shape, f32),
             pltpu.VMEM((nodes + 1, 64, 128), bf16),
-            pltpu.VMEM((columns + 8, values.shape[1]), f32),
-            pltpu.SemaphoreType.DMA((8,)),
+            pltpu.SemaphoreType.DMA((7,)),
         ],
         compiler_params=pltpu.CompilerParams(vmem_limit_bytes=VMEM_BYTES),
         cost_estimate=pl.CostEstimate(flops=400_000_000, bytes_accessed=8_000_000, transcendentals=0),
         name="up_pass",
-    )(points, basis, values, moves)
+    )(basis, values, moves)
 
 
 CHUNK = 32
 
 
-def unbatch_body(matrices, out, held, rows, made, in_sem, out_sem):
+def unbatch_body(part, matrices, out, held, rows, made, in_sem, out_sem):
     nodes = matrices.shape[3]
     pieces = 4
     step = matrices.shape[1] // pieces
     reads = []
-    for h in range(2):
-        for i in range(pieces):
-            at = pl.ds(i * step, step)
-            pair = pl.ds(2 * h, 2)
-            reads.append(
-                pltpu.make_async_copy(
-                    matrices.at[pair, at], held.at[pair, at], in_sem.at[pieces * h + i]
-                )
-            )
-    for read in reads:
-        read.start()
+    for i in range(pieces):
+        at = pl.ds(i * step, step)
+        reads.append(
+            pltpu.make_async_copy(matrices.at[pl.ds(2 * part, 2), at], held.at[:, at], in_sem.at[i])
+        )
+        reads[-1].start()
+    for i in range(pieces):
+        reads[i].wait()
+
+        @pl.loop(i * step, (i + 1) * step, unroll=8)
+        def _(r):
+            x = jnp.concatenate([held[0, r], held[1, r]], axis=0)
+            rows[pl.ds(pl.multiple_of(r * PITCH, 8), nodes)] = jnp.transpose(x)
+
+    def one(n):
+        hi, lo = split(rows[pl.ds(n, 64, stride=PITCH), :])
+        made[n, 0:64] = hi
+        made[n, 64:128] = lo
+
     writes = []
-    for h in range(2):
-        for i in range(pieces):
-            reads[pieces * h + i].wait()
-
-            @pl.loop(i * step, (i + 1) * step, unroll=4)
-            def _(r, h=h):
-                x = jnp.concatenate([held[2 * h, r], held[2 * h + 1, r]], axis=0)
-                rows[pl.ds(pl.multiple_of((h * 64 + r) * PITCH, 8), nodes)] = jnp.transpose(x)
-
-        def one(n, h=h):
-            hi, lo = split(rows[pl.ds(h * 64 * PITCH + n, 64, stride=PITCH), :])
-            made[h, n, 0:64] = hi
-            made[h, n, 64:128] = lo
-
-        for c, begin in enumerate(range(0, nodes, CHUNK)):
-            size = min(CHUNK, nodes - begin)
-            whole = begin + size // 8 * 8
-            pl.loop(begin, whole, unroll=8)(one)
-            for n in range(whole, begin + size):
-                one(n)
-            at = pl.ds(begin, size)
-            writes.append(
-                pltpu.make_async_copy(made.at[h, at], out.at[h, at], out_sem.at[h, c])
-            )
-            writes[-1].start()
+    for c, begin in enumerate(range(0, nodes, CHUNK)):
+        size = min(CHUNK, nodes - begin)
+        whole = begin + size // 8 * 8
+        pl.loop(begin, whole, unroll=8)(one)
+        for n in range(whole, begin + size):
+            one(n)
+        at = pl.ds(begin, size)
+        writes.append(pltpu.make_async_copy(made.at[at], out.at[at], out_sem.at[c]))
+        writes[-1].start()
     for write in writes:
         write.wait()
 
 
-def unbatch(matrices):
+def unbatch(matrices, part):
     nodes = matrices.shape[3]
     return pl.pallas_call(
-        unbatch_body,
-        out_shape=jax.ShapeDtypeStruct((2, nodes, 128, 128), bf16),
+        functools.partial(unbatch_body, part),
+        out_shape=jax.ShapeDtypeStruct((nodes, 128, 128), bf16),
         in_specs=[HBM],
         out_specs=HBM,
         scratch_shapes=[
-            pltpu.VMEM(matrices.shape, f32),
-            pltpu.VMEM((2 * 64 * PITCH, 128), f32),
-            pltpu.VMEM((2, nodes, 128, 128), bf16),
-            pltpu.SemaphoreType.DMA((8,)),
-            pltpu.SemaphoreType.DMA((2, -(-nodes // CHUNK))),
+            pltpu.VMEM((2, *matrices.shape[1:]), f32),
+            pltpu.VMEM((64 * PITCH, 128), f32),
+            pltpu.VMEM((nodes, 128, 128), bf16),
+            pltpu.SemaphoreType.DMA((4,)),
+            pltpu.SemaphoreType.DMA((-(-nodes // CHUNK),)),
         ],
         compiler_params=pltpu.CompilerParams(vmem_limit_bytes=VMEM_BYTES),
         cost_estimate=pl.CostEstimate(flops=1_000, bytes_accessed=1_000, transcendentals=0),
@@ -292,9 +270,9 @@
     )(place, partners, *gathered, moves, matrices)
 
 
-def couple_body(codes, low, own, high, matrices, far, gather, tiles, held, sem):
+def couple_body(codes, low, own, high, first, second, far, gather, tiles, held, sem):
     leaves, columns, _ = own.shape
-    nodes = matrices.shape[1]
+    nodes = first.shape[0]
     takes = []
     for side, ref in enumerate((low, own, high)):
         takes.append(pltpu.make_async_copy(ref, tiles.at[side], sem.at[3 + side]))
@@ -303,8 +281,9 @@
     for i in range(3):
         begin = 42 * i
         at = pl.ds(begin, nodes - begin if i == 2 else 42)
-        reads.append(pltpu.make_async_copy(matrices.at[:, at], held.at[:, at], sem.at[i]))
-        reads[-1].start()
+        for h, x in enumerate((first, second)):
+            reads.append(pltpu.make_async_copy(x.at[at], held.at[h, at], sem.at[6 + 2 * i + h]))
+            reads[-1].start()
     half = low_lanes((columns, 128))
     left = low_lanes((2 * columns, 128))
     for side in range(3):
@@ -332,7 +311,8 @@
         return both(fold(lax.dot_general(x, m, NT, preferred_element_type=f32)))
 
     for i in range(3):
-        reads[i].wait()
+        reads[2 * i].wait()
+        reads[2 * i + 1].wait()
 
         @pl.loop(21 * i, 21 * i + 21, unroll=7)
         def _(t):
@@ -341,23 +321,23 @@
     far[leaves - 1] = one(nodes - 1)
 
 
-def couple_pass(codes, low, own, high, matrices):
+def couple_pass(codes, low, own, high, first, second):
     leaves, columns, _ = own.shape
     return pl.pallas_call(
         couple_body,
         out_shape=jax.ShapeDtypeStruct((leaves, columns, 128), f32),
-        in_specs=[SM] + [HBM] * 4,
+        in_specs=[SM] + [HBM] * 5,
         out_specs=VM,
         scratch_shapes=[
             pltpu.VMEM((2, 3 * leaves, 2 * columns, 128), bf16),
             pltpu.VMEM((3, leaves, columns, 128), f32),
-            pltpu.VMEM(matrices.shape, bf16),
-            pltpu.SemaphoreType.DMA((6,)),
+            pltpu.VMEM((2, *first.shape), bf16),
+            pltpu.SemaphoreType.DMA((12,)),
         ],
         compiler_params=pltpu.CompilerParams(vmem_limit_bytes=VMEM_BYTES),
         cost_estimate=pl.CostEstimate(flops=400_000_000, bytes_accessed=12_000_000, transcendentals=0),
         name="couple_pass",
-    )(codes, low, own, high, matrices)
+    )(codes, low, own, high, first, second)
 
 
 def down_body(core, parent, far_hbm, trans_hbm, basis_hbm, mine, given, out, far, trans, basis, ones, twos, sem):
@@ -443,9 +423,9 @@
 
 def near_body(unroll, chunks, core, lists, counts, targets, *refs):
     origins, refs = refs[: 2 * chunks], refs[2 * chunks :]
-    begin = None
+    begin, spots = None, [targets]
     if chunks == 2:
-        begin, refs = refs[0:2], refs[2:]
+        begin, spots, refs = refs[0:2], refs[2:4], refs[4:]
     mine, other, columns_of, total, weights, places, sem, *sources = refs
     leaves = mine.shape[1] // 128
     width = sources[0].shape[1] // 128
@@ -482,9 +462,9 @@
             for u in range(8):
                 j = 8 * g + u
                 at = pl.ds(pl.multiple_of(j * 128, 128), 128)
-                x = near_weight * jnp.concatenate([near_ref[0:32, at], far_ref[0:32, at]], axis=0)
+                x = near_weight * jnp.concatenate([near_ref[:, at], far_ref[:, at]], axis=0)
                 weights[c * width + j] = stack(x)
-                places[c * width + j, 0:3] = near_ref[32:35, at]
+                places[c * width + j, 0:3] = spots[c][:, at]
 
     items = lax.fori_loop(
         0, leaves, lambda i, s: s + jnp.maximum((counts[i] + PAIR - 1) // PAIR, 1), jnp.int32(0)
@@ -538,16 +518,16 @@
             other[:, at] = begin[1][:, at] + x[32:64]
 
 
-def near_pass(unroll, core, lists, counts, targets, sources, begin=()):
+def near_pass(unroll, core, lists, counts, targets, sources, begin=(), spots=()):
     leaves = lists.shape[0]
     chunks = len(sources) // 2
     held = chunks * (sources[0].shape[1] // 128) + 1
     side = jax.ShapeDtypeStruct((32, leaves * 128), f32)
-    arrays = (targets, *sources, *begin)
+    arrays = (targets, *sources, *begin, *spots)
     return pl.pallas_call(
         functools.partial(near_body, unroll, chunks),
         out_shape=(side, side),
-        in_specs=[SM, SM, SM, VM] + [HBM] * len(sources) + [VM] * len(begin),
+        in_specs=[SM, SM, SM, VM] + [HBM] * len(sources) + [VM] * 2 * len(begin),
         out_specs=(VM, VM),
         scratch_shapes=[
             pltpu.VMEM((leaves, 3, 128, 128), f32),
@@ -609,6 +589,9 @@
     forward = [(i, i + 1) for i in range(count - 1)]
     backward = [(target, source) for source, target in forward]
     swap = [(0, 1), (1, 0)]
+    low = lax.ppermute(values, "leaf", forward)
+    high = lax.ppermute(values, "leaf", backward)
+    spots = (lax.ppermute(points, "leaf", forward), lax.ppermute(points, "leaf", backward))
     across = lax.ppermute(values, "rhs", swap)
     half = leaves // 2
     chosen = lax.dynamic_slice_in_dim(near_list, core * half, half, 0) - position * leaves
@@ -640,41 +623,37 @@
 
     after = lax.optimization_barrier
     core = core[None].astype(jnp.int32)
-    columns = values.shape[0]
-    up, trans, packed = up_pass(points, basis, values, transfer.transpose(1, 2, 0))
-    low = lax.ppermute(packed, "leaf", forward)
-    high = lax.ppermute(packed, "leaf", backward)
+    up, share, trans = up_pass(basis, values, transfer.transpose(1, 2, 0))
     near_ids, far_ids, codes, up = after((near_ids, far_ids, codes, up))
-    begin = near_pass(12, core, near_ids, near_live, points, (packed, across))
-    low, high, coupling, begin = after((low, high, coupling, begin))
-    row = slice(columns + 3, columns + 4)
-    lanes = 128 * columns
-    sibling = jnp.where(position % 2 == 0, high[row, 0:lanes], low[row, 0:lanes])
-    level = (packed[row, 0:lanes] + sibling).reshape(columns, 128)
-    pair = lax.ppermute(level, "leaf", [(i, i ^ 2) for i in range(count)])
+    begin = near_pass(12, core, near_ids, near_live, points, (values, across))
+    low, high, spots, coupling, share, begin = after((low, high, spots, coupling, share, begin))
+    turned, spot = ring(share[None], 1)
     low_across = lax.ppermute(low, "rhs", swap)
     high_across = lax.ppermute(high, "rhs", swap)
-    pair, up, coupling = after((pair, up, coupling))
+    coupling = coupling.transpose(1, 2, 3, 0)
+    first = unbatch(coupling, 0)
+    turned, low_across, high_across, up, coupling, first = after(
+        (turned, low_across, high_across, up, coupling, first)
+    )
+    level = in_order(turned, share[None], spot)
+    level = jnp.where(jnp.arange(128) < 64, level[0] + level[1], level[2] + level[3])[None]
+    turned, spot = ring(level, 4)
     up_low = lax.ppermute(up, "leaf", forward)
     up_high = lax.ppermute(up, "leaf", backward)
-    matrices = unbatch(coupling.transpose(1, 2, 3, 0))
-    pair, far_ids, matrices = after((pair, far_ids, matrices))
-    lower = jnp.arange(128) < 64
-    level = jnp.where(lower == (position & 2 == 0), level, pair)[None]
-    turned, spot = ring(level, 4)
+    second = unbatch(coupling, 1)
+    turned, far_ids, second = after((turned, far_ids, second))
+    level = in_order(turned, level, spot)
+    turned, spot = ring(level, 16)
     mine, other = near_pass(
-        12, core, far_ids, far_live, points, (low, low_across, high, high_across), begin
+        12, core, far_ids, far_live, points, (low, low_across, high, high_across), begin, spots
     )
     turned, mine, other = after((turned, mine, other))
     given = lax.ppermute(other, "rhs", swap)
-    level = in_order(turned, level, spot)
-    turned, spot = ring(level, 16)
-    codes, mine = after((codes, mine))
-    far = couple_pass(codes, up_low, up, up_high, matrices)
-    turned, far = after((turned, far))
     parent = top_pass(
         position[None].astype(jnp.int32), partners_top, (*turned, level), transfer_top, coupling_top
     )
+    up_low, up_high, parent = after((up_low, up_high, parent))
+    far = couple_pass(codes, up_low, up, up_high, first, second)
     return down_pass(core, parent, far, trans, basis, mine, given)
 
 

time: 130 us -> 142 us (1.092)
  the two profiles are of different devices: /device:TPU:4 before, /device:TPU:39 now
where the time goes in v6:
time: 142 us
  Pallas kernels  77.5 us (55%)
  starting transfers between devices  37.7 us (27%)
  waiting for transfers between devices  15.9 us (11%)
  other arithmetic  5.54 us (4%)
  local copies, waits for them, and re-layouts  4.92 us (3%)
    pallas_call x2, Pallas kernels, near_pass(): pl.pallas_call(functools.partial(near_body, unroll, chunks), out_shape=(s...  32.8 us
    ppermute x9, waiting for transfers between devices, ring(): turned.append(lax.ppermute(x, 'leaf', to))  15.9 us
    ppermute x9, starting transfers between devices, ring(): turned.append(lax.ppermute(x, 'leaf', to))  12 us
    pallas_call x1, Pallas kernels, up_pass(): pl.pallas_call(up_body, out_shape=(jax.ShapeDtypeStruct((leaves, columns,...  10.6 us
    pallas_call x1, Pallas kernels, couple_pass(): pl.pallas_call(couple_body, out_shape=jax.ShapeDtypeStruct((leaves, colum...  10.6 us
    pallas_call x2, Pallas kernels, unbatch(): pl.pallas_call(functools.partial(unbatch_body, part), out_shape=jax.Shape...  10.3 us
    pallas_call x1, Pallas kernels, down_pass(): pl.pallas_call(down_body, out_shape=jax.ShapeDtypeStruct((columns, leaves...  8.65 us
    ppermute x1, starting transfers between devices, local(): lax.ppermute(points, 'leaf', backward)  5.47 us
  transfers between devices with their start and end apart: 19, of which 1 were waited for; matrix products, arithmetic and copies ran while one was open for 5% of the time, Pallas kernels for 48%

profile of v6, /device:TPU:39, one launch (start us, length us, event | category | flops | bytes accessed | tf_op | source)
XLA Modules:
  0.0 142.3 jit_solution(12056854764940623144)
XLA Ops:
  0.0 0.7 collective-permute-start.4
  0.7 3.2 %collective-permute-start = (f32[32,8192]{1,0:T(8,128)}, f32[32,8192]{1,0:T(8,128)S(1)}, u32[]{:S(2)}, u32[]{:S(2)}) collective-permute-start(f32[32,8192]{1,0:T(8,128)} %refs_0_.1), channel_id=1, source_target_pairs={{0,2},{2,4},{4,6},{6,8},{8,10},{10,12},{12,14},{14,16},{16,18},{18... | collective-permute-start | bytes 3145736 | tf_op jit(solution)/shard_map/ppermute | solution.py:592
  3.9 4.2 %collective-permute-start.1 = (f32[32,8192]{1,0:T(8,128)}, f32[32,8192]{1,0:T(8,128)S(1)}, u32[]{:S(2)}, u32[]{:S(2)}) collective-permute-start(f32[32,8192]{1,0:T(8,128)} %refs_0_.1), channel_id=1, source_target_pairs={{2,0},{4,2},{6,4},{8,6},{10,8},{12,10},{14,12},{16,14},{18,16},{20... | collective-permute-start | bytes 3145736 | tf_op jit(solution)/shard_map/ppermute | solution.py:593
  8.1 1.9 %collective-permute-start.2 = (f32[3,8192]{1,0:T(4,128)}, f32[3,8192]{1,0:T(4,128)S(1)}, u32[]{:S(2)}, u32[]{:S(2)}) collective-permute-start(f32[3,8192]{1,0:T(4,128)} %targets.3), channel_id=1, source_target_pairs={{0,2},{2,4},{4,6},{6,8},{8,10},{10,12},{12,14},{14,16},{16,18},{18... | collective-permute-start | bytes 294920 | tf_op jit(solution)/shard_map/ppermute | solution.py:594
  10.0 5.5 %collective-permute-start.3 = (f32[3,8192]{1,0:T(4,128)}, f32[3,8192]{1,0:T(4,128)S(1)}, u32[]{:S(2)}, u32[]{:S(2)}) collective-permute-start(f32[3,8192]{1,0:T(4,128)} %targets.3), channel_id=1, source_target_pairs={{2,0},{4,2},{6,4},{8,6},{10,8},{12,10},{14,12},{16,14},{18,16},{20... | collective-permute-start | bytes 294920 | tf_op jit(solution)/shard_map/ppermute | solution.py:594
  15.5 0.7 dynamic_slice.6
  16.2 0.8 convert_reduce_fusion
  17.1 0.3 select_reduce_fusion.1
  17.4 0.1 copy.48
  17.5 0.1 copy.49
  17.6 1.0 select_reduce_fusion
  18.6 0.7 broadcast_multiply_fusion
  19.3 0.7 fusion.4.lists
  19.9 0.7 fusion.5.lists
  20.6 0.7 add_multiply_fusion
  21.3 0.1 copy.50
  21.4 0.1 copy.51
  21.5 0.6 sub.31.codes
  22.2 10.6 %up_pass.1 = (f32[64,32,128]{2,1,0:T(8,128)}, f32[32,128]{1,0:T(8,128)}, bf16[128,64,128]{2,1,0:T(8,128)(2,1)}) custom-call(f32[64,64,128]{2,1,0:T(8,128)} %basis_hbm.3, f32[32,8192]{1,0:T(8,128)} %refs_0_.1, f32[64,64,127]{2,1,0:T(8,128)} %bitcast.8), custom_call_target="tpu_custom_call" | custom-call | flops 400000000 | bytes 8000000 | tf_op jit(solution)/shard_map/up_pass/pallas_call | solution.py:122
  32.9 1.0 copy-done.3
  33.9 16.5 %near_pass.2 = (f32[32,4096]{1,0:T(8,128)}, f32[32,4096]{1,0:T(8,128)}) custom-call(s32[1]{0:T(128)} %bitcast.core, s32[32,28]{1,0:T(8,128)} %fusion.4.lists, s32[32]{0:T(128)} %copy-done.14, f32[3,8192]{1,0:T(4,128)} %targets.3, f32[32,8192]{1,0:T(8,128)} %refs_0_.1, f32[32,8192]{1,0:T(8,128)} %copy-done.3), custom_call_target="tpu_custom_call" | custom-call | flops 1000 | bytes 1000 | tf_op jit(solution)/shard_map/near_pass/pallas_call | solution.py:527
  50.4 0.0 collective-permute-done.3.refs_7_
  50.5 0.0 collective-permute-done.refs_0_
  50.5 0.3 collective-permute-start.8
  50.8 0.2 collective-permute-start.9
  51.1 0.0 collective-permute-start.5
  51.1 0.0 collective-permute-start.6
  51.1 1.5 %collective-permute-start.7 = (f32[1,32,128]{2,1,0:T(8,128)}, f32[1,32,128]{2,1,0:T(8,128)S(1)}, u32[]{:S(2)}, u32[]{:S(2)}) collective-permute-start(f32[1,32,128]{2,1,0:T(8,128)} %bitcast.11), channel_id=1, source_target_pairs={{0,2},{2,4},{4,6},{6,0},{8,10},{10,12},{12,14},{14,8},{16,18},{18,... | collective-permute-start | bytes 49160 | tf_op jit(solution)/shard_map/ppermute | solution.py:611
  52.6 5.2 %unbatch.2.first = bf16[127,128,128]{2,1,0:T(8,128)(2,1)} custom-call(f32[4,64,64,127]{3,2,1,0:T(8,128)} %bitcast.6), custom_call_target="tpu_custom_call" | custom-call | flops 1000 | bytes 1000 | tf_op jit(solution)/shard_map/unbatch/pallas_call | solution.py:188
  57.8 0.0 collective-permute-done.5
  57.8 3.1 %collective-permute-start.10 = (f32[64,32,128]{2,1,0:T(8,128)S(1)}, f32[64,32,128]{2,1,0:T(8,128)S(1)}, u32[]{:S(2)}, u32[]{:S(2)}) collective-permute-start(f32[64,32,128]{2,1,0:T(8,128)S(1)} %copy-done), channel_id=1, source_target_pairs={{0,2},{2,4},{4,6},{6,8},{8,10},{10,12},{12,14},{14,16},{16,18},{18... | collective-permute-start | bytes 3145736 | tf_op jit(solution)/shard_map/ppermute | solution.py:641
  60.9 4.3 %collective-permute-start.11 = (f32[64,32,128]{2,1,0:T(8,128)S(1)}, f32[64,32,128]{2,1,0:T(8,128)S(1)}, u32[]{:S(2)}, u32[]{:S(2)}) collective-permute-start(f32[64,32,128]{2,1,0:T(8,128)S(1)} %copy-done), channel_id=1, source_target_pairs={{2,0},{4,2},{6,4},{8,6},{10,8},{12,10},{14,12},{16,14},{18,16},{20... | collective-permute-start | bytes 3145736 | tf_op jit(solution)/shard_map/ppermute | solution.py:642
  65.3 0.1 collective-permute-start.12
  65.4 5.0 %collective-permute-start.13 = (f32[1,32,128]{2,1,0:T(8,128)S(1)}, f32[1,32,128]{2,1,0:T(8,128)S(1)}, u32[]{:S(2)}, u32[]{:S(2)}) collective-permute-start(f32[1,32,128]{2,1,0:T(8,128)S(1)} %add_select_fusion), channel_id=1, source_target_pairs={{0,16},{2,18},{4,20},{6,22},{8,24},{10,26},{12,28},{14,30},{16,0},... | collective-permute-start | bytes 49160 | tf_op jit(solution)/shard_map/ppermute | solution.py:611
  70.4 5.1 %unbatch.3.second = bf16[127,128,128]{2,1,0:T(8,128)(2,1)} custom-call(f32[4,64,64,127]{3,2,1,0:T(8,128)} %bitcast.7), custom_call_target="tpu_custom_call" | custom-call | flops 1000 | bytes 1000 | tf_op jit(solution)/shard_map/unbatch/pallas_call | solution.py:188
  75.5 0.0 copy-start.15
  75.5 15.9 %collective-permute-done.12 = f32[1,32,128]{2,1,0:T(8,128)S(1)} collective-permute-done((f32[1,32,128]{2,1,0:T(8,128)S(1)}, f32[1,32,128]{2,1,0:T(8,128)S(1)}, u32[]{:S(2)}, u32[]{:S(2)}) %collective-permute-start.12) | collective-permute-done | bytes 16416 | tf_op jit(solution)/shard_map/ppermute | solution.py:611
  91.4 0.1 collective-permute-start.15
  91.5 5.4 %collective-permute-start.16 = (f32[4,32,128]{2,1,0:T(8,128)S(1)}, f32[4,32,128]{2,1,0:T(8,128)S(1)}, u32[]{:S(2)}, u32[]{:S(2)}) collective-permute-start(f32[4,32,128]{2,1,0:T(8,128)S(1)} %pad_maximum_fusion.own), channel_id=1, source_target_pairs={{0,64},{2,66},{4,68},{6,70},{8,72},{10,74},{12,76},{14,78},{16,80}... | collective-permute-start | bytes 196616 | tf_op jit(solution)/shard_map/ppermute | solution.py:611
  96.9 0.0 collective-permute-start.17
  96.9 16.3 %near_pass.3 = (f32[32,4096]{1,0:T(8,128)}, f32[32,4096]{1,0:T(8,128)}) custom-call(s32[1]{0:T(128)} %bitcast.core, s32[32,28]{1,0:T(8,128)} %fusion.5.lists, s32[32]{0:T(128)} %copy-done.13, f32[3,8192]{1,0:T(4,128)} %targets.3, f32[32,8192]{1,0:T(8,128)} %copy-done.4, f32[32,8192]{1,0:T(8,128)} %collective-permute-done.8.refs_1_, f32[32,8192]{1,0:T(8,128)} %copy-done.5, ...), custom_call_target="tpu_custom_call" | custom-call | flops 1000 | bytes 1000 | tf_op jit(solution)/shard_map/near_pass/pallas_call | solution.py:527
  113.2 2.3 %collective-permute-start.18 = (f32[32,4096]{1,0:T(8,128)}, f32[32,4096]{1,0:T(8,128)}, u32[]{:S(2)}, u32[]{:S(2)}) collective-permute-start(f32[32,4096]{1,0:T(8,128)} %get-tuple-element.84), channel_id=1, source_target_pairs={{0,1},{1,0},{2,3},{3,2},{4,5},{5,4},{6,7},{7,6},{8,9},{9,8},{10,11... | collective-permute-start | bytes 1572872 | tf_op jit(solution)/shard_map/ppermute | solution.py:651
  115.5 0.7 copy.52.partners
  116.2 4.6 %top_pass.1.parent = f32[32,128]{1,0:T(8,128)} custom-call(s32[1]{0:T(128)} %bitcast.4.place, s32[60,4]{1,0:T(8,128)} %copy.52.partners, f32[4,32,128]{2,1,0:T(8,128)} %copy-done.9, f32[4,32,128]{2,1,0:T(8,128)} %copy-done.10, f32[4,32,128]{2,1,0:T(8,128)} %copy-done.11, f32[4,32,128]{2,1,0:T(8,128)} %copy-done.6, f32[62,64,64]{2,1,0:T(8,128)} %moves.1, ...), custom_call_target="tpu_custom_call" | custom-call | flops 50000000 | bytes 2000000 | tf_op jit(solution)/shard_map/top_pass/pallas_call | solution.py:261
  120.9 1.0 copy-done.1
  121.8 1.0 copy-done.2
  122.9 10.6 %couple_pass.1.far_hbm = f32[64,32,128]{2,1,0:T(8,128)} custom-call(s32[127,4]{1,0:T(8,128)} %sub.31.codes, f32[64,32,128]{2,1,0:T(8,128)} %copy-done.1, f32[64,32,128]{2,1,0:T(8,128)} %get-tuple-element.55.own, f32[64,32,128]{2,1,0:T(8,128)} %copy-done.2, bf16[127,128,128]{2,1,0:T(8,128)(2,1)} %unbatch.2.first, bf16[127,128,128]{2,1,0:T(8,128)(2,1)} %unbatch.3.second), custom_call_target="tpu_custom_call" | custom-call | flops 400000000 | bytes 12000000 | tf_op jit(solution)/shard_map/couple_pass/pallas_call | solution.py:326
  133.4 8.6 %down_pass.1 = f32[32,8192]{1,0:T(8,128)} custom-call(s32[1]{0:T(128)} %bitcast.core, f32[32,128]{1,0:T(8,128)} %top_pass.1.parent, f32[64,32,128]{2,1,0:T(8,128)} %couple_pass.1.far_hbm, bf16[128,64,128]{2,1,0:T(8,128)(2,1)} %get-tuple-element.82.trans_hbm, f32[64,64,128]{2,1,0:T(8,128)} %basis_hbm.3, f32[32,4096]{1,0:T(8,128)} %get-tuple-element.83.mine, ...), custom_call_target="tpu_custom_call" | custom-call | flops 200000000 | bytes 7000000 | tf_op jit(solution)/shard_map/down_pass/pallas_call | solution.py:400
  (51 shorter events, 0.2 us)
Async XLA Ops:
  0.0 32.8 %collective-permute-start.4 = (f32[32,8192]{1,0:T(8,128)}, f32[32,8192]{1,0:T(8,128)S(1)}, u32[]{:S(2)}, u32[]{:S(2)}) collective-permute-start(f32[32,8192]{1,0:T(8,128)} %refs_0_.1), channel_id=1, source_target_pairs={{0,1},{1,0},{2,3},{3,2},{4,5},{5,4},{6,7},{7,6},{8,9},{9,8},{10,11... | collective-permute-start | bytes 3145736 | tf_op jit(solution)/shard_map/ppermute | solution.py:595
  0.7 49.8 %collective-permute-start = (f32[32,8192]{1,0:T(8,128)}, f32[32,8192]{1,0:T(8,128)S(1)}, u32[]{:S(2)}, u32[]{:S(2)}) collective-permute-start(f32[32,8192]{1,0:T(8,128)} %refs_0_.1), channel_id=1, source_target_pairs={{0,2},{2,4},{4,6},{6,8},{8,10},{10,12},{12,14},{14,16},{16,18},{18... | collective-permute-start | bytes 3145736 | tf_op jit(solution)/shard_map/ppermute | solution.py:592
  3.9 46.6 %collective-permute-start.1 = (f32[32,8192]{1,0:T(8,128)}, f32[32,8192]{1,0:T(8,128)S(1)}, u32[]{:S(2)}, u32[]{:S(2)}) collective-permute-start(f32[32,8192]{1,0:T(8,128)} %refs_0_.1), channel_id=1, source_target_pairs={{2,0},{4,2},{6,4},{8,6},{10,8},{12,10},{14,12},{16,14},{18,16},{20... | collective-permute-start | bytes 3145736 | tf_op jit(solution)/shard_map/ppermute | solution.py:593
  8.1 42.3 %collective-permute-start.2 = (f32[3,8192]{1,0:T(4,128)}, f32[3,8192]{1,0:T(4,128)S(1)}, u32[]{:S(2)}, u32[]{:S(2)}) collective-permute-start(f32[3,8192]{1,0:T(4,128)} %targets.3), channel_id=1, source_target_pairs={{0,2},{2,4},{4,6},{6,8},{8,10},{10,12},{12,14},{14,16},{16,18},{18... | collective-permute-start | bytes 294920 | tf_op jit(solution)/shard_map/ppermute | solution.py:594
  10.0 40.4 %collective-permute-start.3 = (f32[3,8192]{1,0:T(4,128)}, f32[3,8192]{1,0:T(4,128)S(1)}, u32[]{:S(2)}, u32[]{:S(2)}) collective-permute-start(f32[3,8192]{1,0:T(4,128)} %targets.3), channel_id=1, source_target_pairs={{2,0},{4,2},{6,4},{8,6},{10,8},{12,10},{14,12},{16,14},{18,16},{20... | collective-permute-start | bytes 294920 | tf_op jit(solution)/shard_map/ppermute | solution.py:594
  17.1 40.7 %copy-start.13 = (s32[32]{0:T(128)}, s32[32]{0:T(128)S(1)}, u32[]{:S(2)}) copy-start(s32[32]{0:T(128)S(1)} %get-tuple-element.87.counts) | copy-start | bytes 388
  17.1 15.8 %copy-start.14 = (s32[32]{0:T(128)}, s32[32]{0:T(128)S(1)}, u32[]{:S(2)}) copy-start(s32[32]{0:T(128)S(1)} %get-tuple-element.91.counts) | copy-start | bytes 388
  32.8 1.0 copy-start.3
  50.4 7.3 %copy-start.7 = (f32[3,8192]{1,0:T(4,128)}, f32[3,8192]{1,0:T(4,128)S(1)}, u32[]{:S(2)}) copy-start(f32[3,8192]{1,0:T(4,128)S(1)} %collective-permute-done.2.refs_6_) | copy-start | bytes 294916
  50.4 7.3 %copy-start.8 = (f32[3,8192]{1,0:T(4,128)}, f32[3,8192]{1,0:T(4,128)S(1)}, u32[]{:S(2)}) copy-start(f32[3,8192]{1,0:T(4,128)S(1)} %collective-permute-done.3.refs_7_) | copy-start | bytes 294916
  50.5 7.3 %copy-start.4 = (f32[32,8192]{1,0:T(8,128)}, f32[32,8192]{1,0:T(8,128)S(1)}, u32[]{:S(2)}) copy-start(f32[32,8192]{1,0:T(8,128)S(1)} %collective-permute-done.refs_0_) | copy-start | bytes 3145732
  50.5 7.3 %copy-start.5 = (f32[32,8192]{1,0:T(8,128)}, f32[32,8192]{1,0:T(8,128)S(1)}, u32[]{:S(2)}) copy-start(f32[32,8192]{1,0:T(8,128)S(1)} %collective-permute-done.1.refs_2_) | copy-start | bytes 3145732
  50.5 7.3 %collective-permute-start.8 = (f32[32,8192]{1,0:T(8,128)S(1)}, f32[32,8192]{1,0:T(8,128)}, u32[]{:S(2)}, u32[]{:S(2)}) collective-permute-start(f32[32,8192]{1,0:T(8,128)S(1)} %collective-permute-done.refs_0_), channel_id=1, source_target_pairs={{0,1},{1,0},{2,3},{3,2},{4,5},{5,4},{6,7},{7,6},{8,9},{9,8},{10,11... | collective-permute-start | bytes 3145736 | tf_op jit(solution)/shard_map/ppermute | solution.py:631
  50.8 7.0 %collective-permute-start.9 = (f32[32,8192]{1,0:T(8,128)S(1)}, f32[32,8192]{1,0:T(8,128)}, u32[]{:S(2)}, u32[]{:S(2)}) collective-permute-start(f32[32,8192]{1,0:T(8,128)S(1)} %collective-permute-done.1.refs_2_), channel_id=1, source_target_pairs={{0,1},{1,0},{2,3},{3,2},{4,5},{5,4},{6,7},{7,6},{8,9},{9,8},{10,11... | collective-permute-start | bytes 3145736 | tf_op jit(solution)/shard_map/ppermute | solution.py:632
  51.1 6.7 %collective-permute-start.5 = (f32[1,32,128]{2,1,0:T(8,128)}, f32[1,32,128]{2,1,0:T(8,128)S(1)}, u32[]{:S(2)}, u32[]{:S(2)}) collective-permute-start(f32[1,32,128]{2,1,0:T(8,128)} %bitcast.9), channel_id=1, source_target_pairs={{0,6},{2,0},{4,2},{6,4},{8,14},{10,8},{12,10},{14,12},{16,22},{18,... | collective-permute-start | bytes 49160 | tf_op jit(solution)/shard_map/ppermute | solution.py:611
  51.1 6.7 %collective-permute-start.6 = (f32[1,32,128]{2,1,0:T(8,128)}, f32[1,32,128]{2,1,0:T(8,128)S(1)}, u32[]{:S(2)}, u32[]{:S(2)}) collective-permute-start(f32[1,32,128]{2,1,0:T(8,128)} %bitcast.10), channel_id=1, source_target_pairs={{0,4},{2,6},{4,0},{6,2},{8,12},{10,14},{12,8},{14,10},{16,20},{18,... | collective-permute-start | bytes 49160 | tf_op jit(solution)/shard_map/ppermute | solution.py:611
  51.1 6.7 %collective-permute-start.7 = (f32[1,32,128]{2,1,0:T(8,128)}, f32[1,32,128]{2,1,0:T(8,128)S(1)}, u32[]{:S(2)}, u32[]{:S(2)}) collective-permute-start(f32[1,32,128]{2,1,0:T(8,128)} %bitcast.11), channel_id=1, source_target_pairs={{0,2},{2,4},{4,6},{6,0},{8,10},{10,12},{12,14},{14,8},{16,18},{18,... | collective-permute-start | bytes 49160 | tf_op jit(solution)/shard_map/ppermute | solution.py:611
  52.6 5.3 %copy-start = (f32[64,32,128]{2,1,0:T(8,128)S(1)}, f32[64,32,128]{2,1,0:T(8,128)}, u32[]{:S(2)}) copy-start(f32[64,32,128]{2,1,0:T(8,128)} %get-tuple-element.55.own) | copy-start | bytes 3145732
  52.6 12.7 %copy-start.12 = (f32[32,128]{1,0:T(8,128)S(1)}, f32[32,128]{1,0:T(8,128)}, u32[]{:S(2)}) copy-start(f32[32,128]{1,0:T(8,128)} %get-tuple-element.50) | copy-start | bytes 49156
  57.8 63.0 %collective-permute-start.10 = (f32[64,32,128]{2,1,0:T(8,128)S(1)}, f32[64,32,128]{2,1,0:T(8,128)S(1)}, u32[]{:S(2)}, u32[]{:S(2)}) collective-permute-start(f32[64,32,128]{2,1,0:T(8,128)S(1)} %copy-done), channel_id=1, source_target_pairs={{0,2},{2,4},{4,6},{6,8},{8,10},{10,12},{12,14},{14,16},{16,18},{18... | collective-permute-start | bytes 3145736 | tf_op jit(solution)/shard_map/ppermute | solution.py:641
  60.9 59.9 %collective-permute-start.11 = (f32[64,32,128]{2,1,0:T(8,128)S(1)}, f32[64,32,128]{2,1,0:T(8,128)S(1)}, u32[]{:S(2)}, u32[]{:S(2)}) collective-permute-start(f32[64,32,128]{2,1,0:T(8,128)S(1)} %copy-done), channel_id=1, source_target_pairs={{2,0},{4,2},{6,4},{8,6},{10,8},{12,10},{14,12},{16,14},{18,16},{20... | collective-permute-start | bytes 3145736 | tf_op jit(solution)/shard_map/ppermute | solution.py:642
  65.3 26.1 %collective-permute-start.12 = (f32[1,32,128]{2,1,0:T(8,128)S(1)}, f32[1,32,128]{2,1,0:T(8,128)S(1)}, u32[]{:S(2)}, u32[]{:S(2)}) collective-permute-start(f32[1,32,128]{2,1,0:T(8,128)S(1)} %add_select_fusion), channel_id=1, source_target_pairs={{0,24},{2,26},{4,28},{6,30},{8,0},{10,2},{12,4},{14,6},{16,8},{18,... | collective-permute-start | bytes 49160 | tf_op jit(solution)/shard_map/ppermute | solution.py:611
  65.4 26.0 %collective-permute-start.13 = (f32[1,32,128]{2,1,0:T(8,128)S(1)}, f32[1,32,128]{2,1,0:T(8,128)S(1)}, u32[]{:S(2)}, u32[]{:S(2)}) collective-permute-start(f32[1,32,128]{2,1,0:T(8,128)S(1)} %add_select_fusion), channel_id=1, source_target_pairs={{0,16},{2,18},{4,20},{6,22},{8,24},{10,26},{12,28},{14,30},{16,0},... | collective-permute-start | bytes 49160 | tf_op jit(solution)/shard_map/ppermute | solution.py:611
  70.4 21.0 %collective-permute-start.14 = (f32[1,32,128]{2,1,0:T(8,128)S(1)}, f32[1,32,128]{2,1,0:T(8,128)S(1)}, u32[]{:S(2)}, u32[]{:S(2)}) collective-permute-start(f32[1,32,128]{2,1,0:T(8,128)S(1)} %add_select_fusion), channel_id=1, source_target_pairs={{0,8},{2,10},{4,12},{6,14},{8,16},{10,18},{12,20},{14,22},{16,24},... | collective-permute-start | bytes 49160 | tf_op jit(solution)/shard_map/ppermute | solution.py:611
  75.5 40.0 %copy-start.15 = (s32[60,4]{0,1:T(4,128)S(1)}, s32[60,4]{0,1:T(4,128)}, u32[]{:S(2)}) copy-start(s32[60,4]{0,1:T(4,128)} %param.23) | copy-start | bytes 2884
  91.4 24.8 %copy-start.6 = (f32[4,32,128]{2,1,0:T(8,128)}, f32[4,32,128]{2,1,0:T(8,128)S(1)}, u32[]{:S(2)}) copy-start(f32[4,32,128]{2,1,0:T(8,128)S(1)} %pad_maximum_fusion.own) | copy-start | bytes 196612
  91.4 21.8 %collective-permute-start.15 = (f32[4,32,128]{2,1,0:T(8,128)S(1)}, f32[4,32,128]{2,1,0:T(8,128)S(1)}, u32[]{:S(2)}, u32[]{:S(2)}) collective-permute-start(f32[4,32,128]{2,1,0:T(8,128)S(1)} %pad_maximum_fusion.own), channel_id=1, source_target_pairs={{0,96},{2,98},{4,100},{6,102},{8,104},{10,106},{12,108},{14,110},{... | collective-permute-start | bytes 196616 | tf_op jit(solution)/shard_map/ppermute | solution.py:611
  91.5 21.7 %collective-permute-start.16 = (f32[4,32,128]{2,1,0:T(8,128)S(1)}, f32[4,32,128]{2,1,0:T(8,128)S(1)}, u32[]{:S(2)}, u32[]{:S(2)}) collective-permute-start(f32[4,32,128]{2,1,0:T(8,128)S(1)} %pad_maximum_fusion.own), channel_id=1, source_target_pairs={{0,64},{2,66},{4,68},{6,70},{8,72},{10,74},{12,76},{14,78},{16,80}... | collective-permute-start | bytes 196616 | tf_op jit(solution)/shard_map/ppermute | solution.py:611
  96.9 16.3 %collective-permute-start.17 = (f32[4,32,128]{2,1,0:T(8,128)S(1)}, f32[4,32,128]{2,1,0:T(8,128)S(1)}, u32[]{:S(2)}, u32[]{:S(2)}) collective-permute-start(f32[4,32,128]{2,1,0:T(8,128)S(1)} %pad_maximum_fusion.own), channel_id=1, source_target_pairs={{0,32},{2,34},{4,36},{6,38},{8,40},{10,42},{12,44},{14,46},{16,48}... | collective-permute-start | bytes 196616 | tf_op jit(solution)/shard_map/ppermute | solution.py:611
  113.2 3.0 %copy-start.9 = (f32[4,32,128]{2,1,0:T(8,128)}, f32[4,32,128]{2,1,0:T(8,128)S(1)}, u32[]{:S(2)}) copy-start(f32[4,32,128]{2,1,0:T(8,128)S(1)} %collective-permute-done.15.far_three) | copy-start | bytes 196612
  113.2 3.0 %copy-start.10 = (f32[4,32,128]{2,1,0:T(8,128)}, f32[4,32,128]{2,1,0:T(8,128)S(1)}, u32[]{:S(2)}) copy-start(f32[4,32,128]{2,1,0:T(8,128)S(1)} %collective-permute-done.16.far_two) | copy-start | bytes 196612
  113.2 3.0 %copy-start.11 = (f32[4,32,128]{2,1,0:T(8,128)}, f32[4,32,128]{2,1,0:T(8,128)S(1)}, u32[]{:S(2)}) copy-start(f32[4,32,128]{2,1,0:T(8,128)S(1)} %collective-permute-done.17.far_one) | copy-start | bytes 196612
  113.2 20.2 %collective-permute-start.18 = (f32[32,4096]{1,0:T(8,128)}, f32[32,4096]{1,0:T(8,128)}, u32[]{:S(2)}, u32[]{:S(2)}) collective-permute-start(f32[32,4096]{1,0:T(8,128)} %get-tuple-element.84), channel_id=1, source_target_pairs={{0,1},{1,0},{2,3},{3,2},{4,5},{5,4},{6,7},{7,6},{8,9},{9,8},{10,11... | collective-permute-start | bytes 1572872 | tf_op jit(solution)/shard_map/ppermute | solution.py:651
  120.8 1.0 copy-start.1
  121.8 1.0 copy-start.2

commit v7 on v6

--- a/solution.py
+++ b/solution.py
@@ -8,7 +8,8 @@
 VM = pl.BlockSpec(memory_space=pltpu.VMEM)
 HBM = pl.BlockSpec(memory_space=pltpu.HBM)
 PITCH = 136
-VMEM_BYTES = 58 << 20
+VMEM_BYTES = 62 << 20
+SLOTS = 28
 f32 = jnp.float32
 bf16 = jnp.bfloat16
 
@@ -30,7 +31,66 @@
 def low_lanes(shape):
     return lax.broadcasted_iota(jnp.int32, shape, 1) < 64
 
-def up_body(basis_hbm, values_hbm, moves_hbm, up, share, trans_hbm, rows, basis, values, moves, trans, sem):
+def pack_body(points, values, out, sem):
+    columns = values.shape[0]
+    read = pltpu.make_async_copy(values, out.at[pl.ds(0, columns)], sem)
+    read.start()
+    out[columns:] = jnp.concatenate(
+        [points[...], jnp.zeros((out.shape[0] - columns - 3, out.shape[1]), f32)], axis=0
+    )
+    read.wait()
+
+
+def pack(points, values):
+    columns, width = values.shape
+    return pl.pallas_call(
+        pack_body,
+        out_shape=jax.ShapeDtypeStruct((columns + 8, width), f32),
+        in_specs=[VM, HBM],
+        out_specs=VM,
+        scratch_shapes=[pltpu.SemaphoreType.DMA],
+        compiler_params=pltpu.CompilerParams(vmem_limit_bytes=VMEM_BYTES),
+        name="pack",
+    )(points, values)
+
+
+def plan(place, near_list, near_count, partners, lists, live, codes):
+    slots, leaves = near_list.shape
+    local = near_list[...] - place * leaves
+    count = near_count[...]
+    inside = (local >= 0) & (local < leaves)
+    row = lax.broadcasted_iota(jnp.int32, (SLOTS, leaves), 0)
+    for side in range(2):
+        rank = jnp.zeros((1, leaves), jnp.int32)
+        found = jnp.full((SLOTS, leaves), (1 + side) * leaves, jnp.int32)
+        for s in range(slots):
+            here = inside[s : s + 1] if side == 0 else jnp.logical_not(inside[s : s + 1])
+            picked = here & (s < count)
+            ids = local[s : s + 1]
+            if side == 1:
+                ids = jnp.where(ids < 0, ids + leaves, ids)
+            found = jnp.where((row == rank) & picked, ids, found)
+            rank = rank + picked.astype(jnp.int32)
+        lists[side] = found
+        live[side : side + 1] = rank
+    nodes = partners.shape[1]
+    node = lax.broadcasted_iota(jnp.int32, (1, nodes), 1)
+    span = jnp.full((1, nodes), leaves, jnp.int32)
+    start = jnp.zeros((1, nodes), jnp.int32)
+    width, tile, first = leaves // 2, leaves // 2, leaves
+    while width >= 1:
+        span = jnp.where(node >= first, width, span)
+        start = jnp.where(node >= first, 2 * tile, start)
+        tile, first, width = tile + max(1, width // 2), first + width, width // 2
+    shifted = partners[...] - place * span
+    side = jnp.where(shifted < 0, 0, jnp.where(shifted < span, 1, 2))
+    codes[...] = side * (2 * leaves) + start + shifted - (side - 1) * span
+
+
+def up_body(
+    place, near_list, near_count, partners, basis_hbm, values_hbm, moves_hbm,
+    up, share, trans_hbm, lists, live, codes, rows, basis, values, moves, trans, sem,
+):
     leaves = basis.shape[0]
     columns = values.shape[0]
     nodes = moves.shape[2]
@@ -42,6 +102,7 @@
     reads.append(pltpu.make_async_copy(basis_hbm, basis, sem.at[5]))
     for read in reads:
         read.start()
+    plan(place[0], near_list, near_count, partners, lists, live, codes)
     for i in range(4):
         reads[i].wait()
 
@@ -115,7 +176,7 @@
     write.wait()
 
 
-def up_pass(basis, values, moves):
+def up_pass(place, near_list, near_count, partners, basis, values, moves):
     leaves = basis.shape[0]
     columns = values.shape[0]
     nodes = moves.shape[2]
@@ -125,9 +186,12 @@
             jax.ShapeDtypeStruct((leaves, columns, 128), f32),
             jax.ShapeDtypeStruct((columns, 128), f32),
             jax.ShapeDtypeStruct((nodes + 1, 64, 128), bf16),
+            jax.ShapeDtypeStruct((2, SLOTS, leaves), jnp.int32),
+            jax.ShapeDtypeStruct((2, leaves), jnp.int32),
+            jax.ShapeDtypeStruct(partners.shape, jnp.int32),
         ),
-        in_specs=[HBM, HBM, HBM],
-        out_specs=(VM, VM, HBM),
+        in_specs=[SM, VM, VM, VM, HBM, HBM, HBM],
+        out_specs=(VM, VM, HBM, VM, VM, VM),
         scratch_shapes=[
             pltpu.VMEM((64 * PITCH, 128), f32),
             pltpu.VMEM(basis.shape, f32),
@@ -139,7 +203,7 @@
         compiler_params=pltpu.CompilerParams(vmem_limit_bytes=VMEM_BYTES),
         cost_estimate=pl.CostEstimate(flops=400_000_000, bytes_accessed=8_000_000, transcendentals=0),
         name="up_pass",
-    )(basis, values, moves)
+    )(place, near_list, near_count, partners, basis, values, moves)
 
 
 CHUNK = 32
@@ -243,7 +307,7 @@
         index = rows[level] + spot // (2 << level)
         far = jnp.zeros((columns, 64), f32)
         for k in range(4):
-            p = partners[index, k]
+            p = partners[k, index]
             tile = up[tiles[level] + p // 2]
             x = stack(jnp.where(p % 2 == 0, tile, pltpu.roll(tile, 64, 1))[:, 0:64])
             hi, lo = split(block[level, k])
@@ -296,7 +360,7 @@
             gather[1, side * leaves + t] = stack(pltpu.roll(x, 64, 1))
 
     def pick(n, k, side):
-        code = codes[n, k]
+        code = codes[k, n]
         return gather[(code & 1) ^ side, code >> 1]
 
     def one(n):
@@ -418,18 +482,19 @@
 
 near_weight = 0.1
 smoothing = 0.0025
-SLOTS = 28
 PAIR = 2
 
-def near_body(unroll, chunks, core, lists, counts, targets, *refs):
+def near_body(unroll, chunks, core, lists, live, targets, *refs):
     origins, refs = refs[: 2 * chunks], refs[2 * chunks :]
-    begin, spots = None, [targets]
+    begin = None
     if chunks == 2:
-        begin, spots, refs = refs[0:2], refs[2:4], refs[4:]
+        begin, refs = refs[0:2], refs[2:]
     mine, other, columns_of, total, weights, places, sem, *sources = refs
     leaves = mine.shape[1] // 128
     width = sources[0].shape[1] // 128
     core = core[0]
+    side = chunks - 1
+    base = core * leaves
     reads = []
     for i, (origin, source) in enumerate(zip(origins, sources)):
         reads.append(pltpu.make_async_copy(origin, source, sem.at[i]))
@@ -462,18 +527,18 @@
             for u in range(8):
                 j = 8 * g + u
                 at = pl.ds(pl.multiple_of(j * 128, 128), 128)
-                x = near_weight * jnp.concatenate([near_ref[:, at], far_ref[:, at]], axis=0)
+                x = near_weight * jnp.concatenate([near_ref[0:32, at], far_ref[0:32, at]], axis=0)
                 weights[c * width + j] = stack(x)
-                places[c * width + j, 0:3] = spots[c][:, at]
+                places[c * width + j, 0:3] = near_ref[32:35, at]
 
     items = lax.fori_loop(
-        0, leaves, lambda i, s: s + jnp.maximum((counts[i] + PAIR - 1) // PAIR, 1), jnp.int32(0)
+        0, leaves, lambda i, s: s + jnp.maximum((live[side, base + i] + PAIR - 1) // PAIR, 1), jnp.int32(0)
     )
 
     def block(leaf, slot):
         kernels, parts = [], []
         for u in range(PAIR):
-            j = lists[leaf, slot + u]
+            j = lists[side, slot + u, base + leaf]
             s = places[j]
             d = columns_of[leaf, 0] - s[0:1]
             squared = d * d + smoothing
@@ -497,7 +562,7 @@
         for u in range(unroll):
             place = jnp.where(b * unroll + u < items, leaf, leaves)
             made.append((place, block(leaf, slot)))
-            done = slot + PAIR >= counts[leaf]
+            done = slot + PAIR >= live[side, base + leaf]
             leaf = jnp.where(done, jnp.minimum(leaf + 1, leaves - 1), leaf)
             slot = jnp.where(done, 0, slot + PAIR)
         for place, x in made:
@@ -518,16 +583,16 @@
             other[:, at] = begin[1][:, at] + x[32:64]
 
 
-def near_pass(unroll, core, lists, counts, targets, sources, begin=(), spots=()):
-    leaves = lists.shape[0]
+def near_pass(unroll, core, lists, live, targets, sources, begin=()):
+    leaves = lists.shape[2] // 2
     chunks = len(sources) // 2
     held = chunks * (sources[0].shape[1] // 128) + 1
     side = jax.ShapeDtypeStruct((32, leaves * 128), f32)
-    arrays = (targets, *sources, *begin, *spots)
+    arrays = (targets, *sources, *begin)
     return pl.pallas_call(
         functools.partial(near_body, unroll, chunks),
         out_shape=(side, side),
-        in_specs=[SM, SM, SM, VM] + [HBM] * len(sources) + [VM] * 2 * len(begin),
+        in_specs=[SM, SM, SM, VM] + [HBM] * len(sources) + [VM] * len(begin),
         out_specs=(VM, VM),
         scratch_shapes=[
             pltpu.VMEM((leaves, 3, 128, 128), f32),
@@ -540,33 +605,7 @@
         compiler_params=pltpu.CompilerParams(vmem_limit_bytes=VMEM_BYTES),
         cost_estimate=pl.CostEstimate(flops=1_000, bytes_accessed=1_000, transcendentals=0),
         name="near_pass",
-    )(core, lists, counts, *arrays)
-
-
-def arranged(picked, leaf_ids, empty):
-    slots = picked.shape[1]
-    before = jnp.arange(slots)[:, None] < jnp.arange(slots)[None, :]
-    rank = jnp.sum(jnp.where(picked[:, :, None] & before[None], 1, 0), axis=1)
-    to = jnp.arange(SLOTS)[None, None, :]
-    here = picked[:, :, None] & (rank[:, :, None] == to)
-    found = jnp.sum(jnp.where(here, leaf_ids[:, :, None], 0), axis=1)
-    count = jnp.sum(picked.astype(jnp.int32), axis=1)
-    lists = jnp.where(jnp.arange(SLOTS)[None, :] < count[:, None], found, empty)
-    return lists.astype(jnp.int32), count
-
-
-def partner_codes(partners, position, leaves):
-    spans, starts = [], []
-    width, tile = leaves, 0
-    while width >= 1:
-        spans += [width] * width
-        starts += [2 * tile] * width
-        tile, width = tile + max(1, width // 2), width // 2
-    spans = jnp.array(spans, jnp.int32)[:, None]
-    starts = jnp.array(starts, jnp.int32)[:, None]
-    local = partners - position * spans
-    side = jnp.where(local < 0, 0, jnp.where(local < spans, 1, 2))
-    return (side * (2 * leaves) + starts + local - (side - 1) * spans)
+    )(core, lists, live, *arrays)
 
 
 def local(
@@ -589,19 +628,10 @@
     forward = [(i, i + 1) for i in range(count - 1)]
     backward = [(target, source) for source, target in forward]
     swap = [(0, 1), (1, 0)]
-    low = lax.ppermute(values, "leaf", forward)
-    high = lax.ppermute(values, "leaf", backward)
-    spots = (lax.ppermute(points, "leaf", forward), lax.ppermute(points, "leaf", backward))
+    packed = pack(points, values)
+    low = lax.ppermute(packed, "leaf", forward)
+    high = lax.ppermute(packed, "leaf", backward)
     across = lax.ppermute(values, "rhs", swap)
-    half = leaves // 2
-    chosen = lax.dynamic_slice_in_dim(near_list, core * half, half, 0) - position * leaves
-    live = lax.dynamic_slice_in_dim(near_count, core * half, half, 0)
-    alive = jnp.arange(chosen.shape[1])[None, :] < live[:, None]
-    inside = (chosen >= 0) & (chosen < leaves)
-    near_ids, near_live = arranged(alive & inside, chosen, leaves)
-    outside_ids = jnp.where(chosen < 0, chosen + leaves, chosen)
-    far_ids, far_live = arranged(alive & ~inside, outside_ids, 2 * leaves)
-    codes = partner_codes(partners, position, leaves)
 
     def ring(x, stride):
         spot = (position // stride) % 4
@@ -623,10 +653,12 @@
 
     after = lax.optimization_barrier
     core = core[None].astype(jnp.int32)
-    up, share, trans = up_pass(basis, values, transfer.transpose(1, 2, 0))
-    near_ids, far_ids, codes, up = after((near_ids, far_ids, codes, up))
-    begin = near_pass(12, core, near_ids, near_live, points, (values, across))
-    low, high, spots, coupling, share, begin = after((low, high, spots, coupling, share, begin))
+    place = position[None].astype(jnp.int32)
+    up, share, trans, lists, live, codes = up_pass(
+        place, near_list.T, near_count[None], partners.T, basis, values, transfer.transpose(1, 2, 0)
+    )
+    begin = near_pass(12, core, lists, live, points, (packed, across))
+    low, high, coupling, share, begin = after((low, high, coupling, share, begin))
     turned, spot = ring(share[None], 1)
     low_across = lax.ppermute(low, "rhs", swap)
     high_across = lax.ppermute(high, "rhs", swap)
@@ -638,22 +670,20 @@
     level = in_order(turned, share[None], spot)
     level = jnp.where(jnp.arange(128) < 64, level[0] + level[1], level[2] + level[3])[None]
     turned, spot = ring(level, 4)
+    second = unbatch(coupling, 1)
+    turned, lists, up, second = after((turned, lists, up, second))
+    level = in_order(turned, level, spot)
+    turned, spot = ring(level, 16)
     up_low = lax.ppermute(up, "leaf", forward)
     up_high = lax.ppermute(up, "leaf", backward)
-    second = unbatch(coupling, 1)
-    turned, far_ids, second = after((turned, far_ids, second))
-    level = in_order(turned, level, spot)
-    turned, spot = ring(level, 16)
     mine, other = near_pass(
-        12, core, far_ids, far_live, points, (low, low_across, high, high_across), begin, spots
+        12, core, lists, live, points, (low, low_across, high, high_across), begin
     )
-    turned, mine, other = after((turned, mine, other))
     given = lax.ppermute(other, "rhs", swap)
-    parent = top_pass(
-        position[None].astype(jnp.int32), partners_top, (*turned, level), transfer_top, coupling_top
-    )
-    up_low, up_high, parent = after((up_low, up_high, parent))
+    mine, up_low, up_high = after((mine, up_low, up_high))
     far = couple_pass(codes, up_low, up, up_high, first, second)
+    turned, far = after((turned, far))
+    parent = top_pass(place, partners_top.T, (*turned, level), transfer_top, coupling_top)
     return down_pass(core, parent, far, trans, basis, mine, given)
 
 

time: 142 us -> 121 us (0.85)
  the two profiles are of different devices: /device:TPU:39 before, /device:TPU:0 now
where the time goes in v7:
time: 121 us; the launch traced here: 119 us
  Pallas kernels  74.4 us (61%)
  starting transfers between devices  38.4 us (32%)
  waiting for transfers between devices  4.48 us (4%)
  local copies, waits for them, and re-layouts  1.4 us (1%)
    pallas_call x2, Pallas kernels, near_pass(): pl.pallas_call(functools.partial(near_body, unroll, chunks), out_shape=(s...  26.7 us
    ppermute x9, starting transfers between devices, ring(): turned.append(lax.ppermute(x, 'leaf', to))  26 us
    pallas_call x1, Pallas kernels, up_pass(): pl.pallas_call(up_body, out_shape=(jax.ShapeDtypeStruct((leaves, columns,...  11.4 us
    pallas_call x2, Pallas kernels, unbatch(): pl.pallas_call(functools.partial(unbatch_body, part), out_shape=jax.Shape...  10.2 us
    pallas_call x1, Pallas kernels, couple_pass(): pl.pallas_call(couple_body, out_shape=jax.ShapeDtypeStruct((leaves, colum...  9.52 us
    pallas_call x1, Pallas kernels, down_pass(): pl.pallas_call(down_body, out_shape=jax.ShapeDtypeStruct((columns, leaves...  8.64 us
    ppermute x1, starting transfers between devices, local(): low = lax.ppermute(packed, 'leaf', forward)  4.63 us
    ppermute x1, starting transfers between devices, local(): up_low = lax.ppermute(up, 'leaf', forward)  4.6 us
  transfers between devices with their start and end apart: 17, of which 1 were waited for; matrix products, arithmetic and copies ran while one was open for 0% of the time, Pallas kernels for 52%

profile of v7, /device:TPU:0, one launch (start us, length us, event | category | flops | bytes accessed | tf_op | source)
XLA Modules:
  0.0 119.2 jit_solution(3599912502554751543)
XLA Ops:
  0.0 3.3 %pack.1.refs_0_ = f32[40,8192]{1,0:T(8,128)} custom-call(f32[3,8192]{1,0:T(4,128)} %targets.3, f32[32,8192]{1,0:T(8,128)} %values_hbm.1), custom_call_target="tpu_custom_call" | custom-call | tf_op jit(solution)/shard_map/pack/pallas_call | solution.py:46
  3.3 4.6 %collective-permute-start = (f32[40,8192]{1,0:T(8,128)}, f32[40,8192]{1,0:T(8,128)}, u32[]{:S(2)}, u32[]{:S(2)}) collective-permute-start(f32[40,8192]{1,0:T(8,128)} %pack.1.refs_0_), channel_id=1, source_target_pairs={{0,2},{2,4},{4,6},{6,8},{8,10},{10,12},{12,14},{14,16},{16,18},{18... | collective-permute-start | bytes 3932168 | tf_op jit(solution)/shard_map/ppermute | solution.py:632
  7.9 1.3 %collective-permute-start.1 = (f32[40,8192]{1,0:T(8,128)}, f32[40,8192]{1,0:T(8,128)}, u32[]{:S(2)}, u32[]{:S(2)}) collective-permute-start(f32[40,8192]{1,0:T(8,128)} %pack.1.refs_0_), channel_id=1, source_target_pairs={{2,0},{4,2},{6,4},{8,6},{10,8},{12,10},{14,12},{16,14},{18,16},{20... | collective-permute-start | bytes 3932168 | tf_op jit(solution)/shard_map/ppermute | solution.py:633
  9.2 0.1 collective-permute-start.2
  9.3 11.4 %up_pass.1 = (f32[64,32,128]{2,1,0:T(8,128)}, f32[32,128]{1,0:T(8,128)}, bf16[128,64,128]{2,1,0:T(8,128)(2,1)}, s32[2,28,64]{2,1,0:T(8,128)}, s32[2,64]{1,0:T(2,128)}, /*index=5*/s32[4,127]{1,0:T(4,128)}) custom-call(s32[1]{0:T(128)} %bitcast.1.place, s32[27,64]{1,0:T(8,128)} %bitcast.13, s32[1,64]{1,0:T(1,128)} %bitcast.19, s32[4,127]{1,0:T(4,128)} %bitcast.17, ...), custom_call_target="tpu_custom_call" | custom-call | flops 400000000 | bytes 8000000 | tf_op jit(solution)/shard_map/up_pass/pallas_call | solution.py:183
  20.7 0.0 collective-permute-done.2.refs_1_
  20.8 15.2 %near_pass.2 = (f32[32,4096]{1,0:T(8,128)}, f32[32,4096]{1,0:T(8,128)}) custom-call(s32[1]{0:T(128)} %bitcast.core, s32[2,28,64]{2,1,0:T(8,128)} %get-tuple-element.61.lists, s32[2,64]{1,0:T(2,128)} %get-tuple-element.44.live, f32[3,8192]{1,0:T(4,128)} %targets.3, f32[40,8192]{1,0:T(8,128)} %pack.1.refs_0_, f32[32,8192]{1,0:T(8,128)} %collective-permute-done.2.refs_1_), custom_call_target="tpu_custom_call" | custom-call | flops 1000 | bytes 1000 | tf_op jit(solution)/shard_map/near_pass/pallas_call | solution.py:592
  35.9 0.0 collective-permute-done.refs_0_
  35.9 4.4 %collective-permute-done.1.refs_2_ = f32[40,8192]{1,0:T(8,128)} collective-permute-done((f32[40,8192]{1,0:T(8,128)}, f32[40,8192]{1,0:T(8,128)}, u32[]{:S(2)}, u32[]{:S(2)}) %collective-permute-start.1) | collective-permute-done | bytes 1310752 | tf_op jit(solution)/shard_map/ppermute | solution.py:633
  40.4 0.0 collective-permute-start.6
  40.4 0.5 collective-permute-start.7
  40.9 3.7 %collective-permute-start.3 = (f32[1,32,128]{2,1,0:T(8,128)S(1)}, f32[1,32,128]{2,1,0:T(8,128)S(1)}, u32[]{:S(2)}, u32[]{:S(2)}) collective-permute-start(f32[1,32,128]{2,1,0:T(8,128)S(1)} %bitcast.14), channel_id=1, source_target_pairs={{0,6},{2,0},{4,2},{6,4},{8,14},{10,8},{12,10},{14,12},{16,22},{18,... | collective-permute-start | bytes 49160 | tf_op jit(solution)/shard_map/ppermute | solution.py:641
  44.5 0.0 collective-permute-start.4
  44.6 0.9 collective-permute-start.5
  45.4 5.1 %unbatch.2.first = bf16[127,128,128]{2,1,0:T(8,128)(2,1)} custom-call(f32[4,64,64,127]{3,2,1,0:T(8,128)} %bitcast.10), custom_call_target="tpu_custom_call" | custom-call | flops 1000 | bytes 1000 | tf_op jit(solution)/shard_map/unbatch/pallas_call | solution.py:252
  50.5 0.0 collective-permute-done.3
  50.5 0.0 collective-permute-done.4
  50.5 0.0 collective-permute-done.5
  50.5 0.0 collective-permute-done.6.refs_1_
  50.5 0.0 collective-permute-done.7.refs_3_
  50.6 1.6 %collective-permute-start.10 = (f32[1,32,128]{2,1,0:T(8,128)S(1)}, f32[1,32,128]{2,1,0:T(8,128)S(1)}, u32[]{:S(2)}, u32[]{:S(2)}) collective-permute-start(f32[1,32,128]{2,1,0:T(8,128)S(1)} %add_select_fusion), channel_id=1, source_target_pairs={{0,8},{2,10},{4,12},{6,14},{8,16},{10,18},{12,20},{14,22},{16,24},... | collective-permute-start | bytes 49160 | tf_op jit(solution)/shard_map/ppermute | solution.py:641
  52.1 3.8 %collective-permute-start.8 = (f32[1,32,128]{2,1,0:T(8,128)S(1)}, f32[1,32,128]{2,1,0:T(8,128)S(1)}, u32[]{:S(2)}, u32[]{:S(2)}) collective-permute-start(f32[1,32,128]{2,1,0:T(8,128)S(1)} %add_select_fusion), channel_id=1, source_target_pairs={{0,24},{2,26},{4,28},{6,30},{8,0},{10,2},{12,4},{14,6},{16,8},{18,... | collective-permute-start | bytes 49160 | tf_op jit(solution)/shard_map/ppermute | solution.py:641
  55.9 1.4 %collective-permute-start.9 = (f32[1,32,128]{2,1,0:T(8,128)S(1)}, f32[1,32,128]{2,1,0:T(8,128)S(1)}, u32[]{:S(2)}, u32[]{:S(2)}) collective-permute-start(f32[1,32,128]{2,1,0:T(8,128)S(1)} %add_select_fusion), channel_id=1, source_target_pairs={{0,16},{2,18},{4,20},{6,22},{8,24},{10,26},{12,28},{14,30},{16,0},... | collective-permute-start | bytes 49160 | tf_op jit(solution)/shard_map/ppermute | solution.py:641
  57.3 5.1 %unbatch.3.second = bf16[127,128,128]{2,1,0:T(8,128)(2,1)} custom-call(f32[4,64,64,127]{3,2,1,0:T(8,128)} %bitcast.11), custom_call_target="tpu_custom_call" | custom-call | flops 1000 | bytes 1000 | tf_op jit(solution)/shard_map/unbatch/pallas_call | solution.py:252
  62.5 0.0 collective-permute-done.10
  62.5 0.0 collective-permute-done.8
  62.5 0.0 collective-permute-done.9
  62.5 4.6 %collective-permute-start.14 = (f32[64,32,128]{2,1,0:T(8,128)}, f32[64,32,128]{2,1,0:T(8,128)S(1)}, u32[]{:S(2)}, u32[]{:S(2)}) collective-permute-start(f32[64,32,128]{2,1,0:T(8,128)} %get-tuple-element.67.own), channel_id=1, source_target_pairs={{0,2},{2,4},{4,6},{6,8},{8,10},{10,12},{12,14},{14,16},{16,18},{18... | collective-permute-start | bytes 3145736 | tf_op jit(solution)/shard_map/ppermute | solution.py:677
  67.1 1.3 %collective-permute-start.15 = (f32[64,32,128]{2,1,0:T(8,128)}, f32[64,32,128]{2,1,0:T(8,128)}, u32[]{:S(2)}, u32[]{:S(2)}) collective-permute-start(f32[64,32,128]{2,1,0:T(8,128)} %get-tuple-element.67.own), channel_id=1, source_target_pairs={{2,0},{4,2},{6,4},{8,6},{10,8},{12,10},{14,12},{16,14},{18,16},{20... | collective-permute-start | bytes 3145736 | tf_op jit(solution)/shard_map/ppermute | solution.py:678
  68.4 11.6 %near_pass.3 = (f32[32,4096]{1,0:T(8,128)}, f32[32,4096]{1,0:T(8,128)}) custom-call(s32[1]{0:T(128)} %bitcast.core, s32[2,28,64]{2,1,0:T(8,128)} %get-tuple-element.61.lists, s32[2,64]{1,0:T(2,128)} %get-tuple-element.44.live, f32[3,8192]{1,0:T(4,128)} %targets.3, f32[40,8192]{1,0:T(8,128)} %collective-permute-done.refs_0_, f32[40,8192]{1,0:T(8,128)} %copy-done.1, ...), custom_call_target="tpu_custom_call" | custom-call | flops 1000 | bytes 1000 | tf_op jit(solution)/shard_map/near_pass/pallas_call | solution.py:592
  80.0 0.1 collective-permute-start.16
  80.2 8.1 %collective-permute-start.11 = (f32[4,32,128]{2,1,0:T(8,128)S(1)}, f32[4,32,128]{2,1,0:T(8,128)S(1)}, u32[]{:S(2)}, u32[]{:S(2)}) collective-permute-start(f32[4,32,128]{2,1,0:T(8,128)S(1)} %pad_maximum_fusion.own), channel_id=1, source_target_pairs={{0,96},{2,98},{4,100},{6,102},{8,104},{10,106},{12,108},{14,110},{... | collective-permute-start | bytes 196616 | tf_op jit(solution)/shard_map/ppermute | solution.py:641
  88.3 2.5 %collective-permute-start.12 = (f32[4,32,128]{2,1,0:T(8,128)S(1)}, f32[4,32,128]{2,1,0:T(8,128)S(1)}, u32[]{:S(2)}, u32[]{:S(2)}) collective-permute-start(f32[4,32,128]{2,1,0:T(8,128)S(1)} %pad_maximum_fusion.own), channel_id=1, source_target_pairs={{0,64},{2,66},{4,68},{6,70},{8,72},{10,74},{12,76},{14,78},{16,80}... | collective-permute-start | bytes 196616 | tf_op jit(solution)/shard_map/ppermute | solution.py:641
  90.8 0.0 collective-permute-done.14.low
  90.8 4.0 %collective-permute-start.13 = (f32[4,32,128]{2,1,0:T(8,128)S(1)}, f32[4,32,128]{2,1,0:T(8,128)S(1)}, u32[]{:S(2)}, u32[]{:S(2)}) collective-permute-start(f32[4,32,128]{2,1,0:T(8,128)S(1)} %pad_maximum_fusion.own), channel_id=1, source_target_pairs={{0,32},{2,34},{4,36},{6,38},{8,40},{10,42},{12,44},{14,46},{16,48}... | collective-permute-start | bytes 196616 | tf_op jit(solution)/shard_map/ppermute | solution.py:641
  94.9 0.0 collective-permute-done.15.high
  94.9 9.5 %couple_pass.1.far_hbm = f32[64,32,128]{2,1,0:T(8,128)} custom-call(s32[4,127]{1,0:T(4,128)} %get-tuple-element.60.codes, f32[64,32,128]{2,1,0:T(8,128)} %copy-done.2, f32[64,32,128]{2,1,0:T(8,128)} %get-tuple-element.67.own, f32[64,32,128]{2,1,0:T(8,128)} %collective-permute-done.15.high, bf16[127,128,128]{2,1,0:T(8,128)(2,1)} %unbatch.2.first, ...), custom_call_target="tpu_custom_call" | custom-call | flops 400000000 | bytes 12000000 | tf_op jit(solution)/shard_map/couple_pass/pallas_call | solution.py:390
  104.4 0.0 collective-permute-done.11.far_three
  104.4 0.0 copy-start.5
  104.4 0.0 collective-permute-done.12.far_two
  104.4 0.0 collective-permute-done.13.far_one
  104.5 0.6 copy-done.5
  105.0 0.0 copy-done.6
  105.0 0.0 copy-done.7
  105.1 4.6 %top_pass.1.parent = f32[32,128]{1,0:T(8,128)} custom-call(s32[1]{0:T(128)} %bitcast.1.place, s32[4,60]{1,0:T(4,128)} %bitcast.18, f32[4,32,128]{2,1,0:T(8,128)} %copy-done.5, f32[4,32,128]{2,1,0:T(8,128)} %copy-done.6, f32[4,32,128]{2,1,0:T(8,128)} %copy-done.7, f32[4,32,128]{2,1,0:T(8,128)} %copy-done.4, f32[62,64,64]{2,1,0:T(8,128)} %moves.1, ...), custom_call_target="tpu_custom_call" | custom-call | flops 50000000 | bytes 2000000 | tf_op jit(solution)/shard_map/top_pass/pallas_call | solution.py:325
  109.6 0.0 collective-permute-done.16.given
  109.7 0.8 copy-done.3
  110.4 8.6 %down_pass.1 = f32[32,8192]{1,0:T(8,128)} custom-call(s32[1]{0:T(128)} %bitcast.core, f32[32,128]{1,0:T(8,128)} %top_pass.1.parent, f32[64,32,128]{2,1,0:T(8,128)} %couple_pass.1.far_hbm, bf16[128,64,128]{2,1,0:T(8,128)(2,1)} %get-tuple-element.76.trans_hbm, f32[64,64,128]{2,1,0:T(8,128)} %basis_hbm.3, f32[32,4096]{1,0:T(8,128)} %get-tuple-element.77.mine, ...), custom_call_target="tpu_custom_call" | custom-call | flops 200000000 | bytes 7000000 | tf_op jit(solution)/shard_map/down_pass/pallas_call | solution.py:464
  (17 shorter events, 0.1 us)
Async XLA Ops:
  0.0 9.2 %copy-start = (f32[32,8192]{1,0:T(8,128)S(1)}, f32[32,8192]{1,0:T(8,128)}, u32[]{:S(2)}) copy-start(f32[32,8192]{1,0:T(8,128)} %values_hbm.1) | copy-start | bytes 3145732
  3.3 32.6 %collective-permute-start = (f32[40,8192]{1,0:T(8,128)}, f32[40,8192]{1,0:T(8,128)}, u32[]{:S(2)}, u32[]{:S(2)}) collective-permute-start(f32[40,8192]{1,0:T(8,128)} %pack.1.refs_0_), channel_id=1, source_target_pairs={{0,2},{2,4},{4,6},{6,8},{8,10},{10,12},{12,14},{14,16},{16,18},{18... | collective-permute-start | bytes 3932168 | tf_op jit(solution)/shard_map/ppermute | solution.py:632
  7.9 32.4 %collective-permute-start.1 = (f32[40,8192]{1,0:T(8,128)}, f32[40,8192]{1,0:T(8,128)}, u32[]{:S(2)}, u32[]{:S(2)}) collective-permute-start(f32[40,8192]{1,0:T(8,128)} %pack.1.refs_0_), channel_id=1, source_target_pairs={{2,0},{4,2},{6,4},{8,6},{10,8},{12,10},{14,12},{16,14},{18,16},{20... | collective-permute-start | bytes 3932168 | tf_op jit(solution)/shard_map/ppermute | solution.py:633
  9.2 11.5 %collective-permute-start.2 = (f32[32,8192]{1,0:T(8,128)S(1)}, f32[32,8192]{1,0:T(8,128)}, u32[]{:S(2)}, u32[]{:S(2)}) collective-permute-start(f32[32,8192]{1,0:T(8,128)S(1)} %copy-done), channel_id=1, source_target_pairs={{0,1},{1,0},{2,3},{3,2},{4,5},{5,4},{6,7},{7,6},{8,9},{9,8},{10,11... | collective-permute-start | bytes 3145736 | tf_op jit(solution)/shard_map/ppermute | solution.py:634
  20.7 20.2 %copy-start.8 = (f32[32,128]{1,0:T(8,128)S(1)}, f32[32,128]{1,0:T(8,128)}, u32[]{:S(2)}) copy-start(f32[32,128]{1,0:T(8,128)} %get-tuple-element.47) | copy-start | bytes 49156
  40.4 10.1 %collective-permute-start.6 = (f32[40,8192]{1,0:T(8,128)}, f32[40,8192]{1,0:T(8,128)S(1)}, u32[]{:S(2)}, u32[]{:S(2)}) collective-permute-start(f32[40,8192]{1,0:T(8,128)} %collective-permute-done.refs_0_), channel_id=1, source_target_pairs={{0,1},{1,0},{2,3},{3,2},{4,5},{5,4},{6,7},{7,6},{8,9},{9,8},{10,11... | collective-permute-start | bytes 3932168 | tf_op jit(solution)/shard_map/ppermute | solution.py:663
  40.4 10.2 %collective-permute-start.7 = (f32[40,8192]{1,0:T(8,128)}, f32[40,8192]{1,0:T(8,128)}, u32[]{:S(2)}, u32[]{:S(2)}) collective-permute-start(f32[40,8192]{1,0:T(8,128)} %collective-permute-done.1.refs_2_), channel_id=1, source_target_pairs={{0,1},{1,0},{2,3},{3,2},{4,5},{5,4},{6,7},{7,6},{8,9},{9,8},{10,11... | collective-permute-start | bytes 3932168 | tf_op jit(solution)/shard_map/ppermute | solution.py:664
  40.9 9.6 %collective-permute-start.3 = (f32[1,32,128]{2,1,0:T(8,128)S(1)}, f32[1,32,128]{2,1,0:T(8,128)S(1)}, u32[]{:S(2)}, u32[]{:S(2)}) collective-permute-start(f32[1,32,128]{2,1,0:T(8,128)S(1)} %bitcast.14), channel_id=1, source_target_pairs={{0,6},{2,0},{4,2},{6,4},{8,14},{10,8},{12,10},{14,12},{16,22},{18,... | collective-permute-start | bytes 49160 | tf_op jit(solution)/shard_map/ppermute | solution.py:641
  44.5 6.0 %collective-permute-start.4 = (f32[1,32,128]{2,1,0:T(8,128)S(1)}, f32[1,32,128]{2,1,0:T(8,128)S(1)}, u32[]{:S(2)}, u32[]{:S(2)}) collective-permute-start(f32[1,32,128]{2,1,0:T(8,128)S(1)} %bitcast.15), channel_id=1, source_target_pairs={{0,4},{2,6},{4,0},{6,2},{8,12},{10,14},{12,8},{14,10},{16,20},{18,... | collective-permute-start | bytes 49160 | tf_op jit(solution)/shard_map/ppermute | solution.py:641
  44.6 6.0 %collective-permute-start.5 = (f32[1,32,128]{2,1,0:T(8,128)S(1)}, f32[1,32,128]{2,1,0:T(8,128)S(1)}, u32[]{:S(2)}, u32[]{:S(2)}) collective-permute-start(f32[1,32,128]{2,1,0:T(8,128)S(1)} %bitcast.16), channel_id=1, source_target_pairs={{0,2},{2,4},{4,6},{6,0},{8,10},{10,12},{12,14},{14,8},{16,18},{18,... | collective-permute-start | bytes 49160 | tf_op jit(solution)/shard_map/ppermute | solution.py:641
  50.5 11.9 %copy-start.1 = (f32[40,8192]{1,0:T(8,128)}, f32[40,8192]{1,0:T(8,128)S(1)}, u32[]{:S(2)}) copy-start(f32[40,8192]{1,0:T(8,128)S(1)} %collective-permute-done.6.refs_1_) | copy-start | bytes 3932164
  50.6 11.9 %collective-permute-start.10 = (f32[1,32,128]{2,1,0:T(8,128)S(1)}, f32[1,32,128]{2,1,0:T(8,128)S(1)}, u32[]{:S(2)}, u32[]{:S(2)}) collective-permute-start(f32[1,32,128]{2,1,0:T(8,128)S(1)} %add_select_fusion), channel_id=1, source_target_pairs={{0,8},{2,10},{4,12},{6,14},{8,16},{10,18},{12,20},{14,22},{16,24},... | collective-permute-start | bytes 49160 | tf_op jit(solution)/shard_map/ppermute | solution.py:641
  52.1 10.3 %collective-permute-start.8 = (f32[1,32,128]{2,1,0:T(8,128)S(1)}, f32[1,32,128]{2,1,0:T(8,128)S(1)}, u32[]{:S(2)}, u32[]{:S(2)}) collective-permute-start(f32[1,32,128]{2,1,0:T(8,128)S(1)} %add_select_fusion), channel_id=1, source_target_pairs={{0,24},{2,26},{4,28},{6,30},{8,0},{10,2},{12,4},{14,6},{16,8},{18,... | collective-permute-start | bytes 49160 | tf_op jit(solution)/shard_map/ppermute | solution.py:641
  55.9 6.5 %collective-permute-start.9 = (f32[1,32,128]{2,1,0:T(8,128)S(1)}, f32[1,32,128]{2,1,0:T(8,128)S(1)}, u32[]{:S(2)}, u32[]{:S(2)}) collective-permute-start(f32[1,32,128]{2,1,0:T(8,128)S(1)} %add_select_fusion), channel_id=1, source_target_pairs={{0,16},{2,18},{4,20},{6,22},{8,24},{10,26},{12,28},{14,30},{16,0},... | collective-permute-start | bytes 49160 | tf_op jit(solution)/shard_map/ppermute | solution.py:641
  62.5 28.3 %collective-permute-start.14 = (f32[64,32,128]{2,1,0:T(8,128)}, f32[64,32,128]{2,1,0:T(8,128)S(1)}, u32[]{:S(2)}, u32[]{:S(2)}) collective-permute-start(f32[64,32,128]{2,1,0:T(8,128)} %get-tuple-element.67.own), channel_id=1, source_target_pairs={{0,2},{2,4},{4,6},{6,8},{8,10},{10,12},{12,14},{14,16},{16,18},{18... | collective-permute-start | bytes 3145736 | tf_op jit(solution)/shard_map/ppermute | solution.py:677
  67.1 27.8 %collective-permute-start.15 = (f32[64,32,128]{2,1,0:T(8,128)}, f32[64,32,128]{2,1,0:T(8,128)}, u32[]{:S(2)}, u32[]{:S(2)}) collective-permute-start(f32[64,32,128]{2,1,0:T(8,128)} %get-tuple-element.67.own), channel_id=1, source_target_pairs={{2,0},{4,2},{6,4},{8,6},{10,8},{12,10},{14,12},{16,14},{18,16},{20... | collective-permute-start | bytes 3145736 | tf_op jit(solution)/shard_map/ppermute | solution.py:678
  80.0 29.7 %collective-permute-start.16 = (f32[32,4096]{1,0:T(8,128)}, f32[32,4096]{1,0:T(8,128)S(1)}, u32[]{:S(2)}, u32[]{:S(2)}) collective-permute-start(f32[32,4096]{1,0:T(8,128)} %get-tuple-element.78), channel_id=1, source_target_pairs={{0,1},{1,0},{2,3},{3,2},{4,5},{5,4},{6,7},{7,6},{8,9},{9,8},{10,11... | collective-permute-start | bytes 1572872 | tf_op jit(solution)/shard_map/ppermute | solution.py:682
  80.1 24.3 %copy-start.4 = (f32[4,32,128]{2,1,0:T(8,128)}, f32[4,32,128]{2,1,0:T(8,128)S(1)}, u32[]{:S(2)}) copy-start(f32[4,32,128]{2,1,0:T(8,128)S(1)} %pad_maximum_fusion.own) | copy-start | bytes 196612
  80.2 24.2 %collective-permute-start.11 = (f32[4,32,128]{2,1,0:T(8,128)S(1)}, f32[4,32,128]{2,1,0:T(8,128)S(1)}, u32[]{:S(2)}, u32[]{:S(2)}) collective-permute-start(f32[4,32,128]{2,1,0:T(8,128)S(1)} %pad_maximum_fusion.own), channel_id=1, source_target_pairs={{0,96},{2,98},{4,100},{6,102},{8,104},{10,106},{12,108},{14,110},{... | collective-permute-start | bytes 196616 | tf_op jit(solution)/shard_map/ppermute | solution.py:641
  88.3 16.1 %collective-permute-start.12 = (f32[4,32,128]{2,1,0:T(8,128)S(1)}, f32[4,32,128]{2,1,0:T(8,128)S(1)}, u32[]{:S(2)}, u32[]{:S(2)}) collective-permute-start(f32[4,32,128]{2,1,0:T(8,128)S(1)} %pad_maximum_fusion.own), channel_id=1, source_target_pairs={{0,64},{2,66},{4,68},{6,70},{8,72},{10,74},{12,76},{14,78},{16,80}... | collective-permute-start | bytes 196616 | tf_op jit(solution)/shard_map/ppermute | solution.py:641
  90.8 4.0 %copy-start.2 = (f32[64,32,128]{2,1,0:T(8,128)}, f32[64,32,128]{2,1,0:T(8,128)S(1)}, u32[]{:S(2)}) copy-start(f32[64,32,128]{2,1,0:T(8,128)S(1)} %collective-permute-done.14.low) | copy-start | bytes 3145732
  90.8 13.6 %collective-permute-start.13 = (f32[4,32,128]{2,1,0:T(8,128)S(1)}, f32[4,32,128]{2,1,0:T(8,128)S(1)}, u32[]{:S(2)}, u32[]{:S(2)}) collective-permute-start(f32[4,32,128]{2,1,0:T(8,128)S(1)} %pad_maximum_fusion.own), channel_id=1, source_target_pairs={{0,32},{2,34},{4,36},{6,38},{8,40},{10,42},{12,44},{14,46},{16,48}... | collective-permute-start | bytes 196616 | tf_op jit(solution)/shard_map/ppermute | solution.py:641
  104.4 0.6 copy-start.5
  104.4 0.6 copy-start.6
  104.4 0.6 copy-start.7
  109.7 0.8 copy-start.3

commit v8 on v7

--- a/solution.py
+++ b/solution.py
@@ -30,29 +30,6 @@
 
 def low_lanes(shape):
     return lax.broadcasted_iota(jnp.int32, shape, 1) < 64
-
-def pack_body(points, values, out, sem):
-    columns = values.shape[0]
-    read = pltpu.make_async_copy(values, out.at[pl.ds(0, columns)], sem)
-    read.start()
-    out[columns:] = jnp.concatenate(
-        [points[...], jnp.zeros((out.shape[0] - columns - 3, out.shape[1]), f32)], axis=0
-    )
-    read.wait()
-
-
-def pack(points, values):
-    columns, width = values.shape
-    return pl.pallas_call(
-        pack_body,
-        out_shape=jax.ShapeDtypeStruct((columns + 8, width), f32),
-        in_specs=[VM, HBM],
-        out_specs=VM,
-        scratch_shapes=[pltpu.SemaphoreType.DMA],
-        compiler_params=pltpu.CompilerParams(vmem_limit_bytes=VMEM_BYTES),
-        name="pack",
-    )(points, values)
-
 
 def plan(place, near_list, near_count, partners, lists, live, codes):
     slots, leaves = near_list.shape
@@ -88,8 +65,8 @@
 
 
 def up_body(
-    place, near_list, near_count, partners, basis_hbm, values_hbm, moves_hbm,
-    up, share, trans_hbm, lists, live, codes, rows, basis, values, moves, trans, sem,
+    place, near_list, near_count, partners, points, basis_hbm, values_hbm, moves_hbm,
+    up, share, trans_hbm, packed_hbm, lists, live, codes, rows, basis, values, moves, trans, packed, sem,
 ):
     leaves = basis.shape[0]
     columns = values.shape[0]
@@ -130,6 +107,19 @@
 
     for read in reads[4:]:
         read.wait()
+    for c in range(3):
+        for j in range(leaves):
+            row = leaves * c + j
+            packed[leaves + row // columns, row % columns : row % columns + 1] = points[
+                c : c + 1, 128 * j : 128 * j + 128
+            ]
+
+    @pl.loop(0, leaves, unroll=8)
+    def _(j):
+        packed[j] = values[:, pl.ds(pl.multiple_of(j * 128, 128), 128)]
+
+    send = pltpu.make_async_copy(packed, packed_hbm, sem.at[7])
+    send.start()
 
     def leaf_up(i):
         v = stack(values[:, pl.ds(pl.multiple_of(i * 128, 128), 128)])
@@ -174,9 +164,10 @@
     up[leaves - 1] = tiles[0]
     share[...] = both(fold(jnp.dot(stack(tiles[0])[:, 0:64], trans[row], preferred_element_type=f32)))
     write.wait()
-
-
-def up_pass(place, near_list, near_count, partners, basis, values, moves):
+    send.wait()
+
+
+def up_pass(place, near_list, near_count, partners, points, basis, values, moves):
     leaves = basis.shape[0]
     columns = values.shape[0]
     nodes = moves.shape[2]
@@ -186,24 +177,26 @@
             jax.ShapeDtypeStruct((leaves, columns, 128), f32),
             jax.ShapeDtypeStruct((columns, 128), f32),
             jax.ShapeDtypeStruct((nodes + 1, 64, 128), bf16),
+            jax.ShapeDtypeStruct((leaves + 3 * leaves // columns, columns, 128), f32),
             jax.ShapeDtypeStruct((2, SLOTS, leaves), jnp.int32),
             jax.ShapeDtypeStruct((2, leaves), jnp.int32),
             jax.ShapeDtypeStruct(partners.shape, jnp.int32),
         ),
-        in_specs=[SM, VM, VM, VM, HBM, HBM, HBM],
-        out_specs=(VM, VM, HBM, VM, VM, VM),
+        in_specs=[SM, VM, VM, VM, VM, HBM, HBM, HBM],
+        out_specs=(VM, VM, HBM, HBM, VM, VM, VM),
         scratch_shapes=[
             pltpu.VMEM((64 * PITCH, 128), f32),
             pltpu.VMEM(basis.shape, f32),
             pltpu.VMEM(values.shape, f32),
             pltpu.VMEM(moves.shape, f32),
             pltpu.VMEM((nodes + 1, 64, 128), bf16),
-            pltpu.SemaphoreType.DMA((7,)),
+            pltpu.VMEM((leaves + 3 * leaves // columns, columns, 128), f32),
+            pltpu.SemaphoreType.DMA((8,)),
         ],
         compiler_params=pltpu.CompilerParams(vmem_limit_bytes=VMEM_BYTES),
         cost_estimate=pl.CostEstimate(flops=400_000_000, bytes_accessed=8_000_000, transcendentals=0),
         name="up_pass",
-    )(place, near_list, near_count, partners, basis, values, moves)
+    )(place, near_list, near_count, partners, points, basis, values, moves)
 
 
 CHUNK = 32
@@ -491,7 +484,7 @@
         begin, refs = refs[0:2], refs[2:]
     mine, other, columns_of, total, weights, places, sem, *sources = refs
     leaves = mine.shape[1] // 128
-    width = sources[0].shape[1] // 128
+    width = 2 * leaves
     core = core[0]
     side = chunks - 1
     base = core * leaves
@@ -527,9 +520,12 @@
             for u in range(8):
                 j = 8 * g + u
                 at = pl.ds(pl.multiple_of(j * 128, 128), 128)
-                x = near_weight * jnp.concatenate([near_ref[0:32, at], far_ref[0:32, at]], axis=0)
+                beside = far_ref[:, at] if chunks == 1 else far_ref[j]
+                x = near_weight * jnp.concatenate([near_ref[j], beside], axis=0)
                 weights[c * width + j] = stack(x)
-                places[c * width + j, 0:3] = near_ref[32:35, at]
+                for k in range(3):
+                    row = width * k + j
+                    places[c * width + j, k : k + 1] = near_ref[width + row // 32, pl.ds(row % 32, 1)]
 
     items = lax.fori_loop(
         0, leaves, lambda i, s: s + jnp.maximum((live[side, base + i] + PAIR - 1) // PAIR, 1), jnp.int32(0)
@@ -586,7 +582,7 @@
 def near_pass(unroll, core, lists, live, targets, sources, begin=()):
     leaves = lists.shape[2] // 2
     chunks = len(sources) // 2
-    held = chunks * (sources[0].shape[1] // 128) + 1
+    held = chunks * 2 * leaves + 1
     side = jax.ShapeDtypeStruct((32, leaves * 128), f32)
     arrays = (targets, *sources, *begin)
     return pl.pallas_call(
@@ -628,9 +624,6 @@
     forward = [(i, i + 1) for i in range(count - 1)]
     backward = [(target, source) for source, target in forward]
     swap = [(0, 1), (1, 0)]
-    packed = pack(points, values)
-    low = lax.ppermute(packed, "leaf", forward)
-    high = lax.ppermute(packed, "leaf", backward)
     across = lax.ppermute(values, "rhs", swap)
 
     def ring(x, stride):
@@ -654,36 +647,37 @@
     after = lax.optimization_barrier
     core = core[None].astype(jnp.int32)
     place = position[None].astype(jnp.int32)
-    up, share, trans, lists, live, codes = up_pass(
-        place, near_list.T, near_count[None], partners.T, basis, values, transfer.transpose(1, 2, 0)
+    up, share, trans, packed, lists, live, codes = up_pass(
+        place, near_list.T, near_count[None], partners.T, points, basis, values, transfer.transpose(1, 2, 0)
     )
+    turned, spot = ring(share[None], 1)
+    turned, share, packed = after((turned, share, packed))
+    low = lax.ppermute(packed, "leaf", forward)
+    high = lax.ppermute(packed, "leaf", backward)
+    level = in_order(turned, share[None], spot)
+    level = jnp.where(jnp.arange(128) < 64, level[0] + level[1], level[2] + level[3])[None]
+    coupling = coupling.transpose(1, 2, 3, 0)
+    first = unbatch(coupling, 0)
+    lists, first, coupling, level, across = after((lists, first, coupling, level, across))
+    turned, spot = ring(level, 4)
     begin = near_pass(12, core, lists, live, points, (packed, across))
-    low, high, coupling, share, begin = after((low, high, coupling, share, begin))
-    turned, spot = ring(share[None], 1)
+    low, high, turned, up, coupling, begin = after((low, high, turned, up, coupling, begin))
+    level = in_order(turned, level, spot)
     low_across = lax.ppermute(low, "rhs", swap)
     high_across = lax.ppermute(high, "rhs", swap)
-    coupling = coupling.transpose(1, 2, 3, 0)
-    first = unbatch(coupling, 0)
-    turned, low_across, high_across, up, coupling, first = after(
-        (turned, low_across, high_across, up, coupling, first)
-    )
-    level = in_order(turned, share[None], spot)
-    level = jnp.where(jnp.arange(128) < 64, level[0] + level[1], level[2] + level[3])[None]
-    turned, spot = ring(level, 4)
-    second = unbatch(coupling, 1)
-    turned, lists, up, second = after((turned, lists, up, second))
-    level = in_order(turned, level, spot)
-    turned, spot = ring(level, 16)
     up_low = lax.ppermute(up, "leaf", forward)
     up_high = lax.ppermute(up, "leaf", backward)
+    second = unbatch(coupling, 1)
+    low_across, high_across, lists, second, level = after((low_across, high_across, lists, second, level))
+    turned, spot = ring(level, 16)
     mine, other = near_pass(
         12, core, lists, live, points, (low, low_across, high, high_across), begin
     )
+    turned, mine, other = after((turned, mine, other))
     given = lax.ppermute(other, "rhs", swap)
-    mine, up_low, up_high = after((mine, up_low, up_high))
+    parent = top_pass(place, partners_top.T, (*turned, level), transfer_top, coupling_top)
+    parent, up_low, up_high = after((parent, up_low, up_high))
     far = couple_pass(codes, up_low, up, up_high, first, second)
-    turned, far = after((turned, far))
-    parent = top_pass(place, partners_top.T, (*turned, level), transfer_top, coupling_top)
     return down_pass(core, parent, far, trans, basis, mine, given)
 
 

time: 121 us -> 120 us (level)
  starting transfers between devices: 38.4 us -> 32.3 us
  Pallas kernels: 74.4 us -> 78 us
  waiting for transfers between devices: 4.48 us -> 6.56 us
    ppermute x9, waiting for transfers between devices: 0.02 us -> 6.53 us  [ring(): turned.append(lax.ppermute(x, 'leaf', to))]
    pallas_call x2, Pallas kernels: 26.7 us -> 33.2 us  [near_pass(): pl.pallas_call(functools.partial(near_body, unroll, chunks), out_shape=(s...]
    ppermute x1, waiting for transfers between devices: 4.44 us -> 0.01 us  [local(): high = lax.ppermute(packed, 'leaf', backward)]
    pallas_call x1 -> x0, Pallas kernels: 3.3 us -> none  [pack(): pl.pallas_call(pack_body, out_shape=jax.ShapeDtypeStruct((columns + 8, wi...]
    ppermute x1, starting transfers between devices: 4.63 us -> 1.73 us  [local(): low = lax.ppermute(packed, 'leaf', forward)]
    ppermute x1, starting transfers between devices: 4.6 us -> 2.29 us  [local(): up_low = lax.ppermute(up, 'leaf', forward)]
    ppermute x9, starting transfers between devices: 26 us -> 24 us  [ring(): turned.append(lax.ppermute(x, 'leaf', to))]
  transfers between devices with their start and end apart: 17 -> 17, of which waited for: 1 -> 4; matrix products, arithmetic and copies ran while one was open for 0% -> 0% of each run, Pallas kernels for 52% -> 49%
where the time goes in v8:
time: 120 us; the launch traced here: 118 us
  Pallas kernels  78 us (65%)
  starting transfers between devices  32.3 us (27%)
  waiting for transfers between devices  6.56 us (5%)
    pallas_call x2, Pallas kernels, near_pass(): pl.pallas_call(functools.partial(near_body, unroll, chunks), out_shape=(s...  33.2 us
    ppermute x9, starting transfers between devices, ring(): turned.append(lax.ppermute(x, 'leaf', to))  24 us
    pallas_call x1, Pallas kernels, up_pass(): pl.pallas_call(up_body, out_shape=(jax.ShapeDtypeStruct((leaves, columns,...  11.8 us
    pallas_call x2, Pallas kernels, unbatch(): pl.pallas_call(functools.partial(unbatch_body, part), out_shape=jax.Shape...  10.2 us
    pallas_call x1, Pallas kernels, couple_pass(): pl.pallas_call(couple_body, out_shape=jax.ShapeDtypeStruct((leaves, colum...  9.52 us
    pallas_call x1, Pallas kernels, down_pass(): pl.pallas_call(down_body, out_shape=jax.ShapeDtypeStruct((columns, leaves...  8.64 us
    ppermute x9, waiting for transfers between devices, ring(): turned.append(lax.ppermute(x, 'leaf', to))  6.53 us
    pallas_call x1, Pallas kernels, top_pass(): pl.pallas_call(top_body, out_shape=jax.ShapeDtypeStruct((columns, 128), f...  4.58 us
  transfers between devices with their start and end apart: 17, of which 4 were waited for; matrix products, arithmetic and copies ran while one was open for 0% of the time, Pallas kernels for 49%

profile of v8, /device:TPU:0, one launch (start us, length us, event | category | flops | bytes accessed | tf_op | source)
XLA Modules:
  0.0 118.2 jit_solution(2870862376735203390)
XLA Ops:
  0.0 11.8 %up_pass.1 = (f32[64,32,128]{2,1,0:T(8,128)}, f32[32,128]{1,0:T(8,128)}, bf16[128,64,128]{2,1,0:T(8,128)(2,1)}, f32[70,32,128]{2,1,0:T(8,128)}, s32[2,28,64]{2,1...) custom-call(s32[1]{0:T(128)} %bitcast.1.place, s32[27,64]{1,0:T(8,128)} %bitcast.45, s32[1,64]{1,0:T(1,128)} %bitcast.51, ...), custom_call_target="tpu_custom_call" | custom-call | flops 400000000 | bytes 8000000 | tf_op jit(solution)/shard_map/up_pass/pallas_call | solution.py:174
  11.8 3.2 %collective-permute-start = (f32[1,32,128]{2,1,0:T(8,128)}, f32[1,32,128]{2,1,0:T(8,128)S(1)}, u32[]{:S(2)}, u32[]{:S(2)}) collective-permute-start(f32[1,32,128]{2,1,0:T(8,128)} %bitcast.46), channel_id=1, source_target_pairs={{0,6},{2,0},{4,2},{6,4},{8,14},{10,8},{12,10},{14,12},{16,22},{18,... | collective-permute-start | bytes 49160 | tf_op jit(solution)/shard_map/ppermute | solution.py:634
  15.0 0.6 collective-permute-start.1
  15.6 1.0 collective-permute-start.2
  16.6 0.1 collective-permute-done
  16.7 3.8 %collective-permute-done.1 = f32[1,32,128]{2,1,0:T(8,128)S(1)} collective-permute-done((f32[1,32,128]{2,1,0:T(8,128)}, f32[1,32,128]{2,1,0:T(8,128)S(1)}, u32[]{:S(2)}, u32[]{:S(2)}) %collective-permute-start.1) | collective-permute-done | bytes 16416 | tf_op jit(solution)/shard_map/ppermute | solution.py:634
  20.5 0.3 collective-permute-done.2
  20.8 1.7 %collective-permute-start.3 = (f32[70,32,128]{2,1,0:T(8,128)}, f32[70,32,128]{2,1,0:T(8,128)S(1)}, u32[]{:S(2)}, u32[]{:S(2)}) collective-permute-start(f32[70,32,128]{2,1,0:T(8,128)} %get-tuple-element.50.refs_0_), channel_id=1, source_target_pairs={{0,2},{2,4},{4,6},{6,8},{8,10},{10,12},{12,14},{14,16},{16,18},{18... | collective-permute-start | bytes 3440648 | tf_op jit(solution)/shard_map/ppermute | solution.py:655
  22.5 1.3 %collective-permute-start.4 = (f32[70,32,128]{2,1,0:T(8,128)}, f32[70,32,128]{2,1,0:T(8,128)}, u32[]{:S(2)}, u32[]{:S(2)}) collective-permute-start(f32[70,32,128]{2,1,0:T(8,128)} %get-tuple-element.50.refs_0_), channel_id=1, source_target_pairs={{2,0},{4,2},{6,4},{8,6},{10,8},{12,10},{14,12},{16,14},{18,16},{20... | collective-permute-start | bytes 3440648 | tf_op jit(solution)/shard_map/ppermute | solution.py:656
  23.8 0.1 collective-permute-start.5
  23.9 0.0 copy-start.6
  23.9 5.1 %unbatch.2.first = bf16[127,128,128]{2,1,0:T(8,128)(2,1)} custom-call(f32[4,64,64,127]{3,2,1,0:T(8,128)} %bitcast.42), custom_call_target="tpu_custom_call" | custom-call | flops 1000 | bytes 1000 | tf_op jit(solution)/shard_map/unbatch/pallas_call | solution.py:245
  29.0 0.0 copy-done.6
  29.1 0.0 collective-permute-done.5.refs_1_
  29.1 7.8 %collective-permute-start.6 = (f32[1,32,128]{2,1,0:T(8,128)S(1)}, f32[1,32,128]{2,1,0:T(8,128)S(1)}, u32[]{:S(2)}, u32[]{:S(2)}) collective-permute-start(f32[1,32,128]{2,1,0:T(8,128)S(1)} %fusion.3), channel_id=1, source_target_pairs={{0,24},{2,26},{4,28},{6,30},{8,0},{10,2},{12,4},{14,6},{16,8},{18,... | collective-permute-start | bytes 49160 | tf_op jit(solution)/shard_map/ppermute | solution.py:634
  36.8 0.8 collective-permute-start.7
  37.6 0.9 collective-permute-start.8
  38.5 19.5 %near_pass.2 = (f32[32,4096]{1,0:T(8,128)}, f32[32,4096]{1,0:T(8,128)}) custom-call(s32[1]{0:T(128)} %bitcast.core, s32[2,28,64]{2,1,0:T(8,128)} %get-tuple-element.71.lists, s32[2,64]{1,0:T(2,128)} %get-tuple-element.60.live, f32[3,8192]{1,0:T(4,128)} %targets.3, f32[70,32,128]{2,1,0:T(8,128)} %get-tuple-element.50.refs_0_, ...), custom_call_target="tpu_custom_call" | custom-call | flops 1000 | bytes 1000 | tf_op jit(solution)/shard_map/near_pass/pallas_call | solution.py:588
  58.0 0.0 collective-permute-done.6
  58.1 0.0 collective-permute-done.7
  58.1 0.0 collective-permute-done.8
  58.1 0.0 collective-permute-done.3.refs_0_
  58.1 0.0 collective-permute-done.4.refs_2_
  58.1 0.1 collective-permute-start.10
  58.2 0.5 collective-permute-start.9
  58.7 2.3 %collective-permute-start.14 = (f32[64,32,128]{2,1,0:T(8,128)}, f32[64,32,128]{2,1,0:T(8,128)}, u32[]{:S(2)}, u32[]{:S(2)}) collective-permute-start(f32[64,32,128]{2,1,0:T(8,128)} %get-tuple-element.81.own), channel_id=1, source_target_pairs={{0,2},{2,4},{4,6},{6,8},{8,10},{10,12},{12,14},{14,16},{16,18},{18... | collective-permute-start | bytes 3145736 | tf_op jit(solution)/shard_map/ppermute | solution.py:668
  61.0 1.3 %collective-permute-start.15 = (f32[64,32,128]{2,1,0:T(8,128)}, f32[64,32,128]{2,1,0:T(8,128)}, u32[]{:S(2)}, u32[]{:S(2)}) collective-permute-start(f32[64,32,128]{2,1,0:T(8,128)} %get-tuple-element.81.own), channel_id=1, source_target_pairs={{2,0},{4,2},{6,4},{8,6},{10,8},{12,10},{14,12},{16,14},{18,16},{20... | collective-permute-start | bytes 3145736 | tf_op jit(solution)/shard_map/ppermute | solution.py:669
  62.3 5.1 %unbatch.3.second = bf16[127,128,128]{2,1,0:T(8,128)(2,1)} custom-call(f32[4,64,64,127]{3,2,1,0:T(8,128)} %bitcast.43), custom_call_target="tpu_custom_call" | custom-call | flops 1000 | bytes 1000 | tf_op jit(solution)/shard_map/unbatch/pallas_call | solution.py:245
  67.5 0.0 copy-start.2
  67.5 0.0 collective-permute-done.10.refs_3_
  67.5 0.0 collective-permute-done.9.refs_1_
  67.5 8.9 %collective-permute-start.11 = (f32[4,32,128]{2,1,0:T(8,128)S(1)}, f32[4,32,128]{2,1,0:T(8,128)S(1)}, u32[]{:S(2)}, u32[]{:S(2)}) collective-permute-start(f32[4,32,128]{2,1,0:T(8,128)S(1)} %pad_maximum_fusion.own), channel_id=1, source_target_pairs={{0,96},{2,98},{4,100},{6,102},{8,104},{10,106},{12,108},{14,110},{... | collective-permute-start | bytes 196616 | tf_op jit(solution)/shard_map/ppermute | solution.py:634
  76.4 0.0 collective-permute-start.12
  76.4 0.9 collective-permute-start.13
  77.4 13.7 %near_pass.3 = (f32[32,4096]{1,0:T(8,128)}, f32[32,4096]{1,0:T(8,128)}) custom-call(s32[1]{0:T(128)} %bitcast.core, s32[2,28,64]{2,1,0:T(8,128)} %get-tuple-element.71.lists, s32[2,64]{1,0:T(2,128)} %get-tuple-element.60.live, f32[3,8192]{1,0:T(4,128)} %targets.3, f32[70,32,128]{2,1,0:T(8,128)} %copy-done, f32[70,32,128]{2,1,0:T(8,128)} %collective-permute-done.9.refs_1_, ...), custom_call_target="tpu_custom_call" | custom-call | flops 1000 | bytes 1000 | tf_op jit(solution)/shard_map/near_pass/pallas_call | solution.py:588
  91.1 0.0 collective-permute-done.11.far_three
  91.1 0.0 copy-start.3
  91.1 2.3 %collective-permute-done.12.far_two = f32[4,32,128]{2,1,0:T(8,128)S(1)} collective-permute-done((f32[4,32,128]{2,1,0:T(8,128)S(1)}, f32[4,32,128]{2,1,0:T(8,128)S(1)}, u32[]{:S(2)}, u32[]{:S(2)}) %collective-permute-start.12) | collective-permute-done | bytes 65568 | tf_op jit(solution)/shard_map/ppermute | solution.py:634
  93.4 0.0 collective-permute-done.13.far_one
  93.4 1.0 collective-permute-start.16
  94.5 0.0 copy-done.3
  94.5 4.6 %top_pass.1.parent = f32[32,128]{1,0:T(8,128)} custom-call(s32[1]{0:T(128)} %bitcast.1.place, s32[4,60]{1,0:T(4,128)} %bitcast.50, f32[4,32,128]{2,1,0:T(8,128)} %copy-done.3, f32[4,32,128]{2,1,0:T(8,128)} %copy-done.4, f32[4,32,128]{2,1,0:T(8,128)} %copy-done.5, f32[4,32,128]{2,1,0:T(8,128)} %copy-done.2, f32[62,64,64]{2,1,0:T(8,128)} %moves.1, ...), custom_call_target="tpu_custom_call" | custom-call | flops 50000000 | bytes 2000000 | tf_op jit(solution)/shard_map/top_pass/pallas_call | solution.py:318
  99.1 0.0 collective-permute-done.14.low
  99.1 0.0 collective-permute-done.15.high
  99.1 9.5 %couple_pass.1.far_hbm = f32[64,32,128]{2,1,0:T(8,128)} custom-call(s32[4,127]{1,0:T(4,128)} %get-tuple-element.83.codes, f32[64,32,128]{2,1,0:T(8,128)} %collective-permute-done.14.low, f32[64,32,128]{2,1,0:T(8,128)} %get-tuple-element.81.own, f32[64,32,128]{2,1,0:T(8,128)} %collective-permute-done.15.high, bf16[127,128,128]{2,1,0:T(8,128)(2,1)} %unbatch.2.first, ...), custom_call_target="tpu_custom_call" | custom-call | flops 400000000 | bytes 12000000 | tf_op jit(solution)/shard_map/couple_pass/pallas_call | solution.py:383
  108.6 0.0 collective-permute-done.16.given
  108.6 0.8 copy-done.1
  109.4 8.6 %down_pass.1 = f32[32,8192]{1,0:T(8,128)} custom-call(s32[1]{0:T(128)} %bitcast.core, f32[32,128]{1,0:T(8,128)} %top_pass.1.parent, f32[64,32,128]{2,1,0:T(8,128)} %couple_pass.1.far_hbm, bf16[128,64,128]{2,1,0:T(8,128)(2,1)} %get-tuple-element.88.trans_hbm, f32[64,64,128]{2,1,0:T(8,128)} %basis_hbm.3, f32[32,4096]{1,0:T(8,128)} %get-tuple-element.89.mine, ...), custom_call_target="tpu_custom_call" | custom-call | flops 200000000 | bytes 7000000 | tf_op jit(solution)/shard_map/down_pass/pallas_call | solution.py:457
  (12 shorter events, 0.1 us)
Async XLA Ops:
  11.8 4.8 %collective-permute-start = (f32[1,32,128]{2,1,0:T(8,128)}, f32[1,32,128]{2,1,0:T(8,128)S(1)}, u32[]{:S(2)}, u32[]{:S(2)}) collective-permute-start(f32[1,32,128]{2,1,0:T(8,128)} %bitcast.46), channel_id=1, source_target_pairs={{0,6},{2,0},{4,2},{6,4},{8,14},{10,8},{12,10},{14,12},{16,22},{18,... | collective-permute-start | bytes 49160 | tf_op jit(solution)/shard_map/ppermute | solution.py:634
  15.0 5.5 %collective-permute-start.1 = (f32[1,32,128]{2,1,0:T(8,128)}, f32[1,32,128]{2,1,0:T(8,128)S(1)}, u32[]{:S(2)}, u32[]{:S(2)}) collective-permute-start(f32[1,32,128]{2,1,0:T(8,128)} %bitcast.47), channel_id=1, source_target_pairs={{0,4},{2,6},{4,0},{6,2},{8,12},{10,14},{12,8},{14,10},{16,20},{18,... | collective-permute-start | bytes 49160 | tf_op jit(solution)/shard_map/ppermute | solution.py:634
  15.6 5.2 %collective-permute-start.2 = (f32[1,32,128]{2,1,0:T(8,128)}, f32[1,32,128]{2,1,0:T(8,128)S(1)}, u32[]{:S(2)}, u32[]{:S(2)}) collective-permute-start(f32[1,32,128]{2,1,0:T(8,128)} %bitcast.48), channel_id=1, source_target_pairs={{0,2},{2,4},{4,6},{6,0},{8,10},{10,12},{12,14},{14,8},{16,18},{18,... | collective-permute-start | bytes 49160 | tf_op jit(solution)/shard_map/ppermute | solution.py:634
  20.8 37.3 %collective-permute-start.3 = (f32[70,32,128]{2,1,0:T(8,128)}, f32[70,32,128]{2,1,0:T(8,128)S(1)}, u32[]{:S(2)}, u32[]{:S(2)}) collective-permute-start(f32[70,32,128]{2,1,0:T(8,128)} %get-tuple-element.50.refs_0_), channel_id=1, source_target_pairs={{0,2},{2,4},{4,6},{6,8},{8,10},{10,12},{12,14},{14,16},{16,18},{18... | collective-permute-start | bytes 3440648 | tf_op jit(solution)/shard_map/ppermute | solution.py:655
  22.5 35.6 %collective-permute-start.4 = (f32[70,32,128]{2,1,0:T(8,128)}, f32[70,32,128]{2,1,0:T(8,128)}, u32[]{:S(2)}, u32[]{:S(2)}) collective-permute-start(f32[70,32,128]{2,1,0:T(8,128)} %get-tuple-element.50.refs_0_), channel_id=1, source_target_pairs={{2,0},{4,2},{6,4},{8,6},{10,8},{12,10},{14,12},{16,14},{18,16},{20... | collective-permute-start | bytes 3440648 | tf_op jit(solution)/shard_map/ppermute | solution.py:656
  23.8 5.2 %collective-permute-start.5 = (f32[32,8192]{1,0:T(8,128)}, f32[32,8192]{1,0:T(8,128)}, u32[]{:S(2)}, u32[]{:S(2)}) collective-permute-start(f32[32,8192]{1,0:T(8,128)} %values_hbm.1), channel_id=1, source_target_pairs={{0,1},{1,0},{2,3},{3,2},{4,5},{5,4},{6,7},{7,6},{8,9},{9,8},{10,11... | collective-permute-start | bytes 3145736 | tf_op jit(solution)/shard_map/ppermute | solution.py:627
  23.9 5.1 %copy-start.6 = (f32[32,128]{1,0:T(8,128)S(1)}, f32[32,128]{1,0:T(8,128)}, u32[]{:S(2)}) copy-start(f32[32,128]{1,0:T(8,128)} %get-tuple-element.55) | copy-start | bytes 49156
  29.1 29.0 %collective-permute-start.6 = (f32[1,32,128]{2,1,0:T(8,128)S(1)}, f32[1,32,128]{2,1,0:T(8,128)S(1)}, u32[]{:S(2)}, u32[]{:S(2)}) collective-permute-start(f32[1,32,128]{2,1,0:T(8,128)S(1)} %fusion.3), channel_id=1, source_target_pairs={{0,24},{2,26},{4,28},{6,30},{8,0},{10,2},{12,4},{14,6},{16,8},{18,... | collective-permute-start | bytes 49160 | tf_op jit(solution)/shard_map/ppermute | solution.py:634
  36.8 21.2 %collective-permute-start.7 = (f32[1,32,128]{2,1,0:T(8,128)S(1)}, f32[1,32,128]{2,1,0:T(8,128)S(1)}, u32[]{:S(2)}, u32[]{:S(2)}) collective-permute-start(f32[1,32,128]{2,1,0:T(8,128)S(1)} %fusion.3), channel_id=1, source_target_pairs={{0,16},{2,18},{4,20},{6,22},{8,24},{10,26},{12,28},{14,30},{16,0},... | collective-permute-start | bytes 49160 | tf_op jit(solution)/shard_map/ppermute | solution.py:634
  37.6 20.4 %collective-permute-start.8 = (f32[1,32,128]{2,1,0:T(8,128)S(1)}, f32[1,32,128]{2,1,0:T(8,128)S(1)}, u32[]{:S(2)}, u32[]{:S(2)}) collective-permute-start(f32[1,32,128]{2,1,0:T(8,128)S(1)} %fusion.3), channel_id=1, source_target_pairs={{0,8},{2,10},{4,12},{6,14},{8,16},{10,18},{12,20},{14,22},{16,24},... | collective-permute-start | bytes 49160 | tf_op jit(solution)/shard_map/ppermute | solution.py:634
  58.1 9.4 %copy-start = (f32[70,32,128]{2,1,0:T(8,128)}, f32[70,32,128]{2,1,0:T(8,128)S(1)}, u32[]{:S(2)}) copy-start(f32[70,32,128]{2,1,0:T(8,128)S(1)} %collective-permute-done.3.refs_0_) | copy-start | bytes 3440644
  58.1 9.4 %collective-permute-start.10 = (f32[70,32,128]{2,1,0:T(8,128)}, f32[70,32,128]{2,1,0:T(8,128)}, u32[]{:S(2)}, u32[]{:S(2)}) collective-permute-start(f32[70,32,128]{2,1,0:T(8,128)} %collective-permute-done.4.refs_2_), channel_id=1, source_target_pairs={{0,1},{1,0},{2,3},{3,2},{4,5},{5,4},{6,7},{7,6},{8,9},{9,8},{10,11... | collective-permute-start | bytes 3440648 | tf_op jit(solution)/shard_map/ppermute | solution.py:667
  58.2 9.3 %collective-permute-start.9 = (f32[70,32,128]{2,1,0:T(8,128)S(1)}, f32[70,32,128]{2,1,0:T(8,128)}, u32[]{:S(2)}, u32[]{:S(2)}) collective-permute-start(f32[70,32,128]{2,1,0:T(8,128)S(1)} %collective-permute-done.3.refs_0_), channel_id=1, source_target_pairs={{0,1},{1,0},{2,3},{3,2},{4,5},{5,4},{6,7},{7,6},{8,9},{9,8},{10,11... | collective-permute-start | bytes 3440648 | tf_op jit(solution)/shard_map/ppermute | solution.py:666
  58.7 40.4 %collective-permute-start.14 = (f32[64,32,128]{2,1,0:T(8,128)}, f32[64,32,128]{2,1,0:T(8,128)}, u32[]{:S(2)}, u32[]{:S(2)}) collective-permute-start(f32[64,32,128]{2,1,0:T(8,128)} %get-tuple-element.81.own), channel_id=1, source_target_pairs={{0,2},{2,4},{4,6},{6,8},{8,10},{10,12},{12,14},{14,16},{16,18},{18... | collective-permute-start | bytes 3145736 | tf_op jit(solution)/shard_map/ppermute | solution.py:668
  61.0 38.1 %collective-permute-start.15 = (f32[64,32,128]{2,1,0:T(8,128)}, f32[64,32,128]{2,1,0:T(8,128)}, u32[]{:S(2)}, u32[]{:S(2)}) collective-permute-start(f32[64,32,128]{2,1,0:T(8,128)} %get-tuple-element.81.own), channel_id=1, source_target_pairs={{2,0},{4,2},{6,4},{8,6},{10,8},{12,10},{14,12},{16,14},{18,16},{20... | collective-permute-start | bytes 3145736 | tf_op jit(solution)/shard_map/ppermute | solution.py:669
  67.5 23.6 %copy-start.2 = (f32[4,32,128]{2,1,0:T(8,128)}, f32[4,32,128]{2,1,0:T(8,128)S(1)}, u32[]{:S(2)}) copy-start(f32[4,32,128]{2,1,0:T(8,128)S(1)} %pad_maximum_fusion.own) | copy-start | bytes 196612
  67.5 23.6 %collective-permute-start.11 = (f32[4,32,128]{2,1,0:T(8,128)S(1)}, f32[4,32,128]{2,1,0:T(8,128)S(1)}, u32[]{:S(2)}, u32[]{:S(2)}) collective-permute-start(f32[4,32,128]{2,1,0:T(8,128)S(1)} %pad_maximum_fusion.own), channel_id=1, source_target_pairs={{0,96},{2,98},{4,100},{6,102},{8,104},{10,106},{12,108},{14,110},{... | collective-permute-start | bytes 196616 | tf_op jit(solution)/shard_map/ppermute | solution.py:634
  76.4 17.0 %collective-permute-start.12 = (f32[4,32,128]{2,1,0:T(8,128)S(1)}, f32[4,32,128]{2,1,0:T(8,128)S(1)}, u32[]{:S(2)}, u32[]{:S(2)}) collective-permute-start(f32[4,32,128]{2,1,0:T(8,128)S(1)} %pad_maximum_fusion.own), channel_id=1, source_target_pairs={{0,64},{2,66},{4,68},{6,70},{8,72},{10,74},{12,76},{14,78},{16,80}... | collective-permute-start | bytes 196616 | tf_op jit(solution)/shard_map/ppermute | solution.py:634
  76.4 17.0 %collective-permute-start.13 = (f32[4,32,128]{2,1,0:T(8,128)S(1)}, f32[4,32,128]{2,1,0:T(8,128)S(1)}, u32[]{:S(2)}, u32[]{:S(2)}) collective-permute-start(f32[4,32,128]{2,1,0:T(8,128)S(1)} %pad_maximum_fusion.own), channel_id=1, source_target_pairs={{0,32},{2,34},{4,36},{6,38},{8,40},{10,42},{12,44},{14,46},{16,48}... | collective-permute-start | bytes 196616 | tf_op jit(solution)/shard_map/ppermute | solution.py:634
  91.1 3.4 %copy-start.3 = (f32[4,32,128]{2,1,0:T(8,128)}, f32[4,32,128]{2,1,0:T(8,128)S(1)}, u32[]{:S(2)}) copy-start(f32[4,32,128]{2,1,0:T(8,128)S(1)} %collective-permute-done.11.far_three) | copy-start | bytes 196612
  93.4 1.0 copy-start.4
  93.4 1.0 copy-start.5
  93.4 15.2 %collective-permute-start.16 = (f32[32,4096]{1,0:T(8,128)}, f32[32,4096]{1,0:T(8,128)S(1)}, u32[]{:S(2)}, u32[]{:S(2)}) collective-permute-start(f32[32,4096]{1,0:T(8,128)} %get-tuple-element.90), channel_id=1, source_target_pairs={{0,1},{1,0},{2,3},{3,2},{4,5},{5,4},{6,7},{7,6},{8,9},{9,8},{10,11... | collective-permute-start | bytes 1572872 | tf_op jit(solution)/shard_map/ppermute | solution.py:677
  108.6 0.8 copy-start.1

commit v9 on v8

--- a/solution.py
+++ b/solution.py
@@ -65,8 +65,8 @@
 
 
 def up_body(
-    place, near_list, near_count, partners, points, basis_hbm, values_hbm, moves_hbm,
-    up, share, trans_hbm, packed_hbm, lists, live, codes, rows, basis, values, moves, trans, packed, sem,
+    place, near_list, near_count, partners, points, basis_hbm, values_hbm, across_hbm, moves_hbm,
+    up, share, trans_hbm, packed_hbm, lists, live, codes, rows, basis, values, across, moves, trans, packed, sem,
 ):
     leaves = basis.shape[0]
     columns = values.shape[0]
@@ -77,6 +77,7 @@
         reads.append(pltpu.make_async_copy(moves_hbm.at[at], moves.at[at], sem.at[i]))
     reads.append(pltpu.make_async_copy(values_hbm, values, sem.at[4]))
     reads.append(pltpu.make_async_copy(basis_hbm, basis, sem.at[5]))
+    reads.append(pltpu.make_async_copy(across_hbm, across, sem.at[8]))
     for read in reads:
         read.start()
     plan(place[0], near_list, near_count, partners, lists, live, codes)
@@ -107,16 +108,19 @@
 
     for read in reads[4:]:
         read.wait()
+    block = leaves // 2
     for c in range(3):
         for j in range(leaves):
-            row = leaves * c + j
-            packed[leaves + row // columns, row % columns : row % columns + 1] = points[
+            packed[j // block, 2 * block + c, j % block : j % block + 1] = points[
                 c : c + 1, 128 * j : 128 * j + 128
             ]
-
-    @pl.loop(0, leaves, unroll=8)
-    def _(j):
-        packed[j] = values[:, pl.ds(pl.multiple_of(j * 128, 128), 128)]
+    for side in range(2):
+
+        @pl.loop(0, block, unroll=8)
+        def _(j, side=side):
+            at = pl.ds(pl.multiple_of((side * block + j) * 128, 128), 128)
+            packed[side, j] = values[:, at]
+            packed[side, block + j] = across[:, at]
 
     send = pltpu.make_async_copy(packed, packed_hbm, sem.at[7])
     send.start()
@@ -167,7 +171,7 @@
     send.wait()
 
 
-def up_pass(place, near_list, near_count, partners, points, basis, values, moves):
+def up_pass(place, near_list, near_count, partners, points, basis, values, across, moves):
     leaves = basis.shape[0]
     columns = values.shape[0]
     nodes = moves.shape[2]
@@ -177,26 +181,27 @@
             jax.ShapeDtypeStruct((leaves, columns, 128), f32),
             jax.ShapeDtypeStruct((columns, 128), f32),
             jax.ShapeDtypeStruct((nodes + 1, 64, 128), bf16),
-            jax.ShapeDtypeStruct((leaves + 3 * leaves // columns, columns, 128), f32),
+            jax.ShapeDtypeStruct((2, leaves + 3, columns, 128), f32),
             jax.ShapeDtypeStruct((2, SLOTS, leaves), jnp.int32),
             jax.ShapeDtypeStruct((2, leaves), jnp.int32),
             jax.ShapeDtypeStruct(partners.shape, jnp.int32),
         ),
-        in_specs=[SM, VM, VM, VM, VM, HBM, HBM, HBM],
+        in_specs=[SM, VM, VM, VM, VM, HBM, HBM, HBM, HBM],
         out_specs=(VM, VM, HBM, HBM, VM, VM, VM),
         scratch_shapes=[
             pltpu.VMEM((64 * PITCH, 128), f32),
             pltpu.VMEM(basis.shape, f32),
             pltpu.VMEM(values.shape, f32),
+            pltpu.VMEM(values.shape, f32),
             pltpu.VMEM(moves.shape, f32),
             pltpu.VMEM((nodes + 1, 64, 128), bf16),
-            pltpu.VMEM((leaves + 3 * leaves // columns, columns, 128), f32),
-            pltpu.SemaphoreType.DMA((8,)),
+            pltpu.VMEM((2, leaves + 3, columns, 128), f32),
+            pltpu.SemaphoreType.DMA((9,)),
         ],
         compiler_params=pltpu.CompilerParams(vmem_limit_bytes=VMEM_BYTES),
         cost_estimate=pl.CostEstimate(flops=400_000_000, bytes_accessed=8_000_000, transcendentals=0),
         name="up_pass",
-    )(place, near_list, near_count, partners, points, basis, values, moves)
+    )(place, near_list, near_count, partners, points, basis, values, across, moves)
 
 
 CHUNK = 32
@@ -478,7 +483,7 @@
 PAIR = 2
 
 def near_body(unroll, chunks, core, lists, live, targets, *refs):
-    origins, refs = refs[: 2 * chunks], refs[2 * chunks :]
+    origins, refs = refs[:chunks], refs[chunks:]
     begin = None
     if chunks == 2:
         begin, refs = refs[0:2], refs[2:]
@@ -487,7 +492,7 @@
     width = 2 * leaves
     core = core[0]
     side = chunks - 1
-    base = core * leaves
+    mark = core * leaves
     reads = []
     for i, (origin, source) in enumerate(zip(origins, sources)):
         reads.append(pltpu.make_async_copy(origin, source, sem.at[i]))
@@ -510,31 +515,30 @@
 
     for read in reads:
         read.wait()
-    for c in range(chunks):
-        near_ref, far_ref = sources[2 * c], sources[2 * c + 1]
-        lower = 0 if chunks == 1 or c == 1 else core * (leaves // 8)
-        upper = width // 8 if chunks == 1 or c == 0 else (core + 1) * (leaves // 8)
-
-        @pl.loop(lower, upper)
-        def _(g, c=c, near_ref=near_ref, far_ref=far_ref):
+
+    def load(block, base, turn):
+        @pl.loop(0, leaves // 8)
+        def _(g):
             for u in range(8):
                 j = 8 * g + u
-                at = pl.ds(pl.multiple_of(j * 128, 128), 128)
-                beside = far_ref[:, at] if chunks == 1 else far_ref[j]
-                x = near_weight * jnp.concatenate([near_ref[j], beside], axis=0)
-                weights[c * width + j] = stack(x)
-                for k in range(3):
-                    row = width * k + j
-                    places[c * width + j, k : k + 1] = near_ref[width + row // 32, pl.ds(row % 32, 1)]
-
+                x = [block[j], block[leaves + j]]
+                weights[base + j] = stack(near_weight * jnp.concatenate(x[::-1] if turn else x, axis=0))
+                for c in range(3):
+                    places[base + j, c : c + 1] = block[2 * leaves + c, pl.ds(j, 1)]
+
+    base = width * core if chunks == 2 else 0
+    load(sources[0].at[0], base, False)
+    load(sources[0].at[1], base + leaves, False)
+    if chunks == 2:
+        load(sources[1], width - leaves * core, True)
     items = lax.fori_loop(
-        0, leaves, lambda i, s: s + jnp.maximum((live[side, base + i] + PAIR - 1) // PAIR, 1), jnp.int32(0)
+        0, leaves, lambda i, s: s + jnp.maximum((live[side, mark + i] + PAIR - 1) // PAIR, 1), jnp.int32(0)
     )
 
     def block(leaf, slot):
         kernels, parts = [], []
         for u in range(PAIR):
-            j = lists[side, slot + u, base + leaf]
+            j = lists[side, slot + u, mark + leaf]
             s = places[j]
             d = columns_of[leaf, 0] - s[0:1]
             squared = d * d + smoothing
@@ -558,7 +562,7 @@
         for u in range(unroll):
             place = jnp.where(b * unroll + u < items, leaf, leaves)
             made.append((place, block(leaf, slot)))
-            done = slot + PAIR >= live[side, base + leaf]
+            done = slot + PAIR >= live[side, mark + leaf]
             leaf = jnp.where(done, jnp.minimum(leaf + 1, leaves - 1), leaf)
             slot = jnp.where(done, 0, slot + PAIR)
         for place, x in made:
@@ -581,7 +585,7 @@
 
 def near_pass(unroll, core, lists, live, targets, sources, begin=()):
     leaves = lists.shape[2] // 2
-    chunks = len(sources) // 2
+    chunks = len(sources)
     held = chunks * 2 * leaves + 1
     side = jax.ShapeDtypeStruct((32, leaves * 128), f32)
     arrays = (targets, *sources, *begin)
@@ -647,32 +651,39 @@
     after = lax.optimization_barrier
     core = core[None].astype(jnp.int32)
     place = position[None].astype(jnp.int32)
+    coupling = coupling.transpose(1, 2, 3, 0)
+    first = unbatch(coupling, 0)
+    across, first, coupling = after((across, first, coupling))
     up, share, trans, packed, lists, live, codes = up_pass(
-        place, near_list.T, near_count[None], partners.T, points, basis, values, transfer.transpose(1, 2, 0)
+        place,
+        near_list.T,
+        near_count[None],
+        partners.T,
+        points,
+        basis,
+        values,
+        across,
+        transfer.transpose(1, 2, 0),
     )
     turned, spot = ring(share[None], 1)
     turned, share, packed = after((turned, share, packed))
-    low = lax.ppermute(packed, "leaf", forward)
-    high = lax.ppermute(packed, "leaf", backward)
+    outward = [(2 * i, 2 * i + 2) for i in range(count - 1)]
+    outward += [(2 * i + 3, 2 * i + 1) for i in range(count - 1)]
+    beside = lax.ppermute(packed, ("leaf", "rhs"), outward)
     level = in_order(turned, share[None], spot)
     level = jnp.where(jnp.arange(128) < 64, level[0] + level[1], level[2] + level[3])[None]
-    coupling = coupling.transpose(1, 2, 3, 0)
-    first = unbatch(coupling, 0)
-    lists, first, coupling, level, across = after((lists, first, coupling, level, across))
     turned, spot = ring(level, 4)
-    begin = near_pass(12, core, lists, live, points, (packed, across))
-    low, high, turned, up, coupling, begin = after((low, high, turned, up, coupling, begin))
+    begin = near_pass(12, core, lists, live, points, (packed,))
+    coupling, turned, begin = after((coupling, turned, begin))
     level = in_order(turned, level, spot)
-    low_across = lax.ppermute(low, "rhs", swap)
-    high_across = lax.ppermute(high, "rhs", swap)
+    second = unbatch(coupling, 1)
+    beside, up, level, lists, second = after((beside, up, level, lists, second))
+    passed = lax.dynamic_index_in_dim(beside, 1 - core[0], 0, keepdims=False)
+    passed = lax.ppermute(passed, "rhs", swap)
+    turned, spot = ring(level, 16)
     up_low = lax.ppermute(up, "leaf", forward)
     up_high = lax.ppermute(up, "leaf", backward)
-    second = unbatch(coupling, 1)
-    low_across, high_across, lists, second, level = after((low_across, high_across, lists, second, level))
-    turned, spot = ring(level, 16)
-    mine, other = near_pass(
-        12, core, lists, live, points, (low, low_across, high, high_across), begin
-    )
+    mine, other = near_pass(12, core, lists, live, points, (beside, passed), begin)
     turned, mine, other = after((turned, mine, other))
     given = lax.ppermute(other, "rhs", swap)
     parent = top_pass(place, partners_top.T, (*turned, level), transfer_top, coupling_top)

time: 120 us -> 126 us (1.050)
  waiting for transfers between devices: 6.56 us -> 16.2 us
  Pallas kernels: 78 us -> 69 us
  local copies, waits for them, and re-layouts: 0.8 us -> 3.69 us
  starting transfers between devices: 32.3 us -> 34.5 us
    pallas_call x2, Pallas kernels: 33.2 us -> 24 us  [near_pass(): pl.pallas_call(functools.partial(near_body, unroll, chunks), out_shape=(s...]
    ppermute x9, waiting for transfers between devices: 6.53 us -> 15.5 us  [ring(): turned.append(lax.ppermute(x, 'leaf', to))]
    ppermute x4 -> x2, starting transfers between devices: 3.6 us -> 9.53 us  [the longest x1 6.55 us: local(): passed = lax.ppermute(passed, 'rhs', swap)]
    ppermute x9, starting transfers between devices: 24 us -> 21.3 us  [ring(): turned.append(lax.ppermute(x, 'leaf', to))]
    unnamed x14, local copies, waits for them, and re-layouts: 0.8 us -> 2.37 us
    squeeze x0 -> x1, local copies, waits for them, and re-layouts: none -> 1.31 us  [local(): passed = lax.dynamic_index_in_dim(beside, 1 - core[0], 0, keepdims=False)]
  transfers between devices with their start and end apart: 17 -> 15, of which waited for: 4 -> 6; matrix products, arithmetic and copies ran while one was open for 0% -> 1% of each run, Pallas kernels for 49% -> 39%
where the time goes in v9:
time: 126 us; the launch traced here: 125 us
  Pallas kernels  69 us (55%)
  starting transfers between devices  34.5 us (27%)
  waiting for transfers between devices  16.2 us (13%)
  local copies, waits for them, and re-layouts  3.69 us (3%)
    pallas_call x2, Pallas kernels, near_pass(): pl.pallas_call(functools.partial(near_body, unroll, chunks), out_shape=(s...  24 us
    ppermute x9, starting transfers between devices, ring(): turned.append(lax.ppermute(x, 'leaf', to))  21.3 us
    ppermute x9, waiting for transfers between devices, ring(): turned.append(lax.ppermute(x, 'leaf', to))  15.5 us
    pallas_call x1, Pallas kernels, up_pass(): pl.pallas_call(up_body, out_shape=(jax.ShapeDtypeStruct((leaves, columns,...  12 us
    pallas_call x2, Pallas kernels, unbatch(): pl.pallas_call(functools.partial(unbatch_body, part), out_shape=jax.Shape...  10.2 us
    pallas_call x1, Pallas kernels, couple_pass(): pl.pallas_call(couple_body, out_shape=jax.ShapeDtypeStruct((leaves, colum...  9.54 us
    pallas_call x1, Pallas kernels, down_pass(): pl.pallas_call(down_body, out_shape=jax.ShapeDtypeStruct((columns, leaves...  8.64 us
    ppermute x1, starting transfers between devices, local(): passed = lax.ppermute(passed, 'rhs', swap)  6.55 us
  transfers between devices with their start and end apart: 15, of which 6 were waited for; matrix products, arithmetic and copies ran while one was open for 1% of the time, Pallas kernels for 39%

profile of v9, /device:TPU:0, one launch (start us, length us, event | category | flops | bytes accessed | tf_op | source)
XLA Modules:
  0.0 124.5 jit_solution(7543248261861099166)
XLA Ops:
  0.0 0.0 collective-permute-start
  0.0 5.0 %unbatch.2.first = bf16[127,128,128]{2,1,0:T(8,128)(2,1)} custom-call(f32[4,64,64,127]{3,2,1,0:T(8,128)} %bitcast.44), custom_call_target="tpu_custom_call" | custom-call | flops 1000 | bytes 1000 | tf_op jit(solution)/shard_map/unbatch/pallas_call | solution.py:250
  5.1 0.0 collective-permute-done.across_hbm
  5.1 0.0 copy-start.1
  5.1 1.0 copy-done.1
  6.0 12.0 %up_pass.1 = (f32[64,32,128]{2,1,0:T(8,128)}, f32[32,128]{1,0:T(8,128)}, bf16[128,64,128]{2,1,0:T(8,128)(2,1)}, f32[2,67,32,128]{3,2,1,0:T(8,128)}, s32[2,28,64]...) custom-call(s32[1]{0:T(128)} %bitcast.1.place, s32[27,64]{1,0:T(8,128)} %bitcast.47, s32[1,64]{1,0:T(1,128)} %bitcast.53, ...), custom_call_target="tpu_custom_call" | custom-call | flops 400000000 | bytes 8000000 | tf_op jit(solution)/shard_map/up_pass/pallas_call | solution.py:178
  18.1 3.2 %collective-permute-start.1 = (f32[1,32,128]{2,1,0:T(8,128)}, f32[1,32,128]{2,1,0:T(8,128)S(1)}, u32[]{:S(2)}, u32[]{:S(2)}) collective-permute-start(f32[1,32,128]{2,1,0:T(8,128)} %bitcast.48), channel_id=1, source_target_pairs={{0,6},{2,0},{4,2},{6,4},{8,14},{10,8},{12,10},{14,12},{16,22},{18,... | collective-permute-start | bytes 49160 | tf_op jit(solution)/shard_map/ppermute | solution.py:638
  21.2 0.6 collective-permute-start.2
  21.9 1.0 collective-permute-start.3
  22.8 0.1 collective-permute-done.1
  22.9 3.8 %collective-permute-done.2 = f32[1,32,128]{2,1,0:T(8,128)S(1)} collective-permute-done((f32[1,32,128]{2,1,0:T(8,128)}, f32[1,32,128]{2,1,0:T(8,128)S(1)}, u32[]{:S(2)}, u32[]{:S(2)}) %collective-permute-start.2) | collective-permute-done | bytes 16416 | tf_op jit(solution)/shard_map/ppermute | solution.py:638
  26.7 0.3 collective-permute-done.3
  27.0 3.0 %collective-permute-start.4 = (f32[2,67,32,128]{3,2,1,0:T(8,128)}, f32[2,67,32,128]{3,2,1,0:T(8,128)}, u32[]{:S(2)}, u32[]{:S(2)}) collective-permute-start(f32[2,67,32,128]{3,2,1,0:T(8,128)} %get-tuple-element.46.refs_0_), channel_id=1, source_target_pairs={{0,2},{2,4},{4,6},{6,8},{8,10},{10,12},{12,14},{14,16},{16,18},{18... | collective-permute-start | bytes 6586376 | tf_op jit(solution)/shard_map/ppermute | solution.py:672
  30.0 0.7 fusion.3
  30.7 1.8 %collective-permute-start.5 = (f32[1,32,128]{2,1,0:T(8,128)S(1)}, f32[1,32,128]{2,1,0:T(8,128)S(1)}, u32[]{:S(2)}, u32[]{:S(2)}) collective-permute-start(f32[1,32,128]{2,1,0:T(8,128)S(1)} %fusion.3), channel_id=1, source_target_pairs={{0,24},{2,26},{4,28},{6,30},{8,0},{10,2},{12,4},{14,6},{16,8},{18,... | collective-permute-start | bytes 49160 | tf_op jit(solution)/shard_map/ppermute | solution.py:638
  32.5 0.8 collective-permute-start.6
  33.3 0.9 collective-permute-start.7
  34.2 13.4 %near_pass.2 = (f32[32,4096]{1,0:T(8,128)}, f32[32,4096]{1,0:T(8,128)}) custom-call(s32[1]{0:T(128)} %bitcast.core, s32[2,28,64]{2,1,0:T(8,128)} %get-tuple-element.62.lists, s32[2,64]{1,0:T(2,128)} %get-tuple-element.54.live, f32[3,8192]{1,0:T(4,128)} %targets.3, f32[2,67,32,128]{3,2,1,0:T(8,128)} %get-tuple-element.46.refs_0_), custom_call_target="tpu_custom_call" | custom-call | flops 1000 | bytes 1000 | tf_op jit(solution)/shard_map/near_pass/pallas_call | solution.py:592
  47.6 0.0 collective-permute-done.5
  47.6 0.0 collective-permute-done.6
  47.6 0.0 collective-permute-done.7
  47.7 5.2 %unbatch.3.second = bf16[127,128,128]{2,1,0:T(8,128)(2,1)} custom-call(f32[4,64,64,127]{3,2,1,0:T(8,128)} %bitcast.45), custom_call_target="tpu_custom_call" | custom-call | flops 1000 | bytes 1000 | tf_op jit(solution)/shard_map/unbatch/pallas_call | solution.py:250
  52.9 0.0 copy-start.3
  52.9 0.7 collective-permute-done.4.refs_0_
  53.6 1.3 %dynamic-slice_bitcast_fusion = f32[67,32,128]{2,1,0:T(8,128)S(1)} fusion(f32[2,67,32,128]{3,2,1,0:T(8,128)} %collective-permute-done.4.refs_0_, s32[]{:T(128)S(6)} %select_n.175), kind=kLoop, calls=%fused_computation | loop fusion | bytes 2195460 | tf_op jit(solution)/shard_map/jit(dynamic_index_in_dim)/squeeze | solution.py:681
  54.9 6.5 %collective-permute-start.11 = (f32[67,32,128]{2,1,0:T(8,128)S(1)}, f32[67,32,128]{2,1,0:T(8,128)S(1)}, u32[]{:S(2)}, u32[]{:S(2)}) collective-permute-start(f32[67,32,128]{2,1,0:T(8,128)S(1)} %dynamic-slice_bitcast_fusion), channel_id=1, source_target_pairs={{0,1},{1,0},{2,3},{3,2},{4,5},{5,4},{6,7},{7,6},{8,9},{9,8},{10,11... | collective-permute-start | bytes 3293192 | tf_op jit(solution)/shard_map/ppermute | solution.py:682
  61.4 2.3 %collective-permute-start.12 = (f32[64,32,128]{2,1,0:T(8,128)}, f32[64,32,128]{2,1,0:T(8,128)}, u32[]{:S(2)}, u32[]{:S(2)}) collective-permute-start(f32[64,32,128]{2,1,0:T(8,128)} %get-tuple-element.71.own), channel_id=1, source_target_pairs={{0,2},{2,4},{4,6},{6,8},{8,10},{10,12},{12,14},{14,16},{16,18},{18... | collective-permute-start | bytes 3145736 | tf_op jit(solution)/shard_map/ppermute | solution.py:684
  63.8 1.3 %collective-permute-start.13 = (f32[64,32,128]{2,1,0:T(8,128)}, f32[64,32,128]{2,1,0:T(8,128)}, u32[]{:S(2)}, u32[]{:S(2)}) collective-permute-start(f32[64,32,128]{2,1,0:T(8,128)} %get-tuple-element.71.own), channel_id=1, source_target_pairs={{2,0},{4,2},{6,4},{8,6},{10,8},{12,10},{14,12},{16,14},{18,16},{20... | collective-permute-start | bytes 3145736 | tf_op jit(solution)/shard_map/ppermute | solution.py:685
  65.1 9.1 %collective-permute-start.10 = (f32[4,32,128]{2,1,0:T(8,128)S(1)}, f32[4,32,128]{2,1,0:T(8,128)S(1)}, u32[]{:S(2)}, u32[]{:S(2)}) collective-permute-start(f32[4,32,128]{2,1,0:T(8,128)S(1)} %pad_maximum_fusion.own), channel_id=1, source_target_pairs={{0,32},{2,34},{4,36},{6,38},{8,40},{10,42},{12,44},{14,46},{16,48}... | collective-permute-start | bytes 196616 | tf_op jit(solution)/shard_map/ppermute | solution.py:638
  74.2 2.2 %collective-permute-start.8 = (f32[4,32,128]{2,1,0:T(8,128)S(1)}, f32[4,32,128]{2,1,0:T(8,128)S(1)}, u32[]{:S(2)}, u32[]{:S(2)}) collective-permute-start(f32[4,32,128]{2,1,0:T(8,128)S(1)} %pad_maximum_fusion.own), channel_id=1, source_target_pairs={{0,96},{2,98},{4,100},{6,102},{8,104},{10,106},{12,108},{14,110},{... | collective-permute-start | bytes 196616 | tf_op jit(solution)/shard_map/ppermute | solution.py:638
  76.3 0.0 collective-permute-done.11.refs_1_
  76.3 1.8 %collective-permute-start.9 = (f32[4,32,128]{2,1,0:T(8,128)S(1)}, f32[4,32,128]{2,1,0:T(8,128)S(1)}, u32[]{:S(2)}, u32[]{:S(2)}) collective-permute-start(f32[4,32,128]{2,1,0:T(8,128)S(1)} %pad_maximum_fusion.own), channel_id=1, source_target_pairs={{0,64},{2,66},{4,68},{6,70},{8,72},{10,74},{12,76},{14,78},{16,80}... | collective-permute-start | bytes 196616 | tf_op jit(solution)/shard_map/ppermute | solution.py:638
  78.2 0.0 copy-done
  78.2 10.6 %near_pass.3 = (f32[32,4096]{1,0:T(8,128)}, f32[32,4096]{1,0:T(8,128)}) custom-call(s32[1]{0:T(128)} %bitcast.core, s32[2,28,64]{2,1,0:T(8,128)} %get-tuple-element.62.lists, s32[2,64]{1,0:T(2,128)} %get-tuple-element.54.live, f32[3,8192]{1,0:T(4,128)} %targets.3, f32[2,67,32,128]{3,2,1,0:T(8,128)} %collective-permute-done.4.refs_0_, ...), custom_call_target="tpu_custom_call" | custom-call | flops 1000 | bytes 1000 | tf_op jit(solution)/shard_map/near_pass/pallas_call | solution.py:592
  88.8 0.0 copy-done.3
  88.8 6.1 %collective-permute-done.10.far_one = f32[4,32,128]{2,1,0:T(8,128)S(1)} collective-permute-done((f32[4,32,128]{2,1,0:T(8,128)S(1)}, f32[4,32,128]{2,1,0:T(8,128)S(1)}, u32[]{:S(2)}, u32[]{:S(2)}) %collective-permute-start.10) | collective-permute-done | bytes 65568 | tf_op jit(solution)/shard_map/ppermute | solution.py:638
  94.9 0.0 collective-permute-done.8.far_three
  94.9 5.2 %collective-permute-done.9.far_two = f32[4,32,128]{2,1,0:T(8,128)S(1)} collective-permute-done((f32[4,32,128]{2,1,0:T(8,128)S(1)}, f32[4,32,128]{2,1,0:T(8,128)S(1)}, u32[]{:S(2)}, u32[]{:S(2)}) %collective-permute-start.9) | collective-permute-done | bytes 65568 | tf_op jit(solution)/shard_map/ppermute | solution.py:638
  100.1 0.0 collective-permute-start.14
  100.1 0.0 copy-done.5
  100.1 0.6 copy-done.6
  100.7 4.6 %top_pass.1.parent = f32[32,128]{1,0:T(8,128)} custom-call(s32[1]{0:T(128)} %bitcast.1.place, s32[4,60]{1,0:T(4,128)} %bitcast.52, f32[4,32,128]{2,1,0:T(8,128)} %copy-done.5, f32[4,32,128]{2,1,0:T(8,128)} %copy-done.6, f32[4,32,128]{2,1,0:T(8,128)} %copy-done.4, f32[4,32,128]{2,1,0:T(8,128)} %copy-done.3, f32[62,64,64]{2,1,0:T(8,128)} %moves.1, ...), custom_call_target="tpu_custom_call" | custom-call | flops 50000000 | bytes 2000000 | tf_op jit(solution)/shard_map/top_pass/pallas_call | solution.py:323
  105.3 0.0 collective-permute-done.12.low
  105.3 0.0 collective-permute-done.13.high
  105.3 9.5 %couple_pass.1.far_hbm = f32[64,32,128]{2,1,0:T(8,128)} custom-call(s32[4,127]{1,0:T(4,128)} %get-tuple-element.73.codes, f32[64,32,128]{2,1,0:T(8,128)} %collective-permute-done.12.low, f32[64,32,128]{2,1,0:T(8,128)} %get-tuple-element.71.own, f32[64,32,128]{2,1,0:T(8,128)} %collective-permute-done.13.high, bf16[127,128,128]{2,1,0:T(8,128)(2,1)} %unbatch.2.first, ...), custom_call_target="tpu_custom_call" | custom-call | flops 400000000 | bytes 12000000 | tf_op jit(solution)/shard_map/couple_pass/pallas_call | solution.py:388
  114.9 0.0 collective-permute-done.14.given
  114.9 0.8 copy-done.2
  115.7 8.6 %down_pass.1 = f32[32,8192]{1,0:T(8,128)} custom-call(s32[1]{0:T(128)} %bitcast.core, f32[32,128]{1,0:T(8,128)} %top_pass.1.parent, f32[64,32,128]{2,1,0:T(8,128)} %couple_pass.1.far_hbm, bf16[128,64,128]{2,1,0:T(8,128)(2,1)} %get-tuple-element.78.trans_hbm, f32[64,64,128]{2,1,0:T(8,128)} %basis_hbm.3, f32[32,4096]{1,0:T(8,128)} %get-tuple-element.79.mine, ...), custom_call_target="tpu_custom_call" | custom-call | flops 200000000 | bytes 7000000 | tf_op jit(solution)/shard_map/down_pass/pallas_call | solution.py:462
  (9 shorter events, 0.0 us)
Async XLA Ops:
  0.0 5.1 %collective-permute-start = (f32[32,8192]{1,0:T(8,128)}, f32[32,8192]{1,0:T(8,128)S(1)}, u32[]{:S(2)}, u32[]{:S(2)}) collective-permute-start(f32[32,8192]{1,0:T(8,128)} %values_hbm.1), channel_id=1, source_target_pairs={{0,1},{1,0},{2,3},{3,2},{4,5},{5,4},{6,7},{7,6},{8,9},{9,8},{10,11... | collective-permute-start | bytes 3145736 | tf_op jit(solution)/shard_map/ppermute | solution.py:631
  5.1 1.0 copy-start.1
  18.1 4.8 %collective-permute-start.1 = (f32[1,32,128]{2,1,0:T(8,128)}, f32[1,32,128]{2,1,0:T(8,128)S(1)}, u32[]{:S(2)}, u32[]{:S(2)}) collective-permute-start(f32[1,32,128]{2,1,0:T(8,128)} %bitcast.48), channel_id=1, source_target_pairs={{0,6},{2,0},{4,2},{6,4},{8,14},{10,8},{12,10},{14,12},{16,22},{18,... | collective-permute-start | bytes 49160 | tf_op jit(solution)/shard_map/ppermute | solution.py:638
  21.2 5.5 %collective-permute-start.2 = (f32[1,32,128]{2,1,0:T(8,128)}, f32[1,32,128]{2,1,0:T(8,128)S(1)}, u32[]{:S(2)}, u32[]{:S(2)}) collective-permute-start(f32[1,32,128]{2,1,0:T(8,128)} %bitcast.49), channel_id=1, source_target_pairs={{0,4},{2,6},{4,0},{6,2},{8,12},{10,14},{12,8},{14,10},{16,20},{18,... | collective-permute-start | bytes 49160 | tf_op jit(solution)/shard_map/ppermute | solution.py:638
  21.9 5.2 %collective-permute-start.3 = (f32[1,32,128]{2,1,0:T(8,128)}, f32[1,32,128]{2,1,0:T(8,128)S(1)}, u32[]{:S(2)}, u32[]{:S(2)}) collective-permute-start(f32[1,32,128]{2,1,0:T(8,128)} %bitcast.50), channel_id=1, source_target_pairs={{0,2},{2,4},{4,6},{6,0},{8,10},{10,12},{12,14},{14,8},{16,18},{18,... | collective-permute-start | bytes 49160 | tf_op jit(solution)/shard_map/ppermute | solution.py:638
  27.0 26.6 %collective-permute-start.4 = (f32[2,67,32,128]{3,2,1,0:T(8,128)}, f32[2,67,32,128]{3,2,1,0:T(8,128)}, u32[]{:S(2)}, u32[]{:S(2)}) collective-permute-start(f32[2,67,32,128]{3,2,1,0:T(8,128)} %get-tuple-element.46.refs_0_), channel_id=1, source_target_pairs={{0,2},{2,4},{4,6},{6,8},{8,10},{10,12},{12,14},{14,16},{16,18},{18... | collective-permute-start | bytes 6586376 | tf_op jit(solution)/shard_map/ppermute | solution.py:672
  30.7 16.9 %collective-permute-start.5 = (f32[1,32,128]{2,1,0:T(8,128)S(1)}, f32[1,32,128]{2,1,0:T(8,128)S(1)}, u32[]{:S(2)}, u32[]{:S(2)}) collective-permute-start(f32[1,32,128]{2,1,0:T(8,128)S(1)} %fusion.3), channel_id=1, source_target_pairs={{0,24},{2,26},{4,28},{6,30},{8,0},{10,2},{12,4},{14,6},{16,8},{18,... | collective-permute-start | bytes 49160 | tf_op jit(solution)/shard_map/ppermute | solution.py:638
  32.5 15.1 %collective-permute-start.6 = (f32[1,32,128]{2,1,0:T(8,128)S(1)}, f32[1,32,128]{2,1,0:T(8,128)S(1)}, u32[]{:S(2)}, u32[]{:S(2)}) collective-permute-start(f32[1,32,128]{2,1,0:T(8,128)S(1)} %fusion.3), channel_id=1, source_target_pairs={{0,16},{2,18},{4,20},{6,22},{8,24},{10,26},{12,28},{14,30},{16,0},... | collective-permute-start | bytes 49160 | tf_op jit(solution)/shard_map/ppermute | solution.py:638
  33.3 14.3 %collective-permute-start.7 = (f32[1,32,128]{2,1,0:T(8,128)S(1)}, f32[1,32,128]{2,1,0:T(8,128)S(1)}, u32[]{:S(2)}, u32[]{:S(2)}) collective-permute-start(f32[1,32,128]{2,1,0:T(8,128)S(1)} %fusion.3), channel_id=1, source_target_pairs={{0,8},{2,10},{4,12},{6,14},{8,16},{10,18},{12,20},{14,22},{16,24},... | collective-permute-start | bytes 49160 | tf_op jit(solution)/shard_map/ppermute | solution.py:638
  52.9 35.9 %copy-start.3 = (f32[4,32,128]{2,1,0:T(8,128)}, f32[4,32,128]{2,1,0:T(8,128)S(1)}, u32[]{:S(2)}) copy-start(f32[4,32,128]{2,1,0:T(8,128)S(1)} %pad_maximum_fusion.own) | copy-start | bytes 196612
  54.9 21.4 %collective-permute-start.11 = (f32[67,32,128]{2,1,0:T(8,128)S(1)}, f32[67,32,128]{2,1,0:T(8,128)S(1)}, u32[]{:S(2)}, u32[]{:S(2)}) collective-permute-start(f32[67,32,128]{2,1,0:T(8,128)S(1)} %dynamic-slice_bitcast_fusion), channel_id=1, source_target_pairs={{0,1},{1,0},{2,3},{3,2},{4,5},{5,4},{6,7},{7,6},{8,9},{9,8},{10,11... | collective-permute-start | bytes 3293192 | tf_op jit(solution)/shard_map/ppermute | solution.py:682
  61.4 43.9 %collective-permute-start.12 = (f32[64,32,128]{2,1,0:T(8,128)}, f32[64,32,128]{2,1,0:T(8,128)}, u32[]{:S(2)}, u32[]{:S(2)}) collective-permute-start(f32[64,32,128]{2,1,0:T(8,128)} %get-tuple-element.71.own), channel_id=1, source_target_pairs={{0,2},{2,4},{4,6},{6,8},{8,10},{10,12},{12,14},{14,16},{16,18},{18... | collective-permute-start | bytes 3145736 | tf_op jit(solution)/shard_map/ppermute | solution.py:684
  63.8 41.6 %collective-permute-start.13 = (f32[64,32,128]{2,1,0:T(8,128)}, f32[64,32,128]{2,1,0:T(8,128)}, u32[]{:S(2)}, u32[]{:S(2)}) collective-permute-start(f32[64,32,128]{2,1,0:T(8,128)} %get-tuple-element.71.own), channel_id=1, source_target_pairs={{2,0},{4,2},{6,4},{8,6},{10,8},{12,10},{14,12},{16,14},{18,16},{20... | collective-permute-start | bytes 3145736 | tf_op jit(solution)/shard_map/ppermute | solution.py:685
  65.1 29.9 %collective-permute-start.10 = (f32[4,32,128]{2,1,0:T(8,128)S(1)}, f32[4,32,128]{2,1,0:T(8,128)S(1)}, u32[]{:S(2)}, u32[]{:S(2)}) collective-permute-start(f32[4,32,128]{2,1,0:T(8,128)S(1)} %pad_maximum_fusion.own), channel_id=1, source_target_pairs={{0,32},{2,34},{4,36},{6,38},{8,40},{10,42},{12,44},{14,46},{16,48}... | collective-permute-start | bytes 196616 | tf_op jit(solution)/shard_map/ppermute | solution.py:638
  74.2 20.7 %collective-permute-start.8 = (f32[4,32,128]{2,1,0:T(8,128)S(1)}, f32[4,32,128]{2,1,0:T(8,128)S(1)}, u32[]{:S(2)}, u32[]{:S(2)}) collective-permute-start(f32[4,32,128]{2,1,0:T(8,128)S(1)} %pad_maximum_fusion.own), channel_id=1, source_target_pairs={{0,96},{2,98},{4,100},{6,102},{8,104},{10,106},{12,108},{14,110},{... | collective-permute-start | bytes 196616 | tf_op jit(solution)/shard_map/ppermute | solution.py:638
  76.3 1.8 %copy-start = (f32[67,32,128]{2,1,0:T(8,128)}, f32[67,32,128]{2,1,0:T(8,128)S(1)}, u32[]{:S(2)}) copy-start(f32[67,32,128]{2,1,0:T(8,128)S(1)} %collective-permute-done.11.refs_1_) | copy-start | bytes 3293188
  76.3 23.8 %collective-permute-start.9 = (f32[4,32,128]{2,1,0:T(8,128)S(1)}, f32[4,32,128]{2,1,0:T(8,128)S(1)}, u32[]{:S(2)}, u32[]{:S(2)}) collective-permute-start(f32[4,32,128]{2,1,0:T(8,128)S(1)} %pad_maximum_fusion.own), channel_id=1, source_target_pairs={{0,64},{2,66},{4,68},{6,70},{8,72},{10,74},{12,76},{14,78},{16,80}... | collective-permute-start | bytes 196616 | tf_op jit(solution)/shard_map/ppermute | solution.py:638
  94.9 5.2 %copy-start.4 = (f32[4,32,128]{2,1,0:T(8,128)}, f32[4,32,128]{2,1,0:T(8,128)S(1)}, u32[]{:S(2)}) copy-start(f32[4,32,128]{2,1,0:T(8,128)S(1)} %collective-permute-done.10.far_one) | copy-start | bytes 196612
  94.9 5.2 %copy-start.5 = (f32[4,32,128]{2,1,0:T(8,128)}, f32[4,32,128]{2,1,0:T(8,128)S(1)}, u32[]{:S(2)}) copy-start(f32[4,32,128]{2,1,0:T(8,128)S(1)} %collective-permute-done.8.far_three) | copy-start | bytes 196612
  100.1 0.6 copy-start.6
  100.1 14.8 %collective-permute-start.14 = (f32[32,4096]{1,0:T(8,128)}, f32[32,4096]{1,0:T(8,128)S(1)}, u32[]{:S(2)}, u32[]{:S(2)}) collective-permute-start(f32[32,4096]{1,0:T(8,128)} %get-tuple-element.80), channel_id=1, source_target_pairs={{0,1},{1,0},{2,3},{3,2},{4,5},{5,4},{6,7},{7,6},{8,9},{9,8},{10,11... | collective-permute-start | bytes 1572872 | tf_op jit(solution)/shard_map/ppermute | solution.py:688
  114.9 0.8 copy-start.2

commit v10 on v9

--- a/solution.py
+++ b/solution.py
@@ -65,8 +65,8 @@
 
 
 def up_body(
-    place, near_list, near_count, partners, points, basis_hbm, values_hbm, across_hbm, moves_hbm,
-    up, share, trans_hbm, packed_hbm, lists, live, codes, rows, basis, values, across, moves, trans, packed, sem,
+    place, near_list, near_count, partners, basis_hbm, values_hbm, moves_hbm,
+    up, share, trans_hbm, lists, live, codes, rows, basis, values, moves, trans, sem,
 ):
     leaves = basis.shape[0]
     columns = values.shape[0]
@@ -77,7 +77,6 @@
         reads.append(pltpu.make_async_copy(moves_hbm.at[at], moves.at[at], sem.at[i]))
     reads.append(pltpu.make_async_copy(values_hbm, values, sem.at[4]))
     reads.append(pltpu.make_async_copy(basis_hbm, basis, sem.at[5]))
-    reads.append(pltpu.make_async_copy(across_hbm, across, sem.at[8]))
     for read in reads:
         read.start()
     plan(place[0], near_list, near_count, partners, lists, live, codes)
@@ -108,23 +107,6 @@
 
     for read in reads[4:]:
         read.wait()
-    block = leaves // 2
-    for c in range(3):
-        for j in range(leaves):
-            packed[j // block, 2 * block + c, j % block : j % block + 1] = points[
-                c : c + 1, 128 * j : 128 * j + 128
-            ]
-    for side in range(2):
-
-        @pl.loop(0, block, unroll=8)
-        def _(j, side=side):
-            at = pl.ds(pl.multiple_of((side * block + j) * 128, 128), 128)
-            packed[side, j] = values[:, at]
-            packed[side, block + j] = across[:, at]
-
-    send = pltpu.make_async_copy(packed, packed_hbm, sem.at[7])
-    send.start()
-
     def leaf_up(i):
         v = stack(values[:, pl.ds(pl.multiple_of(i * 128, 128), 128)])
         return both(fold(lax.dot_general(v, stack(basis[i]), NT, preferred_element_type=f32)))
@@ -168,10 +150,9 @@
     up[leaves - 1] = tiles[0]
     share[...] = both(fold(jnp.dot(stack(tiles[0])[:, 0:64], trans[row], preferred_element_type=f32)))
     write.wait()
-    send.wait()
-
-
-def up_pass(place, near_list, near_count, partners, points, basis, values, across, moves):
+
+
+def up_pass(place, near_list, near_count, partners, basis, values, moves):
     leaves = basis.shape[0]
     columns = values.shape[0]
     nodes = moves.shape[2]
@@ -181,33 +162,30 @@
             jax.ShapeDtypeStruct((leaves, columns, 128), f32),
             jax.ShapeDtypeStruct((columns, 128), f32),
             jax.ShapeDtypeStruct((nodes + 1, 64, 128), bf16),
-            jax.ShapeDtypeStruct((2, leaves + 3, columns, 128), f32),
             jax.ShapeDtypeStruct((2, SLOTS, leaves), jnp.int32),
             jax.ShapeDtypeStruct((2, leaves), jnp.int32),
             jax.ShapeDtypeStruct(partners.shape, jnp.int32),
         ),
-        in_specs=[SM, VM, VM, VM, VM, HBM, HBM, HBM, HBM],
-        out_specs=(VM, VM, HBM, HBM, VM, VM, VM),
+        in_specs=[SM, VM, VM, VM, HBM, HBM, HBM],
+        out_specs=(VM, VM, HBM, VM, VM, VM),
         scratch_shapes=[
             pltpu.VMEM((64 * PITCH, 128), f32),
             pltpu.VMEM(basis.shape, f32),
             pltpu.VMEM(values.shape, f32),
-            pltpu.VMEM(values.shape, f32),
             pltpu.VMEM(moves.shape, f32),
             pltpu.VMEM((nodes + 1, 64, 128), bf16),
-            pltpu.VMEM((2, leaves + 3, columns, 128), f32),
-            pltpu.SemaphoreType.DMA((9,)),
+            pltpu.SemaphoreType.DMA((7,)),
         ],
         compiler_params=pltpu.CompilerParams(vmem_limit_bytes=VMEM_BYTES),
         cost_estimate=pl.CostEstimate(flops=400_000_000, bytes_accessed=8_000_000, transcendentals=0),
         name="up_pass",
-    )(place, near_list, near_count, partners, points, basis, values, across, moves)
+    )(place, near_list, near_count, partners, basis, values, moves)
 
 
 CHUNK = 32
 
 
-def unbatch_body(part, matrices, out, held, rows, made, in_sem, out_sem):
+def unbatch_body(part, matrices, out, held, rows, made, in_sem, out_sem, between=None):
     nodes = matrices.shape[3]
     pieces = 4
     step = matrices.shape[1] // pieces
@@ -218,6 +196,8 @@
             pltpu.make_async_copy(matrices.at[pl.ds(2 * part, 2), at], held.at[:, at], in_sem.at[i])
         )
         reads[-1].start()
+    if between is not None:
+        between()
     for i in range(pieces):
         reads[i].wait()
 
@@ -245,6 +225,80 @@
         write.wait()
 
 
+def unbatch_pack_body(
+    part, matrices, points, values_hbm, across_hbm, out, packed_hbm,
+    held, rows, made, in_sem, out_sem, values, across, packed, sem,
+):
+    takes = [
+        pltpu.make_async_copy(values_hbm, values, sem.at[0]),
+        pltpu.make_async_copy(across_hbm, across, sem.at[1]),
+    ]
+    for take in takes:
+        take.start()
+    send = pltpu.make_async_copy(packed, packed_hbm, sem.at[2])
+
+    def between():
+        for take in takes:
+            take.wait()
+        arrange(points, values, across, packed)
+        send.start()
+
+    unbatch_body(part, matrices, out, held, rows, made, in_sem, out_sem, between)
+    send.wait()
+
+
+def arrange(points, values, across, packed):
+    leaves = values.shape[1] // 128
+    block = leaves // 2
+    for c in range(3):
+        for j in range(leaves):
+            packed[j // block, 2 * block + c, j % block : j % block + 1] = points[
+                c : c + 1, 128 * j : 128 * j + 128
+            ]
+    for side in range(2):
+
+        @pl.loop(0, block, unroll=8)
+        def _(j, side=side):
+            at = pl.ds(pl.multiple_of((side * block + j) * 128, 128), 128)
+            packed[side, j] = values[:, at]
+            packed[side, block + j] = across[:, at]
+
+
+def unbatch_scratch(matrices):
+    nodes = matrices.shape[3]
+    return [
+        pltpu.VMEM((2, *matrices.shape[1:]), f32),
+        pltpu.VMEM((64 * PITCH, 128), f32),
+        pltpu.VMEM((nodes, 128, 128), bf16),
+        pltpu.SemaphoreType.DMA((4,)),
+        pltpu.SemaphoreType.DMA((-(-nodes // CHUNK),)),
+    ]
+
+
+def unbatch_pack(matrices, part, points, values, across):
+    columns, width = values.shape
+    packed = (2, width // 128 + 3, columns, 128)
+    return pl.pallas_call(
+        functools.partial(unbatch_pack_body, part),
+        out_shape=(
+            jax.ShapeDtypeStruct((matrices.shape[3], 128, 128), bf16),
+            jax.ShapeDtypeStruct(packed, f32),
+        ),
+        in_specs=[HBM, VM, HBM, HBM],
+        out_specs=(HBM, HBM),
+        scratch_shapes=[
+            *unbatch_scratch(matrices),
+            pltpu.VMEM(values.shape, f32),
+            pltpu.VMEM(values.shape, f32),
+            pltpu.VMEM(packed, f32),
+            pltpu.SemaphoreType.DMA((3,)),
+        ],
+        compiler_params=pltpu.CompilerParams(vmem_limit_bytes=VMEM_BYTES),
+        cost_estimate=pl.CostEstimate(flops=1_000, bytes_accessed=1_000, transcendentals=0),
+        name="unbatch_pack",
+    )(matrices, points, values, across)
+
+
 def unbatch(matrices, part):
     nodes = matrices.shape[3]
     return pl.pallas_call(
@@ -252,31 +306,18 @@
         out_shape=jax.ShapeDtypeStruct((nodes, 128, 128), bf16),
         in_specs=[HBM],
         out_specs=HBM,
-        scratch_shapes=[
-            pltpu.VMEM((2, *matrices.shape[1:]), f32),
-            pltpu.VMEM((64 * PITCH, 128), f32),
-            pltpu.VMEM((nodes, 128, 128), bf16),
-            pltpu.SemaphoreType.DMA((4,)),
-            pltpu.SemaphoreType.DMA((-(-nodes // CHUNK),)),
-        ],
+        scratch_shapes=unbatch_scratch(matrices),
         compiler_params=pltpu.CompilerParams(vmem_limit_bytes=VMEM_BYTES),
         cost_estimate=pl.CostEstimate(flops=1_000, bytes_accessed=1_000, transcendentals=0),
         name="unbatch",
     )(matrices)
 
 
-def top_body(place, partners, far_three, far_two, far_one, own, moves, matrices, parent, up, block, sem):
+def top_chain(place, partners, gathered, moves, up, block, arrived):
     spot = place[0]
-    columns = own.shape[1]
-    copies = []
-    width, row = 32, 0
-    for level in range(4):
-        index = row + spot // (2 << level)
-        copies.append(pltpu.make_async_copy(matrices.at[index], block.at[level], sem.at[level]))
-        copies[-1].start()
-        row, width = row + width, width // 2
+    columns = gathered[0].shape[1]
     half = low_lanes((columns, 128))
-    for j, ref in enumerate((far_three, far_two, far_one, own)):
+    for j, ref in enumerate(gathered):
         up[pl.ds(4 * ((spot // 16 + 1 + j) % 4), 4)] = ref[...]
     def lift(tile, r):
         t = jnp.concatenate([moves[r], moves[r + 1]], axis=0)
@@ -298,8 +339,7 @@
         hi, lo = split(moves[r])
         x = stack(d)
         return fold(lax.dot_general(x, hi, NT, preferred_element_type=f32)) + lax.dot_general(x[:columns], lo, NT, preferred_element_type=f32)
-    for copy in copies:
-        copy.wait()
+    arrived()
     fars = []
     for level in range(4):
         index = rows[level] + spot // (2 << level)
@@ -316,36 +356,12 @@
     down = push(down, row + spot // 32)
     for level in range(3, -1, -1):
         down = push(down, rows[level] + spot // (2 << level)) + fars[level]
-    parent[...] = jnp.concatenate([down, down], axis=1)
-
-def top_pass(place, partners, gathered, moves, matrices):
-    columns = gathered[0].shape[1]
-    return pl.pallas_call(
-        top_body,
-        out_shape=jax.ShapeDtypeStruct((columns, 128), f32),
-        in_specs=[SM, SM] + [VM] * 5 + [HBM],
-        out_specs=VM,
-        scratch_shapes=[pltpu.VMEM((32, columns, 128), f32), pltpu.VMEM((4, 4, 64, 64), f32), pltpu.SemaphoreType.DMA((4,))],
-        compiler_params=pltpu.CompilerParams(vmem_limit_bytes=VMEM_BYTES),
-        cost_estimate=pl.CostEstimate(flops=50_000_000, bytes_accessed=2_000_000, transcendentals=0),
-        name="top_pass",
-    )(place, partners, *gathered, moves, matrices)
-
-
-def couple_body(codes, low, own, high, first, second, far, gather, tiles, held, sem):
-    leaves, columns, _ = own.shape
-    nodes = first.shape[0]
-    takes = []
-    for side, ref in enumerate((low, own, high)):
-        takes.append(pltpu.make_async_copy(ref, tiles.at[side], sem.at[3 + side]))
-        takes[-1].start()
-    reads = []
-    for i in range(3):
-        begin = 42 * i
-        at = pl.ds(begin, nodes - begin if i == 2 else 42)
-        for h, x in enumerate((first, second)):
-            reads.append(pltpu.make_async_copy(x.at[at], held.at[h, at], sem.at[6 + 2 * i + h]))
-            reads[-1].start()
+    return jnp.concatenate([down, down], axis=1)
+
+
+def couple(codes, far, gather, tiles, held, takes, reads):
+    _, leaves, columns, _ = tiles.shape
+    nodes = held.shape[1]
     half = low_lanes((columns, 128))
     left = low_lanes((2 * columns, 128))
     for side in range(3):
@@ -383,32 +399,9 @@
     far[leaves - 1] = one(nodes - 1)
 
 
-def couple_pass(codes, low, own, high, first, second):
-    leaves, columns, _ = own.shape
-    return pl.pallas_call(
-        couple_body,
-        out_shape=jax.ShapeDtypeStruct((leaves, columns, 128), f32),
-        in_specs=[SM] + [HBM] * 5,
-        out_specs=VM,
-        scratch_shapes=[
-            pltpu.VMEM((2, 3 * leaves, 2 * columns, 128), bf16),
-            pltpu.VMEM((3, leaves, columns, 128), f32),
-            pltpu.VMEM((2, *first.shape), bf16),
-            pltpu.SemaphoreType.DMA((12,)),
-        ],
-        compiler_params=pltpu.CompilerParams(vmem_limit_bytes=VMEM_BYTES),
-        cost_estimate=pl.CostEstimate(flops=400_000_000, bytes_accessed=12_000_000, transcendentals=0),
-        name="couple_pass",
-    )(codes, low, own, high, first, second)
-
-
-def down_body(core, parent, far_hbm, trans_hbm, basis_hbm, mine, given, out, far, trans, basis, ones, twos, sem):
+def descend(core, parent, far, trans, basis, mine, given, out, ones, twos, moved, based):
     leaves = basis.shape[0]
     columns = out.shape[0]
-    reads = []
-    for i, (source, dest) in enumerate(((far_hbm, far), (trans_hbm, trans), (basis_hbm, basis))):
-        reads.append(pltpu.make_async_copy(source, dest, sem.at[i]))
-        reads[-1].start()
     half = low_lanes((columns, 128))
 
     def push(d, tile):
@@ -420,9 +413,8 @@
         return jnp.where(half, tile, turned), jnp.where(half, turned, tile)
 
     last = leaves - 1
-    above = stack(parent[...])
-    reads[0].wait()
-    reads[1].wait()
+    above = stack(parent)
+    moved.wait()
     t = trans[2 * last]
     t = jnp.concatenate([t, t], axis=0)
     sources = [fold(lax.dot_general(above, t, NT, preferred_element_type=f32)) + far[last]]
@@ -441,7 +433,7 @@
         for u, d in enumerate(spread(ones[i])):
             twos[2 * i + u] = push(d, 2 * i + u)
 
-    reads[2].wait()
+    based.wait()
 
     @pl.loop(0, leaves // 2, unroll=4)
     def _(i):
@@ -456,26 +448,71 @@
     out[:, pl.ds(pl.multiple_of((1 - core[0]) * size, size), size)] += given[...]
 
 
-def down_pass(core, parent, far, trans, basis, mine, given):
-    leaves = basis.shape[0]
-    columns = parent.shape[0]
+def finish_body(
+    core, place, codes, partners, three, two, one, level, mine, given,
+    moves_hbm, matrices, low, own, high, first, second, trans_hbm, basis_hbm, out,
+    moves, block, up, tiles, held, trans, basis, gather, far, ones, twos, sem,
+):
+    spot = place[0]
+    queue = []
+
+    def bring(source, dest):
+        copy = pltpu.make_async_copy(source, dest, sem.at[len(queue)])
+        copy.start()
+        queue.append(copy)
+        return copy
+
+    lifted = bring(moves_hbm, moves)
+    blocks = []
+    width, row = 32, 0
+    for i in range(4):
+        blocks.append(bring(matrices.at[row + spot // (2 << i)], block.at[i]))
+        row, width = row + width, width // 2
+    takes = [bring(ref, tiles.at[side]) for side, ref in enumerate((low, own, high))]
+    nodes = first.shape[0]
+    reads = []
+    for i in range(3):
+        at = pl.ds(42 * i, nodes - 84 if i == 2 else 42)
+        for h, x in enumerate((first, second)):
+            reads.append(bring(x.at[at], held.at[h, at]))
+    moved = bring(trans_hbm, trans)
+    based = bring(basis_hbm, basis)
+
+    def arrived():
+        for copy in blocks:
+            copy.wait()
+
+    lifted.wait()
+    parent = top_chain(place, partners, (three, two, one, level), moves, up, block, arrived)
+    couple(codes, far, gather, tiles, held, takes, reads)
+    descend(core, parent, far, trans, basis, mine, given, out, ones, twos, moved, based)
+
+
+def finish(core, place, codes, partners, gathered, mine, given, moves, matrices, low, own, high, first, second, trans, basis):
+    leaves, columns, _ = own.shape
     return pl.pallas_call(
-        down_body,
+        finish_body,
         out_shape=jax.ShapeDtypeStruct((columns, leaves * 128), f32),
-        in_specs=[SM, VM, HBM, HBM, HBM, VM, VM],
+        in_specs=[SM] * 4 + [VM] * 6 + [HBM] * 9,
         out_specs=VM,
         scratch_shapes=[
-            pltpu.VMEM(far.shape, f32),
+            pltpu.VMEM(moves.shape, f32),
+            pltpu.VMEM((4, *matrices.shape[1:]), f32),
+            pltpu.VMEM((32, columns, 128), f32),
+            pltpu.VMEM((3, leaves, columns, 128), f32),
+            pltpu.VMEM((2, *first.shape), bf16),
             pltpu.VMEM(trans.shape, bf16),
             pltpu.VMEM(basis.shape, f32),
+            pltpu.VMEM((2, 3 * leaves, 2 * columns, 128), bf16),
+            pltpu.VMEM((leaves, columns, 128), f32),
             pltpu.VMEM((leaves // 4, columns, 128), f32),
             pltpu.VMEM((leaves // 2, columns, 128), f32),
-            pltpu.SemaphoreType.DMA((3,)),
+            pltpu.SemaphoreType.DMA((16,)),
         ],
         compiler_params=pltpu.CompilerParams(vmem_limit_bytes=VMEM_BYTES),
-        cost_estimate=pl.CostEstimate(flops=200_000_000, bytes_accessed=7_000_000, transcendentals=0),
-        name="down_pass",
-    )(core, parent, far, trans, basis, mine, given)
+        cost_estimate=pl.CostEstimate(flops=1_000_000_000, bytes_accessed=20_000_000, transcendentals=0),
+        name="finish",
+    )(core, place, codes, partners, *gathered, mine, given, moves, matrices, low, own, high, first, second, trans, basis)
 
 
 near_weight = 0.1
@@ -652,20 +689,12 @@
     core = core[None].astype(jnp.int32)
     place = position[None].astype(jnp.int32)
     coupling = coupling.transpose(1, 2, 3, 0)
-    first = unbatch(coupling, 0)
-    across, first, coupling = after((across, first, coupling))
-    up, share, trans, packed, lists, live, codes = up_pass(
-        place,
-        near_list.T,
-        near_count[None],
-        partners.T,
-        points,
-        basis,
-        values,
-        across,
-        transfer.transpose(1, 2, 0),
+    up, share, trans, lists, live, codes = up_pass(
+        place, near_list.T, near_count[None], partners.T, basis, values, transfer.transpose(1, 2, 0)
     )
     turned, spot = ring(share[None], 1)
+    share, coupling, across = after((share, coupling, across))
+    first, packed = unbatch_pack(coupling, 0, points, values, across)
     turned, share, packed = after((turned, share, packed))
     outward = [(2 * i, 2 * i + 2) for i in range(count - 1)]
     outward += [(2 * i + 3, 2 * i + 1) for i in range(count - 1)]
@@ -674,22 +703,36 @@
     level = jnp.where(jnp.arange(128) < 64, level[0] + level[1], level[2] + level[3])[None]
     turned, spot = ring(level, 4)
     begin = near_pass(12, core, lists, live, points, (packed,))
-    coupling, turned, begin = after((coupling, turned, begin))
+    coupling, turned, beside, begin = after((coupling, turned, beside, begin))
     level = in_order(turned, level, spot)
-    second = unbatch(coupling, 1)
-    beside, up, level, lists, second = after((beside, up, level, lists, second))
+    turned, spot = ring(level, 16)
     passed = lax.dynamic_index_in_dim(beside, 1 - core[0], 0, keepdims=False)
     passed = lax.ppermute(passed, "rhs", swap)
-    turned, spot = ring(level, 16)
+    turned, up, coupling = after((turned, up, coupling))
     up_low = lax.ppermute(up, "leaf", forward)
     up_high = lax.ppermute(up, "leaf", backward)
+    second = unbatch(coupling, 1)
+    passed, lists, second = after((passed, lists, second))
     mine, other = near_pass(12, core, lists, live, points, (beside, passed), begin)
-    turned, mine, other = after((turned, mine, other))
     given = lax.ppermute(other, "rhs", swap)
-    parent = top_pass(place, partners_top.T, (*turned, level), transfer_top, coupling_top)
-    parent, up_low, up_high = after((parent, up_low, up_high))
-    far = couple_pass(codes, up_low, up, up_high, first, second)
-    return down_pass(core, parent, far, trans, basis, mine, given)
+    return finish(
+        core,
+        place,
+        codes,
+        partners_top.T,
+        (*turned, level),
+        mine,
+        given,
+        transfer_top,
+        coupling_top,
+        up_low,
+        up,
+        up_high,
+        first,
+        second,
+        trans,
+        basis,
+    )
 
 
 def solution(mesh):

time: 126 us -> 122 us (0.968)
  the two profiles are of different devices: /device:TPU:0 before, /device:TPU:30 now
where the time goes in v10:
time: 122 us; the launch traced here: 121 us
  Pallas kernels  71.3 us (58%)
  starting transfers between devices  25.6 us (21%)
  waiting for transfers between devices  20.1 us (16%)
  local copies, waits for them, and re-layouts  3.16 us (3%)
    pallas_call x2, Pallas kernels, near_pass(): pl.pallas_call(functools.partial(near_body, unroll, chunks), out_shape=(s...  30 us
    pallas_call x1, Pallas kernels, finish(): pl.pallas_call(finish_body, out_shape=jax.ShapeDtypeStruct((columns, leav...  17.1 us
    ppermute x9, starting transfers between devices, ring(): turned.append(lax.ppermute(x, 'leaf', to))  13.1 us
    pallas_call x1, Pallas kernels, up_pass(): pl.pallas_call(up_body, out_shape=(jax.ShapeDtypeStruct((leaves, columns,...  11.4 us
    ppermute x9, waiting for transfers between devices, ring(): turned.append(lax.ppermute(x, 'leaf', to))  11.3 us
    ppermute x1, waiting for transfers between devices, local(): up_high = lax.ppermute(up, 'leaf', backward)  8.34 us
    pallas_call x1, Pallas kernels, unbatch_pack(): pl.pallas_call(functools.partial(unbatch_pack_body, part), out_shape=(jax...  7.63 us
    pallas_call x1, Pallas kernels, unbatch(): pl.pallas_call(functools.partial(unbatch_body, part), out_shape=jax.Shape...  5.12 us
  transfers between devices with their start and end apart: 15, of which 5 were waited for; matrix products, arithmetic and copies ran while one was open for 0% of the time, Pallas kernels for 45%

profile of v10, /device:TPU:30, one launch (start us, length us, event | category | flops | bytes accessed | tf_op | source)
XLA Modules:
  0.0 120.6 jit_solution(8946481917078553223)
XLA Ops:
  0.0 0.0 collective-permute-start
  0.0 11.4 %up_pass.1 = (f32[64,32,128]{2,1,0:T(8,128)}, f32[32,128]{1,0:T(8,128)}, bf16[128,64,128]{2,1,0:T(8,128)(2,1)}, s32[2,28,64]{2,1,0:T(8,128)}, s32[2,64]{1,0:T(2,128)}, /*index=5*/s32[4,127]{1,0:T(4,128)}) custom-call(s32[1]{0:T(128)} %bitcast.1.place, s32[27,64]{1,0:T(8,128)} %bitcast.47, s32[1,64]{1,0:T(1,128)} %bitcast.53, s32[4,127]{1,0:T(4,128)} %bitcast.51, ...), custom_call_target="tpu_custom_call" | custom-call | flops 400000000 | bytes 8000000 | tf_op jit(solution)/shard_map/up_pass/pallas_call | solution.py:159
  11.4 0.8 collective-permute-start.1
  12.2 0.9 collective-permute-start.2
  13.2 2.2 %collective-permute-start.3 = (f32[1,32,128]{2,1,0:T(8,128)}, f32[1,32,128]{2,1,0:T(8,128)S(1)}, u32[]{:S(2)}, u32[]{:S(2)}) collective-permute-start(f32[1,32,128]{2,1,0:T(8,128)} %bitcast.50), channel_id=1, source_target_pairs={{0,2},{2,4},{4,6},{6,0},{8,10},{10,12},{12,14},{14,8},{16,18},{18,... | collective-permute-start | bytes 49160 | tf_op jit(solution)/shard_map/ppermute | solution.py:675
  15.3 0.0 collective-permute-done.across_hbm
  15.4 0.0 copy-start
  15.4 1.0 copy-done
  16.3 7.6 %unbatch_pack.1 = (bf16[127,128,128]{2,1,0:T(8,128)(2,1)}, f32[2,67,32,128]{3,2,1,0:T(8,128)}) custom-call(f32[4,64,64,127]{3,2,1,0:T(8,128)} %bitcast.44, f32[3,8192]{1,0:T(4,128)} %targets.3, f32[32,8192]{1,0:T(8,128)} %values_hbm.3, f32[32,8192]{1,0:T(8,128)} %copy-done), custom_call_target="tpu_custom_call" | custom-call | flops 1000 | bytes 1000 | tf_op jit(solution)/shard_map/unbatch_pack/pallas_call | solution.py:281
  24.0 0.0 collective-permute-done.1
  24.0 0.0 collective-permute-done.2
  24.0 0.0 collective-permute-done.3
  24.0 4.2 %collective-permute-start.7 = (f32[2,67,32,128]{3,2,1,0:T(8,128)}, f32[2,67,32,128]{3,2,1,0:T(8,128)}, u32[]{:S(2)}, u32[]{:S(2)}) collective-permute-start(f32[2,67,32,128]{3,2,1,0:T(8,128)} %get-tuple-element.50.refs_0_), channel_id=1, source_target_pairs={{0,2},{2,4},{4,6},{6,8},{8,10},{10,12},{12,14},{14,16},{16,18},{18... | collective-permute-start | bytes 6586376 | tf_op jit(solution)/shard_map/ppermute | solution.py:701
  28.2 0.0 copy-done.6
  28.2 0.3 collective-permute-start.4
  28.5 1.4 %collective-permute-start.5 = (f32[1,32,128]{2,1,0:T(8,128)S(1)}, f32[1,32,128]{2,1,0:T(8,128)S(1)}, u32[]{:S(2)}, u32[]{:S(2)}) collective-permute-start(f32[1,32,128]{2,1,0:T(8,128)S(1)} %fusion.3), channel_id=1, source_target_pairs={{0,16},{2,18},{4,20},{6,22},{8,24},{10,26},{12,28},{14,30},{16,0},... | collective-permute-start | bytes 49160 | tf_op jit(solution)/shard_map/ppermute | solution.py:675
  29.9 2.1 %collective-permute-start.6 = (f32[1,32,128]{2,1,0:T(8,128)S(1)}, f32[1,32,128]{2,1,0:T(8,128)S(1)}, u32[]{:S(2)}, u32[]{:S(2)}) collective-permute-start(f32[1,32,128]{2,1,0:T(8,128)S(1)} %fusion.3), channel_id=1, source_target_pairs={{0,8},{2,10},{4,12},{6,14},{8,16},{10,18},{12,20},{14,22},{16,24},... | collective-permute-start | bytes 49160 | tf_op jit(solution)/shard_map/ppermute | solution.py:675
  32.0 15.1 %near_pass.2 = (f32[32,4096]{1,0:T(8,128)}, f32[32,4096]{1,0:T(8,128)}) custom-call(s32[1]{0:T(128)} %bitcast.core, s32[2,28,64]{2,1,0:T(8,128)} %get-tuple-element.65.lists, s32[2,64]{1,0:T(2,128)} %get-tuple-element.52.live, f32[3,8192]{1,0:T(4,128)} %targets.3, f32[2,67,32,128]{3,2,1,0:T(8,128)} %get-tuple-element.50.refs_0_), custom_call_target="tpu_custom_call" | custom-call | flops 1000 | bytes 1000 | tf_op jit(solution)/shard_map/near_pass/pallas_call | solution.py:629
  47.1 0.0 collective-permute-done.4
  47.1 0.0 collective-permute-done.5
  47.2 7.1 %collective-permute-done.6 = f32[1,32,128]{2,1,0:T(8,128)S(1)} collective-permute-done((f32[1,32,128]{2,1,0:T(8,128)S(1)}, f32[1,32,128]{2,1,0:T(8,128)S(1)}, u32[]{:S(2)}, u32[]{:S(2)}) %collective-permute-start.6) | collective-permute-done | bytes 16416 | tf_op jit(solution)/shard_map/ppermute | solution.py:675
  54.3 0.0 collective-permute-done.7.refs_0_
  54.3 1.3 %dynamic-slice_bitcast_fusion = f32[67,32,128]{2,1,0:T(8,128)S(1)} fusion(f32[2,67,32,128]{3,2,1,0:T(8,128)} %collective-permute-done.7.refs_0_, s32[]{:T(128)S(6)} %select_n.175), kind=kLoop, calls=%fused_computation | loop fusion | bytes 2195460 | tf_op jit(solution)/shard_map/jit(dynamic_index_in_dim)/squeeze | solution.py:709
  55.6 2.3 %collective-permute-start.11 = (f32[67,32,128]{2,1,0:T(8,128)S(1)}, f32[67,32,128]{2,1,0:T(8,128)}, u32[]{:S(2)}, u32[]{:S(2)}) collective-permute-start(f32[67,32,128]{2,1,0:T(8,128)S(1)} %dynamic-slice_bitcast_fusion), channel_id=1, source_target_pairs={{0,1},{1,0},{2,3},{3,2},{4,5},{5,4},{6,7},{7,6},{8,9},{9,8},{10,11... | collective-permute-start | bytes 3293192 | tf_op jit(solution)/shard_map/ppermute | solution.py:710
  58.0 0.0 copy-start.2
  58.0 1.9 %collective-permute-start.8 = (f32[4,32,128]{2,1,0:T(8,128)S(1)}, f32[4,32,128]{2,1,0:T(8,128)S(1)}, u32[]{:S(2)}, u32[]{:S(2)}) collective-permute-start(f32[4,32,128]{2,1,0:T(8,128)S(1)} %pad_maximum_fusion.level), channel_id=1, source_target_pairs={{0,96},{2,98},{4,100},{6,102},{8,104},{10,106},{12,108},{14,110},{... | collective-permute-start | bytes 196616 | tf_op jit(solution)/shard_map/ppermute | solution.py:675
  59.9 2.1 %collective-permute-start.9 = (f32[4,32,128]{2,1,0:T(8,128)S(1)}, f32[4,32,128]{2,1,0:T(8,128)S(1)}, u32[]{:S(2)}, u32[]{:S(2)}) collective-permute-start(f32[4,32,128]{2,1,0:T(8,128)S(1)} %pad_maximum_fusion.level), channel_id=1, source_target_pairs={{0,64},{2,66},{4,68},{6,70},{8,72},{10,74},{12,76},{14,78},{16,80}... | collective-permute-start | bytes 196616 | tf_op jit(solution)/shard_map/ppermute | solution.py:675
  62.0 1.3 %collective-permute-start.10 = (f32[4,32,128]{2,1,0:T(8,128)S(1)}, f32[4,32,128]{2,1,0:T(8,128)S(1)}, u32[]{:S(2)}, u32[]{:S(2)}) collective-permute-start(f32[4,32,128]{2,1,0:T(8,128)S(1)} %pad_maximum_fusion.level), channel_id=1, source_target_pairs={{0,32},{2,34},{4,36},{6,38},{8,40},{10,42},{12,44},{14,46},{16,48}... | collective-permute-start | bytes 196616 | tf_op jit(solution)/shard_map/ppermute | solution.py:675
  63.4 0.0 collective-permute-done.8.three
  63.4 0.0 copy-start.3
  63.4 3.0 %collective-permute-done.9.two = f32[4,32,128]{2,1,0:T(8,128)S(1)} collective-permute-done((f32[4,32,128]{2,1,0:T(8,128)S(1)}, f32[4,32,128]{2,1,0:T(8,128)S(1)}, u32[]{:S(2)}, u32[]{:S(2)}) %collective-permute-start.9) | collective-permute-done | bytes 65568 | tf_op jit(solution)/shard_map/ppermute | solution.py:675
  66.4 0.0 copy-start.4
  66.4 1.1 collective-permute-done.10.one
  67.5 4.1 %collective-permute-start.13 = (f32[64,32,128]{2,1,0:T(8,128)}, f32[64,32,128]{2,1,0:T(8,128)}, u32[]{:S(2)}, u32[]{:S(2)}) collective-permute-start(f32[64,32,128]{2,1,0:T(8,128)} %get-tuple-element.71.own), channel_id=1, source_target_pairs={{0,2},{2,4},{4,6},{6,8},{8,10},{10,12},{12,14},{14,16},{16,18},{18... | collective-permute-start | bytes 3145736 | tf_op jit(solution)/shard_map/ppermute | solution.py:712
  71.6 1.9 %collective-permute-start.14 = (f32[64,32,128]{2,1,0:T(8,128)}, f32[64,32,128]{2,1,0:T(8,128)}, u32[]{:S(2)}, u32[]{:S(2)}) collective-permute-start(f32[64,32,128]{2,1,0:T(8,128)} %get-tuple-element.71.own), channel_id=1, source_target_pairs={{2,0},{4,2},{6,4},{8,6},{10,8},{12,10},{14,12},{16,14},{18,16},{20... | collective-permute-start | bytes 3145736 | tf_op jit(solution)/shard_map/ppermute | solution.py:713
  73.5 5.1 %unbatch.1.second = bf16[127,128,128]{2,1,0:T(8,128)(2,1)} custom-call(f32[4,64,64,127]{3,2,1,0:T(8,128)} %bitcast.45), custom_call_target="tpu_custom_call" | custom-call | flops 1000 | bytes 1000 | tf_op jit(solution)/shard_map/unbatch/pallas_call | solution.py:304
  78.7 0.0 copy-done.2
  78.7 0.0 copy-done.3
  78.7 0.0 copy-done.4
  78.7 0.0 copy-done.5
  78.7 0.0 collective-permute-done.11.refs_1_
  78.7 14.9 %near_pass.3 = (f32[32,4096]{1,0:T(8,128)}, f32[32,4096]{1,0:T(8,128)}) custom-call(s32[1]{0:T(128)} %bitcast.core, s32[2,28,64]{2,1,0:T(8,128)} %get-tuple-element.65.lists, s32[2,64]{1,0:T(2,128)} %get-tuple-element.52.live, f32[3,8192]{1,0:T(4,128)} %targets.3, f32[2,67,32,128]{3,2,1,0:T(8,128)} %collective-permute-done.7.refs_0_, ...), custom_call_target="tpu_custom_call" | custom-call | flops 1000 | bytes 1000 | tf_op jit(solution)/shard_map/near_pass/pallas_call | solution.py:629
  93.6 0.1 collective-permute-start.12
  93.7 0.5 collective-permute-done.13.low
  94.1 8.3 %collective-permute-done.14.high = f32[64,32,128]{2,1,0:T(8,128)} collective-permute-done((f32[64,32,128]{2,1,0:T(8,128)}, f32[64,32,128]{2,1,0:T(8,128)}, u32[]{:S(2)}, u32[]{:S(2)}) %collective-permute-start.14) | collective-permute-done | bytes 1048608 | tf_op jit(solution)/shard_map/ppermute | solution.py:713
  102.5 0.0 collective-permute-done.12.given
  102.5 0.9 copy-done.1
  103.3 17.1 %finish.1 = f32[32,8192]{1,0:T(8,128)} custom-call(s32[1]{0:T(128)} %bitcast.core, s32[1]{0:T(128)} %bitcast.1.place, s32[4,127]{1,0:T(4,128)} %get-tuple-element.40.codes, s32[4,60]{1,0:T(4,128)} %bitcast.52, f32[4,32,128]{2,1,0:T(8,128)} %copy-done.3, f32[4,32,128]{2,1,0:T(8,128)} %copy-done.4, f32[4,32,128]{2,1,0:T(8,128)} %copy-done.5, ...), custom_call_target="tpu_custom_call" | custom-call | flops 1000000000 | bytes 20000000 | tf_op jit(solution)/shard_map/finish/pallas_call | solution.py:493
  (7 shorter events, 0.0 us)
Async XLA Ops:
  0.0 15.4 %collective-permute-start = (f32[32,8192]{1,0:T(8,128)}, f32[32,8192]{1,0:T(8,128)S(1)}, u32[]{:S(2)}, u32[]{:S(2)}) collective-permute-start(f32[32,8192]{1,0:T(8,128)} %values_hbm.3), channel_id=1, source_target_pairs={{0,1},{1,0},{2,3},{3,2},{4,5},{5,4},{6,7},{7,6},{8,9},{9,8},{10,11... | collective-permute-start | bytes 3145736 | tf_op jit(solution)/shard_map/ppermute | solution.py:668
  11.4 12.5 %collective-permute-start.1 = (f32[1,32,128]{2,1,0:T(8,128)}, f32[1,32,128]{2,1,0:T(8,128)S(1)}, u32[]{:S(2)}, u32[]{:S(2)}) collective-permute-start(f32[1,32,128]{2,1,0:T(8,128)} %bitcast.48), channel_id=1, source_target_pairs={{0,6},{2,0},{4,2},{6,4},{8,14},{10,8},{12,10},{14,12},{16,22},{18,... | collective-permute-start | bytes 49160 | tf_op jit(solution)/shard_map/ppermute | solution.py:675
  12.2 11.7 %collective-permute-start.2 = (f32[1,32,128]{2,1,0:T(8,128)}, f32[1,32,128]{2,1,0:T(8,128)S(1)}, u32[]{:S(2)}, u32[]{:S(2)}) collective-permute-start(f32[1,32,128]{2,1,0:T(8,128)} %bitcast.49), channel_id=1, source_target_pairs={{0,4},{2,6},{4,0},{6,2},{8,12},{10,14},{12,8},{14,10},{16,20},{18,... | collective-permute-start | bytes 49160 | tf_op jit(solution)/shard_map/ppermute | solution.py:675
  13.2 10.8 %collective-permute-start.3 = (f32[1,32,128]{2,1,0:T(8,128)}, f32[1,32,128]{2,1,0:T(8,128)S(1)}, u32[]{:S(2)}, u32[]{:S(2)}) collective-permute-start(f32[1,32,128]{2,1,0:T(8,128)} %bitcast.50), channel_id=1, source_target_pairs={{0,2},{2,4},{4,6},{6,0},{8,10},{10,12},{12,14},{14,8},{16,18},{18,... | collective-permute-start | bytes 49160 | tf_op jit(solution)/shard_map/ppermute | solution.py:675
  15.4 1.0 copy-start
  16.3 11.9 %copy-start.6 = (f32[32,128]{1,0:T(8,128)S(1)}, f32[32,128]{1,0:T(8,128)}, u32[]{:S(2)}) copy-start(f32[32,128]{1,0:T(8,128)} %get-tuple-element.49) | copy-start | bytes 49156
  24.0 30.3 %collective-permute-start.7 = (f32[2,67,32,128]{3,2,1,0:T(8,128)}, f32[2,67,32,128]{3,2,1,0:T(8,128)}, u32[]{:S(2)}, u32[]{:S(2)}) collective-permute-start(f32[2,67,32,128]{3,2,1,0:T(8,128)} %get-tuple-element.50.refs_0_), channel_id=1, source_target_pairs={{0,2},{2,4},{4,6},{6,8},{8,10},{10,12},{12,14},{14,16},{16,18},{18... | collective-permute-start | bytes 6586376 | tf_op jit(solution)/shard_map/ppermute | solution.py:701
  28.2 18.9 %collective-permute-start.4 = (f32[1,32,128]{2,1,0:T(8,128)S(1)}, f32[1,32,128]{2,1,0:T(8,128)S(1)}, u32[]{:S(2)}, u32[]{:S(2)}) collective-permute-start(f32[1,32,128]{2,1,0:T(8,128)S(1)} %fusion.3), channel_id=1, source_target_pairs={{0,24},{2,26},{4,28},{6,30},{8,0},{10,2},{12,4},{14,6},{16,8},{18,... | collective-permute-start | bytes 49160 | tf_op jit(solution)/shard_map/ppermute | solution.py:675
  28.5 18.7 %collective-permute-start.5 = (f32[1,32,128]{2,1,0:T(8,128)S(1)}, f32[1,32,128]{2,1,0:T(8,128)S(1)}, u32[]{:S(2)}, u32[]{:S(2)}) collective-permute-start(f32[1,32,128]{2,1,0:T(8,128)S(1)} %fusion.3), channel_id=1, source_target_pairs={{0,16},{2,18},{4,20},{6,22},{8,24},{10,26},{12,28},{14,30},{16,0},... | collective-permute-start | bytes 49160 | tf_op jit(solution)/shard_map/ppermute | solution.py:675
  29.9 24.4 %collective-permute-start.6 = (f32[1,32,128]{2,1,0:T(8,128)S(1)}, f32[1,32,128]{2,1,0:T(8,128)S(1)}, u32[]{:S(2)}, u32[]{:S(2)}) collective-permute-start(f32[1,32,128]{2,1,0:T(8,128)S(1)} %fusion.3), channel_id=1, source_target_pairs={{0,8},{2,10},{4,12},{6,14},{8,16},{10,18},{12,20},{14,22},{16,24},... | collective-permute-start | bytes 49160 | tf_op jit(solution)/shard_map/ppermute | solution.py:675
  55.6 23.1 %collective-permute-start.11 = (f32[67,32,128]{2,1,0:T(8,128)S(1)}, f32[67,32,128]{2,1,0:T(8,128)}, u32[]{:S(2)}, u32[]{:S(2)}) collective-permute-start(f32[67,32,128]{2,1,0:T(8,128)S(1)} %dynamic-slice_bitcast_fusion), channel_id=1, source_target_pairs={{0,1},{1,0},{2,3},{3,2},{4,5},{5,4},{6,7},{7,6},{8,9},{9,8},{10,11... | collective-permute-start | bytes 3293192 | tf_op jit(solution)/shard_map/ppermute | solution.py:710
  58.0 20.7 %copy-start.2 = (f32[4,32,128]{2,1,0:T(8,128)}, f32[4,32,128]{2,1,0:T(8,128)S(1)}, u32[]{:S(2)}) copy-start(f32[4,32,128]{2,1,0:T(8,128)S(1)} %pad_maximum_fusion.level) | copy-start | bytes 196612
  58.0 5.4 %collective-permute-start.8 = (f32[4,32,128]{2,1,0:T(8,128)S(1)}, f32[4,32,128]{2,1,0:T(8,128)S(1)}, u32[]{:S(2)}, u32[]{:S(2)}) collective-permute-start(f32[4,32,128]{2,1,0:T(8,128)S(1)} %pad_maximum_fusion.level), channel_id=1, source_target_pairs={{0,96},{2,98},{4,100},{6,102},{8,104},{10,106},{12,108},{14,110},{... | collective-permute-start | bytes 196616 | tf_op jit(solution)/shard_map/ppermute | solution.py:675
  59.9 6.5 %collective-permute-start.9 = (f32[4,32,128]{2,1,0:T(8,128)S(1)}, f32[4,32,128]{2,1,0:T(8,128)S(1)}, u32[]{:S(2)}, u32[]{:S(2)}) collective-permute-start(f32[4,32,128]{2,1,0:T(8,128)S(1)} %pad_maximum_fusion.level), channel_id=1, source_target_pairs={{0,64},{2,66},{4,68},{6,70},{8,72},{10,74},{12,76},{14,78},{16,80}... | collective-permute-start | bytes 196616 | tf_op jit(solution)/shard_map/ppermute | solution.py:675
  62.0 5.5 %collective-permute-start.10 = (f32[4,32,128]{2,1,0:T(8,128)S(1)}, f32[4,32,128]{2,1,0:T(8,128)S(1)}, u32[]{:S(2)}, u32[]{:S(2)}) collective-permute-start(f32[4,32,128]{2,1,0:T(8,128)S(1)} %pad_maximum_fusion.level), channel_id=1, source_target_pairs={{0,32},{2,34},{4,36},{6,38},{8,40},{10,42},{12,44},{14,46},{16,48}... | collective-permute-start | bytes 196616 | tf_op jit(solution)/shard_map/ppermute | solution.py:675
  63.4 15.3 %copy-start.3 = (f32[4,32,128]{2,1,0:T(8,128)}, f32[4,32,128]{2,1,0:T(8,128)S(1)}, u32[]{:S(2)}) copy-start(f32[4,32,128]{2,1,0:T(8,128)S(1)} %collective-permute-done.8.three) | copy-start | bytes 196612
  66.4 12.3 %copy-start.4 = (f32[4,32,128]{2,1,0:T(8,128)}, f32[4,32,128]{2,1,0:T(8,128)S(1)}, u32[]{:S(2)}) copy-start(f32[4,32,128]{2,1,0:T(8,128)S(1)} %collective-permute-done.9.two) | copy-start | bytes 196612
  67.5 11.2 %copy-start.5 = (f32[4,32,128]{2,1,0:T(8,128)}, f32[4,32,128]{2,1,0:T(8,128)S(1)}, u32[]{:S(2)}) copy-start(f32[4,32,128]{2,1,0:T(8,128)S(1)} %collective-permute-done.10.one) | copy-start | bytes 196612
  67.5 26.6 %collective-permute-start.13 = (f32[64,32,128]{2,1,0:T(8,128)}, f32[64,32,128]{2,1,0:T(8,128)}, u32[]{:S(2)}, u32[]{:S(2)}) collective-permute-start(f32[64,32,128]{2,1,0:T(8,128)} %get-tuple-element.71.own), channel_id=1, source_target_pairs={{0,2},{2,4},{4,6},{6,8},{8,10},{10,12},{12,14},{14,16},{16,18},{18... | collective-permute-start | bytes 3145736 | tf_op jit(solution)/shard_map/ppermute | solution.py:712
  71.6 30.9 %collective-permute-start.14 = (f32[64,32,128]{2,1,0:T(8,128)}, f32[64,32,128]{2,1,0:T(8,128)}, u32[]{:S(2)}, u32[]{:S(2)}) collective-permute-start(f32[64,32,128]{2,1,0:T(8,128)} %get-tuple-element.71.own), channel_id=1, source_target_pairs={{2,0},{4,2},{6,4},{8,6},{10,8},{12,10},{14,12},{16,14},{18,16},{20... | collective-permute-start | bytes 3145736 | tf_op jit(solution)/shard_map/ppermute | solution.py:713
  93.6 8.9 %collective-permute-start.12 = (f32[32,4096]{1,0:T(8,128)}, f32[32,4096]{1,0:T(8,128)S(1)}, u32[]{:S(2)}, u32[]{:S(2)}) collective-permute-start(f32[32,4096]{1,0:T(8,128)} %get-tuple-element.70), channel_id=1, source_target_pairs={{0,1},{1,0},{2,3},{3,2},{4,5},{5,4},{6,7},{7,6},{8,9},{9,8},{10,11... | collective-permute-start | bytes 1572872 | tf_op jit(solution)/shard_map/ppermute | solution.py:717
  102.5 0.9 copy-start.1

commit v11 on v10

--- a/solution.py
+++ b/solution.py
@@ -185,7 +185,7 @@
 CHUNK = 32
 
 
-def unbatch_body(part, matrices, out, held, rows, made, in_sem, out_sem, between=None):
+def unbatch_body(part, matrices, out, held, rows, made, in_sem, out_sem):
     nodes = matrices.shape[3]
     pieces = 4
     step = matrices.shape[1] // pieces
@@ -196,8 +196,6 @@
             pltpu.make_async_copy(matrices.at[pl.ds(2 * part, 2), at], held.at[:, at], in_sem.at[i])
         )
         reads[-1].start()
-    if between is not None:
-        between()
     for i in range(pieces):
         reads[i].wait()
 
@@ -225,28 +223,6 @@
         write.wait()
 
 
-def unbatch_pack_body(
-    part, matrices, points, values_hbm, across_hbm, out, packed_hbm,
-    held, rows, made, in_sem, out_sem, values, across, packed, sem,
-):
-    takes = [
-        pltpu.make_async_copy(values_hbm, values, sem.at[0]),
-        pltpu.make_async_copy(across_hbm, across, sem.at[1]),
-    ]
-    for take in takes:
-        take.start()
-    send = pltpu.make_async_copy(packed, packed_hbm, sem.at[2])
-
-    def between():
-        for take in takes:
-            take.wait()
-        arrange(points, values, across, packed)
-        send.start()
-
-    unbatch_body(part, matrices, out, held, rows, made, in_sem, out_sem, between)
-    send.wait()
-
-
 def arrange(points, values, across, packed):
     leaves = values.shape[1] // 128
     block = leaves // 2
@@ -264,39 +240,40 @@
             packed[side, block + j] = across[:, at]
 
 
-def unbatch_scratch(matrices):
-    nodes = matrices.shape[3]
-    return [
-        pltpu.VMEM((2, *matrices.shape[1:]), f32),
-        pltpu.VMEM((64 * PITCH, 128), f32),
-        pltpu.VMEM((nodes, 128, 128), bf16),
-        pltpu.SemaphoreType.DMA((4,)),
-        pltpu.SemaphoreType.DMA((-(-nodes // CHUNK),)),
+def pack_body(points, values_hbm, across_hbm, out_hbm, values, across, packed, sem):
+    takes = [
+        pltpu.make_async_copy(values_hbm, values, sem.at[0]),
+        pltpu.make_async_copy(across_hbm, across, sem.at[1]),
     ]
-
-
-def unbatch_pack(matrices, part, points, values, across):
+    for take in takes:
+        take.start()
+    for take in takes:
+        take.wait()
+    arrange(points, values, across, packed)
+    sends = [pltpu.make_async_copy(packed.at[i], out_hbm.at[i], sem.at[2 + i]) for i in range(2)]
+    for send in sends:
+        send.start()
+    for send in sends:
+        send.wait()
+
+
+def pack(points, values, across):
     columns, width = values.shape
     packed = (2, width // 128 + 3, columns, 128)
     return pl.pallas_call(
-        functools.partial(unbatch_pack_body, part),
-        out_shape=(
-            jax.ShapeDtypeStruct((matrices.shape[3], 128, 128), bf16),
-            jax.ShapeDtypeStruct(packed, f32),
-        ),
-        in_specs=[HBM, VM, HBM, HBM],
-        out_specs=(HBM, HBM),
+        pack_body,
+        out_shape=jax.ShapeDtypeStruct(packed, f32),
+        in_specs=[VM, HBM, HBM],
+        out_specs=HBM,
         scratch_shapes=[
-            *unbatch_scratch(matrices),
             pltpu.VMEM(values.shape, f32),
             pltpu.VMEM(values.shape, f32),
             pltpu.VMEM(packed, f32),
-            pltpu.SemaphoreType.DMA((3,)),
+            pltpu.SemaphoreType.DMA((4,)),
         ],
         compiler_params=pltpu.CompilerParams(vmem_limit_bytes=VMEM_BYTES),
-        cost_estimate=pl.CostEstimate(flops=1_000, bytes_accessed=1_000, transcendentals=0),
-        name="unbatch_pack",
-    )(matrices, points, values, across)
+        name="pack",
+    )(points, values, across)
 
 
 def unbatch(matrices, part):
@@ -306,7 +283,13 @@
         out_shape=jax.ShapeDtypeStruct((nodes, 128, 128), bf16),
         in_specs=[HBM],
         out_specs=HBM,
-        scratch_shapes=unbatch_scratch(matrices),
+        scratch_shapes=[
+            pltpu.VMEM((2, *matrices.shape[1:]), f32),
+            pltpu.VMEM((64 * PITCH, 128), f32),
+            pltpu.VMEM((nodes, 128, 128), bf16),
+            pltpu.SemaphoreType.DMA((4,)),
+            pltpu.SemaphoreType.DMA((-(-nodes // CHUNK),)),
+        ],
         compiler_params=pltpu.CompilerParams(vmem_limit_bytes=VMEM_BYTES),
         cost_estimate=pl.CostEstimate(flops=1_000, bytes_accessed=1_000, transcendentals=0),
         name="unbatch",
@@ -689,32 +672,34 @@
     core = core[None].astype(jnp.int32)
     place = position[None].astype(jnp.int32)
     coupling = coupling.transpose(1, 2, 3, 0)
+    first = unbatch(coupling, 0)
+    across, first, coupling = after((across, first, coupling))
+    packed = pack(points, values, across)
+    outward = [(2 * i, 2 * i + 2) for i in range(count - 1)]
+    outward += [(2 * i + 3, 2 * i + 1) for i in range(count - 1)]
+    beside = lax.ppermute(packed, ("leaf", "rhs"), outward)
+    place, packed = after((place, packed))
     up, share, trans, lists, live, codes = up_pass(
         place, near_list.T, near_count[None], partners.T, basis, values, transfer.transpose(1, 2, 0)
     )
+    begin = near_pass(12, core, lists, live, points, (packed,))
+    share, beside, begin = after((share, beside, begin))
     turned, spot = ring(share[None], 1)
-    share, coupling, across = after((share, coupling, across))
-    first, packed = unbatch_pack(coupling, 0, points, values, across)
-    turned, share, packed = after((turned, share, packed))
-    outward = [(2 * i, 2 * i + 2) for i in range(count - 1)]
-    outward += [(2 * i + 3, 2 * i + 1) for i in range(count - 1)]
-    beside = lax.ppermute(packed, ("leaf", "rhs"), outward)
+    passed = lax.dynamic_index_in_dim(beside, 1 - core[0], 0, keepdims=False)
+    passed = lax.ppermute(passed, "rhs", swap)
+    turned, passed, up = after((turned, passed, up))
     level = in_order(turned, share[None], spot)
     level = jnp.where(jnp.arange(128) < 64, level[0] + level[1], level[2] + level[3])[None]
     turned, spot = ring(level, 4)
-    begin = near_pass(12, core, lists, live, points, (packed,))
-    coupling, turned, beside, begin = after((coupling, turned, beside, begin))
+    up_low = lax.ppermute(up, "leaf", forward)
+    up_high = lax.ppermute(up, "leaf", backward)
+    mine, other = near_pass(12, core, lists, live, points, (beside, passed), begin)
+    turned, mine, other, coupling, up_low = after((turned, mine, other, coupling, up_low))
     level = in_order(turned, level, spot)
     turned, spot = ring(level, 16)
-    passed = lax.dynamic_index_in_dim(beside, 1 - core[0], 0, keepdims=False)
-    passed = lax.ppermute(passed, "rhs", swap)
-    turned, up, coupling = after((turned, up, coupling))
-    up_low = lax.ppermute(up, "leaf", forward)
-    up_high = lax.ppermute(up, "leaf", backward)
+    given = lax.ppermute(other, "rhs", swap)
     second = unbatch(coupling, 1)
-    passed, lists, second = after((passed, lists, second))
-    mine, other = near_pass(12, core, lists, live, points, (beside, passed), begin)
-    given = lax.ppermute(other, "rhs", swap)
+    turned, given, up_low, up_high, second = after((turned, given, up_low, up_high, second))
     return finish(
         core,
         place,

time: 122 us -> 115 us (0.943)
  the two profiles are of different devices: /device:TPU:30 before, /device:TPU:0 now
where the time goes in v11:
time: 115 us; the launch traced here: 114 us
  Pallas kernels  76.3 us (66%)
  starting transfers between devices  23.4 us (20%)
  waiting for transfers between devices  10.7 us (9%)
  local copies, waits for them, and re-layouts  3.1 us (3%)
    pallas_call x2, Pallas kernels, near_pass(): pl.pallas_call(functools.partial(near_body, unroll, chunks), out_shape=(s...  33.3 us
    pallas_call x1, Pallas kernels, finish(): pl.pallas_call(finish_body, out_shape=jax.ShapeDtypeStruct((columns, leav...  17.1 us
    ppermute x9, starting transfers between devices, ring(): turned.append(lax.ppermute(x, 'leaf', to))  12.3 us
    pallas_call x1, Pallas kernels, up_pass(): pl.pallas_call(up_body, out_shape=(jax.ShapeDtypeStruct((leaves, columns,...  11.4 us
    ppermute x9, waiting for transfers between devices, ring(): turned.append(lax.ppermute(x, 'leaf', to))  10.7 us
    pallas_call x2, Pallas kernels, unbatch(): pl.pallas_call(functools.partial(unbatch_body, part), out_shape=jax.Shape...  10.2 us
    ppermute x1, starting transfers between devices, local(): beside = lax.ppermute(packed, ('leaf', 'rhs'), outward)  4.91 us
    ppermute x1, starting transfers between devices, local(): up_low = lax.ppermute(up, 'leaf', forward)  4.83 us
  transfers between devices with their start and end apart: 15, of which 4 were waited for; matrix products, arithmetic and copies ran while one was open for 0% of the time, Pallas kernels for 48%

profile of v11, /device:TPU:0, one launch (start us, length us, event | category | flops | bytes accessed | tf_op | source)
XLA Modules:
  0.0 113.9 jit_solution(2888334510230349888)
XLA Ops:
  0.0 0.0 collective-permute-start
  0.0 5.1 %unbatch.2.first = bf16[127,128,128]{2,1,0:T(8,128)(2,1)} custom-call(f32[4,64,64,127]{3,2,1,0:T(8,128)} %bitcast.12), custom_call_target="tpu_custom_call" | custom-call | flops 1000 | bytes 1000 | tf_op jit(solution)/shard_map/unbatch/pallas_call | solution.py:281
  5.1 0.0 collective-permute-done.across_hbm
  5.1 0.0 copy-start.1
  5.1 1.0 copy-done.1
  6.1 4.3 %pack.1.refs_0_ = f32[2,67,32,128]{3,2,1,0:T(8,128)} custom-call(f32[3,8192]{1,0:T(4,128)} %targets.3, f32[32,8192]{1,0:T(8,128)} %values_hbm.3, f32[32,8192]{1,0:T(8,128)} %copy-done.1), custom_call_target="tpu_custom_call" | custom-call | tf_op jit(solution)/shard_map/pack/pallas_call | solution.py:263
  10.3 4.9 %collective-permute-start.1 = (f32[2,67,32,128]{3,2,1,0:T(8,128)}, f32[2,67,32,128]{3,2,1,0:T(8,128)}, u32[]{:S(2)}, u32[]{:S(2)}) collective-permute-start(f32[2,67,32,128]{3,2,1,0:T(8,128)} %pack.1.refs_0_), channel_id=1, source_target_pairs={{0,2},{2,4},{4,6},{6,8},{8,10},{10,12},{12,14},{14,16},{16,18},{18... | collective-permute-start | bytes 6586376 | tf_op jit(solution)/shard_map/ppermute | solution.py:680
  15.2 11.4 %up_pass.1 = (f32[64,32,128]{2,1,0:T(8,128)}, f32[32,128]{1,0:T(8,128)}, bf16[128,64,128]{2,1,0:T(8,128)(2,1)}, s32[2,28,64]{2,1,0:T(8,128)}, s32[2,64]{1,0:T(2,128)}, /*index=5*/s32[4,127]{1,0:T(4,128)}) custom-call(s32[1]{0:T(128)} %bitcast.1.place, s32[27,64]{1,0:T(8,128)} %bitcast.15, s32[1,64]{1,0:T(1,128)} %bitcast.21, s32[4,127]{1,0:T(4,128)} %bitcast.19, ...), custom_call_target="tpu_custom_call" | custom-call | flops 400000000 | bytes 8000000 | tf_op jit(solution)/shard_map/up_pass/pallas_call | solution.py:159
  26.6 0.0 copy-start.7
  26.6 21.2 %near_pass.2 = (f32[32,4096]{1,0:T(8,128)}, f32[32,4096]{1,0:T(8,128)}) custom-call(s32[1]{0:T(128)} %bitcast.core, s32[2,28,64]{2,1,0:T(8,128)} %get-tuple-element.47.lists, s32[2,64]{1,0:T(2,128)} %get-tuple-element.48.live, f32[3,8192]{1,0:T(4,128)} %targets.3, f32[2,67,32,128]{3,2,1,0:T(8,128)} %pack.1.refs_0_), custom_call_target="tpu_custom_call" | custom-call | flops 1000 | bytes 1000 | tf_op jit(solution)/shard_map/near_pass/pallas_call | solution.py:612
  47.9 0.0 collective-permute-done.1.refs_0_
  47.9 1.3 %dynamic-slice_bitcast_fusion = f32[67,32,128]{2,1,0:T(8,128)S(1)} fusion(f32[2,67,32,128]{3,2,1,0:T(8,128)} %collective-permute-done.1.refs_0_, s32[]{:T(128)S(6)} %select_n.144), kind=kLoop, calls=%fused_computation | loop fusion | bytes 2195460 | tf_op jit(solution)/shard_map/jit(dynamic_index_in_dim)/squeeze | solution.py:688
  49.2 0.1 collective-permute-start.5
  49.3 0.0 copy-done.7
  49.3 0.1 collective-permute-start.4
  49.4 0.1 collective-permute-start.3
  49.5 3.1 %collective-permute-start.2 = (f32[1,32,128]{2,1,0:T(8,128)S(1)}, f32[1,32,128]{2,1,0:T(8,128)S(1)}, u32[]{:S(2)}, u32[]{:S(2)}) collective-permute-start(f32[1,32,128]{2,1,0:T(8,128)S(1)} %bitcast.18), channel_id=1, source_target_pairs={{0,6},{2,0},{4,2},{6,4},{8,14},{10,8},{12,10},{14,12},{16,22},{18,... | collective-permute-start | bytes 49160 | tf_op jit(solution)/shard_map/ppermute | solution.py:658
  52.6 1.7 %collective-permute-done.4 = f32[1,32,128]{2,1,0:T(8,128)S(1)} collective-permute-done((f32[1,32,128]{2,1,0:T(8,128)S(1)}, f32[1,32,128]{2,1,0:T(8,128)S(1)}, u32[]{:S(2)}, u32[]{:S(2)}) %collective-permute-start.4) | collective-permute-done | bytes 16416 | tf_op jit(solution)/shard_map/ppermute | solution.py:658
  54.3 0.4 collective-permute-done.3
  54.7 0.6 collective-permute-done.2
  55.4 0.0 collective-permute-done.5.refs_1_
  55.4 4.8 %collective-permute-start.9 = (f32[64,32,128]{2,1,0:T(8,128)}, f32[64,32,128]{2,1,0:T(8,128)}, u32[]{:S(2)}, u32[]{:S(2)}) collective-permute-start(f32[64,32,128]{2,1,0:T(8,128)} %get-tuple-element.64.own), channel_id=1, source_target_pairs={{0,2},{2,4},{4,6},{6,8},{8,10},{10,12},{12,14},{14,16},{16,18},{18... | collective-permute-start | bytes 3145736 | tf_op jit(solution)/shard_map/ppermute | solution.py:694
  60.2 1.3 %collective-permute-start.14 = (f32[64,32,128]{2,1,0:T(8,128)}, f32[64,32,128]{2,1,0:T(8,128)}, u32[]{:S(2)}, u32[]{:S(2)}) collective-permute-start(f32[64,32,128]{2,1,0:T(8,128)} %get-tuple-element.64.own), channel_id=1, source_target_pairs={{2,0},{4,2},{6,4},{8,6},{10,8},{12,10},{14,12},{16,14},{18,16},{20... | collective-permute-start | bytes 3145736 | tf_op jit(solution)/shard_map/ppermute | solution.py:695
  61.5 1.8 %collective-permute-start.8 = (f32[1,32,128]{2,1,0:T(8,128)S(1)}, f32[1,32,128]{2,1,0:T(8,128)S(1)}, u32[]{:S(2)}, u32[]{:S(2)}) collective-permute-start(f32[1,32,128]{2,1,0:T(8,128)S(1)} %add_select_fusion), channel_id=1, source_target_pairs={{0,8},{2,10},{4,12},{6,14},{8,16},{10,18},{12,20},{14,22},{16,24},... | collective-permute-start | bytes 49160 | tf_op jit(solution)/shard_map/ppermute | solution.py:658
  63.3 1.9 %collective-permute-start.7 = (f32[1,32,128]{2,1,0:T(8,128)S(1)}, f32[1,32,128]{2,1,0:T(8,128)S(1)}, u32[]{:S(2)}, u32[]{:S(2)}) collective-permute-start(f32[1,32,128]{2,1,0:T(8,128)S(1)} %add_select_fusion), channel_id=1, source_target_pairs={{0,16},{2,18},{4,20},{6,22},{8,24},{10,26},{12,28},{14,30},{16,0},... | collective-permute-start | bytes 49160 | tf_op jit(solution)/shard_map/ppermute | solution.py:658
  65.2 0.9 collective-permute-start.6
  66.1 12.1 %near_pass.3 = (f32[32,4096]{1,0:T(8,128)}, f32[32,4096]{1,0:T(8,128)}) custom-call(s32[1]{0:T(128)} %bitcast.core, s32[2,28,64]{2,1,0:T(8,128)} %get-tuple-element.47.lists, s32[2,64]{1,0:T(2,128)} %get-tuple-element.48.live, f32[3,8192]{1,0:T(4,128)} %targets.3, f32[2,67,32,128]{3,2,1,0:T(8,128)} %collective-permute-done.1.refs_0_, ...), custom_call_target="tpu_custom_call" | custom-call | flops 1000 | bytes 1000 | tf_op jit(solution)/shard_map/near_pass/pallas_call | solution.py:612
  78.2 0.0 collective-permute-done.8
  78.2 0.0 collective-permute-done.7
  78.2 7.9 %collective-permute-done.6 = f32[1,32,128]{2,1,0:T(8,128)S(1)} collective-permute-done((f32[1,32,128]{2,1,0:T(8,128)S(1)}, f32[1,32,128]{2,1,0:T(8,128)S(1)}, u32[]{:S(2)}, u32[]{:S(2)}) %collective-permute-start.6) | collective-permute-done | bytes 16416 | tf_op jit(solution)/shard_map/ppermute | solution.py:658
  86.1 0.0 collective-permute-done.9.low
  86.1 0.0 collective-permute-start.13
  86.2 0.0 copy-start.3
  86.2 1.2 %collective-permute-start.12 = (f32[4,32,128]{2,1,0:T(8,128)S(1)}, f32[4,32,128]{2,1,0:T(8,128)S(1)}, u32[]{:S(2)}, u32[]{:S(2)}) collective-permute-start(f32[4,32,128]{2,1,0:T(8,128)S(1)} %pad_maximum_fusion.level), channel_id=1, source_target_pairs={{0,32},{2,34},{4,36},{6,38},{8,40},{10,42},{12,44},{14,46},{16,48}... | collective-permute-start | bytes 196616 | tf_op jit(solution)/shard_map/ppermute | solution.py:658
  87.4 2.2 %collective-permute-start.11 = (f32[4,32,128]{2,1,0:T(8,128)S(1)}, f32[4,32,128]{2,1,0:T(8,128)S(1)}, u32[]{:S(2)}, u32[]{:S(2)}) collective-permute-start(f32[4,32,128]{2,1,0:T(8,128)S(1)} %pad_maximum_fusion.level), channel_id=1, source_target_pairs={{0,64},{2,66},{4,68},{6,70},{8,72},{10,74},{12,76},{14,78},{16,80}... | collective-permute-start | bytes 196616 | tf_op jit(solution)/shard_map/ppermute | solution.py:658
  89.6 1.0 collective-permute-start.10
  90.6 5.2 %unbatch.3.second = bf16[127,128,128]{2,1,0:T(8,128)(2,1)} custom-call(f32[4,64,64,127]{3,2,1,0:T(8,128)} %bitcast.13), custom_call_target="tpu_custom_call" | custom-call | flops 1000 | bytes 1000 | tf_op jit(solution)/shard_map/unbatch/pallas_call | solution.py:281
  95.8 0.0 copy-done.3
  95.8 0.0 collective-permute-done.14.high
  95.8 0.0 collective-permute-done.12.one
  95.8 0.0 collective-permute-done.11.two
  95.8 0.0 collective-permute-done.10.three
  95.9 0.0 collective-permute-done.13.given
  95.9 0.6 copy-done.4
  96.4 0.0 copy-done.5
  96.4 0.0 copy-done.6
  96.5 0.2 copy-done.2
  96.7 17.1 %finish.1 = f32[32,8192]{1,0:T(8,128)} custom-call(s32[1]{0:T(128)} %bitcast.core, s32[1]{0:T(128)} %bitcast.1.place, s32[4,127]{1,0:T(4,128)} %get-tuple-element.45.codes, s32[4,60]{1,0:T(4,128)} %bitcast.20, f32[4,32,128]{2,1,0:T(8,128)} %copy-done.6, f32[4,32,128]{2,1,0:T(8,128)} %copy-done.5, f32[4,32,128]{2,1,0:T(8,128)} %copy-done.4, ...), custom_call_target="tpu_custom_call" | custom-call | flops 1000000000 | bytes 20000000 | tf_op jit(solution)/shard_map/finish/pallas_call | solution.py:476
  (10 shorter events, 0.1 us)
Async XLA Ops:
  0.0 5.1 %collective-permute-start = (f32[32,8192]{1,0:T(8,128)}, f32[32,8192]{1,0:T(8,128)S(1)}, u32[]{:S(2)}, u32[]{:S(2)}) collective-permute-start(f32[32,8192]{1,0:T(8,128)} %values_hbm.3), channel_id=1, source_target_pairs={{0,1},{1,0},{2,3},{3,2},{4,5},{5,4},{6,7},{7,6},{8,9},{9,8},{10,11... | collective-permute-start | bytes 3145736 | tf_op jit(solution)/shard_map/ppermute | solution.py:651
  5.1 1.0 copy-start.1
  10.3 37.6 %collective-permute-start.1 = (f32[2,67,32,128]{3,2,1,0:T(8,128)}, f32[2,67,32,128]{3,2,1,0:T(8,128)}, u32[]{:S(2)}, u32[]{:S(2)}) collective-permute-start(f32[2,67,32,128]{3,2,1,0:T(8,128)} %pack.1.refs_0_), channel_id=1, source_target_pairs={{0,2},{2,4},{4,6},{6,8},{8,10},{10,12},{12,14},{14,16},{16,18},{18... | collective-permute-start | bytes 6586376 | tf_op jit(solution)/shard_map/ppermute | solution.py:680
  26.6 22.7 %copy-start.7 = (f32[32,128]{1,0:T(8,128)S(1)}, f32[32,128]{1,0:T(8,128)}, u32[]{:S(2)}) copy-start(f32[32,128]{1,0:T(8,128)} %get-tuple-element.52) | copy-start | bytes 49156
  49.2 6.2 %collective-permute-start.5 = (f32[67,32,128]{2,1,0:T(8,128)S(1)}, f32[67,32,128]{2,1,0:T(8,128)S(1)}, u32[]{:S(2)}, u32[]{:S(2)}) collective-permute-start(f32[67,32,128]{2,1,0:T(8,128)S(1)} %dynamic-slice_bitcast_fusion), channel_id=1, source_target_pairs={{0,1},{1,0},{2,3},{3,2},{4,5},{5,4},{6,7},{7,6},{8,9},{9,8},{10,11... | collective-permute-start | bytes 3293192 | tf_op jit(solution)/shard_map/ppermute | solution.py:689
  49.3 5.0 %collective-permute-start.4 = (f32[1,32,128]{2,1,0:T(8,128)S(1)}, f32[1,32,128]{2,1,0:T(8,128)S(1)}, u32[]{:S(2)}, u32[]{:S(2)}) collective-permute-start(f32[1,32,128]{2,1,0:T(8,128)S(1)} %bitcast.16), channel_id=1, source_target_pairs={{0,2},{2,4},{4,6},{6,0},{8,10},{10,12},{12,14},{14,8},{16,18},{18,... | collective-permute-start | bytes 49160 | tf_op jit(solution)/shard_map/ppermute | solution.py:658
  49.4 5.3 %collective-permute-start.3 = (f32[1,32,128]{2,1,0:T(8,128)S(1)}, f32[1,32,128]{2,1,0:T(8,128)S(1)}, u32[]{:S(2)}, u32[]{:S(2)}) collective-permute-start(f32[1,32,128]{2,1,0:T(8,128)S(1)} %bitcast.17), channel_id=1, source_target_pairs={{0,4},{2,6},{4,0},{6,2},{8,12},{10,14},{12,8},{14,10},{16,20},{18,... | collective-permute-start | bytes 49160 | tf_op jit(solution)/shard_map/ppermute | solution.py:658
  49.5 5.9 %collective-permute-start.2 = (f32[1,32,128]{2,1,0:T(8,128)S(1)}, f32[1,32,128]{2,1,0:T(8,128)S(1)}, u32[]{:S(2)}, u32[]{:S(2)}) collective-permute-start(f32[1,32,128]{2,1,0:T(8,128)S(1)} %bitcast.18), channel_id=1, source_target_pairs={{0,6},{2,0},{4,2},{6,4},{8,14},{10,8},{12,10},{14,12},{16,22},{18,... | collective-permute-start | bytes 49160 | tf_op jit(solution)/shard_map/ppermute | solution.py:658
  55.4 10.7 %copy-start = (f32[67,32,128]{2,1,0:T(8,128)}, f32[67,32,128]{2,1,0:T(8,128)S(1)}, u32[]{:S(2)}) copy-start(f32[67,32,128]{2,1,0:T(8,128)S(1)} %collective-permute-done.5.refs_1_) | copy-start | bytes 3293188
  55.4 30.7 %collective-permute-start.9 = (f32[64,32,128]{2,1,0:T(8,128)}, f32[64,32,128]{2,1,0:T(8,128)}, u32[]{:S(2)}, u32[]{:S(2)}) collective-permute-start(f32[64,32,128]{2,1,0:T(8,128)} %get-tuple-element.64.own), channel_id=1, source_target_pairs={{0,2},{2,4},{4,6},{6,8},{8,10},{10,12},{12,14},{14,16},{16,18},{18... | collective-permute-start | bytes 3145736 | tf_op jit(solution)/shard_map/ppermute | solution.py:694
  60.2 35.6 %collective-permute-start.14 = (f32[64,32,128]{2,1,0:T(8,128)}, f32[64,32,128]{2,1,0:T(8,128)}, u32[]{:S(2)}, u32[]{:S(2)}) collective-permute-start(f32[64,32,128]{2,1,0:T(8,128)} %get-tuple-element.64.own), channel_id=1, source_target_pairs={{2,0},{4,2},{6,4},{8,6},{10,8},{12,10},{14,12},{16,14},{18,16},{20... | collective-permute-start | bytes 3145736 | tf_op jit(solution)/shard_map/ppermute | solution.py:695
  61.5 16.6 %collective-permute-start.8 = (f32[1,32,128]{2,1,0:T(8,128)S(1)}, f32[1,32,128]{2,1,0:T(8,128)S(1)}, u32[]{:S(2)}, u32[]{:S(2)}) collective-permute-start(f32[1,32,128]{2,1,0:T(8,128)S(1)} %add_select_fusion), channel_id=1, source_target_pairs={{0,8},{2,10},{4,12},{6,14},{8,16},{10,18},{12,20},{14,22},{16,24},... | collective-permute-start | bytes 49160 | tf_op jit(solution)/shard_map/ppermute | solution.py:658
  63.3 14.9 %collective-permute-start.7 = (f32[1,32,128]{2,1,0:T(8,128)S(1)}, f32[1,32,128]{2,1,0:T(8,128)S(1)}, u32[]{:S(2)}, u32[]{:S(2)}) collective-permute-start(f32[1,32,128]{2,1,0:T(8,128)S(1)} %add_select_fusion), channel_id=1, source_target_pairs={{0,16},{2,18},{4,20},{6,22},{8,24},{10,26},{12,28},{14,30},{16,0},... | collective-permute-start | bytes 49160 | tf_op jit(solution)/shard_map/ppermute | solution.py:658
  65.2 20.9 %collective-permute-start.6 = (f32[1,32,128]{2,1,0:T(8,128)S(1)}, f32[1,32,128]{2,1,0:T(8,128)S(1)}, u32[]{:S(2)}, u32[]{:S(2)}) collective-permute-start(f32[1,32,128]{2,1,0:T(8,128)S(1)} %add_select_fusion), channel_id=1, source_target_pairs={{0,24},{2,26},{4,28},{6,30},{8,0},{10,2},{12,4},{14,6},{16,8},{18,... | collective-permute-start | bytes 49160 | tf_op jit(solution)/shard_map/ppermute | solution.py:658
  86.1 9.7 %collective-permute-start.13 = (f32[32,4096]{1,0:T(8,128)}, f32[32,4096]{1,0:T(8,128)S(1)}, u32[]{:S(2)}, u32[]{:S(2)}) collective-permute-start(f32[32,4096]{1,0:T(8,128)} %get-tuple-element.68), channel_id=1, source_target_pairs={{0,1},{1,0},{2,3},{3,2},{4,5},{5,4},{6,7},{7,6},{8,9},{9,8},{10,11... | collective-permute-start | bytes 1572872 | tf_op jit(solution)/shard_map/ppermute | solution.py:700
  86.2 9.6 %copy-start.3 = (f32[4,32,128]{2,1,0:T(8,128)}, f32[4,32,128]{2,1,0:T(8,128)S(1)}, u32[]{:S(2)}) copy-start(f32[4,32,128]{2,1,0:T(8,128)S(1)} %pad_maximum_fusion.level) | copy-start | bytes 196612
  86.2 9.6 %collective-permute-start.12 = (f32[4,32,128]{2,1,0:T(8,128)S(1)}, f32[4,32,128]{2,1,0:T(8,128)S(1)}, u32[]{:S(2)}, u32[]{:S(2)}) collective-permute-start(f32[4,32,128]{2,1,0:T(8,128)S(1)} %pad_maximum_fusion.level), channel_id=1, source_target_pairs={{0,32},{2,34},{4,36},{6,38},{8,40},{10,42},{12,44},{14,46},{16,48}... | collective-permute-start | bytes 196616 | tf_op jit(solution)/shard_map/ppermute | solution.py:658
  87.4 8.4 %collective-permute-start.11 = (f32[4,32,128]{2,1,0:T(8,128)S(1)}, f32[4,32,128]{2,1,0:T(8,128)S(1)}, u32[]{:S(2)}, u32[]{:S(2)}) collective-permute-start(f32[4,32,128]{2,1,0:T(8,128)S(1)} %pad_maximum_fusion.level), channel_id=1, source_target_pairs={{0,64},{2,66},{4,68},{6,70},{8,72},{10,74},{12,76},{14,78},{16,80}... | collective-permute-start | bytes 196616 | tf_op jit(solution)/shard_map/ppermute | solution.py:658
  89.6 6.2 %collective-permute-start.10 = (f32[4,32,128]{2,1,0:T(8,128)S(1)}, f32[4,32,128]{2,1,0:T(8,128)S(1)}, u32[]{:S(2)}, u32[]{:S(2)}) collective-permute-start(f32[4,32,128]{2,1,0:T(8,128)S(1)} %pad_maximum_fusion.level), channel_id=1, source_target_pairs={{0,96},{2,98},{4,100},{6,102},{8,104},{10,106},{12,108},{14,110},{... | collective-permute-start | bytes 196616 | tf_op jit(solution)/shard_map/ppermute | solution.py:658
  95.8 0.6 copy-start.4
  95.8 0.6 copy-start.5
  95.8 0.6 copy-start.6
  95.9 0.8 copy-start.2

commit v12 on v11

--- a/solution.py
+++ b/solution.py
@@ -223,15 +223,26 @@
         write.wait()
 
 
-def arrange(points, values, across, packed):
+def pack_body(points, values_hbm, across_hbm, out_hbm, values, across, packed, sem):
     leaves = values.shape[1] // 128
     block = leaves // 2
+    takes = []
+    for side in range(2):
+        at = pl.ds(side * block * 128, block * 128)
+        for k, (source, dest) in enumerate(((values_hbm, values), (across_hbm, across))):
+            takes.append(
+                pltpu.make_async_copy(source.at[:, at], dest.at[:, at], sem.at[2 * side + k])
+            )
+            takes[-1].start()
     for c in range(3):
         for j in range(leaves):
             packed[j // block, 2 * block + c, j % block : j % block + 1] = points[
                 c : c + 1, 128 * j : 128 * j + 128
             ]
+    sends = []
     for side in range(2):
+        takes[2 * side].wait()
+        takes[2 * side + 1].wait()
 
         @pl.loop(0, block, unroll=8)
         def _(j, side=side):
@@ -239,20 +250,8 @@
             packed[side, j] = values[:, at]
             packed[side, block + j] = across[:, at]
 
-
-def pack_body(points, values_hbm, across_hbm, out_hbm, values, across, packed, sem):
-    takes = [
-        pltpu.make_async_copy(values_hbm, values, sem.at[0]),
-        pltpu.make_async_copy(across_hbm, across, sem.at[1]),
-    ]
-    for take in takes:
-        take.start()
-    for take in takes:
-        take.wait()
-    arrange(points, values, across, packed)
-    sends = [pltpu.make_async_copy(packed.at[i], out_hbm.at[i], sem.at[2 + i]) for i in range(2)]
-    for send in sends:
-        send.start()
+        sends.append(pltpu.make_async_copy(packed.at[side], out_hbm.at[side], sem.at[4 + side]))
+        sends[-1].start()
     for send in sends:
         send.wait()
 
@@ -269,7 +268,7 @@
             pltpu.VMEM(values.shape, f32),
             pltpu.VMEM(values.shape, f32),
             pltpu.VMEM(packed, f32),
-            pltpu.SemaphoreType.DMA((4,)),
+            pltpu.SemaphoreType.DMA((6,)),
         ],
         compiler_params=pltpu.CompilerParams(vmem_limit_bytes=VMEM_BYTES),
         name="pack",
@@ -687,19 +686,19 @@
     turned, spot = ring(share[None], 1)
     passed = lax.dynamic_index_in_dim(beside, 1 - core[0], 0, keepdims=False)
     passed = lax.ppermute(passed, "rhs", swap)
-    turned, passed, up = after((turned, passed, up))
     level = in_order(turned, share[None], spot)
     level = jnp.where(jnp.arange(128) < 64, level[0] + level[1], level[2] + level[3])[None]
     turned, spot = ring(level, 4)
+    level = in_order(turned, level, spot)
+    turned, spot = ring(level, 16)
+    turned, passed, up = after((turned, passed, up))
     up_low = lax.ppermute(up, "leaf", forward)
     up_high = lax.ppermute(up, "leaf", backward)
     mine, other = near_pass(12, core, lists, live, points, (beside, passed), begin)
-    turned, mine, other, coupling, up_low = after((turned, mine, other, coupling, up_low))
-    level = in_order(turned, level, spot)
-    turned, spot = ring(level, 16)
+    mine, other, coupling = after((mine, other, coupling))
     given = lax.ppermute(other, "rhs", swap)
     second = unbatch(coupling, 1)
-    turned, given, up_low, up_high, second = after((turned, given, up_low, up_high, second))
+    given, up_low, up_high, second = after((given, up_low, up_high, second))
     return finish(
         core,
         place,

time: 115 us -> 118 us (1.026)
  the two profiles are of different devices: /device:TPU:0 before, /device:TPU:32 now
where the time goes in v12:
time: 118 us; the launch traced here: 117 us
  Pallas kernels  68.1 us (58%)
  waiting for transfers between devices  24.2 us (21%)
  starting transfers between devices  21.7 us (18%)
  local copies, waits for them, and re-layouts  2.31 us (2%)
    pallas_call x2, Pallas kernels, near_pass(): pl.pallas_call(functools.partial(near_body, unroll, chunks), out_shape=(s...  25.7 us
    pallas_call x1, Pallas kernels, finish(): pl.pallas_call(finish_body, out_shape=jax.ShapeDtypeStruct((columns, leav...  17.1 us
    ppermute x9, waiting for transfers between devices, ring(): turned.append(lax.ppermute(x, 'leaf', to))  11.8 us
    ppermute x9, starting transfers between devices, ring(): turned.append(lax.ppermute(x, 'leaf', to))  11.6 us
    pallas_call x1, Pallas kernels, up_pass(): pl.pallas_call(up_body, out_shape=(jax.ShapeDtypeStruct((leaves, columns,...  11.4 us
    pallas_call x2, Pallas kernels, unbatch(): pl.pallas_call(functools.partial(unbatch_body, part), out_shape=jax.Shape...  10.2 us
    ppermute x1, waiting for transfers between devices, local(): up_low = lax.ppermute(up, 'leaf', forward)  7.34 us
    ppermute x1, waiting for transfers between devices, local(): beside = lax.ppermute(packed, ('leaf', 'rhs'), outward)  5.03 us
  transfers between devices with their start and end apart: 15, of which 8 were waited for; matrix products, arithmetic and copies ran while one was open for 0% of the time, Pallas kernels for 40%

profile of v12, /device:TPU:32, one launch (start us, length us, event | category | flops | bytes accessed | tf_op | source)
XLA Modules:
  0.0 116.7 jit_solution(1678631393971036574)
XLA Ops:
  0.0 0.0 collective-permute-start
  0.0 5.1 %unbatch.2.first = bf16[127,128,128]{2,1,0:T(8,128)(2,1)} custom-call(f32[4,64,64,127]{3,2,1,0:T(8,128)} %bitcast.12), custom_call_target="tpu_custom_call" | custom-call | flops 1000 | bytes 1000 | tf_op jit(solution)/shard_map/unbatch/pallas_call | solution.py:280
  5.1 0.0 collective-permute-done.across_hbm
  5.1 0.0 copy-start.1
  5.1 1.0 copy-done.1
  6.1 3.7 %pack.1.refs_0_ = f32[2,67,32,128]{3,2,1,0:T(8,128)} custom-call(f32[3,8192]{1,0:T(4,128)} %targets.3, f32[32,8192]{1,0:T(8,128)} %values_hbm.3, f32[32,8192]{1,0:T(8,128)} %copy-done.1), custom_call_target="tpu_custom_call" | custom-call | tf_op jit(solution)/shard_map/pack/pallas_call | solution.py:262
  9.8 3.5 %collective-permute-start.1 = (f32[2,67,32,128]{3,2,1,0:T(8,128)}, f32[2,67,32,128]{3,2,1,0:T(8,128)}, u32[]{:S(2)}, u32[]{:S(2)}) collective-permute-start(f32[2,67,32,128]{3,2,1,0:T(8,128)} %pack.1.refs_0_), channel_id=1, source_target_pairs={{0,2},{2,4},{4,6},{6,8},{8,10},{10,12},{12,14},{14,16},{16,18},{18... | collective-permute-start | bytes 6586376 | tf_op jit(solution)/shard_map/ppermute | solution.py:679
  13.3 11.4 %up_pass.1 = (f32[64,32,128]{2,1,0:T(8,128)}, f32[32,128]{1,0:T(8,128)}, bf16[128,64,128]{2,1,0:T(8,128)(2,1)}, s32[2,28,64]{2,1,0:T(8,128)}, s32[2,64]{1,0:T(2,128)}, /*index=5*/s32[4,127]{1,0:T(4,128)}) custom-call(s32[1]{0:T(128)} %bitcast.1.place, s32[27,64]{1,0:T(8,128)} %bitcast.15, s32[1,64]{1,0:T(1,128)} %bitcast.21, s32[4,127]{1,0:T(4,128)} %bitcast.19, ...), custom_call_target="tpu_custom_call" | custom-call | flops 400000000 | bytes 8000000 | tf_op jit(solution)/shard_map/up_pass/pallas_call | solution.py:159
  24.7 0.0 copy-start.7
  24.7 13.6 %near_pass.2 = (f32[32,4096]{1,0:T(8,128)}, f32[32,4096]{1,0:T(8,128)}) custom-call(s32[1]{0:T(128)} %bitcast.core, s32[2,28,64]{2,1,0:T(8,128)} %get-tuple-element.40.lists, s32[2,64]{1,0:T(2,128)} %get-tuple-element.41.live, f32[3,8192]{1,0:T(4,128)} %targets.3, f32[2,67,32,128]{3,2,1,0:T(8,128)} %pack.1.refs_0_), custom_call_target="tpu_custom_call" | custom-call | flops 1000 | bytes 1000 | tf_op jit(solution)/shard_map/near_pass/pallas_call | solution.py:611
  38.3 5.0 %collective-permute-done.1.refs_0_ = f32[2,67,32,128]{3,2,1,0:T(8,128)} collective-permute-done((f32[2,67,32,128]{3,2,1,0:T(8,128)}, f32[2,67,32,128]{3,2,1,0:T(8,128)}, u32[]{:S(2)}, u32[]{:S(2)}) %collective-permute-start.1) | collective-permute-done | bytes 2195488 | tf_op jit(solution)/shard_map/ppermute | solution.py:679
  43.3 1.3 %dynamic-slice_bitcast_fusion = f32[67,32,128]{2,1,0:T(8,128)S(1)} fusion(f32[2,67,32,128]{3,2,1,0:T(8,128)} %collective-permute-done.1.refs_0_, s32[]{:T(128)S(6)} %select_n.175), kind=kLoop, calls=%fused_computation | loop fusion | bytes 2195460 | tf_op jit(solution)/shard_map/jit(dynamic_index_in_dim)/squeeze | solution.py:687
  44.6 0.1 collective-permute-start.11
  44.7 0.0 copy-done.7
  44.7 0.2 collective-permute-start.4
  45.0 0.0 collective-permute-start.3
  45.0 1.9 %collective-permute-start.2 = (f32[1,32,128]{2,1,0:T(8,128)S(1)}, f32[1,32,128]{2,1,0:T(8,128)S(1)}, u32[]{:S(2)}, u32[]{:S(2)}) collective-permute-start(f32[1,32,128]{2,1,0:T(8,128)S(1)} %bitcast.18), channel_id=1, source_target_pairs={{0,2},{2,4},{4,6},{6,0},{8,10},{10,12},{12,14},{14,8},{16,18},{18,... | collective-permute-start | bytes 49160 | tf_op jit(solution)/shard_map/ppermute | solution.py:657
  46.8 1.7 %collective-permute-done.4 = f32[1,32,128]{2,1,0:T(8,128)S(1)} collective-permute-done((f32[1,32,128]{2,1,0:T(8,128)S(1)}, f32[1,32,128]{2,1,0:T(8,128)S(1)}, u32[]{:S(2)}, u32[]{:S(2)}) %collective-permute-start.4) | collective-permute-done | bytes 16416 | tf_op jit(solution)/shard_map/ppermute | solution.py:657
  48.5 1.7 %collective-permute-done.3 = f32[1,32,128]{2,1,0:T(8,128)S(1)} collective-permute-done((f32[1,32,128]{2,1,0:T(8,128)S(1)}, f32[1,32,128]{2,1,0:T(8,128)S(1)}, u32[]{:S(2)}, u32[]{:S(2)}) %collective-permute-start.3) | collective-permute-done | bytes 16416 | tf_op jit(solution)/shard_map/ppermute | solution.py:657
  50.2 1.0 collective-permute-done.2
  51.2 3.9 %collective-permute-start.7 = (f32[1,32,128]{2,1,0:T(8,128)S(1)}, f32[1,32,128]{2,1,0:T(8,128)S(1)}, u32[]{:S(2)}, u32[]{:S(2)}) collective-permute-start(f32[1,32,128]{2,1,0:T(8,128)S(1)} %add_select_fusion), channel_id=1, source_target_pairs={{0,24},{2,26},{4,28},{6,30},{8,0},{10,2},{12,4},{14,6},{16,8},{18,... | collective-permute-start | bytes 49160 | tf_op jit(solution)/shard_map/ppermute | solution.py:657
  55.2 0.0 collective-permute-start.6
  55.2 0.9 collective-permute-start.5
  56.1 0.5 collective-permute-done.7
  56.6 3.8 %collective-permute-done.6 = f32[1,32,128]{2,1,0:T(8,128)S(1)} collective-permute-done((f32[1,32,128]{2,1,0:T(8,128)S(1)}, f32[1,32,128]{2,1,0:T(8,128)S(1)}, u32[]{:S(2)}, u32[]{:S(2)}) %collective-permute-start.6) | collective-permute-done | bytes 16416 | tf_op jit(solution)/shard_map/ppermute | solution.py:657
  60.4 0.0 collective-permute-done.5
  60.4 0.0 copy-start.3
  60.5 2.0 %collective-permute-start.10 = (f32[4,32,128]{2,1,0:T(8,128)S(1)}, f32[4,32,128]{2,1,0:T(8,128)S(1)}, u32[]{:S(2)}, u32[]{:S(2)}) collective-permute-start(f32[4,32,128]{2,1,0:T(8,128)S(1)} %pad_maximum_fusion.level), channel_id=1, source_target_pairs={{0,32},{2,34},{4,36},{6,38},{8,40},{10,42},{12,44},{14,46},{16,48}... | collective-permute-start | bytes 196616 | tf_op jit(solution)/shard_map/ppermute | solution.py:657
  62.4 0.4 collective-permute-start.9
  62.9 2.2 %collective-permute-start.8 = (f32[4,32,128]{2,1,0:T(8,128)S(1)}, f32[4,32,128]{2,1,0:T(8,128)S(1)}, u32[]{:S(2)}, u32[]{:S(2)}) collective-permute-start(f32[4,32,128]{2,1,0:T(8,128)S(1)} %pad_maximum_fusion.level), channel_id=1, source_target_pairs={{0,96},{2,98},{4,100},{6,102},{8,104},{10,106},{12,108},{14,110},{... | collective-permute-start | bytes 196616 | tf_op jit(solution)/shard_map/ppermute | solution.py:657
  65.1 0.0 collective-permute-done.10.one
  65.1 3.1 %collective-permute-done.9.two = f32[4,32,128]{2,1,0:T(8,128)S(1)} collective-permute-done((f32[4,32,128]{2,1,0:T(8,128)S(1)}, f32[4,32,128]{2,1,0:T(8,128)S(1)}, u32[]{:S(2)}, u32[]{:S(2)}) %collective-permute-start.9) | collective-permute-done | bytes 65568 | tf_op jit(solution)/shard_map/ppermute | solution.py:657
  68.2 0.0 collective-permute-done.8.three
  68.2 0.0 collective-permute-done.11.refs_1_
  68.2 0.0 copy-start
  68.2 4.3 %collective-permute-start.14 = (f32[64,32,128]{2,1,0:T(8,128)}, f32[64,32,128]{2,1,0:T(8,128)}, u32[]{:S(2)}, u32[]{:S(2)}) collective-permute-start(f32[64,32,128]{2,1,0:T(8,128)} %get-tuple-element.59.own), channel_id=1, source_target_pairs={{2,0},{4,2},{6,4},{8,6},{10,8},{12,10},{14,12},{16,14},{18,16},{20... | collective-permute-start | bytes 3145736 | tf_op jit(solution)/shard_map/ppermute | solution.py:696
  72.5 1.9 %collective-permute-start.13 = (f32[64,32,128]{2,1,0:T(8,128)}, f32[64,32,128]{2,1,0:T(8,128)}, u32[]{:S(2)}, u32[]{:S(2)}) collective-permute-start(f32[64,32,128]{2,1,0:T(8,128)} %get-tuple-element.59.own), channel_id=1, source_target_pairs={{0,2},{2,4},{4,6},{6,8},{8,10},{10,12},{12,14},{14,16},{16,18},{18... | collective-permute-start | bytes 3145736 | tf_op jit(solution)/shard_map/ppermute | solution.py:695
  74.5 0.0 copy-done
  74.5 12.1 %near_pass.3 = (f32[32,4096]{1,0:T(8,128)}, f32[32,4096]{1,0:T(8,128)}) custom-call(s32[1]{0:T(128)} %bitcast.core, s32[2,28,64]{2,1,0:T(8,128)} %get-tuple-element.40.lists, s32[2,64]{1,0:T(2,128)} %get-tuple-element.41.live, f32[3,8192]{1,0:T(4,128)} %targets.3, f32[2,67,32,128]{3,2,1,0:T(8,128)} %collective-permute-done.1.refs_0_, ...), custom_call_target="tpu_custom_call" | custom-call | flops 1000 | bytes 1000 | tf_op jit(solution)/shard_map/near_pass/pallas_call | solution.py:611
  86.6 0.3 collective-permute-start.12
  86.9 5.1 %unbatch.3.second = bf16[127,128,128]{2,1,0:T(8,128)(2,1)} custom-call(f32[4,64,64,127]{3,2,1,0:T(8,128)} %bitcast.13), custom_call_target="tpu_custom_call" | custom-call | flops 1000 | bytes 1000 | tf_op jit(solution)/shard_map/unbatch/pallas_call | solution.py:280
  92.0 0.0 copy-done.3
  92.0 0.0 copy-done.4
  92.0 0.0 copy-done.5
  92.0 0.0 collective-permute-done.12.given
  92.1 0.0 collective-permute-done.14.high
  92.1 7.3 %collective-permute-done.13.low = f32[64,32,128]{2,1,0:T(8,128)} collective-permute-done((f32[64,32,128]{2,1,0:T(8,128)}, f32[64,32,128]{2,1,0:T(8,128)}, u32[]{:S(2)}, u32[]{:S(2)}) %collective-permute-start.13) | collective-permute-done | bytes 1048608 | tf_op jit(solution)/shard_map/ppermute | solution.py:695
  99.4 17.1 %finish.1 = f32[32,8192]{1,0:T(8,128)} custom-call(s32[1]{0:T(128)} %bitcast.core, s32[1]{0:T(128)} %bitcast.1.place, s32[4,127]{1,0:T(4,128)} %get-tuple-element.38.codes, s32[4,60]{1,0:T(4,128)} %bitcast.20, f32[4,32,128]{2,1,0:T(8,128)} %copy-done.6, f32[4,32,128]{2,1,0:T(8,128)} %copy-done.5, f32[4,32,128]{2,1,0:T(8,128)} %copy-done.4, ...), custom_call_target="tpu_custom_call" | custom-call | flops 1000000000 | bytes 20000000 | tf_op jit(solution)/shard_map/finish/pallas_call | solution.py:475
  (10 shorter events, 0.0 us)
Async XLA Ops:
  0.0 5.1 %collective-permute-start = (f32[32,8192]{1,0:T(8,128)}, f32[32,8192]{1,0:T(8,128)S(1)}, u32[]{:S(2)}, u32[]{:S(2)}) collective-permute-start(f32[32,8192]{1,0:T(8,128)} %values_hbm.3), channel_id=1, source_target_pairs={{0,1},{1,0},{2,3},{3,2},{4,5},{5,4},{6,7},{7,6},{8,9},{9,8},{10,11... | collective-permute-start | bytes 3145736 | tf_op jit(solution)/shard_map/ppermute | solution.py:650
  5.1 1.0 copy-start.1
  9.8 33.5 %collective-permute-start.1 = (f32[2,67,32,128]{3,2,1,0:T(8,128)}, f32[2,67,32,128]{3,2,1,0:T(8,128)}, u32[]{:S(2)}, u32[]{:S(2)}) collective-permute-start(f32[2,67,32,128]{3,2,1,0:T(8,128)} %pack.1.refs_0_), channel_id=1, source_target_pairs={{0,2},{2,4},{4,6},{6,8},{8,10},{10,12},{12,14},{14,16},{16,18},{18... | collective-permute-start | bytes 6586376 | tf_op jit(solution)/shard_map/ppermute | solution.py:679
  24.7 20.0 %copy-start.7 = (f32[32,128]{1,0:T(8,128)S(1)}, f32[32,128]{1,0:T(8,128)}, u32[]{:S(2)}) copy-start(f32[32,128]{1,0:T(8,128)} %get-tuple-element.45) | copy-start | bytes 49156
  44.6 23.6 %collective-permute-start.11 = (f32[67,32,128]{2,1,0:T(8,128)S(1)}, f32[67,32,128]{2,1,0:T(8,128)S(1)}, u32[]{:S(2)}, u32[]{:S(2)}) collective-permute-start(f32[67,32,128]{2,1,0:T(8,128)S(1)} %dynamic-slice_bitcast_fusion), channel_id=1, source_target_pairs={{0,1},{1,0},{2,3},{3,2},{4,5},{5,4},{6,7},{7,6},{8,9},{9,8},{10,11... | collective-permute-start | bytes 3293192 | tf_op jit(solution)/shard_map/ppermute | solution.py:688
  44.7 3.8 %collective-permute-start.4 = (f32[1,32,128]{2,1,0:T(8,128)S(1)}, f32[1,32,128]{2,1,0:T(8,128)S(1)}, u32[]{:S(2)}, u32[]{:S(2)}) collective-permute-start(f32[1,32,128]{2,1,0:T(8,128)S(1)} %bitcast.16), channel_id=1, source_target_pairs={{0,6},{2,0},{4,2},{6,4},{8,14},{10,8},{12,10},{14,12},{16,22},{18,... | collective-permute-start | bytes 49160 | tf_op jit(solution)/shard_map/ppermute | solution.py:657
  45.0 5.2 %collective-permute-start.3 = (f32[1,32,128]{2,1,0:T(8,128)S(1)}, f32[1,32,128]{2,1,0:T(8,128)S(1)}, u32[]{:S(2)}, u32[]{:S(2)}) collective-permute-start(f32[1,32,128]{2,1,0:T(8,128)S(1)} %bitcast.17), channel_id=1, source_target_pairs={{0,4},{2,6},{4,0},{6,2},{8,12},{10,14},{12,8},{14,10},{16,20},{18,... | collective-permute-start | bytes 49160 | tf_op jit(solution)/shard_map/ppermute | solution.py:657
  45.0 6.2 %collective-permute-start.2 = (f32[1,32,128]{2,1,0:T(8,128)S(1)}, f32[1,32,128]{2,1,0:T(8,128)S(1)}, u32[]{:S(2)}, u32[]{:S(2)}) collective-permute-start(f32[1,32,128]{2,1,0:T(8,128)S(1)} %bitcast.18), channel_id=1, source_target_pairs={{0,2},{2,4},{4,6},{6,0},{8,10},{10,12},{12,14},{14,8},{16,18},{18,... | collective-permute-start | bytes 49160 | tf_op jit(solution)/shard_map/ppermute | solution.py:657
  51.2 5.4 %collective-permute-start.7 = (f32[1,32,128]{2,1,0:T(8,128)S(1)}, f32[1,32,128]{2,1,0:T(8,128)S(1)}, u32[]{:S(2)}, u32[]{:S(2)}) collective-permute-start(f32[1,32,128]{2,1,0:T(8,128)S(1)} %add_select_fusion), channel_id=1, source_target_pairs={{0,24},{2,26},{4,28},{6,30},{8,0},{10,2},{12,4},{14,6},{16,8},{18,... | collective-permute-start | bytes 49160 | tf_op jit(solution)/shard_map/ppermute | solution.py:657
  55.2 5.2 %collective-permute-start.6 = (f32[1,32,128]{2,1,0:T(8,128)S(1)}, f32[1,32,128]{2,1,0:T(8,128)S(1)}, u32[]{:S(2)}, u32[]{:S(2)}) collective-permute-start(f32[1,32,128]{2,1,0:T(8,128)S(1)} %add_select_fusion), channel_id=1, source_target_pairs={{0,16},{2,18},{4,20},{6,22},{8,24},{10,26},{12,28},{14,30},{16,0},... | collective-permute-start | bytes 49160 | tf_op jit(solution)/shard_map/ppermute | solution.py:657
  55.2 5.2 %collective-permute-start.5 = (f32[1,32,128]{2,1,0:T(8,128)S(1)}, f32[1,32,128]{2,1,0:T(8,128)S(1)}, u32[]{:S(2)}, u32[]{:S(2)}) collective-permute-start(f32[1,32,128]{2,1,0:T(8,128)S(1)} %add_select_fusion), channel_id=1, source_target_pairs={{0,8},{2,10},{4,12},{6,14},{8,16},{10,18},{12,20},{14,22},{16,24},... | collective-permute-start | bytes 49160 | tf_op jit(solution)/shard_map/ppermute | solution.py:657
  60.4 31.5 %copy-start.3 = (f32[4,32,128]{2,1,0:T(8,128)}, f32[4,32,128]{2,1,0:T(8,128)S(1)}, u32[]{:S(2)}) copy-start(f32[4,32,128]{2,1,0:T(8,128)S(1)} %pad_maximum_fusion.level) | copy-start | bytes 196612
  60.5 4.7 %collective-permute-start.10 = (f32[4,32,128]{2,1,0:T(8,128)S(1)}, f32[4,32,128]{2,1,0:T(8,128)S(1)}, u32[]{:S(2)}, u32[]{:S(2)}) collective-permute-start(f32[4,32,128]{2,1,0:T(8,128)S(1)} %pad_maximum_fusion.level), channel_id=1, source_target_pairs={{0,32},{2,34},{4,36},{6,38},{8,40},{10,42},{12,44},{14,46},{16,48}... | collective-permute-start | bytes 196616 | tf_op jit(solution)/shard_map/ppermute | solution.py:657
  62.4 5.8 %collective-permute-start.9 = (f32[4,32,128]{2,1,0:T(8,128)S(1)}, f32[4,32,128]{2,1,0:T(8,128)S(1)}, u32[]{:S(2)}, u32[]{:S(2)}) collective-permute-start(f32[4,32,128]{2,1,0:T(8,128)S(1)} %pad_maximum_fusion.level), channel_id=1, source_target_pairs={{0,64},{2,66},{4,68},{6,70},{8,72},{10,74},{12,76},{14,78},{16,80}... | collective-permute-start | bytes 196616 | tf_op jit(solution)/shard_map/ppermute | solution.py:657
  62.9 5.4 %collective-permute-start.8 = (f32[4,32,128]{2,1,0:T(8,128)S(1)}, f32[4,32,128]{2,1,0:T(8,128)S(1)}, u32[]{:S(2)}, u32[]{:S(2)}) collective-permute-start(f32[4,32,128]{2,1,0:T(8,128)S(1)} %pad_maximum_fusion.level), channel_id=1, source_target_pairs={{0,96},{2,98},{4,100},{6,102},{8,104},{10,106},{12,108},{14,110},{... | collective-permute-start | bytes 196616 | tf_op jit(solution)/shard_map/ppermute | solution.py:657
  65.1 26.9 %copy-start.4 = (f32[4,32,128]{2,1,0:T(8,128)}, f32[4,32,128]{2,1,0:T(8,128)S(1)}, u32[]{:S(2)}) copy-start(f32[4,32,128]{2,1,0:T(8,128)S(1)} %collective-permute-done.10.one) | copy-start | bytes 196612
  68.2 23.8 %copy-start.5 = (f32[4,32,128]{2,1,0:T(8,128)}, f32[4,32,128]{2,1,0:T(8,128)S(1)}, u32[]{:S(2)}) copy-start(f32[4,32,128]{2,1,0:T(8,128)S(1)} %collective-permute-done.9.two) | copy-start | bytes 196612
  68.2 23.8 %copy-start.6 = (f32[4,32,128]{2,1,0:T(8,128)}, f32[4,32,128]{2,1,0:T(8,128)S(1)}, u32[]{:S(2)}) copy-start(f32[4,32,128]{2,1,0:T(8,128)S(1)} %collective-permute-done.8.three) | copy-start | bytes 196612
  68.2 6.2 %copy-start = (f32[67,32,128]{2,1,0:T(8,128)}, f32[67,32,128]{2,1,0:T(8,128)S(1)}, u32[]{:S(2)}) copy-start(f32[67,32,128]{2,1,0:T(8,128)S(1)} %collective-permute-done.11.refs_1_) | copy-start | bytes 3293188
  68.2 23.8 %collective-permute-start.14 = (f32[64,32,128]{2,1,0:T(8,128)}, f32[64,32,128]{2,1,0:T(8,128)}, u32[]{:S(2)}, u32[]{:S(2)}) collective-permute-start(f32[64,32,128]{2,1,0:T(8,128)} %get-tuple-element.59.own), channel_id=1, source_target_pairs={{2,0},{4,2},{6,4},{8,6},{10,8},{12,10},{14,12},{16,14},{18,16},{20... | collective-permute-start | bytes 3145736 | tf_op jit(solution)/shard_map/ppermute | solution.py:696
  72.5 26.9 %collective-permute-start.13 = (f32[64,32,128]{2,1,0:T(8,128)}, f32[64,32,128]{2,1,0:T(8,128)}, u32[]{:S(2)}, u32[]{:S(2)}) collective-permute-start(f32[64,32,128]{2,1,0:T(8,128)} %get-tuple-element.59.own), channel_id=1, source_target_pairs={{0,2},{2,4},{4,6},{6,8},{8,10},{10,12},{12,14},{14,16},{16,18},{18... | collective-permute-start | bytes 3145736 | tf_op jit(solution)/shard_map/ppermute | solution.py:695
  86.6 5.4 %collective-permute-start.12 = (f32[32,4096]{1,0:T(8,128)}, f32[32,4096]{1,0:T(8,128)S(1)}, u32[]{:S(2)}, u32[]{:S(2)}) collective-permute-start(f32[32,4096]{1,0:T(8,128)} %get-tuple-element.58), channel_id=1, source_target_pairs={{0,1},{1,0},{2,3},{3,2},{4,5},{5,4},{6,7},{7,6},{8,9},{9,8},{10,11... | collective-permute-start | bytes 1572872 | tf_op jit(solution)/shard_map/ppermute | solution.py:699
  92.0 7.4 %copy-start.2 = (f32[32,4096]{1,0:T(8,128)}, f32[32,4096]{1,0:T(8,128)S(1)}, u32[]{:S(2)}) copy-start(f32[32,4096]{1,0:T(8,128)S(1)} %collective-permute-done.12.given) | copy-start | bytes 1572868

commit v13 on v12

--- a/solution.py
+++ b/solution.py
@@ -689,16 +689,16 @@
     level = in_order(turned, share[None], spot)
     level = jnp.where(jnp.arange(128) < 64, level[0] + level[1], level[2] + level[3])[None]
     turned, spot = ring(level, 4)
+    turned, passed, up = after((turned, passed, up))
     level = in_order(turned, level, spot)
-    turned, spot = ring(level, 16)
-    turned, passed, up = after((turned, passed, up))
     up_low = lax.ppermute(up, "leaf", forward)
     up_high = lax.ppermute(up, "leaf", backward)
     mine, other = near_pass(12, core, lists, live, points, (beside, passed), begin)
-    mine, other, coupling = after((mine, other, coupling))
+    level, mine, other, coupling = after((level, mine, other, coupling))
+    turned, spot = ring(level, 16)
     given = lax.ppermute(other, "rhs", swap)
     second = unbatch(coupling, 1)
-    given, up_low, up_high, second = after((given, up_low, up_high, second))
+    turned, given, up_low, up_high, second = after((turned, given, up_low, up_high, second))
     return finish(
         core,
         place,

time: 118 us -> 123 us (1.042)
  the two profiles are of different devices: /device:TPU:32 before, /device:TPU:0 now
where the time goes in v13:
time: 123 us; the launch traced here: 122 us
  Pallas kernels  73.2 us (60%)
  starting transfers between devices  30.9 us (25%)
  waiting for transfers between devices  14.1 us (11%)
  local copies, waits for them, and re-layouts  3.08 us (3%)
    pallas_call x2, Pallas kernels, near_pass(): pl.pallas_call(functools.partial(near_body, unroll, chunks), out_shape=(s...  30.8 us
    ppermute x9, starting transfers between devices, ring(): turned.append(lax.ppermute(x, 'leaf', to))  18.9 us
    pallas_call x1, Pallas kernels, finish(): pl.pallas_call(finish_body, out_shape=jax.ShapeDtypeStruct((columns, leav...  17.1 us
    ppermute x9, waiting for transfers between devices, ring(): turned.append(lax.ppermute(x, 'leaf', to))  14.1 us
    pallas_call x1, Pallas kernels, up_pass(): pl.pallas_call(up_body, out_shape=(jax.ShapeDtypeStruct((leaves, columns,...  11.4 us
    pallas_call x2, Pallas kernels, unbatch(): pl.pallas_call(functools.partial(unbatch_body, part), out_shape=jax.Shape...  10.2 us
    ppermute x1, starting transfers between devices, local(): up_low = lax.ppermute(up, 'leaf', forward)  5.63 us
    ppermute x1, starting transfers between devices, local(): beside = lax.ppermute(packed, ('leaf', 'rhs'), outward)  4.91 us
  transfers between devices with their start and end apart: 15, of which 7 were waited for; matrix products, arithmetic and copies ran while one was open for 0% of the time, Pallas kernels for 43%

profile of v13, /device:TPU:0, one launch (start us, length us, event | category | flops | bytes accessed | tf_op | source)
XLA Modules:
  0.0 121.8 jit_solution(4247986447653193992)
XLA Ops:
  0.0 0.0 collective-permute-start
  0.0 5.1 %unbatch.2.first = bf16[127,128,128]{2,1,0:T(8,128)(2,1)} custom-call(f32[4,64,64,127]{3,2,1,0:T(8,128)} %bitcast.12), custom_call_target="tpu_custom_call" | custom-call | flops 1000 | bytes 1000 | tf_op jit(solution)/shard_map/unbatch/pallas_call | solution.py:280
  5.1 0.0 collective-permute-done.across_hbm
  5.1 0.0 copy-start.1
  5.1 1.0 copy-done.1
  6.1 3.7 %pack.1.refs_0_ = f32[2,67,32,128]{3,2,1,0:T(8,128)} custom-call(f32[3,8192]{1,0:T(4,128)} %targets.3, f32[32,8192]{1,0:T(8,128)} %values_hbm.3, f32[32,8192]{1,0:T(8,128)} %copy-done.1), custom_call_target="tpu_custom_call" | custom-call | tf_op jit(solution)/shard_map/pack/pallas_call | solution.py:262
  9.8 4.9 %collective-permute-start.1 = (f32[2,67,32,128]{3,2,1,0:T(8,128)}, f32[2,67,32,128]{3,2,1,0:T(8,128)}, u32[]{:S(2)}, u32[]{:S(2)}) collective-permute-start(f32[2,67,32,128]{3,2,1,0:T(8,128)} %pack.1.refs_0_), channel_id=1, source_target_pairs={{0,2},{2,4},{4,6},{6,8},{8,10},{10,12},{12,14},{14,16},{16,18},{18... | collective-permute-start | bytes 6586376 | tf_op jit(solution)/shard_map/ppermute | solution.py:679
  14.7 11.4 %up_pass.1 = (f32[64,32,128]{2,1,0:T(8,128)}, f32[32,128]{1,0:T(8,128)}, bf16[128,64,128]{2,1,0:T(8,128)(2,1)}, s32[2,28,64]{2,1,0:T(8,128)}, s32[2,64]{1,0:T(2,128)}, /*index=5*/s32[4,127]{1,0:T(4,128)}) custom-call(s32[1]{0:T(128)} %bitcast.1.place, s32[27,64]{1,0:T(8,128)} %bitcast.15, s32[1,64]{1,0:T(1,128)} %bitcast.21, s32[4,127]{1,0:T(4,128)} %bitcast.19, ...), custom_call_target="tpu_custom_call" | custom-call | flops 400000000 | bytes 8000000 | tf_op jit(solution)/shard_map/up_pass/pallas_call | solution.py:159
  26.1 0.0 copy-start.7
  26.1 18.7 %near_pass.2 = (f32[32,4096]{1,0:T(8,128)}, f32[32,4096]{1,0:T(8,128)}) custom-call(s32[1]{0:T(128)} %bitcast.core, s32[2,28,64]{2,1,0:T(8,128)} %get-tuple-element.44.lists, s32[2,64]{1,0:T(2,128)} %get-tuple-element.45.live, f32[3,8192]{1,0:T(4,128)} %targets.3, f32[2,67,32,128]{3,2,1,0:T(8,128)} %pack.1.refs_0_), custom_call_target="tpu_custom_call" | custom-call | flops 1000 | bytes 1000 | tf_op jit(solution)/shard_map/near_pass/pallas_call | solution.py:611
  44.8 0.0 collective-permute-done.1.refs_0_
  44.8 1.3 %dynamic-slice_bitcast_fusion = f32[67,32,128]{2,1,0:T(8,128)S(1)} fusion(f32[2,67,32,128]{3,2,1,0:T(8,128)} %collective-permute-done.1.refs_0_, s32[]{:T(128)S(6)} %select_n.160), kind=kLoop, calls=%fused_computation | loop fusion | bytes 2195460 | tf_op jit(solution)/shard_map/jit(dynamic_index_in_dim)/squeeze | solution.py:687
  46.1 0.1 collective-permute-start.8
  46.2 0.0 copy-done.7
  46.2 0.1 collective-permute-start.4
  46.3 0.1 collective-permute-start.3
  46.4 1.9 %collective-permute-start.2 = (f32[1,32,128]{2,1,0:T(8,128)S(1)}, f32[1,32,128]{2,1,0:T(8,128)S(1)}, u32[]{:S(2)}, u32[]{:S(2)}) collective-permute-start(f32[1,32,128]{2,1,0:T(8,128)S(1)} %bitcast.18), channel_id=1, source_target_pairs={{0,2},{2,4},{4,6},{6,0},{8,10},{10,12},{12,14},{14,8},{16,18},{18,... | collective-permute-start | bytes 49160 | tf_op jit(solution)/shard_map/ppermute | solution.py:657
  48.3 1.7 %collective-permute-done.4 = f32[1,32,128]{2,1,0:T(8,128)S(1)} collective-permute-done((f32[1,32,128]{2,1,0:T(8,128)S(1)}, f32[1,32,128]{2,1,0:T(8,128)S(1)}, u32[]{:S(2)}, u32[]{:S(2)}) %collective-permute-start.4) | collective-permute-done | bytes 16416 | tf_op jit(solution)/shard_map/ppermute | solution.py:657
  50.0 1.6 %collective-permute-done.3 = f32[1,32,128]{2,1,0:T(8,128)S(1)} collective-permute-done((f32[1,32,128]{2,1,0:T(8,128)S(1)}, f32[1,32,128]{2,1,0:T(8,128)S(1)}, u32[]{:S(2)}, u32[]{:S(2)}) %collective-permute-start.3) | collective-permute-done | bytes 16416 | tf_op jit(solution)/shard_map/ppermute | solution.py:657
  51.6 1.1 collective-permute-done.2
  52.7 0.1 collective-permute-start.7
  52.8 3.9 %collective-permute-start.6 = (f32[1,32,128]{2,1,0:T(8,128)S(1)}, f32[1,32,128]{2,1,0:T(8,128)S(1)}, u32[]{:S(2)}, u32[]{:S(2)}) collective-permute-start(f32[1,32,128]{2,1,0:T(8,128)S(1)} %add_select_fusion), channel_id=1, source_target_pairs={{0,16},{2,18},{4,20},{6,22},{8,24},{10,26},{12,28},{14,30},{16,0},... | collective-permute-start | bytes 49160 | tf_op jit(solution)/shard_map/ppermute | solution.py:657
  56.7 0.0 collective-permute-start.5
  56.7 1.0 collective-permute-done.7
  57.8 0.8 collective-permute-done.6
  58.6 1.9 %collective-permute-done.5 = f32[1,32,128]{2,1,0:T(8,128)S(1)} collective-permute-done((f32[1,32,128]{2,1,0:T(8,128)S(1)}, f32[1,32,128]{2,1,0:T(8,128)S(1)}, u32[]{:S(2)}, u32[]{:S(2)}) %collective-permute-start.5) | collective-permute-done | bytes 16416 | tf_op jit(solution)/shard_map/ppermute | solution.py:657
  60.5 0.0 collective-permute-done.8.refs_1_
  60.5 1.3 %collective-permute-start.14 = (f32[64,32,128]{2,1,0:T(8,128)}, f32[64,32,128]{2,1,0:T(8,128)}, u32[]{:S(2)}, u32[]{:S(2)}) collective-permute-start(f32[64,32,128]{2,1,0:T(8,128)} %get-tuple-element.63.own), channel_id=1, source_target_pairs={{2,0},{4,2},{6,4},{8,6},{10,8},{12,10},{14,12},{16,14},{18,16},{20... | collective-permute-start | bytes 3145736 | tf_op jit(solution)/shard_map/ppermute | solution.py:695
  61.8 5.6 %collective-permute-start.13 = (f32[64,32,128]{2,1,0:T(8,128)}, f32[64,32,128]{2,1,0:T(8,128)}, u32[]{:S(2)}, u32[]{:S(2)}) collective-permute-start(f32[64,32,128]{2,1,0:T(8,128)} %get-tuple-element.63.own), channel_id=1, source_target_pairs={{0,2},{2,4},{4,6},{6,8},{8,10},{10,12},{12,14},{14,16},{16,18},{18... | collective-permute-start | bytes 3145736 | tf_op jit(solution)/shard_map/ppermute | solution.py:694
  67.4 0.0 copy-done
  67.4 12.1 %near_pass.3 = (f32[32,4096]{1,0:T(8,128)}, f32[32,4096]{1,0:T(8,128)}) custom-call(s32[1]{0:T(128)} %bitcast.core, s32[2,28,64]{2,1,0:T(8,128)} %get-tuple-element.44.lists, s32[2,64]{1,0:T(2,128)} %get-tuple-element.45.live, f32[3,8192]{1,0:T(4,128)} %targets.3, f32[2,67,32,128]{3,2,1,0:T(8,128)} %collective-permute-done.1.refs_0_, ...), custom_call_target="tpu_custom_call" | custom-call | flops 1000 | bytes 1000 | tf_op jit(solution)/shard_map/near_pass/pallas_call | solution.py:611
  79.5 0.2 collective-permute-start.12
  79.7 0.0 collective-permute-start.11
  79.7 7.8 %collective-permute-start.10 = (f32[4,32,128]{2,1,0:T(8,128)S(1)}, f32[4,32,128]{2,1,0:T(8,128)S(1)}, u32[]{:S(2)}, u32[]{:S(2)}) collective-permute-start(f32[4,32,128]{2,1,0:T(8,128)S(1)} %pad_maximum_fusion.level), channel_id=1, source_target_pairs={{0,64},{2,66},{4,68},{6,70},{8,72},{10,74},{12,76},{14,78},{16,80}... | collective-permute-start | bytes 196616 | tf_op jit(solution)/shard_map/ppermute | solution.py:657
  87.5 6.0 %collective-permute-done.11.one = f32[4,32,128]{2,1,0:T(8,128)S(1)} collective-permute-done((f32[4,32,128]{2,1,0:T(8,128)S(1)}, f32[4,32,128]{2,1,0:T(8,128)S(1)}, u32[]{:S(2)}, u32[]{:S(2)}) %collective-permute-start.11) | collective-permute-done | bytes 65568 | tf_op jit(solution)/shard_map/ppermute | solution.py:657
  93.5 5.0 %collective-permute-start.9 = (f32[4,32,128]{2,1,0:T(8,128)S(1)}, f32[4,32,128]{2,1,0:T(8,128)S(1)}, u32[]{:S(2)}, u32[]{:S(2)}) collective-permute-start(f32[4,32,128]{2,1,0:T(8,128)S(1)} %pad_maximum_fusion.level), channel_id=1, source_target_pairs={{0,96},{2,98},{4,100},{6,102},{8,104},{10,106},{12,108},{14,110},{... | collective-permute-start | bytes 196616 | tf_op jit(solution)/shard_map/ppermute | solution.py:657
  98.5 5.2 %unbatch.3.second = bf16[127,128,128]{2,1,0:T(8,128)(2,1)} custom-call(f32[4,64,64,127]{3,2,1,0:T(8,128)} %bitcast.13), custom_call_target="tpu_custom_call" | custom-call | flops 1000 | bytes 1000 | tf_op jit(solution)/shard_map/unbatch/pallas_call | solution.py:280
  103.7 0.0 copy-done.3
  103.7 0.0 copy-done.4
  103.7 0.0 collective-permute-done.10.two
  103.7 0.0 collective-permute-done.9.three
  103.7 0.0 collective-permute-done.12.given
  103.8 0.0 collective-permute-done.14.high
  103.8 0.0 collective-permute-done.13.low
  103.8 0.5 copy-done.5
  104.3 0.0 copy-done.6
  104.4 0.2 copy-done.2
  104.6 17.1 %finish.1 = f32[32,8192]{1,0:T(8,128)} custom-call(s32[1]{0:T(128)} %bitcast.core, s32[1]{0:T(128)} %bitcast.1.place, s32[4,127]{1,0:T(4,128)} %get-tuple-element.42.codes, s32[4,60]{1,0:T(4,128)} %bitcast.20, f32[4,32,128]{2,1,0:T(8,128)} %copy-done.6, f32[4,32,128]{2,1,0:T(8,128)} %copy-done.5, f32[4,32,128]{2,1,0:T(8,128)} %copy-done.4, ...), custom_call_target="tpu_custom_call" | custom-call | flops 1000000000 | bytes 20000000 | tf_op jit(solution)/shard_map/finish/pallas_call | solution.py:475
  (10 shorter events, 0.1 us)
Async XLA Ops:
  0.0 5.1 %collective-permute-start = (f32[32,8192]{1,0:T(8,128)}, f32[32,8192]{1,0:T(8,128)S(1)}, u32[]{:S(2)}, u32[]{:S(2)}) collective-permute-start(f32[32,8192]{1,0:T(8,128)} %values_hbm.3), channel_id=1, source_target_pairs={{0,1},{1,0},{2,3},{3,2},{4,5},{5,4},{6,7},{7,6},{8,9},{9,8},{10,11... | collective-permute-start | bytes 3145736 | tf_op jit(solution)/shard_map/ppermute | solution.py:650
  5.1 1.0 copy-start.1
  9.8 35.0 %collective-permute-start.1 = (f32[2,67,32,128]{3,2,1,0:T(8,128)}, f32[2,67,32,128]{3,2,1,0:T(8,128)}, u32[]{:S(2)}, u32[]{:S(2)}) collective-permute-start(f32[2,67,32,128]{3,2,1,0:T(8,128)} %pack.1.refs_0_), channel_id=1, source_target_pairs={{0,2},{2,4},{4,6},{6,8},{8,10},{10,12},{12,14},{14,16},{16,18},{18... | collective-permute-start | bytes 6586376 | tf_op jit(solution)/shard_map/ppermute | solution.py:679
  26.1 20.1 %copy-start.7 = (f32[32,128]{1,0:T(8,128)S(1)}, f32[32,128]{1,0:T(8,128)}, u32[]{:S(2)}) copy-start(f32[32,128]{1,0:T(8,128)} %get-tuple-element.49) | copy-start | bytes 49156
  46.1 14.3 %collective-permute-start.8 = (f32[67,32,128]{2,1,0:T(8,128)S(1)}, f32[67,32,128]{2,1,0:T(8,128)S(1)}, u32[]{:S(2)}, u32[]{:S(2)}) collective-permute-start(f32[67,32,128]{2,1,0:T(8,128)S(1)} %dynamic-slice_bitcast_fusion), channel_id=1, source_target_pairs={{0,1},{1,0},{2,3},{3,2},{4,5},{5,4},{6,7},{7,6},{8,9},{9,8},{10,11... | collective-permute-start | bytes 3293192 | tf_op jit(solution)/shard_map/ppermute | solution.py:688
  46.2 3.8 %collective-permute-start.4 = (f32[1,32,128]{2,1,0:T(8,128)S(1)}, f32[1,32,128]{2,1,0:T(8,128)S(1)}, u32[]{:S(2)}, u32[]{:S(2)}) collective-permute-start(f32[1,32,128]{2,1,0:T(8,128)S(1)} %bitcast.16), channel_id=1, source_target_pairs={{0,6},{2,0},{4,2},{6,4},{8,14},{10,8},{12,10},{14,12},{16,22},{18,... | collective-permute-start | bytes 49160 | tf_op jit(solution)/shard_map/ppermute | solution.py:657
  46.3 5.3 %collective-permute-start.3 = (f32[1,32,128]{2,1,0:T(8,128)S(1)}, f32[1,32,128]{2,1,0:T(8,128)S(1)}, u32[]{:S(2)}, u32[]{:S(2)}) collective-permute-start(f32[1,32,128]{2,1,0:T(8,128)S(1)} %bitcast.17), channel_id=1, source_target_pairs={{0,4},{2,6},{4,0},{6,2},{8,12},{10,14},{12,8},{14,10},{16,20},{18,... | collective-permute-start | bytes 49160 | tf_op jit(solution)/shard_map/ppermute | solution.py:657
  46.4 6.3 %collective-permute-start.2 = (f32[1,32,128]{2,1,0:T(8,128)S(1)}, f32[1,32,128]{2,1,0:T(8,128)S(1)}, u32[]{:S(2)}, u32[]{:S(2)}) collective-permute-start(f32[1,32,128]{2,1,0:T(8,128)S(1)} %bitcast.18), channel_id=1, source_target_pairs={{0,2},{2,4},{4,6},{6,0},{8,10},{10,12},{12,14},{14,8},{16,18},{18,... | collective-permute-start | bytes 49160 | tf_op jit(solution)/shard_map/ppermute | solution.py:657
  52.7 5.0 %collective-permute-start.7 = (f32[1,32,128]{2,1,0:T(8,128)S(1)}, f32[1,32,128]{2,1,0:T(8,128)S(1)}, u32[]{:S(2)}, u32[]{:S(2)}) collective-permute-start(f32[1,32,128]{2,1,0:T(8,128)S(1)} %add_select_fusion), channel_id=1, source_target_pairs={{0,8},{2,10},{4,12},{6,14},{8,16},{10,18},{12,20},{14,22},{16,24},... | collective-permute-start | bytes 49160 | tf_op jit(solution)/shard_map/ppermute | solution.py:657
  52.8 5.8 %collective-permute-start.6 = (f32[1,32,128]{2,1,0:T(8,128)S(1)}, f32[1,32,128]{2,1,0:T(8,128)S(1)}, u32[]{:S(2)}, u32[]{:S(2)}) collective-permute-start(f32[1,32,128]{2,1,0:T(8,128)S(1)} %add_select_fusion), channel_id=1, source_target_pairs={{0,16},{2,18},{4,20},{6,22},{8,24},{10,26},{12,28},{14,30},{16,0},... | collective-permute-start | bytes 49160 | tf_op jit(solution)/shard_map/ppermute | solution.py:657
  56.7 3.7 %collective-permute-start.5 = (f32[1,32,128]{2,1,0:T(8,128)S(1)}, f32[1,32,128]{2,1,0:T(8,128)S(1)}, u32[]{:S(2)}, u32[]{:S(2)}) collective-permute-start(f32[1,32,128]{2,1,0:T(8,128)S(1)} %add_select_fusion), channel_id=1, source_target_pairs={{0,24},{2,26},{4,28},{6,30},{8,0},{10,2},{12,4},{14,6},{16,8},{18,... | collective-permute-start | bytes 49160 | tf_op jit(solution)/shard_map/ppermute | solution.py:657
  60.5 6.9 %copy-start = (f32[67,32,128]{2,1,0:T(8,128)}, f32[67,32,128]{2,1,0:T(8,128)S(1)}, u32[]{:S(2)}) copy-start(f32[67,32,128]{2,1,0:T(8,128)S(1)} %collective-permute-done.8.refs_1_) | copy-start | bytes 3293188
  60.5 43.3 %collective-permute-start.14 = (f32[64,32,128]{2,1,0:T(8,128)}, f32[64,32,128]{2,1,0:T(8,128)}, u32[]{:S(2)}, u32[]{:S(2)}) collective-permute-start(f32[64,32,128]{2,1,0:T(8,128)} %get-tuple-element.63.own), channel_id=1, source_target_pairs={{2,0},{4,2},{6,4},{8,6},{10,8},{12,10},{14,12},{16,14},{18,16},{20... | collective-permute-start | bytes 3145736 | tf_op jit(solution)/shard_map/ppermute | solution.py:695
  61.8 42.0 %collective-permute-start.13 = (f32[64,32,128]{2,1,0:T(8,128)}, f32[64,32,128]{2,1,0:T(8,128)}, u32[]{:S(2)}, u32[]{:S(2)}) collective-permute-start(f32[64,32,128]{2,1,0:T(8,128)} %get-tuple-element.63.own), channel_id=1, source_target_pairs={{0,2},{2,4},{4,6},{6,8},{8,10},{10,12},{12,14},{14,16},{16,18},{18... | collective-permute-start | bytes 3145736 | tf_op jit(solution)/shard_map/ppermute | solution.py:694
  79.5 24.2 %copy-start.3 = (f32[4,32,128]{2,1,0:T(8,128)}, f32[4,32,128]{2,1,0:T(8,128)S(1)}, u32[]{:S(2)}) copy-start(f32[4,32,128]{2,1,0:T(8,128)S(1)} %pad_maximum_fusion.level) | copy-start | bytes 196612
  79.5 24.2 %collective-permute-start.12 = (f32[32,4096]{1,0:T(8,128)}, f32[32,4096]{1,0:T(8,128)S(1)}, u32[]{:S(2)}, u32[]{:S(2)}) collective-permute-start(f32[32,4096]{1,0:T(8,128)} %get-tuple-element.62), channel_id=1, source_target_pairs={{0,1},{1,0},{2,3},{3,2},{4,5},{5,4},{6,7},{7,6},{8,9},{9,8},{10,11... | collective-permute-start | bytes 1572872 | tf_op jit(solution)/shard_map/ppermute | solution.py:699
  79.7 13.8 %collective-permute-start.11 = (f32[4,32,128]{2,1,0:T(8,128)S(1)}, f32[4,32,128]{2,1,0:T(8,128)S(1)}, u32[]{:S(2)}, u32[]{:S(2)}) collective-permute-start(f32[4,32,128]{2,1,0:T(8,128)S(1)} %pad_maximum_fusion.level), channel_id=1, source_target_pairs={{0,32},{2,34},{4,36},{6,38},{8,40},{10,42},{12,44},{14,46},{16,48}... | collective-permute-start | bytes 196616 | tf_op jit(solution)/shard_map/ppermute | solution.py:657
  79.7 24.0 %collective-permute-start.10 = (f32[4,32,128]{2,1,0:T(8,128)S(1)}, f32[4,32,128]{2,1,0:T(8,128)S(1)}, u32[]{:S(2)}, u32[]{:S(2)}) collective-permute-start(f32[4,32,128]{2,1,0:T(8,128)S(1)} %pad_maximum_fusion.level), channel_id=1, source_target_pairs={{0,64},{2,66},{4,68},{6,70},{8,72},{10,74},{12,76},{14,78},{16,80}... | collective-permute-start | bytes 196616 | tf_op jit(solution)/shard_map/ppermute | solution.py:657
  93.5 10.2 %copy-start.4 = (f32[4,32,128]{2,1,0:T(8,128)}, f32[4,32,128]{2,1,0:T(8,128)S(1)}, u32[]{:S(2)}) copy-start(f32[4,32,128]{2,1,0:T(8,128)S(1)} %collective-permute-done.11.one) | copy-start | bytes 196612
  93.5 10.2 %collective-permute-start.9 = (f32[4,32,128]{2,1,0:T(8,128)S(1)}, f32[4,32,128]{2,1,0:T(8,128)S(1)}, u32[]{:S(2)}, u32[]{:S(2)}) collective-permute-start(f32[4,32,128]{2,1,0:T(8,128)S(1)} %pad_maximum_fusion.level), channel_id=1, source_target_pairs={{0,96},{2,98},{4,100},{6,102},{8,104},{10,106},{12,108},{14,110},{... | collective-permute-start | bytes 196616 | tf_op jit(solution)/shard_map/ppermute | solution.py:657
  103.7 0.6 copy-start.5
  103.7 0.6 copy-start.6
  103.8 0.8 copy-start.2

commit v14 on v12

--- a/solution.py
+++ b/solution.py
@@ -689,16 +689,16 @@
     level = in_order(turned, share[None], spot)
     level = jnp.where(jnp.arange(128) < 64, level[0] + level[1], level[2] + level[3])[None]
     turned, spot = ring(level, 4)
+    turned, passed, up = after((turned, passed, up))
     level = in_order(turned, level, spot)
     turned, spot = ring(level, 16)
-    turned, passed, up = after((turned, passed, up))
     up_low = lax.ppermute(up, "leaf", forward)
     up_high = lax.ppermute(up, "leaf", backward)
     mine, other = near_pass(12, core, lists, live, points, (beside, passed), begin)
     mine, other, coupling = after((mine, other, coupling))
+    second = unbatch(coupling, 1)
+    turned, other, second = after((turned, other, second))
     given = lax.ppermute(other, "rhs", swap)
-    second = unbatch(coupling, 1)
-    given, up_low, up_high, second = after((given, up_low, up_high, second))
     return finish(
         core,
         place,

time: 118 us -> 119 us (level)
  the two profiles are of different devices: /device:TPU:32 before, /device:TPU:0 now
where the time goes in v14:
time: 119 us; the launch traced here: 117 us
  Pallas kernels  63.3 us (53%)
  starting transfers between devices  30.3 us (25%)
  waiting for transfers between devices  20.2 us (17%)
  local copies, waits for them, and re-layouts  3.08 us (3%)
    pallas_call x2, Pallas kernels, near_pass(): pl.pallas_call(functools.partial(near_body, unroll, chunks), out_shape=(s...  20.7 us
    ppermute x9, starting transfers between devices, ring(): turned.append(lax.ppermute(x, 'leaf', to))  18.1 us
    ppermute x9, waiting for transfers between devices, ring(): turned.append(lax.ppermute(x, 'leaf', to))  17.2 us
    pallas_call x1, Pallas kernels, finish(): pl.pallas_call(finish_body, out_shape=jax.ShapeDtypeStruct((columns, leav...  17.1 us
    pallas_call x1, Pallas kernels, up_pass(): pl.pallas_call(up_body, out_shape=(jax.ShapeDtypeStruct((leaves, columns,...  11.4 us
    pallas_call x2, Pallas kernels, unbatch(): pl.pallas_call(functools.partial(unbatch_body, part), out_shape=jax.Shape...  10.3 us
    ppermute x1, starting transfers between devices, local(): up_low = lax.ppermute(up, 'leaf', forward)  5.64 us
    ppermute x1, starting transfers between devices, local(): beside = lax.ppermute(packed, ('leaf', 'rhs'), outward)  4.94 us
  transfers between devices with their start and end apart: 15, of which 9 were waited for; matrix products, arithmetic and copies ran while one was open for 0% of the time, Pallas kernels for 36%

profile of v14, /device:TPU:0, one launch (start us, length us, event | category | flops | bytes accessed | tf_op | source)
XLA Modules:
  0.0 117.2 jit_solution(11342579361142544371)
XLA Ops:
  0.0 0.0 collective-permute-start
  0.0 5.1 %unbatch.2.first = bf16[127,128,128]{2,1,0:T(8,128)(2,1)} custom-call(f32[4,64,64,127]{3,2,1,0:T(8,128)} %bitcast.12), custom_call_target="tpu_custom_call" | custom-call | flops 1000 | bytes 1000 | tf_op jit(solution)/shard_map/unbatch/pallas_call | solution.py:280
  5.1 0.0 collective-permute-done.across_hbm
  5.1 0.0 copy-start.1
  5.1 1.0 copy-done.1
  6.0 3.7 %pack.1.refs_0_ = f32[2,67,32,128]{3,2,1,0:T(8,128)} custom-call(f32[3,8192]{1,0:T(4,128)} %targets.3, f32[32,8192]{1,0:T(8,128)} %values_hbm.3, f32[32,8192]{1,0:T(8,128)} %copy-done.1), custom_call_target="tpu_custom_call" | custom-call | tf_op jit(solution)/shard_map/pack/pallas_call | solution.py:262
  9.8 4.9 %collective-permute-start.1 = (f32[2,67,32,128]{3,2,1,0:T(8,128)}, f32[2,67,32,128]{3,2,1,0:T(8,128)}, u32[]{:S(2)}, u32[]{:S(2)}) collective-permute-start(f32[2,67,32,128]{3,2,1,0:T(8,128)} %pack.1.refs_0_), channel_id=1, source_target_pairs={{0,2},{2,4},{4,6},{6,8},{8,10},{10,12},{12,14},{14,16},{16,18},{18... | collective-permute-start | bytes 6586376 | tf_op jit(solution)/shard_map/ppermute | solution.py:679
  14.7 11.4 %up_pass.1 = (f32[64,32,128]{2,1,0:T(8,128)}, f32[32,128]{1,0:T(8,128)}, bf16[128,64,128]{2,1,0:T(8,128)(2,1)}, s32[2,28,64]{2,1,0:T(8,128)}, s32[2,64]{1,0:T(2,128)}, /*index=5*/s32[4,127]{1,0:T(4,128)}) custom-call(s32[1]{0:T(128)} %bitcast.1.place, s32[27,64]{1,0:T(8,128)} %bitcast.15, s32[1,64]{1,0:T(1,128)} %bitcast.21, s32[4,127]{1,0:T(4,128)} %bitcast.19, ...), custom_call_target="tpu_custom_call" | custom-call | flops 400000000 | bytes 8000000 | tf_op jit(solution)/shard_map/up_pass/pallas_call | solution.py:159
  26.1 0.0 copy-start.7
  26.1 11.0 %near_pass.2 = (f32[32,4096]{1,0:T(8,128)}, f32[32,4096]{1,0:T(8,128)}) custom-call(s32[1]{0:T(128)} %bitcast.core, s32[2,28,64]{2,1,0:T(8,128)} %get-tuple-element.41.lists, s32[2,64]{1,0:T(2,128)} %get-tuple-element.42.live, f32[3,8192]{1,0:T(4,128)} %targets.3, f32[2,67,32,128]{3,2,1,0:T(8,128)} %pack.1.refs_0_), custom_call_target="tpu_custom_call" | custom-call | flops 1000 | bytes 1000 | tf_op jit(solution)/shard_map/near_pass/pallas_call | solution.py:611
  37.2 1.1 collective-permute-done.1.refs_0_
  38.3 1.3 %dynamic-slice_bitcast_fusion = f32[67,32,128]{2,1,0:T(8,128)S(1)} fusion(f32[2,67,32,128]{3,2,1,0:T(8,128)} %collective-permute-done.1.refs_0_, s32[]{:T(128)S(6)} %select_n.160), kind=kLoop, calls=%fused_computation | loop fusion | bytes 2195460 | tf_op jit(solution)/shard_map/jit(dynamic_index_in_dim)/squeeze | solution.py:687
  39.6 0.3 collective-permute-start.8
  39.8 0.0 copy-done.7
  39.9 5.2 %collective-permute-start.4 = (f32[1,32,128]{2,1,0:T(8,128)S(1)}, f32[1,32,128]{2,1,0:T(8,128)S(1)}, u32[]{:S(2)}, u32[]{:S(2)}) collective-permute-start(f32[1,32,128]{2,1,0:T(8,128)S(1)} %bitcast.16), channel_id=1, source_target_pairs={{0,6},{2,0},{4,2},{6,4},{8,14},{10,8},{12,10},{14,12},{16,22},{18,... | collective-permute-start | bytes 49160 | tf_op jit(solution)/shard_map/ppermute | solution.py:657
  45.1 0.0 collective-permute-start.3
  45.1 0.9 collective-permute-start.2
  45.9 0.6 collective-permute-done.4
  46.5 3.8 %collective-permute-done.3 = f32[1,32,128]{2,1,0:T(8,128)S(1)} collective-permute-done((f32[1,32,128]{2,1,0:T(8,128)S(1)}, f32[1,32,128]{2,1,0:T(8,128)S(1)}, u32[]{:S(2)}, u32[]{:S(2)}) %collective-permute-start.3) | collective-permute-done | bytes 16416 | tf_op jit(solution)/shard_map/ppermute | solution.py:657
  50.3 0.0 collective-permute-done.2
  50.3 1.7 %collective-permute-start.7 = (f32[1,32,128]{2,1,0:T(8,128)S(1)}, f32[1,32,128]{2,1,0:T(8,128)S(1)}, u32[]{:S(2)}, u32[]{:S(2)}) collective-permute-start(f32[1,32,128]{2,1,0:T(8,128)S(1)} %add_select_fusion), channel_id=1, source_target_pairs={{0,8},{2,10},{4,12},{6,14},{8,16},{10,18},{12,20},{14,22},{16,24},... | collective-permute-start | bytes 49160 | tf_op jit(solution)/shard_map/ppermute | solution.py:657
  52.1 4.7 %collective-permute-start.6 = (f32[1,32,128]{2,1,0:T(8,128)S(1)}, f32[1,32,128]{2,1,0:T(8,128)S(1)}, u32[]{:S(2)}, u32[]{:S(2)}) collective-permute-start(f32[1,32,128]{2,1,0:T(8,128)S(1)} %add_select_fusion), channel_id=1, source_target_pairs={{0,16},{2,18},{4,20},{6,22},{8,24},{10,26},{12,28},{14,30},{16,0},... | collective-permute-start | bytes 49160 | tf_op jit(solution)/shard_map/ppermute | solution.py:657
  56.7 0.1 collective-permute-start.5
  56.8 0.2 collective-permute-done.7
  57.0 1.6 %collective-permute-done.6 = f32[1,32,128]{2,1,0:T(8,128)S(1)} collective-permute-done((f32[1,32,128]{2,1,0:T(8,128)S(1)}, f32[1,32,128]{2,1,0:T(8,128)S(1)}, u32[]{:S(2)}, u32[]{:S(2)}) %collective-permute-start.6) | collective-permute-done | bytes 16416 | tf_op jit(solution)/shard_map/ppermute | solution.py:657
  58.6 1.9 %collective-permute-done.5 = f32[1,32,128]{2,1,0:T(8,128)S(1)} collective-permute-done((f32[1,32,128]{2,1,0:T(8,128)S(1)}, f32[1,32,128]{2,1,0:T(8,128)S(1)}, u32[]{:S(2)}, u32[]{:S(2)}) %collective-permute-start.5) | collective-permute-done | bytes 16416 | tf_op jit(solution)/shard_map/ppermute | solution.py:657
  60.5 0.0 collective-permute-done.8.refs_1_
  60.5 1.3 %collective-permute-start.14 = (f32[64,32,128]{2,1,0:T(8,128)}, f32[64,32,128]{2,1,0:T(8,128)}, u32[]{:S(2)}, u32[]{:S(2)}) collective-permute-start(f32[64,32,128]{2,1,0:T(8,128)} %get-tuple-element.65.own), channel_id=1, source_target_pairs={{2,0},{4,2},{6,4},{8,6},{10,8},{12,10},{14,12},{16,14},{18,16},{20... | collective-permute-start | bytes 3145736 | tf_op jit(solution)/shard_map/ppermute | solution.py:696
  61.8 5.6 %collective-permute-start.13 = (f32[64,32,128]{2,1,0:T(8,128)}, f32[64,32,128]{2,1,0:T(8,128)}, u32[]{:S(2)}, u32[]{:S(2)}) collective-permute-start(f32[64,32,128]{2,1,0:T(8,128)} %get-tuple-element.65.own), channel_id=1, source_target_pairs={{0,2},{2,4},{4,6},{6,8},{8,10},{10,12},{12,14},{14,16},{16,18},{18... | collective-permute-start | bytes 3145736 | tf_op jit(solution)/shard_map/ppermute | solution.py:695
  67.4 0.0 copy-start.3
  67.4 0.9 collective-permute-start.11
  68.4 3.4 %collective-permute-start.10 = (f32[4,32,128]{2,1,0:T(8,128)S(1)}, f32[4,32,128]{2,1,0:T(8,128)S(1)}, u32[]{:S(2)}, u32[]{:S(2)}) collective-permute-start(f32[4,32,128]{2,1,0:T(8,128)S(1)} %pad_maximum_fusion.level), channel_id=1, source_target_pairs={{0,64},{2,66},{4,68},{6,70},{8,72},{10,74},{12,76},{14,78},{16,80}... | collective-permute-start | bytes 196616 | tf_op jit(solution)/shard_map/ppermute | solution.py:657
  71.8 1.2 %collective-permute-start.9 = (f32[4,32,128]{2,1,0:T(8,128)S(1)}, f32[4,32,128]{2,1,0:T(8,128)S(1)}, u32[]{:S(2)}, u32[]{:S(2)}) collective-permute-start(f32[4,32,128]{2,1,0:T(8,128)S(1)} %pad_maximum_fusion.level), channel_id=1, source_target_pairs={{0,96},{2,98},{4,100},{6,102},{8,104},{10,106},{12,108},{14,110},{... | collective-permute-start | bytes 196616 | tf_op jit(solution)/shard_map/ppermute | solution.py:657
  73.0 0.0 copy-done
  73.0 9.7 %near_pass.3 = (f32[32,4096]{1,0:T(8,128)}, f32[32,4096]{1,0:T(8,128)}) custom-call(s32[1]{0:T(128)} %bitcast.core, s32[2,28,64]{2,1,0:T(8,128)} %get-tuple-element.41.lists, s32[2,64]{1,0:T(2,128)} %get-tuple-element.42.live, f32[3,8192]{1,0:T(4,128)} %targets.3, f32[2,67,32,128]{3,2,1,0:T(8,128)} %collective-permute-done.1.refs_0_, ...), custom_call_target="tpu_custom_call" | custom-call | flops 1000 | bytes 1000 | tf_op jit(solution)/shard_map/near_pass/pallas_call | solution.py:611
  82.7 0.0 copy-done.3
  82.7 0.0 copy-start.8
  82.7 5.3 %unbatch.3.second = bf16[127,128,128]{2,1,0:T(8,128)(2,1)} custom-call(f32[4,64,64,127]{3,2,1,0:T(8,128)} %bitcast.13), custom_call_target="tpu_custom_call" | custom-call | flops 1000 | bytes 1000 | tf_op jit(solution)/shard_map/unbatch/pallas_call | solution.py:280
  88.0 4.2 %collective-permute-done.11.one = f32[4,32,128]{2,1,0:T(8,128)S(1)} collective-permute-done((f32[4,32,128]{2,1,0:T(8,128)S(1)}, f32[4,32,128]{2,1,0:T(8,128)S(1)}, u32[]{:S(2)}, u32[]{:S(2)}) %collective-permute-start.11) | collective-permute-done | bytes 65568 | tf_op jit(solution)/shard_map/ppermute | solution.py:657
  92.3 4.9 %collective-permute-done.10.two = f32[4,32,128]{2,1,0:T(8,128)S(1)} collective-permute-done((f32[4,32,128]{2,1,0:T(8,128)S(1)}, f32[4,32,128]{2,1,0:T(8,128)S(1)}, u32[]{:S(2)}, u32[]{:S(2)}) %collective-permute-start.10) | collective-permute-done | bytes 65568 | tf_op jit(solution)/shard_map/ppermute | solution.py:657
  97.1 0.0 collective-permute-done.9.three
  97.1 0.0 copy-done.8
  97.1 0.1 collective-permute-start.12
  97.2 1.9 %collective-permute-done.12.given = f32[32,4096]{1,0:T(8,128)S(1)} collective-permute-done((f32[32,4096]{1,0:T(8,128)S(1)}, f32[32,4096]{1,0:T(8,128)S(1)}, u32[]{:S(2)}, u32[]{:S(2)}) %collective-permute-start.12) | collective-permute-done | bytes 524320 | tf_op jit(solution)/shard_map/ppermute | solution.py:701
  99.1 0.0 collective-permute-done.14.high
  99.1 0.0 collective-permute-done.13.low
  99.2 0.8 copy-done.2
  99.9 17.1 %finish.1 = f32[32,8192]{1,0:T(8,128)} custom-call(s32[1]{0:T(128)} %bitcast.core, s32[1]{0:T(128)} %bitcast.1.place, s32[4,127]{1,0:T(4,128)} %get-tuple-element.39.codes, s32[4,60]{1,0:T(4,128)} %bitcast.20, f32[4,32,128]{2,1,0:T(8,128)} %copy-done.6, f32[4,32,128]{2,1,0:T(8,128)} %copy-done.5, f32[4,32,128]{2,1,0:T(8,128)} %copy-done.4, ...), custom_call_target="tpu_custom_call" | custom-call | flops 1000000000 | bytes 20000000 | tf_op jit(solution)/shard_map/finish/pallas_call | solution.py:475
  (12 shorter events, 0.1 us)
Async XLA Ops:
  0.0 5.1 %collective-permute-start = (f32[32,8192]{1,0:T(8,128)}, f32[32,8192]{1,0:T(8,128)S(1)}, u32[]{:S(2)}, u32[]{:S(2)}) collective-permute-start(f32[32,8192]{1,0:T(8,128)} %values_hbm.3), channel_id=1, source_target_pairs={{0,1},{1,0},{2,3},{3,2},{4,5},{5,4},{6,7},{7,6},{8,9},{9,8},{10,11... | collective-permute-start | bytes 3145736 | tf_op jit(solution)/shard_map/ppermute | solution.py:650
  5.1 1.0 copy-start.1
  9.8 28.5 %collective-permute-start.1 = (f32[2,67,32,128]{3,2,1,0:T(8,128)}, f32[2,67,32,128]{3,2,1,0:T(8,128)}, u32[]{:S(2)}, u32[]{:S(2)}) collective-permute-start(f32[2,67,32,128]{3,2,1,0:T(8,128)} %pack.1.refs_0_), channel_id=1, source_target_pairs={{0,2},{2,4},{4,6},{6,8},{8,10},{10,12},{12,14},{14,16},{16,18},{18... | collective-permute-start | bytes 6586376 | tf_op jit(solution)/shard_map/ppermute | solution.py:679
  26.1 13.7 %copy-start.7 = (f32[32,128]{1,0:T(8,128)S(1)}, f32[32,128]{1,0:T(8,128)}, u32[]{:S(2)}) copy-start(f32[32,128]{1,0:T(8,128)} %get-tuple-element.46) | copy-start | bytes 49156
  39.6 20.9 %collective-permute-start.8 = (f32[67,32,128]{2,1,0:T(8,128)S(1)}, f32[67,32,128]{2,1,0:T(8,128)S(1)}, u32[]{:S(2)}, u32[]{:S(2)}) collective-permute-start(f32[67,32,128]{2,1,0:T(8,128)S(1)} %dynamic-slice_bitcast_fusion), channel_id=1, source_target_pairs={{0,1},{1,0},{2,3},{3,2},{4,5},{5,4},{6,7},{7,6},{8,9},{9,8},{10,11... | collective-permute-start | bytes 3293192 | tf_op jit(solution)/shard_map/ppermute | solution.py:688
  39.9 6.7 %collective-permute-start.4 = (f32[1,32,128]{2,1,0:T(8,128)S(1)}, f32[1,32,128]{2,1,0:T(8,128)S(1)}, u32[]{:S(2)}, u32[]{:S(2)}) collective-permute-start(f32[1,32,128]{2,1,0:T(8,128)S(1)} %bitcast.16), channel_id=1, source_target_pairs={{0,6},{2,0},{4,2},{6,4},{8,14},{10,8},{12,10},{14,12},{16,22},{18,... | collective-permute-start | bytes 49160 | tf_op jit(solution)/shard_map/ppermute | solution.py:657
  45.1 5.2 %collective-permute-start.3 = (f32[1,32,128]{2,1,0:T(8,128)S(1)}, f32[1,32,128]{2,1,0:T(8,128)S(1)}, u32[]{:S(2)}, u32[]{:S(2)}) collective-permute-start(f32[1,32,128]{2,1,0:T(8,128)S(1)} %bitcast.17), channel_id=1, source_target_pairs={{0,4},{2,6},{4,0},{6,2},{8,12},{10,14},{12,8},{14,10},{16,20},{18,... | collective-permute-start | bytes 49160 | tf_op jit(solution)/shard_map/ppermute | solution.py:657
  45.1 5.2 %collective-permute-start.2 = (f32[1,32,128]{2,1,0:T(8,128)S(1)}, f32[1,32,128]{2,1,0:T(8,128)S(1)}, u32[]{:S(2)}, u32[]{:S(2)}) collective-permute-start(f32[1,32,128]{2,1,0:T(8,128)S(1)} %bitcast.18), channel_id=1, source_target_pairs={{0,2},{2,4},{4,6},{6,0},{8,10},{10,12},{12,14},{14,8},{16,18},{18,... | collective-permute-start | bytes 49160 | tf_op jit(solution)/shard_map/ppermute | solution.py:657
  50.3 6.7 %collective-permute-start.7 = (f32[1,32,128]{2,1,0:T(8,128)S(1)}, f32[1,32,128]{2,1,0:T(8,128)S(1)}, u32[]{:S(2)}, u32[]{:S(2)}) collective-permute-start(f32[1,32,128]{2,1,0:T(8,128)S(1)} %add_select_fusion), channel_id=1, source_target_pairs={{0,8},{2,10},{4,12},{6,14},{8,16},{10,18},{12,20},{14,22},{16,24},... | collective-permute-start | bytes 49160 | tf_op jit(solution)/shard_map/ppermute | solution.py:657
  52.1 6.6 %collective-permute-start.6 = (f32[1,32,128]{2,1,0:T(8,128)S(1)}, f32[1,32,128]{2,1,0:T(8,128)S(1)}, u32[]{:S(2)}, u32[]{:S(2)}) collective-permute-start(f32[1,32,128]{2,1,0:T(8,128)S(1)} %add_select_fusion), channel_id=1, source_target_pairs={{0,16},{2,18},{4,20},{6,22},{8,24},{10,26},{12,28},{14,30},{16,0},... | collective-permute-start | bytes 49160 | tf_op jit(solution)/shard_map/ppermute | solution.py:657
  56.7 3.7 %collective-permute-start.5 = (f32[1,32,128]{2,1,0:T(8,128)S(1)}, f32[1,32,128]{2,1,0:T(8,128)S(1)}, u32[]{:S(2)}, u32[]{:S(2)}) collective-permute-start(f32[1,32,128]{2,1,0:T(8,128)S(1)} %add_select_fusion), channel_id=1, source_target_pairs={{0,24},{2,26},{4,28},{6,30},{8,0},{10,2},{12,4},{14,6},{16,8},{18,... | collective-permute-start | bytes 49160 | tf_op jit(solution)/shard_map/ppermute | solution.py:657
  60.5 12.5 %copy-start = (f32[67,32,128]{2,1,0:T(8,128)}, f32[67,32,128]{2,1,0:T(8,128)S(1)}, u32[]{:S(2)}) copy-start(f32[67,32,128]{2,1,0:T(8,128)S(1)} %collective-permute-done.8.refs_1_) | copy-start | bytes 3293188
  60.5 38.7 %collective-permute-start.14 = (f32[64,32,128]{2,1,0:T(8,128)}, f32[64,32,128]{2,1,0:T(8,128)}, u32[]{:S(2)}, u32[]{:S(2)}) collective-permute-start(f32[64,32,128]{2,1,0:T(8,128)} %get-tuple-element.65.own), channel_id=1, source_target_pairs={{2,0},{4,2},{6,4},{8,6},{10,8},{12,10},{14,12},{16,14},{18,16},{20... | collective-permute-start | bytes 3145736 | tf_op jit(solution)/shard_map/ppermute | solution.py:696
  61.8 37.4 %collective-permute-start.13 = (f32[64,32,128]{2,1,0:T(8,128)}, f32[64,32,128]{2,1,0:T(8,128)}, u32[]{:S(2)}, u32[]{:S(2)}) collective-permute-start(f32[64,32,128]{2,1,0:T(8,128)} %get-tuple-element.65.own), channel_id=1, source_target_pairs={{0,2},{2,4},{4,6},{6,8},{8,10},{10,12},{12,14},{14,16},{16,18},{18... | collective-permute-start | bytes 3145736 | tf_op jit(solution)/shard_map/ppermute | solution.py:695
  67.4 15.3 %copy-start.3 = (f32[4,32,128]{2,1,0:T(8,128)}, f32[4,32,128]{2,1,0:T(8,128)S(1)}, u32[]{:S(2)}) copy-start(f32[4,32,128]{2,1,0:T(8,128)S(1)} %pad_maximum_fusion.level) | copy-start | bytes 196612
  67.4 24.8 %collective-permute-start.11 = (f32[4,32,128]{2,1,0:T(8,128)S(1)}, f32[4,32,128]{2,1,0:T(8,128)S(1)}, u32[]{:S(2)}, u32[]{:S(2)}) collective-permute-start(f32[4,32,128]{2,1,0:T(8,128)S(1)} %pad_maximum_fusion.level), channel_id=1, source_target_pairs={{0,32},{2,34},{4,36},{6,38},{8,40},{10,42},{12,44},{14,46},{16,48}... | collective-permute-start | bytes 196616 | tf_op jit(solution)/shard_map/ppermute | solution.py:657
  68.4 28.7 %collective-permute-start.10 = (f32[4,32,128]{2,1,0:T(8,128)S(1)}, f32[4,32,128]{2,1,0:T(8,128)S(1)}, u32[]{:S(2)}, u32[]{:S(2)}) collective-permute-start(f32[4,32,128]{2,1,0:T(8,128)S(1)} %pad_maximum_fusion.level), channel_id=1, source_target_pairs={{0,64},{2,66},{4,68},{6,70},{8,72},{10,74},{12,76},{14,78},{16,80}... | collective-permute-start | bytes 196616 | tf_op jit(solution)/shard_map/ppermute | solution.py:657
  71.8 25.3 %collective-permute-start.9 = (f32[4,32,128]{2,1,0:T(8,128)S(1)}, f32[4,32,128]{2,1,0:T(8,128)S(1)}, u32[]{:S(2)}, u32[]{:S(2)}) collective-permute-start(f32[4,32,128]{2,1,0:T(8,128)S(1)} %pad_maximum_fusion.level), channel_id=1, source_target_pairs={{0,96},{2,98},{4,100},{6,102},{8,104},{10,106},{12,108},{14,110},{... | collective-permute-start | bytes 196616 | tf_op jit(solution)/shard_map/ppermute | solution.py:657
  82.7 14.4 %copy-start.8 = (f32[32,4096]{1,0:T(8,128)S(1)}, f32[32,4096]{1,0:T(8,128)}, u32[]{:S(2)}) copy-start(f32[32,4096]{1,0:T(8,128)} %get-tuple-element.64) | copy-start | bytes 1572868
  92.2 6.9 %copy-start.4 = (f32[4,32,128]{2,1,0:T(8,128)}, f32[4,32,128]{2,1,0:T(8,128)S(1)}, u32[]{:S(2)}) copy-start(f32[4,32,128]{2,1,0:T(8,128)S(1)} %collective-permute-done.11.one) | copy-start | bytes 196612
  97.1 2.0 %copy-start.5 = (f32[4,32,128]{2,1,0:T(8,128)}, f32[4,32,128]{2,1,0:T(8,128)S(1)}, u32[]{:S(2)}) copy-start(f32[4,32,128]{2,1,0:T(8,128)S(1)} %collective-permute-done.10.two) | copy-start | bytes 196612
  97.1 2.0 %copy-start.6 = (f32[4,32,128]{2,1,0:T(8,128)}, f32[4,32,128]{2,1,0:T(8,128)S(1)}, u32[]{:S(2)}) copy-start(f32[4,32,128]{2,1,0:T(8,128)S(1)} %collective-permute-done.9.three) | copy-start | bytes 196612
  97.1 2.0 %collective-permute-start.12 = (f32[32,4096]{1,0:T(8,128)S(1)}, f32[32,4096]{1,0:T(8,128)S(1)}, u32[]{:S(2)}, u32[]{:S(2)}) collective-permute-start(f32[32,4096]{1,0:T(8,128)S(1)} %copy-done.8), channel_id=1, source_target_pairs={{0,1},{1,0},{2,3},{3,2},{4,5},{5,4},{6,7},{7,6},{8,9},{9,8},{10,11... | collective-permute-start | bytes 1572872 | tf_op jit(solution)/shard_map/ppermute | solution.py:701
  99.1 0.8 copy-start.2
